TPU v7x, 32 devices: a whole 2x2x4 slice. The times are simulated.
32 devices in a mesh: wide: 8 (over z, y), narrow: 4 (over x, core).
Axes of the slice: x: 2, y: 2, z: 4, core: 2. Of those that a mesh axis runs over, the one named last changes fastest.
Arguments:
- raw_ints: bfloat16 [4, 640, 8, 2, 384], P('narrow', 'wide'), may hold values from -5 to 5
- metric_root: bfloat16 [640, 640], P('wide'), may hold values from -0.25 to 0.25
- occ_energy: float32 [8, 2], replicated, may hold values from -1.6 to -0.4
- vir_energy: float32 [4, 384], replicated, may hold values from 0.3 to 2.5
- block_kpoint: int32 [4, 8], replicated, may hold values from 0 to 7
- occ_count: int32 [4, 8], replicated, may hold values from 1 to 2, as said below
Outputs:
- gamma: bfloat16 [4, 640, 8, 2, 384], P('narrow', None, 'wide')
- virt_density: float32 [147456], P(('wide', 'narrow'))
Inputs may be any that keep to these rules, and one draw needn't show every extreme that they name: `occ_count`: slot o of a block is live when o is less than its count; some block has all 2 slots live.
All inputs are finite; a program needn't handle non-finite values.
Results may differ from a plain program's by a relative error of at most 0.0043.
Values may be sent and summed in bfloat16 or wider, within the bound.
No kernel may reach another device: no remote copies, remote signals or barrier semaphores. Data moves between devices by JAX's collectives and lax.ppermute only.
A program may use at most 64 MiB of HBM per device.

v0:
```python
import jax
import jax.numpy as jnp
from jax import lax
from jax.sharding import PartitionSpec as P

WINDOW = 3


def from_behind(value, axis, steps):
    count = lax.axis_size(axis)
    pairs = [(source, (source + steps) % count) for source in range(count)]
    return lax.ppermute(value, axis, pairs)


def partner(value, axis, bit):
    mask = 2**bit
    pairs = [(source, source ^ mask) for source in range(lax.axis_size(axis))]
    return lax.ppermute(value, axis, pairs)


def shards(raw_ints, metric_root, occ_energy, vir_energy, block_kpoint, occ_count):
    occ_slots = raw_ints.shape[3]
    vir_count = raw_ints.shape[4]
    row_width = occ_slots * vir_count
    wide_count = lax.axis_size("wide")
    group_count = lax.axis_size("narrow")
    my_block = lax.axis_index("wide")
    my_group = lax.axis_index("narrow")
    partner_group = (my_group + group_count // 2) % group_count
    flip_bit = group_count.bit_length() - 2
    regrouped = lax.all_to_all(raw_ints, "wide", split_axis=2, concat_axis=1, tiled=True)
    aux_count = regrouped.shape[1]
    aux_rows = regrouped.reshape(aux_count, row_width)
    fitted = lax.dot_general(
        lax.all_gather(metric_root, "wide", axis=0, tiled=True),
        aux_rows,
        (((0,), (0,)), ((), ())),
        preferred_element_type=jnp.float32,
    ).astype(jnp.bfloat16)

    def window_blocks(source):
        shifted = [from_behind(source, "wide", -offset) for offset in range(1, WINDOW)]
        return shifted

    facing = partner(fitted, "narrow", flip_bit)
    paired = [facing] + window_blocks(facing)

    def block_state(group_index, block_index):
        k_point = lax.dynamic_slice(block_kpoint, (group_index, block_index), (1, 1))[0, 0]
        picked = jnp.sum(
            jnp.where(jnp.arange(occ_energy.shape[0])[:, None] == k_point, occ_energy, 0.0), axis=0
        )
        live_count = lax.dynamic_slice(occ_count, (group_index, block_index), (1, 1))[0, 0]
        live_slots = (jnp.arange(occ_slots) < live_count).astype(jnp.float32)
        return (picked, live_slots)

    vir_own = lax.dynamic_index_in_dim(vir_energy, my_group, 0, keepdims=False)
    vir_partner = lax.dynamic_index_in_dim(vir_energy, partner_group, 0, keepdims=False)
    occ_own, live_own = block_state(my_group, my_block)
    gamma_sum = jnp.zeros((aux_count, row_width), jnp.float32)
    density = jnp.zeros((vir_count, vir_count), jnp.float32)
    for offset in range(WINDOW):
        far_rows = paired[offset]
        occ_other, live_other = block_state(partner_group, (my_block + offset) % wide_count)
        coulomb = lax.dot_general(
            fitted, far_rows, (((0,), (0,)), ((), ())), preferred_element_type=jnp.float32
        )
        coulomb = coulomb.reshape(occ_slots, vir_count, occ_slots, vir_count)
        denominator = (
            occ_own[:, None, None, None]
            + occ_other[None, None, :, None]
            - vir_own[None, :, None, None]
            - vir_partner[None, None, None, :]
        )
        amplitude = (
            coulomb / denominator * live_own[:, None, None, None] * live_other[None, None, :, None]
        )
        mixed_amp = 2.0 * amplitude - jnp.transpose(amplitude, (0, 3, 2, 1))
        amp_half = amplitude.astype(jnp.bfloat16)
        mixed_half = mixed_amp.astype(jnp.bfloat16)
        gamma_sum = gamma_sum + lax.dot_general(
            far_rows,
            mixed_half.reshape(row_width, row_width),
            (((1,), (1,)), ((), ())),
            preferred_element_type=jnp.float32,
        )
        density = density + jnp.einsum(
            "iajc,ibjc->ab", mixed_half, amp_half, preferred_element_type=jnp.float32
        )
    norm_scale = 1.0 / (group_count * wide_count * vir_count)
    virt_density = (
        lax.psum_scatter(density.reshape(-1), ("wide", "narrow"), scatter_dimension=0, tiled=True)
        * norm_scale
    )
    return (
        gamma_sum.astype(jnp.bfloat16).reshape(1, aux_count, 1, occ_slots, vir_count),
        virt_density,
    )


def solution(mesh):
    placed = (P("narrow", "wide", None, None, None), P("wide", None), P(), P(), P(), P())
    return jax.shard_map(
        shards,
        mesh=mesh,
        in_specs=placed,
        out_specs=(P("narrow", None, "wide", None, None), P(("wide", "narrow"))),
        check_vma=False,
    )
```

profile of v0, /device:TPU:0, one launch (start us, length us, event | category | flops | bytes accessed | tf_op | source)
XLA Modules:
  0.0 301.7 jit_solution(15917331955978879491)
XLA Ops:
  7.2 2.9 copy.61
  10.0 7.3 %all-to-all-start = ((bf16[1,80,8,2,384]{4,3,1,0,2:T(2,128)(2,1)}), bf16[1,80,8,2,384]{4,3,1,0,2:T(2,128)(2,1)S(1)}, u32[]{:S(2)}, u32[]{:S(2)}) async-start(bf16[1,80,8,2,384]{4,3,1,0,2:T(2,128)(2,1)} %copy.61), calls=%async_computation | async-start | bytes 1966080 | tf_op jit(solution)/shard_map/all_to_all | solution.py:31
  17.4 47.4 %all_gather.3 = bf16[640,640]{1,0:T(8,128)(2,1)S(1)} all-gather(bf16[80,640]{1,0:T(8,128)(2,1)S(1)} %copy-done.7), channel_id=1, replica_groups=mesh['wide'=8,'narrow'=4] {'wide'}, dimensions={0}, use_global_device_ids=true | all-gather | bytes 921600 | tf_op jit(solution)/shard_map/all_gather | solution.py:35
  65.0 1.0 convolution_convert_fusion
  66.0 1.6 collective-permute-start
  67.6 0.7 fusion.14
  68.2 0.6 iota_compare_fusion
  68.9 0.6 iota_compare_fusion.1
  69.5 0.6 iota_compare_fusion.2
  70.2 0.6 iota_compare_fusion.3
  70.8 0.7 compare_convert_fusion
  71.5 0.7 compare_convert_fusion.1
  72.3 11.2 %collective-permute-done = bf16[640,768]{1,0:T(8,128)(2,1)} collective-permute-done((bf16[640,768]{1,0:T(8,128)(2,1)S(1)}, bf16[640,768]{1,0:T(8,128)(2,1)}, u32[]{:S(2)}, u32[]{:S(2)}) %collective-permute-start) | collective-permute-done | bytes 983072 | tf_op jit(solution)/shard_map/ppermute | solution.py:18
  83.5 2.3 collective-permute-start.1
  85.8 0.7 compare_convert_fusion.2
  86.8 0.6 compare_convert_fusion.3
  87.4 2.6 fusion.16
  90.0 2.4 reshape.176
  92.4 15.9 %collective-permute-done.1 = bf16[640,768]{1,0:T(8,128)(2,1)} collective-permute-done((bf16[640,768]{1,0:T(8,128)(2,1)}, bf16[640,768]{1,0:T(8,128)(2,1)}, u32[]{:S(2)}, u32[]{:S(2)}) %collective-permute-start.1) | collective-permute-done | bytes 983072 | tf_op jit(solution)/shard_map/ppermute | solution.py:12
  108.3 2.6 fusion.18
  110.9 2.4 reshape.178
  113.3 8.1 %collective-permute-done.2 = bf16[640,768]{1,0:T(8,128)(2,1)S(1)} collective-permute-done((bf16[640,768]{1,0:T(8,128)(2,1)}, bf16[640,768]{1,0:T(8,128)(2,1)S(1)}, u32[]{:S(2)}, u32[]{:S(2)}) %collective-permute-start.2) | collective-permute-done | bytes 983072 | tf_op jit(solution)/shard_map/ppermute | solution.py:12
  121.4 2.7 fusion.20
  124.1 2.3 reshape.180
  126.4 5.6 %fusion.4 = (f32[2,384,2,384]{3,1,2,0:T(8,128)}, f32[2,384,2,384]{3,1,2,0:T(8,128)}, f32[2,384,2,384]{3,1,2,0:T(8,128)S(1)}) fusion(f32[2,384,2,384]{3,2,1,0:T(2,128)} %reshape.180, f32[2]{0:T(128)S(1)} %compare_convert_fusion, f32[2,384,2]{1,2,0:T(2,128)S(1)} %get-tuple-element.21, f32[2]{0:T(128)S(1)} %compare_convert_fusion.3, ...), kind=kLoop, calls=%fused_computation.8 | loop fusion | flops 7077888 | bytes 14175776 | tf_op jit(solution)/shard_map/mul | solution.py:76
  132.1 3.1 %copy.71 = f32[2,384,2,384]{1,3,2,0:T(8,128)} copy(f32[2,384,2,384]{3,1,2,0:T(8,128)} %get-tuple-element.18) | data formatting | bytes 4718592 | tf_op jit(solution)/shard_map/mul | solution.py:76
  135.1 2.8 fusion
  137.9 0.3 copy-done.1
  138.2 1.7 convolution_bitcast_fusion
  139.9 2.9 copy.73
  142.8 3.1 %copy.67 = f32[2,384,2,384]{1,3,2,0:T(8,128)} copy(f32[2,384,2,384]{3,1,2,0:T(8,128)} %get-tuple-element.19) | data formatting | bytes 4718592 | tf_op jit(solution)/shard_map/mul | solution.py:76
  145.8 2.8 fusion.1
  148.6 0.3 copy-done
  148.9 1.7 convolution_bitcast_fusion.1
  150.6 2.9 copy.69
  153.4 1.9 copy.63
  155.4 1.9 fusion.2
  157.3 2.9 copy.65
  160.2 2.9 fusion.10
  163.1 2.1 reshape.183
  165.7 0.8 copy-done.4
  166.5 0.2 copy.85
  166.7 2.2 fusion.19
  168.9 2.3 fusion.17
  171.2 1.0 add_convert_fusion
  172.1 1.2 reshape.182
  173.3 120.2 %all-reduce.3.cloned.1.call-done = f32[147456]{0:T(1024)} async-done(((f32[147456]{0:T(1024)}), f32[147456]{0:T(1024)}) %all-reduce.3.cloned.1.call-update) | async-done | bytes 589840
  293.5 1.4 dynamic-slice_multiply_fusion
  (34 shorter events, 1.2 us)
Async XLA Ops:
  7.2 10.2 %copy-start.7 = (bf16[80,640]{1,0:T(8,128)(2,1)S(1)}, bf16[80,640]{1,0:T(8,128)(2,1)}, u32[]{:S(2)}) copy-start(bf16[80,640]{1,0:T(8,128)(2,1)} %param.7) | copy-start | bytes 307204
  10.0 54.7 %all-to-all-start = ((bf16[1,80,8,2,384]{4,3,1,0,2:T(2,128)(2,1)}), bf16[1,80,8,2,384]{4,3,1,0,2:T(2,128)(2,1)S(1)}, u32[]{:S(2)}, u32[]{:S(2)}) async-start(bf16[1,80,8,2,384]{4,3,1,0,2:T(2,128)(2,1)} %copy.61), calls=%async_computation | async-start | bytes 1966080 | tf_op jit(solution)/shard_map/all_to_all | solution.py:31
  17.3 276.2 %all-reduce.3.cloned.1.call-start = ((), (), s32[]{:S(2)}) async-start(), calls=%async_computation.1 | async-start | bytes 1179648
  64.9 2.6 copy-start.10
  64.9 2.6 copy-start.8
  65.0 2.6 copy-start.9
  65.0 7.2 %copy-start.11 = (f32[8,2]{0,1:T(2,128)S(1)}, f32[8,2]{0,1:T(2,128)}, u32[]{:S(2)}) copy-start(f32[8,2]{0,1:T(2,128)} %param.8) | copy-start | bytes 196
  65.9 20.5 %copy-start.12 = (bf16[640,768]{1,0:T(8,128)(2,1)}, bf16[640,768]{1,0:T(8,128)(2,1)S(1)}, u32[]{:S(2)}) copy-start(bf16[640,768]{1,0:T(8,128)(2,1)S(1)} %convolution_convert_fusion) | copy-start | bytes 2949124
  66.0 17.6 %collective-permute-start = (bf16[640,768]{1,0:T(8,128)(2,1)S(1)}, bf16[640,768]{1,0:T(8,128)(2,1)}, u32[]{:S(2)}, u32[]{:S(2)}) collective-permute-start(bf16[640,768]{1,0:T(8,128)(2,1)S(1)} %convolution_convert_fusion), channel_id=1, source_target_pairs={{0,2},{1,3},{2,0},{3,1},{4,6},{5,7},{6,4},{7,5},{8,10},{9,11},{10,... | collective-permute-start | bytes 2949128 | tf_op jit(solution)/shard_map/ppermute | solution.py:18
  83.5 24.8 %collective-permute-start.1 = (bf16[640,768]{1,0:T(8,128)(2,1)}, bf16[640,768]{1,0:T(8,128)(2,1)}, u32[]{:S(2)}, u32[]{:S(2)}) collective-permute-start(bf16[640,768]{1,0:T(8,128)(2,1)} %collective-permute-done), channel_id=1, source_target_pairs={{0,28},{4,0},{8,4},{12,8},{16,12},{20,16},{24,20},{28,24},{1,29},{... | collective-permute-start | bytes 2949128 | tf_op jit(solution)/shard_map/ppermute | solution.py:12
  86.6 34.8 %collective-permute-start.2 = (bf16[640,768]{1,0:T(8,128)(2,1)}, bf16[640,768]{1,0:T(8,128)(2,1)S(1)}, u32[]{:S(2)}, u32[]{:S(2)}) collective-permute-start(bf16[640,768]{1,0:T(8,128)(2,1)} %collective-permute-done), channel_id=1, source_target_pairs={{0,24},{4,28},{8,0},{12,4},{16,8},{20,12},{24,16},{28,20},{1,25},{... | collective-permute-start | bytes 2949128 | tf_op jit(solution)/shard_map/ppermute | solution.py:12
  121.4 2.7 copy-start.5
  135.1 3.1 %copy-start.1 = (f32[2,384,2,384]{3,1,2,0:T(8,128)S(1)}, f32[2,384,2,384]{3,1,2,0:T(8,128)}, u32[]{:S(2)}) copy-start(f32[2,384,2,384]{3,1,2,0:T(8,128)} %get-tuple-element.18) | copy-start | bytes 7077892
  145.8 3.1 %copy-start = (f32[2,384,2,384]{3,1,2,0:T(8,128)S(1)}, f32[2,384,2,384]{3,1,2,0:T(8,128)}, u32[]{:S(2)}) copy-start(f32[2,384,2,384]{3,1,2,0:T(8,128)} %get-tuple-element.19) | copy-start | bytes 7077892
  163.1 2.1 copy-start.2
  163.1 2.4 copy-start.3
  165.2 1.3 copy-start.4
  168.9 2.3 copy-start.6
Sparse Core Ops, SparseCore 0:
  165.3 128.1 all-reduce.2
where the time goes:
time: 302 us
  waiting for transfers between devices  155 us (51%)
  blocking collectives  47.4 us (16%)
  local copies, waits for them, and re-layouts  32.9 us (11%)
  matrix products  20.5 us (7%)
  other arithmetic  20 us (7%)
  between operations  14.3 us (5%)
  starting transfers between devices  11.3 us (4%)
    unnamed x2, waiting for transfers between devices  120 us
    all_gather x1, blocking collectives, shards(): lax.all_gather(metric_root, 'wide', axis=0, tiled=True)  47.4 us
    ppermute x2, waiting for transfers between devices, from_behind(): return lax.ppermute(value, axis, pairs)  24 us
    ppermute x1, waiting for transfers between devices, partner(): return lax.ppermute(value, axis, pairs)  11.2 us
    convert_element_type x3, local copies, waits for them, and re-layouts, shards(): mixed_half = mixed_amp.astype(jnp.bfloat16)  8.6 us
    mul x3, local copies, waits for them, and re-layouts, shards(): coulomb / denominator * live_own[:, None, None, None]  8.07 us
    dot_general x3, matrix products, shards(): lax.dot_general(fitted, far_rows, (((0,), (0,)), ((), ())), preferred_ele...  7.9 us
    convert_element_type x3, other arithmetic, shards(): mixed_half = mixed_amp.astype(jnp.bfloat16)  7.52 us
  transfers between devices with their start and end apart: 5, of which 4 were waited for; matrix products, arithmetic and copies ran while one was open for 8% of the time, Pallas kernels for 0%

commit v1 on v0

v1 whole, which is shorter than its diff:
```python
import functools

import jax
import jax.numpy as jnp
from jax import lax
from jax.experimental import pallas as pl
from jax.experimental.pallas import tpu as pltpu
from jax.sharding import PartitionSpec as P

WINDOW = 3
DIRECT = 8


def flip(value, axis, mask):
    pairs = [(source, source ^ mask) for source in range(lax.axis_size(axis))]
    return lax.ppermute(value, axis, pairs)


def from_ahead(value, axis, steps):
    count = lax.axis_size(axis)
    pairs = [(source, (source - steps) % count) for source in range(count)]
    return lax.ppermute(value, axis, pairs)


def is_power(count):
    return count & (count - 1) == 0


def bits_of(count):
    return [1 << bit for bit in reversed(range(count.bit_length() - 1))]


def doubled(count):
    order = [0]
    for mask in bits_of(count):
        order = order + [place ^ mask for place in order]
    return order


def pair_kernel(
    offset, slot, occ_ref, kpoint_ref, count_ref, row_ref, column_ref, own_ref, far_ref, *rest
):
    density_in, mixed_ref, density_ref = rest if len(rest) == 3 else (None, *rest)
    group_count, wide_count = kpoint_ref.shape
    occ_slots = occ_ref.shape[1]
    vir_count = row_ref.shape[1]
    group = lax.axis_index("narrow")
    block = lax.axis_index("wide")
    partner = lax.rem(group + group_count // 2, group_count)
    other = lax.rem(block + offset, wide_count)
    spot = lax.broadcasted_iota(jnp.int32, column_ref.shape, 1)
    vir_own = jnp.sum(jnp.where(spot == group, column_ref[...], 0.0), axis=1, keepdims=True)
    vir_far = row_ref[pl.ds(partner, 1), :]
    occ_far = occ_ref[kpoint_ref[partner, other], slot]
    live_far = slot < count_ref[partner, other]
    far = far_ref[...]
    total = None
    for i in range(occ_slots):
        columns = slice(i * vir_count, (i + 1) * vir_count)
        coulomb = lax.dot_general(
            own_ref[:, columns], far, (((0,), (0,)), ((), ())), preferred_element_type=jnp.float32
        )
        occ = occ_ref[kpoint_ref[group, block], i] + occ_far
        live = jnp.logical_and(i < count_ref[group, block], live_far)
        scale = jnp.where(live, 1.0, 0.0).astype(jnp.float32)
        amplitude = coulomb * (scale / ((occ - vir_own) - vir_far))
        mixed = (2.0 * amplitude - amplitude.T).astype(jnp.bfloat16)
        mixed_ref[columns, :] = mixed
        term = lax.dot_general(
            mixed,
            amplitude.astype(jnp.bfloat16),
            (((1,), (1,)), ((), ())),
            preferred_element_type=jnp.float32,
        )
        total = term if total is None else total + term
    density_ref[...] = total if density_in is None else density_in[...] + total


def gamma_kernel(far_count, *refs):
    fars, mixeds, out_ref = refs[:far_count], refs[far_count:-1], refs[-1]
    vir_count = fars[0].shape[1]
    for i in range(out_ref.shape[1] // vir_count):
        columns = slice(i * vir_count, (i + 1) * vir_count)
        total = None
        for far, mixed in zip(fars, mixeds):
            term = lax.dot_general(
                far[...], mixed[columns, :], (((1,), (1,)), ((), ())), preferred_element_type=jnp.float32
            )
            total = term if total is None else total + term
        out_ref[:, columns] = total.astype(out_ref.dtype)


VMEM = pl.BlockSpec(memory_space=pltpu.VMEM)
SMEM = pl.BlockSpec(memory_space=pltpu.SMEM)


def pair_terms(offset, slot, small, own, far, density):
    vir_count = far.shape[1]
    width = own.shape[1]
    operands = [*small, own, far] + ([] if density is None else [density])
    specs = [SMEM] * 3 + [VMEM] * (len(operands) - 3)
    flops = 2 * own.shape[0] * width * vir_count + 2 * width * vir_count * vir_count
    moved = 2 * (own.size + far.size + width * vir_count) + 8 * vir_count * vir_count
    return pl.pallas_call(
        functools.partial(pair_kernel, offset, slot),
        out_shape=(
            jax.ShapeDtypeStruct((width, vir_count), jnp.bfloat16),
            jax.ShapeDtypeStruct((vir_count, vir_count), jnp.float32),
        ),
        in_specs=specs,
        out_specs=(VMEM, VMEM),
        compiler_params=pltpu.CompilerParams(vmem_limit_bytes=32 * 1024 * 1024),
        cost_estimate=pl.CostEstimate(flops=flops, bytes_accessed=moved, transcendentals=0),
    )(*operands)


def three_index(fars, mixeds):
    aux_count = fars[0].shape[0]
    width = mixeds[0].shape[0]
    flops = sum(2 * far.size * width for far in fars)
    moved = 2 * (sum(far.size for far in fars) + sum(mixed.size for mixed in mixeds) + aux_count * width)
    return pl.pallas_call(
        functools.partial(gamma_kernel, len(fars)),
        out_shape=jax.ShapeDtypeStruct((aux_count, width), jnp.bfloat16),
        in_specs=[VMEM] * (len(fars) + len(mixeds)),
        out_specs=VMEM,
        compiler_params=pltpu.CompilerParams(vmem_limit_bytes=48 * 1024 * 1024),
        cost_estimate=pl.CostEstimate(flops=flops, bytes_accessed=moved, transcendentals=0),
    )(*fars, *mixeds)


def gathered_metric(metric):
    wide_count = lax.axis_size("wide")
    columns = metric.shape[1]
    half = columns // 2
    low_bit = lax.axis_index("narrow") % 2
    part = lax.dynamic_slice_in_dim(metric, low_bit * half, half, 1)
    for mask in bits_of(wide_count):
        part = jnp.concatenate([part, flip(part, "wide", mask)], axis=0)
    other = flip(part, "narrow", 1)
    first = jnp.where(low_bit == 0, part, other)
    second = jnp.where(low_bit == 0, other, part)
    return jnp.concatenate([first, second], axis=1)


def scattered_sum(density):
    wide_count = lax.axis_size("wide")
    group_count = lax.axis_size("narrow")
    wide_bits, narrow_bits = bits_of(wide_count), bits_of(group_count)
    part = density.size // (wide_count * group_count)
    lane = 128 if part % 128 == 0 else part
    value = density.reshape([2] * (len(wide_bits) + len(narrow_bits)) + [part // lane, lane])
    stages = [("narrow", mask, len(wide_bits) + place) for place, mask in enumerate(narrow_bits)]
    stages = stages[::-1] + [("wide", mask, place) for place, mask in reversed(list(enumerate(wide_bits)))]
    for axis, mask, dim in stages:
        bit = (lax.axis_index(axis) // mask) % 2
        sent = lax.dynamic_index_in_dim(value, 1 - bit, dim, keepdims=False).astype(jnp.bfloat16)
        kept = lax.dynamic_index_in_dim(value, bit, dim, keepdims=False)
        value = kept + flip(sent, axis, mask).astype(jnp.float32)
    return value.reshape(-1)


def shards(raw_ints, metric_root, occ_energy, vir_energy, block_kpoint, occ_count):
    _, aux_rows, block_count, occ_slots, vir_count = raw_ints.shape
    row_width = occ_slots * vir_count
    wide_count = lax.axis_size("wide")
    group_count = lax.axis_size("narrow")
    my_block = lax.axis_index("wide")
    direct = wide_count <= DIRECT and is_power(wide_count)
    small = (occ_energy, block_kpoint, occ_count, vir_energy, vir_energy.T)
    if direct:
        metric = gathered_metric(metric_root)
    else:
        metric = lax.all_gather(metric_root, "wide", axis=0, tiled=True)

    fitted = []
    for slot in range(occ_slots):
        blocks = jnp.transpose(raw_ints[0, :, :, slot, :], (1, 0, 2))
        if direct:
            pieces = []
            for place in doubled(wide_count):
                piece = lax.dynamic_index_in_dim(blocks, my_block ^ place, 0, keepdims=False)
                pieces.append(flip(piece, "wide", place) if place else piece)
            rows = jnp.concatenate(pieces, axis=0)
        else:
            rows = lax.all_to_all(blocks, "wide", split_axis=0, concat_axis=0, tiled=True)
            rows = rows.reshape(wide_count * aux_rows, vir_count)
        fitted.append(
            lax.dot_general(
                metric, rows, (((0,), (0,)), ((), ())), preferred_element_type=jnp.float32
            ).astype(jnp.bfloat16)
        )
    own = jnp.concatenate(fitted, axis=1)
    aux_count = own.shape[0]

    half_turn = [(source, (source + group_count // 2) % group_count) for source in range(group_count)]
    facing = [lax.ppermute(part, "narrow", half_turn) for part in fitted]
    odd = my_block % 2 == 1
    window = {}
    for slot in range(occ_slots):
        window[0, slot] = facing[slot]
        second = from_ahead(facing[slot], "wide", 2)
        window[2, slot] = second
        if wide_count % 2 == 0:
            window[1, slot] = flip(jnp.where(odd, facing[slot], second), "wide", 1)
        else:
            window[1, slot] = from_ahead(facing[slot], "wide", 1)

    fars, mixeds = [], []
    density = None
    for offset in (0, 2, 1):
        for slot in range(occ_slots):
            far = window[offset, slot]
            mixed, density = pair_terms(offset, slot, small, own, far, density)
            fars.append(far)
            mixeds.append(mixed)
    gamma = three_index(fars, mixeds)
    norm_scale = 1.0 / (group_count * wide_count * vir_count)
    virt_density = scattered_sum(density * norm_scale)
    return gamma.reshape(1, aux_count, 1, occ_slots, vir_count), virt_density


def solution(mesh):
    placed = (P("narrow", "wide", None, None, None), P("wide", None), P(), P(), P(), P())
    return jax.shard_map(
        shards,
        mesh=mesh,
        in_specs=placed,
        out_specs=(P("narrow", None, "wide", None, None), P(("wide", "narrow"))),
        check_vma=False,
    )
```

time: 302 us -> 144 us (0.48)
  waiting for transfers between devices: 155 us -> 50.3 us
  blocking collectives: 47.4 us -> 0 us
  starting transfers between devices: 11.3 us -> 44.5 us
  matrix products: 20.5 us -> 1.59 us
  Pallas kernels: 0 us -> 17.9 us
  other arithmetic: 20 us -> 6.7 us
  between operations: 14.3 us -> 1.35 us
  local copies, waits for them, and re-layouts: 32.9 us -> 21.5 us
    unnamed x2 -> x0, waiting for transfers between devices: 120 us -> none
    all_gather x1 -> x0, blocking collectives: 47.4 us -> none  [shards(): lax.all_gather(metric_root, 'wide', axis=0, tiled=True)]
    ppermute x3 -> x29, starting transfers between devices: 4 us -> 44.5 us  [the longest x25 36.4 us: flip(): return lax.ppermute(value, axis, pairs)]
    dot_general x10 -> x2, matrix products: 20.5 us -> 1.59 us  [shards(): lax.dot_general(metric, rows, (((0,), (0,)), ((), ())), preferred_element...]
    pallas_call x0 -> x7, Pallas kernels: none -> 17.9 us  [the longest x6 12 us: pair_terms(): pl.pallas_call(functools.partial(pair_kernel, offset, slot), out_shape=(j...]
    ppermute x3 -> x29, waiting for transfers between devices: 35.2 us -> 50.3 us  [the longest x25 25.1 us: flip(): return lax.ppermute(value, axis, pairs)]
    convert_element_type x7 -> x0, other arithmetic: 10.1 us -> none  [the longest x3 7.52 us: shards(): mixed_half = mixed_amp.astype(jnp.bfloat16)]
    mul x3 -> x0, local copies, waits for them, and re-layouts: 8.07 us -> none  [shards(): coulomb / denominator * live_own[:, None, None, None]]
  transfers between devices with their start and end apart: 5 -> 29, of which waited for: 4 -> 12; matrix products, arithmetic and copies ran while one was open for 8% -> 6% of each run, Pallas kernels for 0% -> 11%
where the time goes in v1:
time: 144 us
  waiting for transfers between devices  50.3 us (35%)
  starting transfers between devices  44.5 us (31%)
  local copies, waits for them, and re-layouts  21.5 us (15%)
  Pallas kernels  17.9 us (12%)
  other arithmetic  6.7 us (5%)
  matrix products  1.59 us (1%)
    ppermute x25, starting transfers between devices, flip(): return lax.ppermute(value, axis, pairs)  36.4 us
    ppermute x25, waiting for transfers between devices, flip(): return lax.ppermute(value, axis, pairs)  25.1 us
    ppermute x2, waiting for transfers between devices, shards(): facing = [lax.ppermute(part, 'narrow', half_turn) for part in fitted]  16.9 us
    pallas_call x6, Pallas kernels, pair_terms(): pl.pallas_call(functools.partial(pair_kernel, offset, slot), out_shape=(j...  12 us
    unnamed x68, local copies, waits for them, and re-layouts  9.85 us
    ppermute x2, waiting for transfers between devices, from_ahead(): return lax.ppermute(value, axis, pairs)  8.26 us
    pallas_call x1, Pallas kernels, three_index(): pl.pallas_call(functools.partial(gamma_kernel, len(fars)), out_shape=jax....  5.85 us
    ppermute x2, starting transfers between devices, from_ahead(): return lax.ppermute(value, axis, pairs)  5 us
  transfers between devices with their start and end apart: 29, of which 12 were waited for; matrix products, arithmetic and copies ran while one was open for 6% of the time, Pallas kernels for 11%

profile of v1, /device:TPU:0, one launch (start us, length us, event | category | flops | bytes accessed | tf_op | source)
XLA Modules:
  0.0 143.9 jit_solution(17615168083973152791)
XLA Ops:
  0.7 3.2 %fusion.10 = (bf16[1,80,8,1,384]{4,3,2,1,0:T(2,128)(2,1)S(1)}, bf16[1,80,8,1,384]{4,3,2,1,0:T(2,128)(2,1)S(1)}) fusion(bf16[1,80,8,2,384]{4,3,2,1,0:T(2,128)(2,1)} %param.6), kind=kLoop, calls=%fused_computation.79 | loop fusion | bytes 1966080 | tf_op jit(solution)/shard_map/slice | solution.py:178
  3.9 2.3 %constant_dynamic-slice_fusion = (bf16[1,80,1,1,384]{4,3,2,1,0:T(2,128)(2,1)S(1)}, bf16[1,80,1,1,384]{4,3,2,1,0:T(2,128)(2,1)S(1)}, bf16[1,80,1,1,384]{4,3,2,1,0...) fusion(bf16[1,80,8,1,384]{4,3,2,1,0:T(2,128)(2,1)S(1)} %get-tup, ...), kind=kLoop, calls=%fused_computation.60 | loop fusion | bytes 1966112 | tf_op jit(solution)/shard_map/dynamic-slice.31
  6.2 4.1 %collective-permute-start.4 = (bf16[80,384]{1,0:T(8,128)(2,1)S(1)}, bf16[80,384]{1,0:T(8,128)(2,1)S(1)}, u32[]{:S(2)}, u32[]{:S(2)}) collective-permute-start(bf16[80,384]{1,0:T(8,128)(2,1)S(1)} %bitcast.95), channel_id=1, source_target_pairs={{0,16},{4,20},{8,24},{12,28},{16,0},{20,4},{24,8},{28,12},{1,17},{... | collective-permute-start | bytes 184328 | tf_op jit(solution)/shard_map/ppermute | solution.py:16
  10.3 1.6 %collective-permute-start.5 = (bf16[80,384]{1,0:T(8,128)(2,1)S(1)}, bf16[80,384]{1,0:T(8,128)(2,1)S(1)}, u32[]{:S(2)}, u32[]{:S(2)}) collective-permute-start(bf16[80,384]{1,0:T(8,128)(2,1)S(1)} %bitcast.94), channel_id=1, source_target_pairs={{0,8},{4,12},{8,0},{12,4},{16,24},{20,28},{24,16},{28,20},{1,9},{5... | collective-permute-start | bytes 184328 | tf_op jit(solution)/shard_map/ppermute | solution.py:16
  12.1 1.8 %collective-permute-start.7 = (bf16[80,384]{1,0:T(8,128)(2,1)S(1)}, bf16[80,384]{1,0:T(8,128)(2,1)S(1)}, u32[]{:S(2)}, u32[]{:S(2)}) collective-permute-start(bf16[80,384]{1,0:T(8,128)(2,1)S(1)} %bitcast.91), channel_id=1, source_target_pairs={{0,4},{4,0},{8,12},{12,8},{16,20},{20,16},{24,28},{28,24},{1,5},{5... | collective-permute-start | bytes 184328 | tf_op jit(solution)/shard_map/ppermute | solution.py:16
  14.0 1.8 %collective-permute-start = (bf16[80,320]{1,0:T(8,128)(2,1)S(1)}, bf16[80,320]{1,0:T(8,128)(2,1)S(1)}, u32[]{:S(2)}, u32[]{:S(2)}) collective-permute-start(bf16[80,320]{1,0:T(8,128)(2,1)S(1)} %constant_dynamic-slice_fusion.16), channel_id=1, source_target_pairs={{0,16},{4,20},{8,24},{12,28},{16,0},{20,4},{24,8},{28,12},{1,17},{... | collective-permute-start | bytes 153608 | tf_op jit(solution)/shard_map/ppermute | solution.py:16
  16.6 3.5 %collective-permute-done = bf16[80,320]{1,0:T(8,128)(2,1)S(1)} collective-permute-done((bf16[80,320]{1,0:T(8,128)(2,1)S(1)}, bf16[80,320]{1,0:T(8,128)(2,1)S(1)}, u32[]{:S(2)}, u32[]{:S(2)}) %collective-permute-start) | collective-permute-done | bytes 51232 | tf_op jit(solution)/shard_map/ppermute | solution.py:16
  20.9 3.4 %collective-permute-start.9 = (bf16[80,384]{1,0:T(8,128)(2,1)S(1)}, bf16[80,384]{1,0:T(8,128)(2,1)S(1)}, u32[]{:S(2)}, u32[]{:S(2)}) collective-permute-start(bf16[80,384]{1,0:T(8,128)(2,1)S(1)} %bitcast.97), channel_id=1, source_target_pairs={{0,12},{4,8},{8,4},{12,0},{16,28},{20,24},{24,20},{28,16},{1,13},{... | collective-permute-start | bytes 184328 | tf_op jit(solution)/shard_map/ppermute | solution.py:16
  24.3 2.0 %collective-permute-start.10 = (bf16[80,384]{1,0:T(8,128)(2,1)S(1)}, bf16[80,384]{1,0:T(8,128)(2,1)S(1)}, u32[]{:S(2)}, u32[]{:S(2)}) collective-permute-start(bf16[80,384]{1,0:T(8,128)(2,1)S(1)} %bitcast.96), channel_id=1, source_target_pairs={{0,28},{4,24},{8,20},{12,16},{16,12},{20,8},{24,4},{28,0},{1,29},{... | collective-permute-start | bytes 184328 | tf_op jit(solution)/shard_map/ppermute | solution.py:16
  26.5 3.1 %collective-permute-start.13 = (bf16[80,384]{1,0:T(8,128)(2,1)S(1)}, bf16[80,384]{1,0:T(8,128)(2,1)S(1)}, u32[]{:S(2)}, u32[]{:S(2)}) collective-permute-start(bf16[80,384]{1,0:T(8,128)(2,1)S(1)} %bitcast.90), channel_id=1, source_target_pairs={{0,8},{4,12},{8,0},{12,4},{16,24},{20,28},{24,16},{28,20},{1,9},{5... | collective-permute-start | bytes 184328 | tf_op jit(solution)/shard_map/ppermute | solution.py:16
  29.6 1.4 collective-permute-start.14
  31.9 5.1 %collective-permute-done.1 = bf16[160,320]{1,0:T(8,128)(2,1)S(1)} collective-permute-done((bf16[160,320]{1,0:T(8,128)(2,1)S(1)}, bf16[160,320]{1,0:T(8,128)(2,1)S(1)}, u32[]{:S(2)}, u32[]{:S(2)}) %collective-permute-start.1) | collective-permute-done | bytes 102432 | tf_op jit(solution)/shard_map/ppermute | solution.py:16
  37.0 1.6 %collective-permute-start.16 = (bf16[80,384]{1,0:T(8,128)(2,1)S(1)}, bf16[80,384]{1,0:T(8,128)(2,1)S(1)}, u32[]{:S(2)}, u32[]{:S(2)}) collective-permute-start(bf16[80,384]{1,0:T(8,128)(2,1)S(1)} %bitcast.87), channel_id=1, source_target_pairs={{0,20},{4,16},{8,28},{12,24},{16,4},{20,0},{24,12},{28,8},{1,21},{... | collective-permute-start | bytes 184328 | tf_op jit(solution)/shard_map/ppermute | solution.py:16
  39.6 2.7 %collective-permute-start.17 = (bf16[80,384]{1,0:T(8,128)(2,1)S(1)}, bf16[80,384]{1,0:T(8,128)(2,1)S(1)}, u32[]{:S(2)}, u32[]{:S(2)}) collective-permute-start(bf16[80,384]{1,0:T(8,128)(2,1)S(1)} %bitcast.86), channel_id=1, source_target_pairs={{0,12},{4,8},{8,4},{12,0},{16,28},{20,24},{24,20},{28,16},{1,13},{... | collective-permute-start | bytes 184328 | tf_op jit(solution)/shard_map/ppermute | solution.py:16
  42.3 3.9 %collective-permute-done.2 = bf16[320,320]{1,0:T(8,128)(2,1)S(1)} collective-permute-done((bf16[320,320]{1,0:T(8,128)(2,1)S(1)}, bf16[320,320]{1,0:T(8,128)(2,1)S(1)}, u32[]{:S(2)}, u32[]{:S(2)}) %collective-permute-start.2) | collective-permute-done | bytes 204832 | tf_op jit(solution)/shard_map/ppermute | solution.py:16
  46.2 1.9 %collective-permute-start.18 = (bf16[80,384]{1,0:T(8,128)(2,1)S(1)}, bf16[80,384]{1,0:T(8,128)(2,1)S(1)}, u32[]{:S(2)}, u32[]{:S(2)}) collective-permute-start(bf16[80,384]{1,0:T(8,128)(2,1)S(1)} %bitcast.85), channel_id=1, source_target_pairs={{0,28},{4,24},{8,20},{12,16},{16,12},{20,8},{24,4},{28,0},{1,29},{... | collective-permute-start | bytes 184328 | tf_op jit(solution)/shard_map/ppermute | solution.py:16
  48.4 1.7 %collective-permute-done.3 = bf16[640,320]{1,0:T(8,128)(2,1)S(1)} collective-permute-done((bf16[640,320]{1,0:T(8,128)(2,1)S(1)}, bf16[640,320]{1,0:T(8,128)(2,1)S(1)}, u32[]{:S(2)}, u32[]{:S(2)}) %collective-permute-start.3) | collective-permute-done | bytes 409632 | tf_op jit(solution)/shard_map/ppermute | solution.py:16
  51.2 1.6 %collective-permute-start.11 = (bf16[640,384]{1,0:T(8,128)(2,1)S(1)}, bf16[640,384]{1,0:T(8,128)(2,1)S(1)}, u32[]{:S(2)}, u32[]{:S(2)}) collective-permute-start(bf16[640,384]{1,0:T(8,128)(2,1)S(1)} %convolution_convert_fusion.1), channel_id=1, source_target_pairs={{0,2},{1,3},{2,0},{3,1},{4,6},{5,7},{6,4},{7,5},{8,10},{9,11},{10,... | collective-permute-start | bytes 1474568 | tf_op jit(solution)/shard_map/ppermute | solution.py:197
  54.1 1.6 %collective-permute-start.19 = (bf16[640,384]{1,0:T(8,128)(2,1)S(1)}, bf16[640,384]{1,0:T(8,128)(2,1)S(1)}, u32[]{:S(2)}, u32[]{:S(2)}) collective-permute-start(bf16[640,384]{1,0:T(8,128)(2,1)S(1)} %convolution_convert_fusion), channel_id=1, source_target_pairs={{0,2},{1,3},{2,0},{3,1},{4,6},{5,7},{6,4},{7,5},{8,10},{9,11},{10,... | collective-permute-start | bytes 1474568 | tf_op jit(solution)/shard_map/ppermute | solution.py:197
  55.6 9.7 %collective-permute-done.11.far_ref.refs_0_ = bf16[640,384]{1,0:T(8,128)(2,1)S(1)} collective-permute-done((bf16[640,384]{1,0:T(8,128)(2,1)S(1)}, bf16[640,384]{1,0:T(8,128)(2,1)S(1)}, u32[]{:S(2)}, u32[]{:S(2)}) %collective-permute-start.11) | collective-permute-done | bytes 491552 | tf_op jit(solution)/shard_map/ppermute | solution.py:197
  65.3 2.5 %collective-permute-start.20 = (bf16[640,384]{1,0:T(8,128)(2,1)S(1)}, bf16[640,384]{1,0:T(8,128)(2,1)S(1)}, u32[]{:S(2)}, u32[]{:S(2)}) collective-permute-start(bf16[640,384]{1,0:T(8,128)(2,1)S(1)} %collective-permute-done.11.far_ref.refs_0_), channel_id=1, source_target_pairs={{0,24},{4,28},{8,0},{12,4},{16,8},{20,12},{24,16},{28,20},{1,25},{... | collective-permute-start | bytes 1474568 | tf_op jit(solution)/shard_map/ppermute | solution.py:22
  67.8 7.2 %collective-permute-done.19.far_ref.refs_1_ = bf16[640,384]{1,0:T(8,128)(2,1)S(1)} collective-permute-done((bf16[640,384]{1,0:T(8,128)(2,1)S(1)}, bf16[640,384]{1,0:T(8,128)(2,1)S(1)}, u32[]{:S(2)}, u32[]{:S(2)}) %collective-permute-start.19) | collective-permute-done | bytes 491552 | tf_op jit(solution)/shard_map/ppermute | solution.py:197
  75.1 2.5 %collective-permute-start.21 = (bf16[640,384]{1,0:T(8,128)(2,1)S(1)}, bf16[640,384]{1,0:T(8,128)(2,1)S(1)}, u32[]{:S(2)}, u32[]{:S(2)}) collective-permute-start(bf16[640,384]{1,0:T(8,128)(2,1)S(1)} %collective-permute-done.19.far_ref.refs_1_), channel_id=1, source_target_pairs={{0,24},{4,28},{8,0},{12,4},{16,8},{20,12},{24,16},{28,20},{1,25},{... | collective-permute-start | bytes 1474568 | tf_op jit(solution)/shard_map/ppermute | solution.py:22
  79.3 8.3 %collective-permute-done.21.far_ref.refs_3_ = bf16[640,384]{1,0:T(8,128)(2,1)S(1)} collective-permute-done((bf16[640,384]{1,0:T(8,128)(2,1)S(1)}, bf16[640,384]{1,0:T(8,128)(2,1)S(1)}, u32[]{:S(2)}, u32[]{:S(2)}) %collective-permute-start.21) | collective-permute-done | bytes 491552 | tf_op jit(solution)/shard_map/ppermute | solution.py:22
  89.6 1.3 pad_maximum_fusion.own_ref
  90.9 2.0 %shard_map.77 = (bf16[768,384]{1,0:T(8,128)(2,1)S(1)}, f32[384,384]{1,0:T(8,128)S(1)}) custom-call(f32[8,2]{1,0:T(8,128)S(1)} %copy.23.occ_ref, s32[4,8]{1,0:T(4,128)S(1)} %copy-done.2, s32[4,8]{1,0:T(4,128)S(1)} %copy-done.3, f32[4,384]{1,0:T(4,128)S(1)} %copy-done.1, f32[384,4]{1,0:T(8,128)S(1)} %bitcast.78, bf16[640,768]{1,0:T(8,128)(2,1)S(1)} %pad_maximum_fusion.own_ref, ...), custom_call_target="tpu_custom_call" | custom-call | flops 603979776 | bytes 3244032 | tf_op jit(solution)/shard_map/pallas_call | solution.py:104
  93.7 2.0 %shard_map.78 = (bf16[768,384]{1,0:T(8,128)(2,1)S(1)}, f32[384,384]{1,0:T(8,128)S(1)}) custom-call(f32[8,2]{1,0:T(8,128)S(1)} %copy.23.occ_ref, s32[4,8]{1,0:T(4,128)S(1)} %copy-done.2, s32[4,8]{1,0:T(4,128)S(1)} %copy-done.3, f32[4,384]{1,0:T(4,128)S(1)} %copy-done.1, f32[384,4]{1,0:T(8,128)S(1)} %bitcast.79, bf16[640,768]{1,0:T(8,128)(2,1)S(1)} %pad_maximum_fusion.own_ref, ...), custom_call_target="tpu_custom_call" | custom-call | flops 603979776 | bytes 3244032 | tf_op jit(solution)/shard_map/pallas_call | solution.py:104
  95.7 2.0 %shard_map.79 = (bf16[768,384]{1,0:T(8,128)(2,1)S(1)}, f32[384,384]{1,0:T(8,128)S(1)}) custom-call(f32[8,2]{1,0:T(8,128)S(1)} %copy.23.occ_ref, s32[4,8]{1,0:T(4,128)S(1)} %copy-done.2, s32[4,8]{1,0:T(4,128)S(1)} %copy-done.3, f32[4,384]{1,0:T(4,128)S(1)} %copy-done.1, f32[384,4]{1,0:T(8,128)S(1)} %bitcast.80, bf16[640,768]{1,0:T(8,128)(2,1)S(1)} %pad_maximum_fusion.own_ref, ...), custom_call_target="tpu_custom_call" | custom-call | flops 603979776 | bytes 3244032 | tf_op jit(solution)/shard_map/pallas_call | solution.py:104
  98.6 2.0 %shard_map.80 = (bf16[768,384]{1,0:T(8,128)(2,1)S(1)}, f32[384,384]{1,0:T(8,128)S(1)}) custom-call(f32[8,2]{1,0:T(8,128)S(1)} %copy.23.occ_ref, s32[4,8]{1,0:T(4,128)S(1)} %copy-done.2, s32[4,8]{1,0:T(4,128)S(1)} %copy-done.3, f32[4,384]{1,0:T(4,128)S(1)} %copy-done.1, f32[384,4]{1,0:T(8,128)S(1)} %bitcast.81, bf16[640,768]{1,0:T(8,128)(2,1)S(1)} %pad_maximum_fusion.own_ref, ...), custom_call_target="tpu_custom_call" | custom-call | flops 603979776 | bytes 3244032 | tf_op jit(solution)/shard_map/pallas_call | solution.py:104
  101.4 2.0 %shard_map.81 = (bf16[768,384]{1,0:T(8,128)(2,1)S(1)}, f32[384,384]{1,0:T(8,128)S(1)}) custom-call(f32[8,2]{1,0:T(8,128)S(1)} %copy.23.occ_ref, s32[4,8]{1,0:T(4,128)S(1)} %copy-done.2, s32[4,8]{1,0:T(4,128)S(1)} %copy-done.3, f32[4,384]{1,0:T(4,128)S(1)} %copy-done.1, f32[384,4]{1,0:T(8,128)S(1)} %bitcast.82, bf16[640,768]{1,0:T(8,128)(2,1)S(1)} %pad_maximum_fusion.own_ref, ...), custom_call_target="tpu_custom_call" | custom-call | flops 603979776 | bytes 3244032 | tf_op jit(solution)/shard_map/pallas_call | solution.py:104
  103.4 2.0 %shard_map.82 = (bf16[768,384]{1,0:T(8,128)(2,1)S(1)}, f32[384,384]{1,0:T(8,128)S(1)}) custom-call(f32[8,2]{1,0:T(8,128)S(1)} %copy.23.occ_ref, s32[4,8]{1,0:T(4,128)S(1)} %copy-done.2, s32[4,8]{1,0:T(4,128)S(1)} %copy-done.3, f32[4,384]{1,0:T(4,128)S(1)} %copy-done.1, f32[384,4]{1,0:T(8,128)S(1)} %bitcast.83, bf16[640,768]{1,0:T(8,128)(2,1)S(1)} %pad_maximum_fusion.own_ref, ...), custom_call_target="tpu_custom_call" | custom-call | flops 603979776 | bytes 3244032 | tf_op jit(solution)/shard_map/pallas_call | solution.py:104
  107.2 2.0 %reshape.83 = f32[2,2,2,2,2,36,128]{6,5,4,3,2,1,0:T(8,128)} reshape(f32[384,384]{1,0:T(8,128)} %broadcast_multiply_fusion) | data formatting | bytes 1179648 | tf_op jit(solution)/shard_map/reshape | solution.py:152
  109.1 1.0 fusion
  110.2 1.3 collective-permute-done.24
  111.6 1.0 bitcast_add_fusion
  112.6 1.6 %collective-permute-start.25 = (bf16[2,2,2,36,128]{4,3,2,1,0:T(8,128)(2,1)S(1)}, bf16[2,2,2,36,128]{4,3,2,1,0:T(8,128)(2,1)}, u32[]{:S(2)}, u32[]{:S(2)}) collective-permute-start(bf16[2,2,2,36,128]{4,3,2,1,0:T(8,128)(2,1)S(1)} %fusion.1), channel_id=1, source_target_pairs={{0,2},{1,3},{2,0},{3,1},{4,6},{5,7},{6,4},{7,5},{8,10},{9,11},{10,... | collective-permute-start | bytes 221192 | tf_op jit(solution)/shard_map/ppermute | solution.py:16
  114.2 3.1 %collective-permute-done.25 = bf16[2,2,2,36,128]{4,3,2,1,0:T(8,128)(2,1)} collective-permute-done((bf16[2,2,2,36,128]{4,3,2,1,0:T(8,128)(2,1)S(1)}, bf16[2,2,2,36,128]{4,3,2,1,0:T(8,128)(2,1)}, u32[]{:S(2)}, u32[]{:S(2)}) %collective-permute-start.25) | collective-permute-done | bytes 73760 | tf_op jit(solution)/shard_map/ppermute | solution.py:16
  118.2 1.2 collective-permute-start.26
  119.4 2.9 %collective-permute-done.26 = bf16[2,2,36,128]{3,2,1,0:T(8,128)(2,1)S(1)} collective-permute-done((bf16[2,2,36,128]{3,2,1,0:T(8,128)(2,1)S(1)}, bf16[2,2,36,128]{3,2,1,0:T(8,128)(2,1)S(1)}, u32[]{:S(2)}, u32[]{:S(2)}) %collective-permute-start.26) | collective-permute-done | bytes 36896 | tf_op jit(solution)/shard_map/ppermute | solution.py:16
  123.2 2.9 %collective-permute-done.27 = bf16[2,36,128]{2,1,0:T(8,128)(2,1)S(1)} collective-permute-done((bf16[2,36,128]{2,1,0:T(8,128)(2,1)S(1)}, bf16[2,36,128]{2,1,0:T(8,128)(2,1)S(1)}, u32[]{:S(2)}, u32[]{:S(2)}) %collective-permute-start.27) | collective-permute-done | bytes 18464 | tf_op jit(solution)/shard_map/ppermute | solution.py:16
  126.2 2.8 %collective-permute-start.28 = (bf16[36,128]{1,0:T(8,128)(2,1)S(1)}, bf16[36,128]{1,0:T(8,128)(2,1)S(1)}, u32[]{:S(2)}, u32[]{:S(2)}) collective-permute-start(bf16[36,128]{1,0:T(8,128)(2,1)S(1)} %fusion.7), channel_id=1, source_target_pairs={{0,16},{4,20},{8,24},{12,28},{16,0},{20,4},{24,8},{28,12},{1,17},{... | collective-permute-start | bytes 27656 | tf_op jit(solution)/shard_map/ppermute | solution.py:16
  129.0 1.1 copy-done.5
  130.1 1.1 copy-done.7
  131.1 1.1 copy-done.9
  132.2 1.1 copy-done.11
  133.3 1.1 copy-done.14
  134.3 5.9 %shard_map.83 = bf16[640,768]{1,0:T(8,128)(2,1)} custom-call(bf16[640,384]{1,0:T(8,128)(2,1)S(1)} %collective-permute-done.11.far_ref.refs_0_, bf16[640,384]{1,0:T(8,128)(2,1)S(1)} %collective-permute-done.19.far_ref.refs_1_, bf16[640,384]{1,0:T(8,128)(2,1)S(1)} %collective-permute-done.20.far_ref.refs_2_, ...), custom_call_target="tpu_custom_call" | custom-call | flops 2264924160 | bytes 7471104 | tf_op jit(solution)/shard_map/pallas_call | solution.py:122
  140.2 3.0 %reshape.82 = bf16[1,640,1,2,384]{4,3,1,2,0:T(2,128)(2,1)} reshape(bf16[640,768]{1,0:T(8,128)(2,1)} %shard_map.83) | data formatting | bytes 1966080 | tf_op jit(solution)/shard_map/reshape | solution.py:220
  (112 shorter events, 16.7 us)
Async XLA Ops:
  0.6 13.2 %copy-start = (bf16[80,640]{1,0:T(8,128)(2,1)S(1)}, bf16[80,640]{1,0:T(8,128)(2,1)}, u32[]{:S(2)}) copy-start(bf16[80,640]{1,0:T(8,128)(2,1)} %param.7) | copy-start | bytes 307204
  6.2 14.7 %collective-permute-start.4 = (bf16[80,384]{1,0:T(8,128)(2,1)S(1)}, bf16[80,384]{1,0:T(8,128)(2,1)S(1)}, u32[]{:S(2)}, u32[]{:S(2)}) collective-permute-start(bf16[80,384]{1,0:T(8,128)(2,1)S(1)} %bitcast.95), channel_id=1, source_target_pairs={{0,16},{4,20},{8,24},{12,28},{16,0},{20,4},{24,8},{28,12},{1,17},{... | collective-permute-start | bytes 184328 | tf_op jit(solution)/shard_map/ppermute | solution.py:16
  10.3 14.0 %collective-permute-start.5 = (bf16[80,384]{1,0:T(8,128)(2,1)S(1)}, bf16[80,384]{1,0:T(8,128)(2,1)S(1)}, u32[]{:S(2)}, u32[]{:S(2)}) collective-permute-start(bf16[80,384]{1,0:T(8,128)(2,1)S(1)} %bitcast.94), channel_id=1, source_target_pairs={{0,8},{4,12},{8,0},{12,4},{16,24},{20,28},{24,16},{28,20},{1,9},{5... | collective-permute-start | bytes 184328 | tf_op jit(solution)/shard_map/ppermute | solution.py:16
  12.0 14.4 %collective-permute-start.6 = (bf16[80,384]{1,0:T(8,128)(2,1)S(1)}, bf16[80,384]{1,0:T(8,128)(2,1)S(1)}, u32[]{:S(2)}, u32[]{:S(2)}) collective-permute-start(bf16[80,384]{1,0:T(8,128)(2,1)S(1)} %bitcast.93), channel_id=1, source_target_pairs={{0,24},{4,28},{8,16},{12,20},{16,8},{20,12},{24,0},{28,4},{1,25},{... | collective-permute-start | bytes 184328 | tf_op jit(solution)/shard_map/ppermute | solution.py:16
  12.1 14.4 %collective-permute-start.7 = (bf16[80,384]{1,0:T(8,128)(2,1)S(1)}, bf16[80,384]{1,0:T(8,128)(2,1)S(1)}, u32[]{:S(2)}, u32[]{:S(2)}) collective-permute-start(bf16[80,384]{1,0:T(8,128)(2,1)S(1)} %bitcast.91), channel_id=1, source_target_pairs={{0,4},{4,0},{8,12},{12,8},{16,20},{20,16},{24,28},{28,24},{1,5},{5... | collective-permute-start | bytes 184328 | tf_op jit(solution)/shard_map/ppermute | solution.py:16
  14.0 6.1 %collective-permute-start = (bf16[80,320]{1,0:T(8,128)(2,1)S(1)}, bf16[80,320]{1,0:T(8,128)(2,1)S(1)}, u32[]{:S(2)}, u32[]{:S(2)}) collective-permute-start(bf16[80,320]{1,0:T(8,128)(2,1)S(1)} %constant_dynamic-slice_fusion.16), channel_id=1, source_target_pairs={{0,16},{4,20},{8,24},{12,28},{16,0},{20,4},{24,8},{28,12},{1,17},{... | collective-permute-start | bytes 153608 | tf_op jit(solution)/shard_map/ppermute | solution.py:16
  16.4 7.9 %copy-start.17 = (bf16[640,384]{1,0:T(8,128)(2,1)S(1)}, bf16[640,384]{1,0:T(8,128)(2,1)}, u32[]{:S(2)}) copy-start(bf16[640,384]{1,0:T(8,128)(2,1)} %fusion.3) | copy-start | bytes 1474564
  20.1 9.5 %collective-permute-start.8 = (bf16[80,384]{1,0:T(8,128)(2,1)S(1)}, bf16[80,384]{1,0:T(8,128)(2,1)S(1)}, u32[]{:S(2)}, u32[]{:S(2)}) collective-permute-start(bf16[80,384]{1,0:T(8,128)(2,1)S(1)} %bitcast.98), channel_id=1, source_target_pairs={{0,20},{4,16},{8,28},{12,24},{16,4},{20,0},{24,12},{28,8},{1,21},{... | collective-permute-start | bytes 184328 | tf_op jit(solution)/shard_map/ppermute | solution.py:16
  20.9 10.1 %collective-permute-start.9 = (bf16[80,384]{1,0:T(8,128)(2,1)S(1)}, bf16[80,384]{1,0:T(8,128)(2,1)S(1)}, u32[]{:S(2)}, u32[]{:S(2)}) collective-permute-start(bf16[80,384]{1,0:T(8,128)(2,1)S(1)} %bitcast.97), channel_id=1, source_target_pairs={{0,12},{4,8},{8,4},{12,0},{16,28},{20,24},{24,20},{28,16},{1,13},{... | collective-permute-start | bytes 184328 | tf_op jit(solution)/shard_map/ppermute | solution.py:16
  24.3 7.5 %collective-permute-start.10 = (bf16[80,384]{1,0:T(8,128)(2,1)S(1)}, bf16[80,384]{1,0:T(8,128)(2,1)S(1)}, u32[]{:S(2)}, u32[]{:S(2)}) collective-permute-start(bf16[80,384]{1,0:T(8,128)(2,1)S(1)} %bitcast.96), channel_id=1, source_target_pairs={{0,28},{4,24},{8,20},{12,16},{16,12},{20,8},{24,4},{28,0},{1,29},{... | collective-permute-start | bytes 184328 | tf_op jit(solution)/shard_map/ppermute | solution.py:16
  26.4 12.3 %collective-permute-start.12 = (bf16[80,384]{1,0:T(8,128)(2,1)S(1)}, bf16[80,384]{1,0:T(8,128)(2,1)S(1)}, u32[]{:S(2)}, u32[]{:S(2)}) collective-permute-start(bf16[80,384]{1,0:T(8,128)(2,1)S(1)} %bitcast.92), channel_id=1, source_target_pairs={{0,16},{4,20},{8,24},{12,28},{16,0},{20,4},{24,8},{28,12},{1,17},{... | collective-permute-start | bytes 184328 | tf_op jit(solution)/shard_map/ppermute | solution.py:16
  26.5 13.1 %collective-permute-start.13 = (bf16[80,384]{1,0:T(8,128)(2,1)S(1)}, bf16[80,384]{1,0:T(8,128)(2,1)S(1)}, u32[]{:S(2)}, u32[]{:S(2)}) collective-permute-start(bf16[80,384]{1,0:T(8,128)(2,1)S(1)} %bitcast.90), channel_id=1, source_target_pairs={{0,8},{4,12},{8,0},{12,4},{16,24},{20,28},{24,16},{28,20},{1,9},{5... | collective-permute-start | bytes 184328 | tf_op jit(solution)/shard_map/ppermute | solution.py:16
  29.6 18.6 %collective-permute-start.14 = (bf16[80,384]{1,0:T(8,128)(2,1)S(1)}, bf16[80,384]{1,0:T(8,128)(2,1)S(1)}, u32[]{:S(2)}, u32[]{:S(2)}) collective-permute-start(bf16[80,384]{1,0:T(8,128)(2,1)S(1)} %bitcast.89), channel_id=1, source_target_pairs={{0,24},{4,28},{8,16},{12,20},{16,8},{20,12},{24,0},{28,4},{1,25},{... | collective-permute-start | bytes 184328 | tf_op jit(solution)/shard_map/ppermute | solution.py:16
  31.0 17.3 %collective-permute-start.15 = (bf16[80,384]{1,0:T(8,128)(2,1)S(1)}, bf16[80,384]{1,0:T(8,128)(2,1)S(1)}, u32[]{:S(2)}, u32[]{:S(2)}) collective-permute-start(bf16[80,384]{1,0:T(8,128)(2,1)S(1)} %bitcast.88), channel_id=1, source_target_pairs={{0,4},{4,0},{8,12},{12,8},{16,20},{20,16},{24,28},{28,24},{1,5},{5... | collective-permute-start | bytes 184328 | tf_op jit(solution)/shard_map/ppermute | solution.py:16
  31.8 5.2 %collective-permute-start.1 = (bf16[160,320]{1,0:T(8,128)(2,1)S(1)}, bf16[160,320]{1,0:T(8,128)(2,1)S(1)}, u32[]{:S(2)}, u32[]{:S(2)}) collective-permute-start(bf16[160,320]{1,0:T(8,128)(2,1)S(1)} %pad_maximum_fusion.6), channel_id=1, source_target_pairs={{0,8},{4,12},{8,0},{12,4},{16,24},{20,28},{24,16},{28,20},{1,9},{5... | collective-permute-start | bytes 307208 | tf_op jit(solution)/shard_map/ppermute | solution.py:16
  37.0 11.3 %collective-permute-start.16 = (bf16[80,384]{1,0:T(8,128)(2,1)S(1)}, bf16[80,384]{1,0:T(8,128)(2,1)S(1)}, u32[]{:S(2)}, u32[]{:S(2)}) collective-permute-start(bf16[80,384]{1,0:T(8,128)(2,1)S(1)} %bitcast.87), channel_id=1, source_target_pairs={{0,20},{4,16},{8,28},{12,24},{16,4},{20,0},{24,12},{28,8},{1,21},{... | collective-permute-start | bytes 184328 | tf_op jit(solution)/shard_map/ppermute | solution.py:16
  38.6 7.6 %collective-permute-start.2 = (bf16[320,320]{1,0:T(8,128)(2,1)S(1)}, bf16[320,320]{1,0:T(8,128)(2,1)S(1)}, u32[]{:S(2)}, u32[]{:S(2)}) collective-permute-start(bf16[320,320]{1,0:T(8,128)(2,1)S(1)} %pad_maximum_fusion.5), channel_id=1, source_target_pairs={{0,4},{4,0},{8,12},{12,8},{16,20},{20,16},{24,28},{28,24},{1,5},{5... | collective-permute-start | bytes 614408 | tf_op jit(solution)/shard_map/ppermute | solution.py:16
  39.6 8.8 %collective-permute-start.17 = (bf16[80,384]{1,0:T(8,128)(2,1)S(1)}, bf16[80,384]{1,0:T(8,128)(2,1)S(1)}, u32[]{:S(2)}, u32[]{:S(2)}) collective-permute-start(bf16[80,384]{1,0:T(8,128)(2,1)S(1)} %bitcast.86), channel_id=1, source_target_pairs={{0,12},{4,8},{8,4},{12,0},{16,28},{20,24},{24,20},{28,16},{1,13},{... | collective-permute-start | bytes 184328 | tf_op jit(solution)/shard_map/ppermute | solution.py:16
  46.2 7.0 %collective-permute-start.18 = (bf16[80,384]{1,0:T(8,128)(2,1)S(1)}, bf16[80,384]{1,0:T(8,128)(2,1)S(1)}, u32[]{:S(2)}, u32[]{:S(2)}) collective-permute-start(bf16[80,384]{1,0:T(8,128)(2,1)S(1)} %bitcast.85), channel_id=1, source_target_pairs={{0,28},{4,24},{8,20},{12,16},{16,12},{20,8},{24,4},{28,0},{1,29},{... | collective-permute-start | bytes 184328 | tf_op jit(solution)/shard_map/ppermute | solution.py:16
  48.2 1.9 %collective-permute-start.3 = (bf16[640,320]{1,0:T(8,128)(2,1)S(1)}, bf16[640,320]{1,0:T(8,128)(2,1)S(1)}, u32[]{:S(2)}, u32[]{:S(2)}) collective-permute-start(bf16[640,320]{1,0:T(8,128)(2,1)S(1)} %pad_maximum_fusion.2), channel_id=1, source_target_pairs={{0,1},{1,0},{2,3},{3,2},{4,5},{5,4},{6,7},{7,6},{8,9},{9,8},{10,11... | collective-permute-start | bytes 1228808 | tf_op jit(solution)/shard_map/ppermute | solution.py:16
  51.2 23.9 %copy-start.15 = (bf16[640,384]{1,0:T(8,128)(2,1)}, bf16[640,384]{1,0:T(8,128)(2,1)S(1)}, u32[]{:S(2)}) copy-start(bf16[640,384]{1,0:T(8,128)(2,1)S(1)} %convolution_convert_fusion.1) | copy-start | bytes 1474564
  51.2 14.1 %collective-permute-start.11 = (bf16[640,384]{1,0:T(8,128)(2,1)S(1)}, bf16[640,384]{1,0:T(8,128)(2,1)S(1)}, u32[]{:S(2)}, u32[]{:S(2)}) collective-permute-start(bf16[640,384]{1,0:T(8,128)(2,1)S(1)} %convolution_convert_fusion.1), channel_id=1, source_target_pairs={{0,2},{1,3},{2,0},{3,1},{4,6},{5,7},{6,4},{7,5},{8,10},{9,11},{10,... | collective-permute-start | bytes 1474568 | tf_op jit(solution)/shard_map/ppermute | solution.py:197
  54.1 21.0 %copy-start.16 = (bf16[640,384]{1,0:T(8,128)(2,1)}, bf16[640,384]{1,0:T(8,128)(2,1)S(1)}, u32[]{:S(2)}) copy-start(bf16[640,384]{1,0:T(8,128)(2,1)S(1)} %convolution_convert_fusion) | copy-start | bytes 1474564
  54.1 21.0 %collective-permute-start.19 = (bf16[640,384]{1,0:T(8,128)(2,1)S(1)}, bf16[640,384]{1,0:T(8,128)(2,1)S(1)}, u32[]{:S(2)}, u32[]{:S(2)}) collective-permute-start(bf16[640,384]{1,0:T(8,128)(2,1)S(1)} %convolution_convert_fusion), channel_id=1, source_target_pairs={{0,2},{1,3},{2,0},{3,1},{4,6},{5,7},{6,4},{7,5},{8,10},{9,11},{10,... | collective-permute-start | bytes 1474568 | tf_op jit(solution)/shard_map/ppermute | solution.py:197
  65.3 12.2 %collective-permute-start.20 = (bf16[640,384]{1,0:T(8,128)(2,1)S(1)}, bf16[640,384]{1,0:T(8,128)(2,1)S(1)}, u32[]{:S(2)}, u32[]{:S(2)}) collective-permute-start(bf16[640,384]{1,0:T(8,128)(2,1)S(1)} %collective-permute-done.11.far_ref.refs_0_), channel_id=1, source_target_pairs={{0,24},{4,28},{8,0},{12,4},{16,8},{20,12},{24,16},{28,20},{1,25},{... | collective-permute-start | bytes 1474568 | tf_op jit(solution)/shard_map/ppermute | solution.py:22
  75.1 12.5 %collective-permute-start.21 = (bf16[640,384]{1,0:T(8,128)(2,1)S(1)}, bf16[640,384]{1,0:T(8,128)(2,1)S(1)}, u32[]{:S(2)}, u32[]{:S(2)}) collective-permute-start(bf16[640,384]{1,0:T(8,128)(2,1)S(1)} %collective-permute-done.19.far_ref.refs_1_), channel_id=1, source_target_pairs={{0,24},{4,28},{8,0},{12,4},{16,8},{20,12},{24,16},{28,20},{1,25},{... | collective-permute-start | bytes 1474568 | tf_op jit(solution)/shard_map/ppermute | solution.py:22
  78.4 10.9 %copy-start.18 = (f32[8,2]{0,1:T(2,128)S(1)}, f32[8,2]{0,1:T(2,128)}, u32[]{:S(2)}) copy-start(f32[8,2]{0,1:T(2,128)} %param.8) | copy-start | bytes 196
  78.4 11.0 %copy-start.1 = (f32[4,384]{1,0:T(4,128)S(1)}, f32[4,384]{1,0:T(4,128)}, u32[]{:S(2)}) copy-start(f32[4,384]{1,0:T(4,128)} %row_ref.11) | copy-start | bytes 18436
  78.4 23.0 %collective-permute-start.22 = (bf16[640,384]{1,0:T(8,128)(2,1)}, bf16[640,384]{1,0:T(8,128)(2,1)S(1)}, u32[]{:S(2)}, u32[]{:S(2)}) collective-permute-start(bf16[640,384]{1,0:T(8,128)(2,1)} %broadcast_select_fusion.1), channel_id=1, source_target_pairs={{0,4},{4,0},{8,12},{12,8},{16,20},{20,16},{24,28},{28,24},{1,5},{5... | collective-permute-start | bytes 1474568 | tf_op jit(solution)/shard_map/ppermute | solution.py:16
  88.4 15.1 %collective-permute-start.23 = (bf16[640,384]{1,0:T(8,128)(2,1)}, bf16[640,384]{1,0:T(8,128)(2,1)S(1)}, u32[]{:S(2)}, u32[]{:S(2)}) collective-permute-start(bf16[640,384]{1,0:T(8,128)(2,1)} %broadcast_select_fusion), channel_id=1, source_target_pairs={{0,4},{4,0},{8,12},{12,8},{16,20},{20,16},{24,28},{28,24},{1,5},{5... | collective-permute-start | bytes 1474568 | tf_op jit(solution)/shard_map/ppermute | solution.py:16
  89.5 1.3 copy-start.2
  89.6 1.3 copy-start.3
  92.9 0.8 copy-start.13
  95.7 2.0 %copy-start.4 = (bf16[768,384]{1,0:T(8,128)(2,1)}, bf16[768,384]{1,0:T(8,128)(2,1)S(1)}, u32[]{:S(2)}) copy-start(bf16[768,384]{1,0:T(8,128)(2,1)S(1)} %get-tuple-element.16.refs_7_) | copy-start | bytes 1769476
  97.8 0.8 copy-start.6
  100.6 0.8 copy-start.8
  103.4 2.0 %copy-start.10 = (bf16[768,384]{1,0:T(8,128)(2,1)}, bf16[768,384]{1,0:T(8,128)(2,1)S(1)}, u32[]{:S(2)}) copy-start(bf16[768,384]{1,0:T(8,128)(2,1)S(1)} %get-tuple-element.22.refs_10_) | copy-start | bytes 1769476
  105.5 0.8 copy-start.12
  110.1 1.5 %collective-permute-start.24 = (bf16[2,2,2,2,36,128]{5,4,3,2,1,0:T(8,128)(2,1)S(1)}, bf16[2,2,2,2,36,128]{5,4,3,2,1,0:T(8,128)(2,1)S(1)}, u32[]{:S(2)}, u32[]{:S(2)}) collective-permute-start(bf16[2,2,2,2,36,128]{5,4,3,2,1,0:T(8,128)(2,1)S(1)} %fusion), channel_id=1, source_target_pairs={{0,1},{1,0},{2,3},{3,2},{4,5},{5,4},{6,7},{7,6},{8,9},{9,8},{10,11... | collective-permute-start | bytes 442376 | tf_op jit(solution)/shard_map/ppermute | solution.py:16
  112.6 4.7 %collective-permute-start.25 = (bf16[2,2,2,36,128]{4,3,2,1,0:T(8,128)(2,1)S(1)}, bf16[2,2,2,36,128]{4,3,2,1,0:T(8,128)(2,1)}, u32[]{:S(2)}, u32[]{:S(2)}) collective-permute-start(bf16[2,2,2,36,128]{4,3,2,1,0:T(8,128)(2,1)S(1)} %fusion.1), channel_id=1, source_target_pairs={{0,2},{1,3},{2,0},{3,1},{4,6},{5,7},{6,4},{7,5},{8,10},{9,11},{10,... | collective-permute-start | bytes 221192 | tf_op jit(solution)/shard_map/ppermute | solution.py:16
  118.2 4.1 %collective-permute-start.26 = (bf16[2,2,36,128]{3,2,1,0:T(8,128)(2,1)S(1)}, bf16[2,2,36,128]{3,2,1,0:T(8,128)(2,1)S(1)}, u32[]{:S(2)}, u32[]{:S(2)}) collective-permute-start(bf16[2,2,36,128]{3,2,1,0:T(8,128)(2,1)S(1)} %fusion.4), channel_id=1, source_target_pairs={{0,4},{4,0},{8,12},{12,8},{16,20},{20,16},{24,28},{28,24},{1,5},{5... | collective-permute-start | bytes 110600 | tf_op jit(solution)/shard_map/ppermute | solution.py:16
  122.3 3.8 %collective-permute-start.27 = (bf16[2,36,128]{2,1,0:T(8,128)(2,1)S(1)}, bf16[2,36,128]{2,1,0:T(8,128)(2,1)S(1)}, u32[]{:S(2)}, u32[]{:S(2)}) collective-permute-start(bf16[2,36,128]{2,1,0:T(8,128)(2,1)S(1)} %fusion.5), channel_id=1, source_target_pairs={{0,8},{4,12},{8,0},{12,4},{16,24},{20,28},{24,16},{28,20},{1,9},{5... | collective-permute-start | bytes 55304 | tf_op jit(solution)/shard_map/ppermute | solution.py:16
  126.2 17.0 %collective-permute-start.28 = (bf16[36,128]{1,0:T(8,128)(2,1)S(1)}, bf16[36,128]{1,0:T(8,128)(2,1)S(1)}, u32[]{:S(2)}, u32[]{:S(2)}) collective-permute-start(bf16[36,128]{1,0:T(8,128)(2,1)S(1)} %fusion.7), channel_id=1, source_target_pairs={{0,16},{4,20},{8,24},{12,28},{16,0},{20,4},{24,8},{28,12},{1,17},{... | collective-permute-start | bytes 27656 | tf_op jit(solution)/shard_map/ppermute | solution.py:16
  129.0 1.1 copy-start.5
  130.1 1.1 copy-start.7
  131.1 1.1 copy-start.9
  132.2 1.1 copy-start.11
  133.3 1.1 copy-start.14

commit v2 on v1

v2 whole, which is shorter than its diff:
```python
import functools

import jax
import jax.numpy as jnp
from jax import lax
from jax.experimental import pallas as pl
from jax.experimental.pallas import tpu as pltpu
from jax.sharding import PartitionSpec as P

WINDOW = 3
DIRECT = 8


def flip(value, axis, mask):
    pairs = [(source, source ^ mask) for source in range(lax.axis_size(axis))]
    return lax.ppermute(value, axis, pairs)


def from_ahead(value, axis, steps):
    count = lax.axis_size(axis)
    pairs = [(source, (source - steps) % count) for source in range(count)]
    return lax.ppermute(value, axis, pairs)


def is_power(count):
    return count & (count - 1) == 0


def bits_of(count):
    return [1 << bit for bit in reversed(range(count.bit_length() - 1))]


def doubled(count):
    order = [0]
    for mask in bits_of(count):
        order = order + [place ^ mask for place in order]
    return order


def rows_of(refs):
    return refs[0][...] if len(refs) == 1 else jnp.concatenate([ref[...] for ref in refs], axis=0)


def product(left, right, dims):
    return lax.dot_general(left, right, ((dims[0], dims[1]), ((), ())), preferred_element_type=jnp.float32)


def fit_kernel(halves, own_count, *refs):
    metric_refs, refs = refs[:halves], refs[halves:]
    own_refs, facing_refs, outs = refs[:own_count], refs[own_count:-2], refs[-2:]
    low_bit = lax.axis_index("narrow") % 2
    for sources, out_ref in zip((own_refs, facing_refs), outs):
        rows = rows_of(sources)
        for place, metric_ref in enumerate(metric_refs):
            part = product(metric_ref[...], rows, ((0,), (0,))).astype(out_ref.dtype)
            if halves == 1:
                out_ref[...] = part
            else:
                start = (low_bit if place == 0 else 1 - low_bit) * part.shape[0]
                out_ref[pl.ds(pl.multiple_of(start, part.shape[0]), part.shape[0]), :] = part


def fit(metric, own, facing):
    aux_count = sum(part.shape[1] for part in metric)
    shape = jax.ShapeDtypeStruct((aux_count, own[0].shape[1]), own[0].dtype)
    flops = 4 * aux_count * aux_count * own[0].shape[1]
    moved = 2 * (aux_count * aux_count + 4 * aux_count * own[0].shape[1])
    operands = [*metric, *own, *facing]
    return pl.pallas_call(
        functools.partial(fit_kernel, len(metric), len(own)),
        out_shape=(shape, shape),
        in_specs=[VMEM] * len(operands),
        out_specs=(VMEM, VMEM),
        compiler_params=pltpu.CompilerParams(vmem_limit_bytes=32 * 1024 * 1024),
        cost_estimate=pl.CostEstimate(flops=flops, bytes_accessed=moved, transcendentals=0),
    )(*operands)


def far_rows(refs):
    if len(refs) == 1:
        return refs[0][...]
    odd = lax.axis_index("wide") % 2 == 1
    return jnp.where(odd, refs[0][...], refs[1][...])


def pair_kernel(offset, slot, fars, sums, last, scale_by, *refs):
    occ_ref, kpoint_ref, count_ref, row_ref, column_ref = refs[:5]
    occ_slots = occ_ref.shape[1]
    own_refs, refs = refs[5 : 5 + occ_slots], refs[5 + occ_slots :]
    far_refs, refs = refs[:fars], refs[fars:]
    sum_refs, outs = refs[:sums], refs[sums:]
    group_count, wide_count = kpoint_ref.shape
    vir_count = row_ref.shape[1]
    group = lax.axis_index("narrow")
    block = lax.axis_index("wide")
    partner = lax.rem(group + group_count // 2, group_count)
    other = lax.rem(block + offset, wide_count)
    spot = lax.broadcasted_iota(jnp.int32, column_ref.shape, 1)
    vir_own = jnp.sum(jnp.where(spot == group, column_ref[...], 0.0), axis=1, keepdims=True)
    vir_far = row_ref[pl.ds(partner, 1), :]
    occ_far = occ_ref[kpoint_ref[partner, other], slot]
    live_far = slot < count_ref[partner, other]
    far = far_rows(far_refs)
    total = None
    for i in range(occ_slots):
        columns = slice(i * vir_count, (i + 1) * vir_count)
        coulomb = product(own_refs[i][...], far, ((0,), (0,)))
        occ = occ_ref[kpoint_ref[group, block], i] + occ_far
        live = jnp.logical_and(i < count_ref[group, block], live_far)
        scale = jnp.where(live, 1.0, 0.0).astype(jnp.float32)
        amplitude = coulomb * (scale / ((occ - vir_own) - vir_far))
        mixed = (2.0 * amplitude - amplitude.T).astype(jnp.bfloat16)
        if last:
            outs[-1][columns, :] = mixed
        else:
            three = product(far, mixed, ((1,), (1,)))
            outs[-1][:, columns] = three if not sums else sum_refs[1][:, columns] + three
        term = product(mixed, amplitude.astype(jnp.bfloat16), ((1,), (1,)))
        total = term if total is None else total + term
    if sums:
        total = sum_refs[0][...] + total
    if not last:
        outs[0][...] = total
        return
    total = total * scale_by
    if len(outs) == 2:
        outs[0][...] = total
        return
    sent_ref, kept_ref = outs[:2]
    part = vir_count // (wide_count * group_count)
    order = halving_order(wide_count, group_count)
    total = jnp.concatenate([total[part * place : part * (place + 1)] for place in order], axis=0)
    half = vir_count // 2
    low = group % 2 == 0
    sent_ref[...] = jnp.where(low, total[half:], total[:half]).astype(jnp.bfloat16)
    kept_ref[...] = jnp.where(low, total[:half], total[half:])


def gamma_kernel(sum_ref, mixed_ref, *refs):
    far = far_rows(refs[:-1])
    refs[-1][...] = (sum_ref[...] + product(far, mixed_ref[...], ((1,), (1,)))).astype(refs[-1].dtype)


VMEM = pl.BlockSpec(memory_space=pltpu.VMEM)
SMEM = pl.BlockSpec(memory_space=pltpu.SMEM)


def pair_terms(offset, slot, small, own, far, sums, last=False, scale_by=1.0):
    aux_count, vir_count = far[0].shape
    width = len(own) * vir_count
    density = jax.ShapeDtypeStruct((vir_count, vir_count), jnp.float32)
    gamma = jax.ShapeDtypeStruct((aux_count, width), jnp.float32)
    mixed = jax.ShapeDtypeStruct((width, vir_count), jnp.bfloat16)
    halves = [jax.ShapeDtypeStruct((vir_count // 2, vir_count), kind) for kind in (jnp.bfloat16, jnp.float32)]
    split = vir_count % (lax.axis_size("wide") * lax.axis_size("narrow")) == 0
    shapes = ((*halves, mixed) if split else (density, mixed)) if last else (density, gamma)
    sums = sums[:1] if last else sums
    operands = [*small, *own, *far, *sums]
    flops = 4 * aux_count * width * vir_count + 2 * width * vir_count * vir_count
    moved = 2 * aux_count * (width + vir_count) + 8 * vir_count * vir_count + 8 * aux_count * width
    return pl.pallas_call(
        functools.partial(pair_kernel, offset, slot, len(far), len(sums), last, scale_by),
        out_shape=shapes,
        in_specs=[SMEM] * 3 + [VMEM] * (len(operands) - 3),
        out_specs=tuple([VMEM] * len(shapes)),
        compiler_params=pltpu.CompilerParams(vmem_limit_bytes=32 * 1024 * 1024),
        cost_estimate=pl.CostEstimate(flops=flops, bytes_accessed=moved, transcendentals=0),
    )(*operands)


def three_index(gamma, mixed, far):
    aux_count, width = gamma.shape
    vir_count = mixed.shape[1]
    return pl.pallas_call(
        gamma_kernel,
        out_shape=jax.ShapeDtypeStruct((aux_count, width), jnp.bfloat16),
        in_specs=[VMEM] * (2 + len(far)),
        out_specs=VMEM,
        compiler_params=pltpu.CompilerParams(vmem_limit_bytes=32 * 1024 * 1024),
        cost_estimate=pl.CostEstimate(
            flops=2 * aux_count * width * vir_count, bytes_accessed=6 * gamma.size, transcendentals=0
        ),
    )(gamma, mixed, *far)


def halving_stages(wide_count, group_count):
    stages = [("narrow", mask) for mask in reversed(bits_of(group_count))]
    return stages + [("wide", mask) for mask in reversed(bits_of(wide_count))]


def halving_order(wide_count, group_count):
    order = [0]
    for axis, mask in reversed(halving_stages(wide_count, group_count)):
        step = mask * group_count if axis == "wide" else mask
        order = order + [place + step for place in order]
    return order


def halved_sum(sent, kept, beside):
    stages = halving_stages(lax.axis_size("wide"), lax.axis_size("narrow"))
    for position, (axis, mask) in enumerate(stages):
        value = kept + flip(sent, axis, mask).astype(jnp.float32)
        if position + 1 < len(stages):
            axis, mask = stages[position + 1]
            bit = (lax.axis_index(axis) // mask) % 2
            half = value.shape[0] // 2
            sent = lax.dynamic_slice_in_dim(value, (1 - bit) * half, half, 0).astype(jnp.bfloat16)
            kept = lax.dynamic_slice_in_dim(value, bit * half, half, 0)
            sent = after(sent, beside) if position == 1 else sent
    return value.reshape(-1)


def pack_kernel(slot, raw_ref, *outs):
    block = lax.axis_index("wide")
    for place, out_ref in zip(doubled(raw_ref.shape[1]), outs):
        for part in range(2):
            out_ref[part] = raw_ref[:, jnp.bitwise_xor(block, place ^ part), slot, :]


def packed(raw, slot):
    rows, block_count, _, vir_count = raw.shape
    shape = jax.ShapeDtypeStruct((2, rows, vir_count), raw.dtype)
    count = block_count // 2
    return pl.pallas_call(
        functools.partial(pack_kernel, slot),
        out_shape=tuple([shape] * count),
        in_specs=[VMEM],
        out_specs=tuple([VMEM] * count),
        compiler_params=pltpu.CompilerParams(vmem_limit_bytes=32 * 1024 * 1024),
        cost_estimate=pl.CostEstimate(flops=0, bytes_accessed=6 * raw.size, transcendentals=0),
    )(raw)


def after(value, *earlier):
    return lax.optimization_barrier((value, *earlier))[0]


def gathered_rows(raw, metric):
    wide_count, group_count = lax.axis_size("wide"), lax.axis_size("narrow")
    half_turn = [(source, (source + group_count // 2) % group_count) for source in range(group_count)]
    occ_slots = raw.shape[2]
    half = metric.shape[1] // 2
    places = doubled(wide_count)[: wide_count // 2]
    stages = bits_of(wide_count)
    part = lax.dynamic_slice_in_dim(metric, lax.axis_index("narrow") % 2 * half, half, 1)
    steps = []
    for mask in stages:
        steps.append(flip(part, "wide", mask))
        part = jnp.concatenate([part, steps[-1]], axis=0)
    own, facing = [], []
    for slot in range(occ_slots):
        source = after(raw, steps[0], *earliest) if slot else raw
        messages = packed(source, slot)
        arrived = [flip(message, "wide", place) for message, place in zip(messages[1:], places[1:])]
        earliest = arrived[-1:]
        arrived = [messages[0], *arrived]
        mine, theirs = [jnp.concatenate([message[part] for message in arrived], axis=0) for part in range(2)]
        if slot:
            mine = after(mine, facing[-1][0])
        else:
            theirs = after(theirs, steps[-2])
        first = lax.ppermute(mine, "narrow", half_turn)
        received = flip(theirs, "wide", 1)
        if slot == 0:
            sent = after(received, first, steps[-1])
        else:
            sent = after(received, first)
        own.append([mine, received])
        facing.append([first, lax.ppermute(sent, "narrow", half_turn)])
    return own, facing, [part, flip(part, "narrow", 1)]


def scattered_sum(density):
    wide_count = lax.axis_size("wide")
    group_count = lax.axis_size("narrow")
    wide_bits, narrow_bits = bits_of(wide_count), bits_of(group_count)
    part = density.size // (wide_count * group_count)
    lane = 128 if part % 128 == 0 else part
    value = density.reshape([2] * (len(wide_bits) + len(narrow_bits)) + [part // lane, lane])
    stages = [("narrow", mask, len(wide_bits) + place) for place, mask in enumerate(narrow_bits)]
    stages = stages[::-1] + [("wide", mask, place) for place, mask in reversed(list(enumerate(wide_bits)))]
    for axis, mask, dim in stages:
        bit = (lax.axis_index(axis) // mask) % 2
        sent = lax.dynamic_index_in_dim(value, 1 - bit, dim, keepdims=False).astype(jnp.bfloat16)
        kept = lax.dynamic_index_in_dim(value, bit, dim, keepdims=False)
        value = kept + flip(sent, axis, mask).astype(jnp.float32)
    return value.reshape(-1)


def shards(raw_ints, metric_root, occ_energy, vir_energy, block_kpoint, occ_count):
    _, aux_rows, block_count, occ_slots, vir_count = raw_ints.shape
    wide_count = lax.axis_size("wide")
    group_count = lax.axis_size("narrow")
    my_block = lax.axis_index("wide")
    direct = wide_count <= DIRECT and is_power(wide_count) and wide_count > 2 and group_count % 2 == 0
    small = (occ_energy, block_kpoint, occ_count, vir_energy, vir_energy.T)
    half_turn = [(source, (source + group_count // 2) % group_count) for source in range(group_count)]
    to_even = [(source, source - 1) for source in range(1, wide_count, 2)]
    to_odd = [(source, source + 1) for source in range(0, wide_count, 2)]

    own_rows, facing_rows = [], []
    if direct:
        own_rows, facing_rows, metric = gathered_rows(raw_ints[0], metric_root)
    else:
        metric = [lax.all_gather(metric_root, "wide", axis=0, tiled=True)]
        for slot in range(occ_slots):
            blocks = jnp.transpose(raw_ints[0, :, :, slot, :], (1, 0, 2))
            rows = lax.all_to_all(blocks, "wide", split_axis=0, concat_axis=0, tiled=True)
            rows = rows.reshape(wide_count * aux_rows, vir_count)
            own_rows.append([rows])
            facing_rows.append([lax.ppermute(rows, "narrow", half_turn)])

    own, facing = zip(*[fit(metric, *rows) for rows in zip(own_rows, facing_rows)])
    aux_count = own[0].shape[0]
    pair = functools.partial(pair_terms, small=small, own=own)
    second, first = [], []
    sums = ()
    for slot in range(occ_slots):
        source = after(facing[slot], *sums) if slot else facing[slot]
        second.append(from_ahead(source, "wide", 2))
        if wide_count % 2 == 0:
            first.append([lax.ppermute(facing[slot], "wide", to_even)])
        else:
            first.append([from_ahead(facing[slot], "wide", 1)])
        sums = pair(0, slot, far=[facing[slot]], sums=sums)
    for slot in range(occ_slots):
        if wide_count % 2 == 0:
            source = after(second[slot], *sums)
            first[slot].insert(0, lax.ppermute(source, "wide", to_odd))
        sums = pair(2, slot, far=[second[slot]], sums=sums)
    for slot in range(occ_slots - 1):
        sums = pair(1, slot, far=first[slot], sums=sums)
    norm_scale = 1.0 / (group_count * wide_count * vir_count)
    *terms, mixed = pair(1, occ_slots - 1, far=first[-1], sums=sums, last=True, scale_by=norm_scale)
    gamma = three_index(sums[1], mixed, first[-1])
    if len(terms) == 2:
        virt_density = halved_sum(*terms, gamma)
    else:
        virt_density = scattered_sum(*terms)
    return gamma.reshape(1, aux_count, 1, occ_slots, vir_count), virt_density


def solution(mesh):
    placed = (P("narrow", "wide", None, None, None), P("wide", None), P(), P(), P(), P())
    return jax.shard_map(
        shards,
        mesh=mesh,
        in_specs=placed,
        out_specs=(P("narrow", None, "wide", None, None), P(("wide", "narrow"))),
        check_vma=False,
    )
```

time: 144 us -> 114 us (0.79)
  local copies, waits for them, and re-layouts: 21.5 us -> 7.88 us
  starting transfers between devices: 44.5 us -> 37.4 us
  waiting for transfers between devices: 50.3 us -> 43.5 us
  other arithmetic: 6.7 us -> 2.16 us
  Pallas kernels: 17.9 us -> 21.7 us
  matrix products: 1.59 us -> 0 us
    ppermute x25 -> x17, starting transfers between devices: 36.4 us -> 21.9 us  [flip(): return lax.ppermute(value, axis, pairs)]
    ppermute x2 -> x8, starting transfers between devices: 3.11 us -> 11.9 us  [the longest x2 6.68 us: shards(): first[slot].insert(0, lax.ppermute(source, 'wide', to_odd))]
    ppermute x2, waiting for transfers between devices: 8.26 us -> 0.01 us  [from_ahead(): return lax.ppermute(value, axis, pairs)]
    unnamed x68 -> x28, local copies, waits for them, and re-layouts: 9.85 us -> 5.13 us
    ppermute x25 -> x17, waiting for transfers between devices: 25.1 us -> 29.5 us  [flip(): return lax.ppermute(value, axis, pairs)]
    pallas_call x7 -> x11, Pallas kernels: 17.9 us -> 21.7 us  [the longest x6 16.5 us: pair_terms(): pl.pallas_call(functools.partial(pair_kernel, offset, slot, len(far), len...]
    slice x1 -> x0, local copies, waits for them, and re-layouts: 3.19 us -> none  [shards(): blocks = jnp.transpose(raw_ints[0, :, :, slot, :], (1, 0, 2))]
    ppermute x2 -> x8, waiting for transfers between devices: 16.9 us -> 14 us  [the longest x2 7.38 us: shards(): first[slot].insert(0, lax.ppermute(source, 'wide', to_odd))]
  transfers between devices with their start and end apart: 29 -> 27, of which waited for: 12 -> 13; matrix products, arithmetic and copies ran while one was open for 6% -> 2% of each run, Pallas kernels for 11% -> 17%
where the time goes in v2:
time: 114 us
  waiting for transfers between devices  43.5 us (38%)
  starting transfers between devices  37.4 us (33%)
  Pallas kernels  21.7 us (19%)
  local copies, waits for them, and re-layouts  7.88 us (7%)
  other arithmetic  2.16 us (2%)
    ppermute x17, waiting for transfers between devices, flip(): return lax.ppermute(value, axis, pairs)  29.5 us
    ppermute x17, starting transfers between devices, flip(): return lax.ppermute(value, axis, pairs)  21.9 us
    pallas_call x6, Pallas kernels, pair_terms(): pl.pallas_call(functools.partial(pair_kernel, offset, slot, len(far), len...  16.5 us
    ppermute x2, waiting for transfers between devices, shards(): first[slot].insert(0, lax.ppermute(source, 'wide', to_odd))  7.38 us
    ppermute x2, starting transfers between devices, shards(): first[slot].insert(0, lax.ppermute(source, 'wide', to_odd))  6.68 us
    unnamed x28, local copies, waits for them, and re-layouts  5.13 us
    ppermute x2, waiting for transfers between devices, gathered_rows(): facing.append([first, lax.ppermute(sent, 'narrow', half_turn)])  5.01 us
    ppermute x2, starting transfers between devices, from_ahead(): return lax.ppermute(value, axis, pairs)  3.62 us
  transfers between devices with their start and end apart: 27, of which 13 were waited for; matrix products, arithmetic and copies ran while one was open for 2% of the time, Pallas kernels for 17%

profile of v2, /device:TPU:0, one launch (start us, length us, event | category | flops | bytes accessed | tf_op | source)
XLA Modules:
  0.0 113.8 jit_solution(14032610991099325835)
XLA Ops:
  0.7 0.9 copy-done
  1.6 4.1 %collective-permute-start = (bf16[80,320]{1,0:T(8,128)(2,1)S(1)}, bf16[80,320]{1,0:T(8,128)(2,1)S(1)}, u32[]{:S(2)}, u32[]{:S(2)}) collective-permute-start(bf16[80,320]{1,0:T(8,128)(2,1)S(1)} %constant_dynamic-slice_fusion), channel_id=1, source_target_pairs={{0,16},{4,20},{8,24},{12,28},{16,0},{20,4},{24,8},{28,12},{1,17},{... | collective-permute-start | bytes 153608 | tf_op jit(solution)/shard_map/ppermute | solution.py:16
  5.7 1.2 %copy-done.1 = bf16[1,80,8,2,384]{4,3,2,1,0:T(2,128)(2,1)S(1)} copy-done((bf16[1,80,8,2,384]{4,3,2,1,0:T(2,128)(2,1)S(1)}, bf16[1,80,8,2,384]{4,3,2,1,0:T(2,128)(2,1)}, u32[]{:S(2)}) %copy-start.1) | copy-done | bytes 983064
  6.9 1.1 shard_map.77
  8.1 1.9 %collective-permute-start.5 = (bf16[2,80,384]{2,1,0:T(8,128)(2,1)S(1)}, bf16[2,80,384]{2,1,0:T(8,128)(2,1)S(1)}, u32[]{:S(2)}, u32[]{:S(2)}) collective-permute-start(bf16[2,80,384]{2,1,0:T(8,128)(2,1)S(1)} %get-tuple-element.38), channel_id=1, source_target_pairs={{0,8},{4,12},{8,0},{12,4},{16,24},{20,28},{24,16},{28,20},{1,9},{5... | collective-permute-start | bytes 368648 | tf_op jit(solution)/shard_map/ppermute | solution.py:16
  10.0 2.5 %collective-permute-start.6 = (bf16[2,80,384]{2,1,0:T(8,128)(2,1)S(1)}, bf16[2,80,384]{2,1,0:T(8,128)(2,1)S(1)}, u32[]{:S(2)}, u32[]{:S(2)}) collective-permute-start(bf16[2,80,384]{2,1,0:T(8,128)(2,1)S(1)} %get-tuple-element.39), channel_id=1, source_target_pairs={{0,24},{4,28},{8,16},{12,20},{16,8},{20,12},{24,0},{28,4},{1,25},{... | collective-permute-start | bytes 368648 | tf_op jit(solution)/shard_map/ppermute | solution.py:16
  13.3 8.2 %collective-permute-done.6 = bf16[2,80,384]{2,1,0:T(8,128)(2,1)S(1)} collective-permute-done((bf16[2,80,384]{2,1,0:T(8,128)(2,1)S(1)}, bf16[2,80,384]{2,1,0:T(8,128)(2,1)S(1)}, u32[]{:S(2)}, u32[]{:S(2)}) %collective-permute-start.6) | collective-permute-done | bytes 122912 | tf_op jit(solution)/shard_map/ppermute | solution.py:16
  21.6 1.6 %collective-permute-start.8 = (bf16[320,384]{1,0:T(8,128)(2,1)S(1)}, bf16[320,384]{1,0:T(8,128)(2,1)S(1)}, u32[]{:S(2)}, u32[]{:S(2)}) collective-permute-start(bf16[320,384]{1,0:T(8,128)(2,1)S(1)} %pad_maximum_fusion.2.refs_2_), channel_id=1, source_target_pairs={{0,2},{1,3},{2,0},{3,1},{4,6},{5,7},{6,4},{7,5},{8,10},{9,11},{10,... | collective-permute-start | bytes 737288 | tf_op jit(solution)/shard_map/ppermute | solution.py:262
  23.1 1.1 shard_map.79
  24.3 0.9 collective-permute-start.10
  25.2 1.0 collective-permute-start.11
  26.2 2.6 %collective-permute-start.12 = (bf16[2,80,384]{2,1,0:T(8,128)(2,1)S(1)}, bf16[2,80,384]{2,1,0:T(8,128)(2,1)S(1)}, u32[]{:S(2)}, u32[]{:S(2)}) collective-permute-start(bf16[2,80,384]{2,1,0:T(8,128)(2,1)S(1)} %get-tuple-element.47), channel_id=1, source_target_pairs={{0,24},{4,28},{8,16},{12,20},{16,8},{20,12},{24,0},{28,4},{1,25},{... | collective-permute-start | bytes 368648 | tf_op jit(solution)/shard_map/ppermute | solution.py:16
  28.8 1.6 %collective-permute-start.2 = (bf16[320,320]{1,0:T(8,128)(2,1)S(1)}, bf16[320,320]{1,0:T(8,128)(2,1)S(1)}, u32[]{:S(2)}, u32[]{:S(2)}) collective-permute-start(bf16[320,320]{1,0:T(8,128)(2,1)S(1)} %pad_maximum_fusion.1), channel_id=1, source_target_pairs={{0,4},{4,0},{8,12},{12,8},{16,20},{20,16},{24,28},{28,24},{1,5},{5... | collective-permute-start | bytes 614408 | tf_op jit(solution)/shard_map/ppermute | solution.py:16
  30.4 4.7 %collective-permute-done.10 = bf16[2,80,384]{2,1,0:T(8,128)(2,1)S(1)} collective-permute-done((bf16[2,80,384]{2,1,0:T(8,128)(2,1)S(1)}, bf16[2,80,384]{2,1,0:T(8,128)(2,1)S(1)}, u32[]{:S(2)}, u32[]{:S(2)}) %collective-permute-start.10) | collective-permute-done | bytes 122912 | tf_op jit(solution)/shard_map/ppermute | solution.py:16
  35.1 1.5 %collective-permute-start.7 = (bf16[320,384]{1,0:T(8,128)(2,1)S(1)}, bf16[320,384]{1,0:T(8,128)(2,1)S(1)}, u32[]{:S(2)}, u32[]{:S(2)}) collective-permute-start(bf16[320,384]{1,0:T(8,128)(2,1)S(1)} %pad_maximum_fusion.3), channel_id=1, source_target_pairs={{0,4},{4,0},{8,12},{12,8},{16,20},{20,16},{24,28},{28,24},{1,5},{5... | collective-permute-start | bytes 737288 | tf_op jit(solution)/shard_map/ppermute | solution.py:16
  38.0 3.8 %collective-permute-done.7.refs_3_ = bf16[320,384]{1,0:T(8,128)(2,1)S(1)} collective-permute-done((bf16[320,384]{1,0:T(8,128)(2,1)S(1)}, bf16[320,384]{1,0:T(8,128)(2,1)S(1)}, u32[]{:S(2)}, u32[]{:S(2)}) %collective-permute-start.7) | collective-permute-done | bytes 245792 | tf_op jit(solution)/shard_map/ppermute | solution.py:16
  42.4 2.1 %collective-permute-done.13.refs_3_ = bf16[320,384]{1,0:T(8,128)(2,1)S(1)} collective-permute-done((bf16[320,384]{1,0:T(8,128)(2,1)S(1)}, bf16[320,384]{1,0:T(8,128)(2,1)S(1)}, u32[]{:S(2)}, u32[]{:S(2)}) %collective-permute-start.13) | collective-permute-done | bytes 245792 | tf_op jit(solution)/shard_map/ppermute | solution.py:16
  44.5 1.6 %collective-permute-done.14.refs_4_ = bf16[320,384]{1,0:T(8,128)(2,1)S(1)} collective-permute-done((bf16[320,384]{1,0:T(8,128)(2,1)S(1)}, bf16[320,384]{1,0:T(8,128)(2,1)S(1)}, u32[]{:S(2)}, u32[]{:S(2)}) %collective-permute-start.14) | collective-permute-done | bytes 245792 | tf_op jit(solution)/shard_map/ppermute | solution.py:262
  46.3 5.0 %collective-permute-done.9.refs_5_ = bf16[320,384]{1,0:T(8,128)(2,1)S(1)} collective-permute-done((bf16[320,384]{1,0:T(8,128)(2,1)S(1)}, bf16[320,384]{1,0:T(8,128)(2,1)S(1)}, u32[]{:S(2)}, u32[]{:S(2)}) %collective-permute-start.9) | collective-permute-done | bytes 245792 | tf_op jit(solution)/shard_map/ppermute | solution.py:269
  51.3 1.1 shard_map.78
  52.5 1.9 %collective-permute-start.16 = (bf16[640,384]{1,0:T(8,128)(2,1)S(1)}, bf16[640,384]{1,0:T(8,128)(2,1)S(1)}, u32[]{:S(2)}, u32[]{:S(2)}) collective-permute-start(bf16[640,384]{1,0:T(8,128)(2,1)S(1)} %get-tuple-element.51.refs_7_), channel_id=1, source_target_pairs={{0,24},{4,28},{8,0},{12,4},{16,8},{20,12},{24,16},{28,20},{1,25},{... | collective-permute-start | bytes 1474568 | tf_op jit(solution)/shard_map/ppermute | solution.py:22
  54.4 1.1 shard_map.80
  55.6 2.9 %shard_map.81 = (f32[384,384]{1,0:T(8,128)S(1)}, f32[640,768]{1,0:T(8,128)S(1)}) custom-call(f32[8,2]{1,0:T(8,128)S(1)} %copy.13.refs_0_, s32[4,8]{1,0:T(4,128)S(1)} %copy-done.8, s32[4,8]{1,0:T(4,128)S(1)} %copy-done.9, f32[4,384]{1,0:T(4,128)S(1)} %copy-done.7, f32[384,4]{1,0:T(8,128)S(1)} %bitcast.35, bf16[640,384]{1,0:T(8,128)(2,1)S(1)} %get-tuple-element.42.refs_5_, ...), custom_call_target="tpu_custom_call" | custom-call | flops 981467136 | bytes 6586368 | tf_op jit(solution)/shard_map/pallas_call | solution.py:161
  58.5 1.7 %collective-permute-start.19 = (bf16[640,384]{1,0:T(8,128)(2,1)S(1)}, bf16[640,384]{1,0:T(8,128)(2,1)S(1)}, u32[]{:S(2)}, u32[]{:S(2)}) collective-permute-start(bf16[640,384]{1,0:T(8,128)(2,1)S(1)} %get-tuple-element.58.refs_7_), channel_id=1, source_target_pairs={{0,24},{4,28},{8,0},{12,4},{16,8},{20,12},{24,16},{28,20},{1,25},{... | collective-permute-start | bytes 1474568 | tf_op jit(solution)/shard_map/ppermute | solution.py:22
  60.2 1.3 %collective-permute-start.18 = (bf16[640,384]{1,0:T(8,128)(2,1)S(1)}, bf16[640,384]{1,0:T(8,128)(2,1)S(1)}, u32[]{:S(2)}, u32[]{:S(2)}) collective-permute-start(bf16[640,384]{1,0:T(8,128)(2,1)S(1)} %get-tuple-element.51.refs_7_), channel_id=1, source_target_pairs={{4,0},{12,8},{20,16},{28,24},{5,1},{13,9},{21,17},{29,25},{6,2},{1... | collective-permute-start | bytes 1474568 | tf_op jit(solution)/shard_map/ppermute | solution.py:322
  61.4 1.3 %collective-permute-start.21 = (bf16[640,384]{1,0:T(8,128)(2,1)S(1)}, bf16[640,384]{1,0:T(8,128)(2,1)S(1)}, u32[]{:S(2)}, u32[]{:S(2)}) collective-permute-start(bf16[640,384]{1,0:T(8,128)(2,1)S(1)} %get-tuple-element.58.refs_7_), channel_id=1, source_target_pairs={{4,0},{12,8},{20,16},{28,24},{5,1},{13,9},{21,17},{29,25},{6,2},{1... | collective-permute-start | bytes 1474568 | tf_op jit(solution)/shard_map/ppermute | solution.py:322
  62.7 2.9 %shard_map.82 = (f32[384,384]{1,0:T(8,128)S(1)}, f32[640,768]{1,0:T(8,128)S(1)}) custom-call(f32[8,2]{1,0:T(8,128)S(1)} %copy.13.refs_0_, s32[4,8]{1,0:T(4,128)S(1)} %copy-done.8, s32[4,8]{1,0:T(4,128)S(1)} %copy-done.9, f32[4,384]{1,0:T(4,128)S(1)} %copy-done.7, f32[384,4]{1,0:T(8,128)S(1)} %bitcast.36, bf16[640,384]{1,0:T(8,128)(2,1)S(1)} %get-tuple-element.42.refs_5_, ...), custom_call_target="tpu_custom_call" | custom-call | flops 981467136 | bytes 6586368 | tf_op jit(solution)/shard_map/pallas_call | solution.py:161
  65.7 4.8 %collective-permute-start.17 = (bf16[640,384]{1,0:T(8,128)(2,1)S(1)}, bf16[640,384]{1,0:T(8,128)(2,1)S(1)}, u32[]{:S(2)}, u32[]{:S(2)}) collective-permute-start(bf16[640,384]{1,0:T(8,128)(2,1)S(1)} %collective-permute-done.16.refs_7_), channel_id=1, source_target_pairs={{0,4},{8,12},{16,20},{24,28},{1,5},{9,13},{17,21},{25,29},{2,6},{1... | collective-permute-start | bytes 1474568 | tf_op jit(solution)/shard_map/ppermute | solution.py:329
  70.5 2.9 %shard_map.83 = (f32[384,384]{1,0:T(8,128)S(1)}, f32[640,768]{1,0:T(8,128)S(1)}) custom-call(f32[8,2]{1,0:T(8,128)S(1)} %copy.13.refs_0_, s32[4,8]{1,0:T(4,128)S(1)} %copy-done.8, s32[4,8]{1,0:T(4,128)S(1)} %copy-done.9, f32[4,384]{1,0:T(4,128)S(1)} %copy-done.7, f32[384,4]{1,0:T(8,128)S(1)} %bitcast.37, bf16[640,384]{1,0:T(8,128)(2,1)S(1)} %get-tuple-element.42.refs_5_, ...), custom_call_target="tpu_custom_call" | custom-call | flops 981467136 | bytes 6586368 | tf_op jit(solution)/shard_map/pallas_call | solution.py:161
  73.4 1.9 %collective-permute-start.20 = (bf16[640,384]{1,0:T(8,128)(2,1)S(1)}, bf16[640,384]{1,0:T(8,128)(2,1)S(1)}, u32[]{:S(2)}, u32[]{:S(2)}) collective-permute-start(bf16[640,384]{1,0:T(8,128)(2,1)S(1)} %collective-permute-done.19.refs_7_), channel_id=1, source_target_pairs={{0,4},{8,12},{16,20},{24,28},{1,5},{9,13},{17,21},{25,29},{2,6},{1... | collective-permute-start | bytes 1474568 | tf_op jit(solution)/shard_map/ppermute | solution.py:329
  75.3 2.9 %shard_map.84 = (f32[384,384]{1,0:T(8,128)S(1)}, f32[640,768]{1,0:T(8,128)S(1)}) custom-call(f32[8,2]{1,0:T(8,128)S(1)} %copy.13.refs_0_, s32[4,8]{1,0:T(4,128)S(1)} %copy-done.8, s32[4,8]{1,0:T(4,128)S(1)} %copy-done.9, f32[4,384]{1,0:T(4,128)S(1)} %copy-done.7, f32[384,4]{1,0:T(8,128)S(1)} %bitcast.38, bf16[640,384]{1,0:T(8,128)(2,1)S(1)} %get-tuple-element.42.refs_5_, ...), custom_call_target="tpu_custom_call" | custom-call | flops 981467136 | bytes 6586368 | tf_op jit(solution)/shard_map/pallas_call | solution.py:161
  78.2 3.7 %collective-permute-done.17.refs_7_ = bf16[640,384]{1,0:T(8,128)(2,1)S(1)} collective-permute-done((bf16[640,384]{1,0:T(8,128)(2,1)S(1)}, bf16[640,384]{1,0:T(8,128)(2,1)S(1)}, u32[]{:S(2)}, u32[]{:S(2)}) %collective-permute-start.17) | collective-permute-done | bytes 491552 | tf_op jit(solution)/shard_map/ppermute | solution.py:329
  82.0 2.9 %shard_map.85 = (f32[384,384]{1,0:T(8,128)S(1)}, f32[640,768]{1,0:T(8,128)S(1)}) custom-call(f32[8,2]{1,0:T(8,128)S(1)} %copy.13.refs_0_, s32[4,8]{1,0:T(4,128)S(1)} %copy-done.8, s32[4,8]{1,0:T(4,128)S(1)} %copy-done.9, f32[4,384]{1,0:T(4,128)S(1)} %copy-done.7, f32[384,4]{1,0:T(8,128)S(1)} %bitcast.39, bf16[640,384]{1,0:T(8,128)(2,1)S(1)} %get-tuple-element.42.refs_5_, ...), custom_call_target="tpu_custom_call" | custom-call | flops 981467136 | bytes 6586368 | tf_op jit(solution)/shard_map/pallas_call | solution.py:161
  84.9 3.7 %collective-permute-done.20.refs_7_.refs_0_ = bf16[640,384]{1,0:T(8,128)(2,1)S(1)} collective-permute-done((bf16[640,384]{1,0:T(8,128)(2,1)S(1)}, bf16[640,384]{1,0:T(8,128)(2,1)S(1)}, u32[]{:S(2)}, u32[]{:S(2)}) %collective-permute-start.20) | collective-permute-done | bytes 491552 | tf_op jit(solution)/shard_map/ppermute | solution.py:329
  88.5 2.0 %shard_map.86 = (bf16[192,384]{1,0:T(8,128)(2,1)S(1)}, f32[192,384]{1,0:T(8,128)S(1)}, bf16[768,384]{1,0:T(8,128)(2,1)S(1)}) custom-call(f32[8,2]{1,0:T(8,128)S(1)} %copy.13.refs_0_, s32[4,8]{1,0:T(4,128)S(1)} %copy-done.8, s32[4,8]{1,0:T(4,128)S(1)} %copy-done.9, f32[4,384]{1,0:T(4,128)S(1)} %copy-done.7, f32[384,4]{1,0:T(8,128)S(1)} %bitcast.40, ...), custom_call_target="tpu_custom_call" | custom-call | flops 981467136 | bytes 6586368 | tf_op jit(solution)/shard_map/pallas_call | solution.py:161
  91.3 1.5 %collective-permute-done.22 = bf16[192,384]{1,0:T(8,128)(2,1)} collective-permute-done((bf16[192,384]{1,0:T(8,128)(2,1)S(1)}, bf16[192,384]{1,0:T(8,128)(2,1)}, u32[]{:S(2)}, u32[]{:S(2)}) %collective-permute-start.22) | collective-permute-done | bytes 147488 | tf_op jit(solution)/shard_map/ppermute | solution.py:16
  92.8 1.0 convert_add_fusion
  94.5 0.8 collective-permute-start.23
  95.3 1.1 copy-done.3
  96.4 1.0 copy-done.5
  98.1 1.1 collective-permute-done.23
  99.2 0.9 convert_add_fusion.1
  100.1 2.5 %collective-permute-start.24 = (bf16[48,384]{1,0:T(8,128)(2,1)S(1)}, bf16[48,384]{1,0:T(8,128)(2,1)S(1)}, u32[]{:S(2)}, u32[]{:S(2)}) collective-permute-start(bf16[48,384]{1,0:T(8,128)(2,1)S(1)} %dynamic-slice_convert_fusion.1), channel_id=1, source_target_pairs={{0,4},{4,0},{8,12},{12,8},{16,20},{20,16},{24,28},{28,24},{1,5},{5... | collective-permute-start | bytes 110600 | tf_op jit(solution)/shard_map/ppermute | solution.py:16
  102.7 1.9 %collective-permute-done.24 = bf16[48,384]{1,0:T(8,128)(2,1)S(1)} collective-permute-done((bf16[48,384]{1,0:T(8,128)(2,1)S(1)}, bf16[48,384]{1,0:T(8,128)(2,1)S(1)}, u32[]{:S(2)}, u32[]{:S(2)}) %collective-permute-start.24) | collective-permute-done | bytes 36896 | tf_op jit(solution)/shard_map/ppermute | solution.py:16
  104.8 3.7 %collective-permute-done.25 = bf16[24,384]{1,0:T(8,128)(2,1)S(1)} collective-permute-done((bf16[24,384]{1,0:T(8,128)(2,1)S(1)}, bf16[24,384]{1,0:T(8,128)(2,1)S(1)}, u32[]{:S(2)}, u32[]{:S(2)}) %collective-permute-start.25) | collective-permute-done | bytes 18464 | tf_op jit(solution)/shard_map/ppermute | solution.py:16
  108.5 1.0 collective-permute-start.26
  109.5 1.2 %reshape.10 = bf16[1,640,1,2,384]{4,3,1,2,0:T(2,128)(2,1)} reshape(bf16[640,768]{1,0:T(8,128)(2,1)S(1)} %shard_map.87) | data formatting | bytes 1966080 | tf_op jit(solution)/shard_map/reshape | solution.py:340
  110.6 2.5 %collective-permute-done.26 = bf16[12,384]{1,0:T(8,128)(2,1)S(1)} collective-permute-done((bf16[12,384]{1,0:T(8,128)(2,1)S(1)}, bf16[12,384]{1,0:T(8,128)(2,1)S(1)}, u32[]{:S(2)}, u32[]{:S(2)}) %collective-permute-start.26) | collective-permute-done | bytes 9248 | tf_op jit(solution)/shard_map/ppermute | solution.py:16
  (72 shorter events, 6.2 us)
Async XLA Ops:
  0.6 0.9 copy-start
  1.6 10.9 %collective-permute-start = (bf16[80,320]{1,0:T(8,128)(2,1)S(1)}, bf16[80,320]{1,0:T(8,128)(2,1)S(1)}, u32[]{:S(2)}, u32[]{:S(2)}) collective-permute-start(bf16[80,320]{1,0:T(8,128)(2,1)S(1)} %constant_dynamic-slice_fusion), channel_id=1, source_target_pairs={{0,16},{4,20},{8,24},{12,28},{16,0},{20,4},{24,8},{28,12},{1,17},{... | collective-permute-start | bytes 153608 | tf_op jit(solution)/shard_map/ppermute | solution.py:16
  5.7 1.2 %copy-start.1 = (bf16[1,80,8,2,384]{4,3,2,1,0:T(2,128)(2,1)S(1)}, bf16[1,80,8,2,384]{4,3,2,1,0:T(2,128)(2,1)}, u32[]{:S(2)}) copy-start(bf16[1,80,8,2,384]{4,3,2,1,0:T(2,128)(2,1)} %param.6) | copy-start | bytes 2949124
  8.1 13.4 %collective-permute-start.4 = (bf16[2,80,384]{2,1,0:T(8,128)(2,1)S(1)}, bf16[2,80,384]{2,1,0:T(8,128)(2,1)S(1)}, u32[]{:S(2)}, u32[]{:S(2)}) collective-permute-start(bf16[2,80,384]{2,1,0:T(8,128)(2,1)S(1)} %get-tuple-element.37), channel_id=1, source_target_pairs={{0,16},{4,20},{8,24},{12,28},{16,0},{20,4},{24,8},{28,12},{1,17},{... | collective-permute-start | bytes 368648 | tf_op jit(solution)/shard_map/ppermute | solution.py:16
  8.1 13.4 %collective-permute-start.5 = (bf16[2,80,384]{2,1,0:T(8,128)(2,1)S(1)}, bf16[2,80,384]{2,1,0:T(8,128)(2,1)S(1)}, u32[]{:S(2)}, u32[]{:S(2)}) collective-permute-start(bf16[2,80,384]{2,1,0:T(8,128)(2,1)S(1)} %get-tuple-element.38), channel_id=1, source_target_pairs={{0,8},{4,12},{8,0},{12,4},{16,24},{20,28},{24,16},{28,20},{1,9},{5... | collective-permute-start | bytes 368648 | tf_op jit(solution)/shard_map/ppermute | solution.py:16
  10.0 11.4 %collective-permute-start.6 = (bf16[2,80,384]{2,1,0:T(8,128)(2,1)S(1)}, bf16[2,80,384]{2,1,0:T(8,128)(2,1)S(1)}, u32[]{:S(2)}, u32[]{:S(2)}) collective-permute-start(bf16[2,80,384]{2,1,0:T(8,128)(2,1)S(1)} %get-tuple-element.39), channel_id=1, source_target_pairs={{0,24},{4,28},{8,16},{12,20},{16,8},{20,12},{24,0},{28,4},{1,25},{... | collective-permute-start | bytes 368648 | tf_op jit(solution)/shard_map/ppermute | solution.py:16
  12.6 16.2 %collective-permute-start.1 = (bf16[160,320]{1,0:T(8,128)(2,1)S(1)}, bf16[160,320]{1,0:T(8,128)(2,1)S(1)}, u32[]{:S(2)}, u32[]{:S(2)}) collective-permute-start(bf16[160,320]{1,0:T(8,128)(2,1)S(1)} %pad_maximum_fusion.6), channel_id=1, source_target_pairs={{0,8},{4,12},{8,0},{12,4},{16,24},{20,28},{24,16},{28,20},{1,9},{5... | collective-permute-start | bytes 307208 | tf_op jit(solution)/shard_map/ppermute | solution.py:16
  21.6 15.8 %collective-permute-start.8 = (bf16[320,384]{1,0:T(8,128)(2,1)S(1)}, bf16[320,384]{1,0:T(8,128)(2,1)S(1)}, u32[]{:S(2)}, u32[]{:S(2)}) collective-permute-start(bf16[320,384]{1,0:T(8,128)(2,1)S(1)} %pad_maximum_fusion.2.refs_2_), channel_id=1, source_target_pairs={{0,2},{1,3},{2,0},{3,1},{4,6},{5,7},{6,4},{7,5},{8,10},{9,11},{10,... | collective-permute-start | bytes 737288 | tf_op jit(solution)/shard_map/ppermute | solution.py:262
  24.3 21.8 %copy-start.12 = (f32[8,2]{0,1:T(2,128)S(1)}, f32[8,2]{0,1:T(2,128)}, u32[]{:S(2)}) copy-start(f32[8,2]{0,1:T(2,128)} %param.8) | copy-start | bytes 196
  24.3 21.9 %copy-start.7 = (f32[4,384]{1,0:T(4,128)S(1)}, f32[4,384]{1,0:T(4,128)}, u32[]{:S(2)}) copy-start(f32[4,384]{1,0:T(4,128)} %refs_3_.11) | copy-start | bytes 18436
  24.3 10.8 %collective-permute-start.10 = (bf16[2,80,384]{2,1,0:T(8,128)(2,1)S(1)}, bf16[2,80,384]{2,1,0:T(8,128)(2,1)S(1)}, u32[]{:S(2)}, u32[]{:S(2)}) collective-permute-start(bf16[2,80,384]{2,1,0:T(8,128)(2,1)S(1)} %get-tuple-element.45), channel_id=1, source_target_pairs={{0,16},{4,20},{8,24},{12,28},{16,0},{20,4},{24,8},{28,12},{1,17},{... | collective-permute-start | bytes 368648 | tf_op jit(solution)/shard_map/ppermute | solution.py:16
  25.2 11.4 %collective-permute-start.11 = (bf16[2,80,384]{2,1,0:T(8,128)(2,1)S(1)}, bf16[2,80,384]{2,1,0:T(8,128)(2,1)S(1)}, u32[]{:S(2)}, u32[]{:S(2)}) collective-permute-start(bf16[2,80,384]{2,1,0:T(8,128)(2,1)S(1)} %get-tuple-element.46), channel_id=1, source_target_pairs={{0,8},{4,12},{8,0},{12,4},{16,24},{20,28},{24,16},{28,20},{1,9},{5... | collective-permute-start | bytes 368648 | tf_op jit(solution)/shard_map/ppermute | solution.py:16
  26.2 10.5 %collective-permute-start.12 = (bf16[2,80,384]{2,1,0:T(8,128)(2,1)S(1)}, bf16[2,80,384]{2,1,0:T(8,128)(2,1)S(1)}, u32[]{:S(2)}, u32[]{:S(2)}) collective-permute-start(bf16[2,80,384]{2,1,0:T(8,128)(2,1)S(1)} %get-tuple-element.47), channel_id=1, source_target_pairs={{0,24},{4,28},{8,16},{12,20},{16,8},{20,12},{24,0},{28,4},{1,25},{... | collective-permute-start | bytes 368648 | tf_op jit(solution)/shard_map/ppermute | solution.py:16
  28.8 9.1 %collective-permute-start.2 = (bf16[320,320]{1,0:T(8,128)(2,1)S(1)}, bf16[320,320]{1,0:T(8,128)(2,1)S(1)}, u32[]{:S(2)}, u32[]{:S(2)}) collective-permute-start(bf16[320,320]{1,0:T(8,128)(2,1)S(1)} %pad_maximum_fusion.1), channel_id=1, source_target_pairs={{0,4},{4,0},{8,12},{12,8},{16,20},{20,16},{24,28},{28,24},{1,5},{5... | collective-permute-start | bytes 614408 | tf_op jit(solution)/shard_map/ppermute | solution.py:16
  35.1 6.8 %collective-permute-start.7 = (bf16[320,384]{1,0:T(8,128)(2,1)S(1)}, bf16[320,384]{1,0:T(8,128)(2,1)S(1)}, u32[]{:S(2)}, u32[]{:S(2)}) collective-permute-start(bf16[320,384]{1,0:T(8,128)(2,1)S(1)} %pad_maximum_fusion.3), channel_id=1, source_target_pairs={{0,4},{4,0},{8,12},{12,8},{16,20},{20,16},{24,28},{28,24},{1,5},{5... | collective-permute-start | bytes 737288 | tf_op jit(solution)/shard_map/ppermute | solution.py:16
  36.7 7.8 %collective-permute-start.13 = (bf16[320,384]{1,0:T(8,128)(2,1)S(1)}, bf16[320,384]{1,0:T(8,128)(2,1)S(1)}, u32[]{:S(2)}, u32[]{:S(2)}) collective-permute-start(bf16[320,384]{1,0:T(8,128)(2,1)S(1)} %pad_maximum_fusion.5), channel_id=1, source_target_pairs={{0,4},{4,0},{8,12},{12,8},{16,20},{20,16},{24,28},{28,24},{1,5},{5... | collective-permute-start | bytes 737288 | tf_op jit(solution)/shard_map/ppermute | solution.py:16
  37.3 8.7 %collective-permute-start.14 = (bf16[320,384]{1,0:T(8,128)(2,1)S(1)}, bf16[320,384]{1,0:T(8,128)(2,1)S(1)}, u32[]{:S(2)}, u32[]{:S(2)}) collective-permute-start(bf16[320,384]{1,0:T(8,128)(2,1)S(1)} %pad_maximum_fusion.4.refs_2_), channel_id=1, source_target_pairs={{0,2},{1,3},{2,0},{3,1},{4,6},{5,7},{6,4},{7,5},{8,10},{9,11},{10,... | collective-permute-start | bytes 737288 | tf_op jit(solution)/shard_map/ppermute | solution.py:262
  38.0 13.4 %collective-permute-start.3 = (bf16[640,320]{1,0:T(8,128)(2,1)S(1)}, bf16[640,320]{1,0:T(8,128)(2,1)S(1)}, u32[]{:S(2)}, u32[]{:S(2)}) collective-permute-start(bf16[640,320]{1,0:T(8,128)(2,1)S(1)} %pad_maximum_fusion.refs_0_), channel_id=1, source_target_pairs={{0,1},{1,0},{2,3},{3,2},{4,5},{5,4},{6,7},{7,6},{8,9},{9,8},{10,11... | collective-permute-start | bytes 1228808 | tf_op jit(solution)/shard_map/ppermute | solution.py:16
  41.9 9.5 %collective-permute-start.9 = (bf16[320,384]{1,0:T(8,128)(2,1)S(1)}, bf16[320,384]{1,0:T(8,128)(2,1)S(1)}, u32[]{:S(2)}, u32[]{:S(2)}) collective-permute-start(bf16[320,384]{1,0:T(8,128)(2,1)S(1)} %collective-permute-done.7.refs_3_), channel_id=1, source_target_pairs={{0,2},{1,3},{2,0},{3,1},{4,6},{5,7},{6,4},{7,5},{8,10},{9,11},{10,... | collective-permute-start | bytes 737288 | tf_op jit(solution)/shard_map/ppermute | solution.py:269
  46.1 8.4 %collective-permute-start.15 = (bf16[320,384]{1,0:T(8,128)(2,1)S(1)}, bf16[320,384]{1,0:T(8,128)(2,1)S(1)}, u32[]{:S(2)}, u32[]{:S(2)}) collective-permute-start(bf16[320,384]{1,0:T(8,128)(2,1)S(1)} %collective-permute-done.13.refs_3_), channel_id=1, source_target_pairs={{0,2},{1,3},{2,0},{3,1},{4,6},{5,7},{6,4},{7,5},{8,10},{9,11},{10,... | collective-permute-start | bytes 737288 | tf_op jit(solution)/shard_map/ppermute | solution.py:269
  46.3 9.3 %copy-start.8 = (s32[4,8]{1,0:T(4,128)S(1)}, s32[4,8]{1,0:T(4,128)}, u32[]{:S(2)}) copy-start(s32[4,8]{1,0:T(4,128)} %refs_1_.11) | copy-start | bytes 388
  46.3 9.3 %copy-start.9 = (s32[4,8]{1,0:T(4,128)S(1)}, s32[4,8]{1,0:T(4,128)}, u32[]{:S(2)}) copy-start(s32[4,8]{1,0:T(4,128)} %refs_2_.11) | copy-start | bytes 388
  52.5 13.2 %collective-permute-start.16 = (bf16[640,384]{1,0:T(8,128)(2,1)S(1)}, bf16[640,384]{1,0:T(8,128)(2,1)S(1)}, u32[]{:S(2)}, u32[]{:S(2)}) collective-permute-start(bf16[640,384]{1,0:T(8,128)(2,1)S(1)} %get-tuple-element.51.refs_7_), channel_id=1, source_target_pairs={{0,24},{4,28},{8,0},{12,4},{16,8},{20,12},{24,16},{28,20},{1,25},{... | collective-permute-start | bytes 1474568 | tf_op jit(solution)/shard_map/ppermute | solution.py:22
  58.5 14.9 %collective-permute-start.19 = (bf16[640,384]{1,0:T(8,128)(2,1)S(1)}, bf16[640,384]{1,0:T(8,128)(2,1)S(1)}, u32[]{:S(2)}, u32[]{:S(2)}) collective-permute-start(bf16[640,384]{1,0:T(8,128)(2,1)S(1)} %get-tuple-element.58.refs_7_), channel_id=1, source_target_pairs={{0,24},{4,28},{8,0},{12,4},{16,8},{20,12},{24,16},{28,20},{1,25},{... | collective-permute-start | bytes 1474568 | tf_op jit(solution)/shard_map/ppermute | solution.py:22
  60.2 18.1 %collective-permute-start.18 = (bf16[640,384]{1,0:T(8,128)(2,1)S(1)}, bf16[640,384]{1,0:T(8,128)(2,1)S(1)}, u32[]{:S(2)}, u32[]{:S(2)}) collective-permute-start(bf16[640,384]{1,0:T(8,128)(2,1)S(1)} %get-tuple-element.51.refs_7_), channel_id=1, source_target_pairs={{4,0},{12,8},{20,16},{28,24},{5,1},{13,9},{21,17},{29,25},{6,2},{1... | collective-permute-start | bytes 1474568 | tf_op jit(solution)/shard_map/ppermute | solution.py:322
  61.4 23.4 %collective-permute-start.21 = (bf16[640,384]{1,0:T(8,128)(2,1)S(1)}, bf16[640,384]{1,0:T(8,128)(2,1)S(1)}, u32[]{:S(2)}, u32[]{:S(2)}) collective-permute-start(bf16[640,384]{1,0:T(8,128)(2,1)S(1)} %get-tuple-element.58.refs_7_), channel_id=1, source_target_pairs={{4,0},{12,8},{20,16},{28,24},{5,1},{13,9},{21,17},{29,25},{6,2},{1... | collective-permute-start | bytes 1474568 | tf_op jit(solution)/shard_map/ppermute | solution.py:322
  65.7 16.3 %collective-permute-start.17 = (bf16[640,384]{1,0:T(8,128)(2,1)S(1)}, bf16[640,384]{1,0:T(8,128)(2,1)S(1)}, u32[]{:S(2)}, u32[]{:S(2)}) collective-permute-start(bf16[640,384]{1,0:T(8,128)(2,1)S(1)} %collective-permute-done.16.refs_7_), channel_id=1, source_target_pairs={{0,4},{8,12},{16,20},{24,28},{1,5},{9,13},{17,21},{25,29},{2,6},{1... | collective-permute-start | bytes 1474568 | tf_op jit(solution)/shard_map/ppermute | solution.py:329
  73.4 15.1 %collective-permute-start.20 = (bf16[640,384]{1,0:T(8,128)(2,1)S(1)}, bf16[640,384]{1,0:T(8,128)(2,1)S(1)}, u32[]{:S(2)}, u32[]{:S(2)}) collective-permute-start(bf16[640,384]{1,0:T(8,128)(2,1)S(1)} %collective-permute-done.19.refs_7_), channel_id=1, source_target_pairs={{0,4},{8,12},{16,20},{24,28},{1,5},{9,13},{17,21},{25,29},{2,6},{1... | collective-permute-start | bytes 1474568 | tf_op jit(solution)/shard_map/ppermute | solution.py:329
  88.5 2.0 %copy-start.4 = (bf16[640,384]{1,0:T(8,128)(2,1)}, bf16[640,384]{1,0:T(8,128)(2,1)S(1)}, u32[]{:S(2)}) copy-start(bf16[640,384]{1,0:T(8,128)(2,1)S(1)} %collective-permute-done.20.refs_7_.refs_0_) | copy-start | bytes 1474564
  90.6 0.7 copy-start.6
  91.3 4.0 %copy-start.2 = (bf16[768,384]{1,0:T(8,128)(2,1)}, bf16[768,384]{1,0:T(8,128)(2,1)S(1)}, u32[]{:S(2)}) copy-start(bf16[768,384]{1,0:T(8,128)(2,1)S(1)} %get-tuple-element.66.mixed_ref) | copy-start | bytes 1769476
  91.3 1.5 %collective-permute-start.22 = (bf16[192,384]{1,0:T(8,128)(2,1)S(1)}, bf16[192,384]{1,0:T(8,128)(2,1)}, u32[]{:S(2)}, u32[]{:S(2)}) collective-permute-start(bf16[192,384]{1,0:T(8,128)(2,1)S(1)} %get-tuple-element.68), channel_id=1, source_target_pairs={{0,1},{1,0},{2,3},{3,2},{4,5},{5,4},{6,7},{7,6},{8,9},{9,8},{10,11... | collective-permute-start | bytes 442376 | tf_op jit(solution)/shard_map/ppermute | solution.py:16
  93.8 1.5 %copy-start.10 = (f32[192,384]{1,0:T(8,128)}, f32[192,384]{1,0:T(8,128)S(1)}, u32[]{:S(2)}) copy-start(f32[192,384]{1,0:T(8,128)S(1)} %convert_add_fusion) | copy-start | bytes 884740
  94.5 4.7 %collective-permute-start.23 = (bf16[96,384]{1,0:T(8,128)(2,1)}, bf16[96,384]{1,0:T(8,128)(2,1)}, u32[]{:S(2)}, u32[]{:S(2)}) collective-permute-start(bf16[96,384]{1,0:T(8,128)(2,1)} %dynamic-slice_convert_fusion), channel_id=1, source_target_pairs={{0,2},{1,3},{2,0},{3,1},{4,6},{5,7},{6,4},{7,5},{8,10},{9,11},{10,... | collective-permute-start | bytes 221192 | tf_op jit(solution)/shard_map/ppermute | solution.py:16
  95.3 1.1 copy-start.3
  96.4 1.0 copy-start.5
  97.4 1.8 %copy-start.11 = (f32[192,384]{1,0:T(8,128)S(1)}, f32[192,384]{1,0:T(8,128)}, u32[]{:S(2)}) copy-start(f32[192,384]{1,0:T(8,128)} %copy-done.10) | copy-start | bytes 884740
  100.1 4.5 %collective-permute-start.24 = (bf16[48,384]{1,0:T(8,128)(2,1)S(1)}, bf16[48,384]{1,0:T(8,128)(2,1)S(1)}, u32[]{:S(2)}, u32[]{:S(2)}) collective-permute-start(bf16[48,384]{1,0:T(8,128)(2,1)S(1)} %dynamic-slice_convert_fusion.1), channel_id=1, source_target_pairs={{0,4},{4,0},{8,12},{12,8},{16,20},{20,16},{24,28},{28,24},{1,5},{5... | collective-permute-start | bytes 110600 | tf_op jit(solution)/shard_map/ppermute | solution.py:16
  104.7 3.8 %collective-permute-start.25 = (bf16[24,384]{1,0:T(8,128)(2,1)S(1)}, bf16[24,384]{1,0:T(8,128)(2,1)S(1)}, u32[]{:S(2)}, u32[]{:S(2)}) collective-permute-start(bf16[24,384]{1,0:T(8,128)(2,1)S(1)} %dynamic-slice_convert_fusion.2), channel_id=1, source_target_pairs={{0,8},{4,12},{8,0},{12,4},{16,24},{20,28},{24,16},{28,20},{1,9},{5... | collective-permute-start | bytes 55304 | tf_op jit(solution)/shard_map/ppermute | solution.py:16
  108.5 4.7 %collective-permute-start.26 = (bf16[12,384]{1,0:T(8,128)(2,1)S(1)}, bf16[12,384]{1,0:T(8,128)(2,1)S(1)}, u32[]{:S(2)}, u32[]{:S(2)}) collective-permute-start(bf16[12,384]{1,0:T(8,128)(2,1)S(1)} %dynamic-slice_convert_fusion.3), channel_id=1, source_target_pairs={{0,16},{4,20},{8,24},{12,28},{16,0},{20,4},{24,8},{28,12},{1,17},{... | collective-permute-start | bytes 27656 | tf_op jit(solution)/shard_map/ppermute | solution.py:16

commit v3 on v2

--- a/solution.py
+++ b/solution.py
@@ -9,6 +9,7 @@
 
 WINDOW = 3
 DIRECT = 8
+FAR_PARTS = 1
 
 
 def flip(value, axis, mask):
@@ -45,42 +46,63 @@
     return lax.dot_general(left, right, ((dims[0], dims[1]), ((), ())), preferred_element_type=jnp.float32)
 
 
-def fit_kernel(halves, own_count, *refs):
+def fit_kernel(halves, parts, cuts, *refs):
     metric_refs, refs = refs[:halves], refs[halves:]
-    own_refs, facing_refs, outs = refs[:own_count], refs[own_count:-2], refs[-2:]
-    low_bit = lax.axis_index("narrow") % 2
-    for sources, out_ref in zip((own_refs, facing_refs), outs):
-        rows = rows_of(sources)
-        for place, metric_ref in enumerate(metric_refs):
-            part = product(metric_ref[...], rows, ((0,), (0,))).astype(out_ref.dtype)
-            if halves == 1:
-                out_ref[...] = part
-            else:
-                start = (low_bit if place == 0 else 1 - low_bit) * part.shape[0]
-                out_ref[pl.ds(pl.multiple_of(start, part.shape[0]), part.shape[0]), :] = part
-
-
-def fit(metric, own, facing):
-    aux_count = sum(part.shape[1] for part in metric)
-    shape = jax.ShapeDtypeStruct((aux_count, own[0].shape[1]), own[0].dtype)
-    flops = 4 * aux_count * aux_count * own[0].shape[1]
-    moved = 2 * (aux_count * aux_count + 4 * aux_count * own[0].shape[1])
-    operands = [*metric, *own, *facing]
-    return pl.pallas_call(
-        functools.partial(fit_kernel, len(metric), len(own)),
-        out_shape=(shape, shape),
+    sources, outs = refs[: parts * len(cuts)], refs[parts * len(cuts) :]
+    low = lax.axis_index("narrow") % 2 == 0
+    for source, cut in enumerate(cuts):
+        rows = rows_of(sources[source * parts : (source + 1) * parts])
+        fitted = [product(metric_ref[...], rows, ((0,), (0,))) for metric_ref in metric_refs]
+        if halves == 2:
+            fitted = [jnp.where(low, fitted[0], fitted[1]), jnp.where(low, fitted[1], fitted[0])]
+        fitted = jnp.concatenate([part.astype(outs[0].dtype) for part in fitted], axis=0)
+        size = fitted.shape[0] // cut
+        for place, out_ref in enumerate(outs[:cut]):
+            out_ref[...] = fitted[place * size : (place + 1) * size]
+        outs = outs[cut:]
+
+
+def fit(metric, sources, cuts):
+    aux_count = sum(half.shape[1] for half in metric)
+    vir_count = sources[0][0].shape[1]
+    shapes = [
+        jax.ShapeDtypeStruct((aux_count // cut, vir_count), sources[0][0].dtype) for cut in cuts for _ in range(cut)
+    ]
+    operands = [*metric, *[part for source in sources for part in source]]
+    flops = 2 * len(sources) * aux_count * aux_count * vir_count
+    moved = 2 * aux_count * (aux_count + 2 * len(sources) * vir_count)
+    results = pl.pallas_call(
+        functools.partial(fit_kernel, len(metric), len(sources[0]), cuts),
+        out_shape=tuple(shapes),
         in_specs=[VMEM] * len(operands),
-        out_specs=(VMEM, VMEM),
+        out_specs=tuple([VMEM] * len(shapes)),
         compiler_params=pltpu.CompilerParams(vmem_limit_bytes=32 * 1024 * 1024),
         cost_estimate=pl.CostEstimate(flops=flops, bytes_accessed=moved, transcendentals=0),
     )(*operands)
-
-
-def far_rows(refs):
-    if len(refs) == 1:
-        return refs[0][...]
+    return [list(results[sum(cuts[:place]) : sum(cuts[: place + 1])]) for place in range(len(cuts))]
+
+
+def choice_kernel(odd_ref, even_ref, out_ref):
     odd = lax.axis_index("wide") % 2 == 1
-    return jnp.where(odd, refs[0][...], refs[1][...])
+
+    @pl.when(odd)
+    def _():
+        out_ref[...] = odd_ref[...]
+
+    @pl.when(jnp.logical_not(odd))
+    def _():
+        out_ref[...] = even_ref[...]
+
+
+def choice(odd, even):
+    return pl.pallas_call(
+        choice_kernel,
+        out_shape=jax.ShapeDtypeStruct(odd.shape, odd.dtype),
+        in_specs=[VMEM] * 2,
+        out_specs=VMEM,
+        compiler_params=pltpu.CompilerParams(vmem_limit_bytes=32 * 1024 * 1024),
+        cost_estimate=pl.CostEstimate(flops=0, bytes_accessed=6 * odd.size, transcendentals=0),
+    )(odd, even)
 
 
 def pair_kernel(offset, slot, fars, sums, last, scale_by, *refs):
@@ -100,7 +122,7 @@
     vir_far = row_ref[pl.ds(partner, 1), :]
     occ_far = occ_ref[kpoint_ref[partner, other], slot]
     live_far = slot < count_ref[partner, other]
-    far = far_rows(far_refs)
+    far = rows_of(far_refs)
     total = None
     for i in range(occ_slots):
         columns = slice(i * vir_count, (i + 1) * vir_count)
@@ -137,7 +159,7 @@
 
 
 def gamma_kernel(sum_ref, mixed_ref, *refs):
-    far = far_rows(refs[:-1])
+    far = rows_of(refs[:-1])
     refs[-1][...] = (sum_ref[...] + product(far, mixed_ref[...], ((1,), (1,)))).astype(refs[-1].dtype)
 
 
@@ -146,7 +168,7 @@
 
 
 def pair_terms(offset, slot, small, own, far, sums, last=False, scale_by=1.0):
-    aux_count, vir_count = far[0].shape
+    aux_count, vir_count = own[0].shape
     width = len(own) * vir_count
     density = jax.ShapeDtypeStruct((vir_count, vir_count), jnp.float32)
     gamma = jax.ShapeDtypeStruct((aux_count, width), jnp.float32)
@@ -210,25 +232,48 @@
     return value.reshape(-1)
 
 
-def pack_kernel(slot, raw_ref, *outs):
+def pack_kernel(slot, sets, raw_ref, *outs):
     block = lax.axis_index("wide")
-    for place, out_ref in zip(doubled(raw_ref.shape[1]), outs):
-        for part in range(2):
-            out_ref[part] = raw_ref[:, jnp.bitwise_xor(block, place ^ part), slot, :]
-
-
-def packed(raw, slot):
-    rows, block_count, _, vir_count = raw.shape
-    shape = jax.ShapeDtypeStruct((2, rows, vir_count), raw.dtype)
-    count = block_count // 2
+    for offsets, out_ref in zip(sets, outs):
+        for place, offset in enumerate(offsets):
+            out_ref[place] = raw_ref[:, jnp.bitwise_xor(block, offset), slot, :]
+
+
+def packed(raw, slot, sets):
+    rows, _, _, vir_count = raw.shape
     return pl.pallas_call(
-        functools.partial(pack_kernel, slot),
-        out_shape=tuple([shape] * count),
+        functools.partial(pack_kernel, slot, sets),
+        out_shape=tuple(jax.ShapeDtypeStruct((len(offsets), rows, vir_count), raw.dtype) for offsets in sets),
         in_specs=[VMEM],
-        out_specs=tuple([VMEM] * count),
+        out_specs=tuple([VMEM] * len(sets)),
         compiler_params=pltpu.CompilerParams(vmem_limit_bytes=32 * 1024 * 1024),
         cost_estimate=pl.CostEstimate(flops=0, bytes_accessed=6 * raw.size, transcendentals=0),
     )(raw)
+
+
+def sent_direct(raw, slot):
+    places = doubled(lax.axis_size("wide"))
+    places = places[: len(places) // 2]
+    messages = packed(raw, slot, [[place, place ^ 1] for place in places])
+    arrived = [flip(message, "wide", place) if place else message for message, place in zip(messages, places)]
+    return [jnp.concatenate([message[part] for message in arrived], axis=0) for part in range(2)]
+
+
+def sent_halving(raw, slot, earlier):
+    count = lax.axis_size("wide")
+    kept, message = packed(raw, slot, [list(range(count // 2)), list(range(count // 2, count))])
+    held = {offset: [kept[offset]] for offset in range(count // 2)}
+    for mask in bits_of(count)[:-1]:
+        if message is None:
+            sent = [offset for offset in held if offset & mask]
+            message = jnp.stack([piece for offset in sent for piece in held.pop(offset)])
+            message = after(message, *earlier)
+        pieces = list(flip(message, "wide", mask))
+        message = None
+        depth = len(pieces) // len(held)
+        for place, offset in enumerate(sorted(held)):
+            held[offset] = held[offset] + pieces[place * depth : (place + 1) * depth]
+    return [jnp.concatenate(held[part], axis=0) for part in range(2)]
 
 
 def after(value, *earlier):
@@ -238,36 +283,31 @@
 def gathered_rows(raw, metric):
     wide_count, group_count = lax.axis_size("wide"), lax.axis_size("narrow")
     half_turn = [(source, (source + group_count // 2) % group_count) for source in range(group_count)]
-    occ_slots = raw.shape[2]
     half = metric.shape[1] // 2
-    places = doubled(wide_count)[: wide_count // 2]
-    stages = bits_of(wide_count)
     part = lax.dynamic_slice_in_dim(metric, lax.axis_index("narrow") % 2 * half, half, 1)
     steps = []
-    for mask in stages:
+    for mask in bits_of(wide_count):
         steps.append(flip(part, "wide", mask))
         part = jnp.concatenate([part, steps[-1]], axis=0)
-    own, facing = [], []
-    for slot in range(occ_slots):
-        source = after(raw, steps[0], *earliest) if slot else raw
-        messages = packed(source, slot)
-        arrived = [flip(message, "wide", place) for message, place in zip(messages[1:], places[1:])]
-        earliest = arrived[-1:]
-        arrived = [messages[0], *arrived]
-        mine, theirs = [jnp.concatenate([message[part] for message in arrived], axis=0) for part in range(2)]
+    metric = [part, flip(part, "narrow", 1)]
+    rest = []
+    for slot in range(raw.shape[2]):
         if slot:
-            mine = after(mine, facing[-1][0])
+            mine, theirs = sent_halving(after(raw, mine_sent), slot, [mine])
+            mine, theirs = after(mine, *facing_rows), after(theirs, own_rows[1])
         else:
-            theirs = after(theirs, steps[-2])
+            mine, theirs = sent_direct(raw, slot)
+            mine_sent = steps[0]
         first = lax.ppermute(mine, "narrow", half_turn)
         received = flip(theirs, "wide", 1)
-        if slot == 0:
-            sent = after(received, first, steps[-1])
+        own_rows = [mine, received]
+        facing_rows = [first, lax.ppermute(after(received, *facing) if slot else after(received, first), "narrow", half_turn)]
+        if slot:
+            own += fit(metric, [own_rows], [1])[0]
+            rest.append(facing_rows)
         else:
-            sent = after(received, first)
-        own.append([mine, received])
-        facing.append([first, lax.ppermute(sent, "narrow", half_turn)])
-    return own, facing, [part, flip(part, "narrow", 1)]
+            own, facing = fit(metric, [own_rows, facing_rows], [1, FAR_PARTS])
+    return own, facing, metric, rest
 
 
 def scattered_sum(density):
@@ -295,39 +335,42 @@
     direct = wide_count <= DIRECT and is_power(wide_count) and wide_count > 2 and group_count % 2 == 0
     small = (occ_energy, block_kpoint, occ_count, vir_energy, vir_energy.T)
     half_turn = [(source, (source + group_count // 2) % group_count) for source in range(group_count)]
-    to_even = [(source, source - 1) for source in range(1, wide_count, 2)]
-    to_odd = [(source, source + 1) for source in range(0, wide_count, 2)]
-
-    own_rows, facing_rows = [], []
+
     if direct:
-        own_rows, facing_rows, metric = gathered_rows(raw_ints[0], metric_root)
+        own, facing, metric, rest = gathered_rows(raw_ints[0], metric_root)
     else:
         metric = [lax.all_gather(metric_root, "wide", axis=0, tiled=True)]
+        own, rest = [], []
         for slot in range(occ_slots):
             blocks = jnp.transpose(raw_ints[0, :, :, slot, :], (1, 0, 2))
             rows = lax.all_to_all(blocks, "wide", split_axis=0, concat_axis=0, tiled=True)
             rows = rows.reshape(wide_count * aux_rows, vir_count)
-            own_rows.append([rows])
-            facing_rows.append([lax.ppermute(rows, "narrow", half_turn)])
-
-    own, facing = zip(*[fit(metric, *rows) for rows in zip(own_rows, facing_rows)])
+            own += fit(metric, [[rows]], [1])[0]
+            rest.append([lax.ppermute(rows, "narrow", half_turn)])
+        (facing,) = fit(metric, [rest.pop(0)], [FAR_PARTS])
     aux_count = own[0].shape[0]
+
     pair = functools.partial(pair_terms, small=small, own=own)
-    second, first = [], []
+    ahead, second, first = [], [], []
     sums = ()
     for slot in range(occ_slots):
-        source = after(facing[slot], *sums) if slot else facing[slot]
-        second.append(from_ahead(source, "wide", 2))
-        if wide_count % 2 == 0:
-            first.append([lax.ppermute(facing[slot], "wide", to_even)])
-        else:
-            first.append([from_ahead(facing[slot], "wide", 1)])
-        sums = pair(0, slot, far=[facing[slot]], sums=sums)
+        if slot:
+            part, *parts = rest[slot - 1]
+            (facing,) = fit(metric, [[after(part, *sums), *parts]], [FAR_PARTS])
+        ahead.append(facing)
+        second.append([from_ahead(part, "wide", 2) for part in facing])
+        if slot == 0:
+            sums = pair(0, slot, far=facing, sums=sums)
     for slot in range(occ_slots):
         if wide_count % 2 == 0:
-            source = after(second[slot], *sums)
-            first[slot].insert(0, lax.ppermute(source, "wide", to_odd))
-        sums = pair(2, slot, far=[second[slot]], sums=sums)
+            chosen = [choice(after(odd, *sums), even) for odd, even in zip(ahead[slot], second[slot])]
+            first.append([flip(part, "wide", 1) for part in chosen])
+        else:
+            chosen = ()
+            first.append([from_ahead(part, "wide", 1) for part in ahead[slot]])
+        if slot + 1 < occ_slots:
+            sums = pair(0, slot + 1, far=[after(part, *chosen) for part in ahead[slot + 1]], sums=sums)
+        sums = pair(2, slot, far=second[slot], sums=sums)
     for slot in range(occ_slots - 1):
         sums = pair(1, slot, far=first[slot], sums=sums)
     norm_scale = 1.0 / (group_count * wide_count * vir_count)

time: 114 us -> 109 us (0.956)
  waiting for transfers between devices: 43.5 us -> 36 us
  starting transfers between devices: 37.4 us -> 39.6 us
  Pallas kernels: 21.7 us -> 23.9 us
    ppermute x6 -> x2, waiting for transfers between devices: 12.4 us -> 2.17 us  [gathered_rows(): lax.ppermute(after(received, *facing) if slot else after(received, first)...]
    ppermute x6 -> x2, starting transfers between devices: 9.75 us -> 2.53 us  [gathered_rows(): lax.ppermute(after(received, *facing) if slot else after(received, first)...]
    ppermute x17 -> x18, starting transfers between devices: 21.9 us -> 26.7 us  [flip(): return lax.ppermute(value, axis, pairs)]
    ppermute x2, starting transfers between devices: 3.62 us -> 7.86 us  [from_ahead(): return lax.ppermute(value, axis, pairs)]
    ppermute x2, waiting for transfers between devices: 0.01 us -> 3.28 us  [from_ahead(): return lax.ppermute(value, axis, pairs)]
    ppermute x2, waiting for transfers between devices: 1.58 us -> 0.01 us  [gathered_rows(): first = lax.ppermute(mine, 'narrow', half_turn)]
    pallas_call x4 -> x7, Pallas kernels: 4.52 us -> 5.96 us  [the longest x3 3.43 us: fit(): pl.pallas_call(functools.partial(fit_kernel, len(metric), len(sources[0])...]
    ppermute x17 -> x18, waiting for transfers between devices: 29.5 us -> 30.5 us  [flip(): return lax.ppermute(value, axis, pairs)]
  transfers between devices with their start and end apart: 27 -> 24, of which waited for: 13 -> 14; matrix products, arithmetic and copies ran while one was open for 2% -> 2% of each run, Pallas kernels for 17% -> 20%
where the time goes in v3:
time: 109 us
  starting transfers between devices  39.6 us (36%)
  waiting for transfers between devices  36 us (33%)
  Pallas kernels  23.9 us (22%)
  local copies, waits for them, and re-layouts  6.96 us (6%)
  other arithmetic  1.21 us (1%)
    ppermute x18, waiting for transfers between devices, flip(): return lax.ppermute(value, axis, pairs)  30.5 us
    ppermute x18, starting transfers between devices, flip(): return lax.ppermute(value, axis, pairs)  26.7 us
    pallas_call x6, Pallas kernels, pair_terms(): pl.pallas_call(functools.partial(pair_kernel, offset, slot, len(far), len...  17.2 us
    ppermute x2, starting transfers between devices, from_ahead(): return lax.ppermute(value, axis, pairs)  7.86 us
    unnamed x26, local copies, waits for them, and re-layouts  4.22 us
    pallas_call x3, Pallas kernels, fit(): pl.pallas_call(functools.partial(fit_kernel, len(metric), len(sources[0])...  3.43 us
    ppermute x2, waiting for transfers between devices, from_ahead(): return lax.ppermute(value, axis, pairs)  3.28 us
    ppermute x2, starting transfers between devices, gathered_rows(): lax.ppermute(after(received, *facing) if slot else after(received, first)...  2.53 us
  transfers between devices with their start and end apart: 24, of which 14 were waited for; matrix products, arithmetic and copies ran while one was open for 2% of the time, Pallas kernels for 20%

profile of v3, /device:TPU:0, one launch (start us, length us, event | category | flops | bytes accessed | tf_op | source)
XLA Modules:
  0.0 108.6 jit_solution(7360659162956212221)
XLA Ops:
  0.7 0.9 copy-done
  1.6 4.1 %collective-permute-start = (bf16[80,320]{1,0:T(8,128)(2,1)S(1)}, bf16[80,320]{1,0:T(8,128)(2,1)S(1)}, u32[]{:S(2)}, u32[]{:S(2)}) collective-permute-start(bf16[80,320]{1,0:T(8,128)(2,1)S(1)} %constant_dynamic-slice_fusion), channel_id=1, source_target_pairs={{0,16},{4,20},{8,24},{12,28},{16,0},{20,4},{24,8},{28,12},{1,17},{... | collective-permute-start | bytes 153608 | tf_op jit(solution)/shard_map/ppermute | solution.py:17
  5.7 1.2 %copy-done.1 = bf16[1,80,8,2,384]{4,3,2,1,0:T(2,128)(2,1)S(1)} copy-done((bf16[1,80,8,2,384]{4,3,2,1,0:T(2,128)(2,1)S(1)}, bf16[1,80,8,2,384]{4,3,2,1,0:T(2,128)(2,1)}, u32[]{:S(2)}) %copy-start.1) | copy-done | bytes 983064
  6.9 1.1 %shard_map.77 = (bf16[2,80,384]{2,1,0:T(8,128)(2,1)S(1)}, bf16[2,80,384]{2,1,0:T(8,128)(2,1)S(1)}, bf16[2,80,384]{2,1,0:T(8,128)(2,1)S(1)}, bf16[2,80,384]{2,1,0:T(8,128)(2,1)S(1)}) custom-call(bf16[80,8,2,384]{3,2,1,0:T(2,128)(2,1)S(1)} %bitcast.41), custom_call_target="tpu_custom_call" | custom-call | bytes 2949120 | tf_op jit(solution)/shard_map/pallas_call | solution.py:244
  8.1 1.9 %collective-permute-start.5 = (bf16[2,80,384]{2,1,0:T(8,128)(2,1)S(1)}, bf16[2,80,384]{2,1,0:T(8,128)(2,1)S(1)}, u32[]{:S(2)}, u32[]{:S(2)}) collective-permute-start(bf16[2,80,384]{2,1,0:T(8,128)(2,1)S(1)} %get-tuple-element.36), channel_id=1, source_target_pairs={{0,8},{4,12},{8,0},{12,4},{16,24},{20,28},{24,16},{28,20},{1,9},{5... | collective-permute-start | bytes 368648 | tf_op jit(solution)/shard_map/ppermute | solution.py:17
  10.0 2.5 %collective-permute-start.6 = (bf16[2,80,384]{2,1,0:T(8,128)(2,1)S(1)}, bf16[2,80,384]{2,1,0:T(8,128)(2,1)S(1)}, u32[]{:S(2)}, u32[]{:S(2)}) collective-permute-start(bf16[2,80,384]{2,1,0:T(8,128)(2,1)S(1)} %get-tuple-element.37), channel_id=1, source_target_pairs={{0,24},{4,28},{8,16},{12,20},{16,8},{20,12},{24,0},{28,4},{1,25},{... | collective-permute-start | bytes 368648 | tf_op jit(solution)/shard_map/ppermute | solution.py:17
  12.5 1.1 %shard_map.79 = (bf16[4,80,384]{2,1,0:T(8,128)(2,1)S(1)}, bf16[4,80,384]{2,1,0:T(8,128)(2,1)S(1)}) custom-call(bf16[80,8,2,384]{3,2,1,0:T(2,128)(2,1)S(1)} %bitcast.42), custom_call_target="tpu_custom_call" | custom-call | bytes 2949120 | tf_op jit(solution)/shard_map/pallas_call | solution.py:244
  13.9 2.4 %collective-permute-start.1 = (bf16[160,320]{1,0:T(8,128)(2,1)S(1)}, bf16[160,320]{1,0:T(8,128)(2,1)S(1)}, u32[]{:S(2)}, u32[]{:S(2)}) collective-permute-start(bf16[160,320]{1,0:T(8,128)(2,1)S(1)} %pad_maximum_fusion.7), channel_id=1, source_target_pairs={{0,8},{4,12},{8,0},{12,4},{16,24},{20,28},{24,16},{28,20},{1,9},{5... | collective-permute-start | bytes 307208 | tf_op jit(solution)/shard_map/ppermute | solution.py:17
  16.3 7.9 %collective-permute-done.4 = bf16[2,80,384]{2,1,0:T(8,128)(2,1)S(1)} collective-permute-done((bf16[2,80,384]{2,1,0:T(8,128)(2,1)S(1)}, bf16[2,80,384]{2,1,0:T(8,128)(2,1)S(1)}, u32[]{:S(2)}, u32[]{:S(2)}) %collective-permute-start.4) | collective-permute-done | bytes 122912 | tf_op jit(solution)/shard_map/ppermute | solution.py:17
  24.3 1.6 %collective-permute-start.7 = (bf16[320,384]{1,0:T(8,128)(2,1)S(1)}, bf16[320,384]{1,0:T(8,128)(2,1)S(1)}, u32[]{:S(2)}, u32[]{:S(2)}) collective-permute-start(bf16[320,384]{1,0:T(8,128)(2,1)S(1)} %pad_maximum_fusion.3), channel_id=1, source_target_pairs={{0,4},{4,0},{8,12},{12,8},{16,20},{20,16},{24,28},{28,24},{1,5},{5... | collective-permute-start | bytes 737288 | tf_op jit(solution)/shard_map/ppermute | solution.py:17
  25.9 1.6 %collective-permute-start.8 = (bf16[320,384]{1,0:T(8,128)(2,1)S(1)}, bf16[320,384]{1,0:T(8,128)(2,1)S(1)}, u32[]{:S(2)}, u32[]{:S(2)}) collective-permute-start(bf16[320,384]{1,0:T(8,128)(2,1)S(1)} %pad_maximum_fusion.2.refs_2_), channel_id=1, source_target_pairs={{0,2},{1,3},{2,0},{3,1},{4,6},{5,7},{6,4},{7,5},{8,10},{9,11},{10,... | collective-permute-start | bytes 737288 | tf_op jit(solution)/shard_map/ppermute | solution.py:301
  28.1 4.2 %collective-permute-done.10 = bf16[4,80,384]{2,1,0:T(8,128)(2,1)S(1)} collective-permute-done((bf16[4,80,384]{2,1,0:T(8,128)(2,1)S(1)}, bf16[4,80,384]{2,1,0:T(8,128)(2,1)S(1)}, u32[]{:S(2)}, u32[]{:S(2)}) %collective-permute-start.10) | collective-permute-done | bytes 245792 | tf_op jit(solution)/shard_map/ppermute | solution.py:17
  32.7 1.1 %collective-permute-done.2 = bf16[320,320]{1,0:T(8,128)(2,1)S(1)} collective-permute-done((bf16[320,320]{1,0:T(8,128)(2,1)S(1)}, bf16[320,320]{1,0:T(8,128)(2,1)S(1)}, u32[]{:S(2)}, u32[]{:S(2)}) %collective-permute-start.2) | collective-permute-done | bytes 204832 | tf_op jit(solution)/shard_map/ppermute | solution.py:17
  34.0 1.0 collective-permute-start.9
  35.0 4.3 %collective-permute-done.11 = bf16[4,80,384]{2,1,0:T(8,128)(2,1)S(1)} collective-permute-done((bf16[4,80,384]{2,1,0:T(8,128)(2,1)S(1)}, bf16[4,80,384]{2,1,0:T(8,128)(2,1)S(1)}, u32[]{:S(2)}, u32[]{:S(2)}) %collective-permute-start.11) | collective-permute-done | bytes 245792 | tf_op jit(solution)/shard_map/ppermute | solution.py:17
  39.3 1.6 %collective-permute-start.12 = (bf16[320,384]{1,0:T(8,128)(2,1)S(1)}, bf16[320,384]{1,0:T(8,128)(2,1)S(1)}, u32[]{:S(2)}, u32[]{:S(2)}) collective-permute-start(bf16[320,384]{1,0:T(8,128)(2,1)S(1)} %pad_maximum_fusion.6), channel_id=1, source_target_pairs={{0,4},{4,0},{8,12},{12,8},{16,20},{20,16},{24,28},{28,24},{1,5},{5... | collective-permute-start | bytes 737288 | tf_op jit(solution)/shard_map/ppermute | solution.py:17
  41.0 1.3 %collective-permute-done.9.refs_5_ = bf16[320,384]{1,0:T(8,128)(2,1)S(1)} collective-permute-done((bf16[320,384]{1,0:T(8,128)(2,1)S(1)}, bf16[320,384]{1,0:T(8,128)(2,1)S(1)}, u32[]{:S(2)}, u32[]{:S(2)}) %collective-permute-start.9) | collective-permute-done | bytes 245792 | tf_op jit(solution)/shard_map/ppermute | solution.py:304
  42.3 1.0 collective-permute-start.15
  43.3 1.1 %shard_map.78 = (bf16[640,384]{1,0:T(8,128)(2,1)S(1)}, bf16[640,384]{1,0:T(8,128)(2,1)S(1)}) custom-call(bf16[640,320]{1,0:T(8,128)(2,1)S(1)} %pad_maximum_fusion.refs_0_, bf16[640,320]{1,0:T(8,128)(2,1)S(1)} %collective-permute-done.3.refs_1_, bf16[320,384]{1,0:T(8,128)(2,1)S(1)} %pad_maximum_fusion.2.refs_2_, ...), custom_call_target="tpu_custom_call" | custom-call | flops 629145600 | bytes 2785280 | tf_op jit(solution)/shard_map/pallas_call | solution.py:74
  44.4 1.2 %collective-permute-done.12.refs_3_ = bf16[320,384]{1,0:T(8,128)(2,1)S(1)} collective-permute-done((bf16[320,384]{1,0:T(8,128)(2,1)S(1)}, bf16[320,384]{1,0:T(8,128)(2,1)S(1)}, u32[]{:S(2)}, u32[]{:S(2)}) %collective-permute-start.12) | collective-permute-done | bytes 245792 | tf_op jit(solution)/shard_map/ppermute | solution.py:17
  45.6 1.5 %collective-permute-start.16 = (bf16[320,384]{1,0:T(8,128)(2,1)S(1)}, bf16[320,384]{1,0:T(8,128)(2,1)}, u32[]{:S(2)}, u32[]{:S(2)}) collective-permute-start(bf16[320,384]{1,0:T(8,128)(2,1)S(1)} %collective-permute-done.12.refs_3_), channel_id=1, source_target_pairs={{0,2},{1,3},{2,0},{3,1},{4,6},{5,7},{6,4},{7,5},{8,10},{9,11},{10,... | collective-permute-start | bytes 737288 | tf_op jit(solution)/shard_map/ppermute | solution.py:304
  47.1 3.4 %collective-permute-start.13 = (bf16[640,384]{1,0:T(8,128)(2,1)S(1)}, bf16[640,384]{1,0:T(8,128)(2,1)S(1)}, u32[]{:S(2)}, u32[]{:S(2)}) collective-permute-start(bf16[640,384]{1,0:T(8,128)(2,1)S(1)} %get-tuple-element.49.refs_7_.odd_ref), channel_id=1, source_target_pairs={{0,24},{4,28},{8,0},{12,4},{16,8},{20,12},{24,16},{28,20},{1,25},{... | collective-permute-start | bytes 1474568 | tf_op jit(solution)/shard_map/ppermute | solution.py:23
  51.4 2.9 %shard_map.81 = (f32[384,384]{1,0:T(8,128)S(1)}, f32[640,768]{1,0:T(8,128)S(1)}) custom-call(f32[8,2]{1,0:T(8,128)S(1)} %copy.13.refs_0_, s32[4,8]{1,0:T(4,128)S(1)} %copy-done.5, s32[4,8]{1,0:T(4,128)S(1)} %copy-done.7, f32[4,384]{1,0:T(4,128)S(1)} %copy-done.4, f32[384,4]{1,0:T(8,128)S(1)} %bitcast.35, bf16[640,384]{1,0:T(8,128)(2,1)S(1)} %get-tuple-element.39.refs_5_, ...), custom_call_target="tpu_custom_call" | custom-call | flops 981467136 | bytes 6586368 | tf_op jit(solution)/shard_map/pallas_call | solution.py:183
  54.3 0.8 collective-permute-done.16.refs_3_
  55.2 1.6 %shard_map.83.refs_7_.odd_ref = bf16[640,384]{1,0:T(8,128)(2,1)S(1)} custom-call(bf16[640,320]{1,0:T(8,128)(2,1)S(1)} %pad_maximum_fusion.refs_0_, bf16[640,320]{1,0:T(8,128)(2,1)S(1)} %collective-permute-done.3.refs_1_, bf16[320,384]{1,0:T(8,128)(2,1)S(1)} %collective-permute-done.15.refs_2_, bf16[320,384]{1,0:T(8,128)(2,1)} %collective-permute-done.16.refs_3_), custom_call_target="tpu_custom_call" | custom-call | flops 314572800 | bytes 1802240 | tf_op jit(solution)/shard_map/pallas_call | solution.py:74
  56.8 4.5 %collective-permute-start.17 = (bf16[640,384]{1,0:T(8,128)(2,1)S(1)}, bf16[640,384]{1,0:T(8,128)(2,1)S(1)}, u32[]{:S(2)}, u32[]{:S(2)}) collective-permute-start(bf16[640,384]{1,0:T(8,128)(2,1)S(1)} %shard_map.83.refs_7_.odd_ref), channel_id=1, source_target_pairs={{0,24},{4,28},{8,0},{12,4},{16,8},{20,12},{24,16},{28,20},{1,25},{... | collective-permute-start | bytes 1474568 | tf_op jit(solution)/shard_map/ppermute | solution.py:23
  61.5 1.5 %collective-permute-start.14 = (bf16[640,384]{1,0:T(8,128)(2,1)S(1)}, bf16[640,384]{1,0:T(8,128)(2,1)S(1)}, u32[]{:S(2)}, u32[]{:S(2)}) collective-permute-start(bf16[640,384]{1,0:T(8,128)(2,1)S(1)} %shard_map.82), channel_id=1, source_target_pairs={{0,4},{4,0},{8,12},{12,8},{16,20},{20,16},{24,28},{28,24},{1,5},{5... | collective-permute-start | bytes 1474568 | tf_op jit(solution)/shard_map/ppermute | solution.py:17
  63.0 2.9 %shard_map.84 = (f32[384,384]{1,0:T(8,128)S(1)}, f32[640,768]{1,0:T(8,128)S(1)}) custom-call(f32[8,2]{1,0:T(8,128)S(1)} %copy.13.refs_0_, s32[4,8]{1,0:T(4,128)S(1)} %copy-done.5, s32[4,8]{1,0:T(4,128)S(1)} %copy-done.7, f32[4,384]{1,0:T(4,128)S(1)} %copy-done.4, f32[384,4]{1,0:T(8,128)S(1)} %bitcast.36, bf16[640,384]{1,0:T(8,128)(2,1)S(1)} %get-tuple-element.39.refs_5_, ...), custom_call_target="tpu_custom_call" | custom-call | flops 981467136 | bytes 6586368 | tf_op jit(solution)/shard_map/pallas_call | solution.py:183
  66.0 2.9 %shard_map.85 = (f32[384,384]{1,0:T(8,128)S(1)}, f32[640,768]{1,0:T(8,128)S(1)}) custom-call(f32[8,2]{1,0:T(8,128)S(1)} %copy.13.refs_0_, s32[4,8]{1,0:T(4,128)S(1)} %copy-done.5, s32[4,8]{1,0:T(4,128)S(1)} %copy-done.7, f32[4,384]{1,0:T(4,128)S(1)} %copy-done.4, f32[384,4]{1,0:T(8,128)S(1)} %bitcast.37, bf16[640,384]{1,0:T(8,128)(2,1)S(1)} %get-tuple-element.39.refs_5_, ...), custom_call_target="tpu_custom_call" | custom-call | flops 981467136 | bytes 6586368 | tf_op jit(solution)/shard_map/pallas_call | solution.py:183
  68.9 3.3 %collective-permute-done.17.refs_7_.even_ref = bf16[640,384]{1,0:T(8,128)(2,1)S(1)} collective-permute-done((bf16[640,384]{1,0:T(8,128)(2,1)S(1)}, bf16[640,384]{1,0:T(8,128)(2,1)S(1)}, u32[]{:S(2)}, u32[]{:S(2)}) %collective-permute-start.17) | collective-permute-done | bytes 491552 | tf_op jit(solution)/shard_map/ppermute | solution.py:23
  72.2 1.6 %collective-permute-start.18 = (bf16[640,384]{1,0:T(8,128)(2,1)S(1)}, bf16[640,384]{1,0:T(8,128)(2,1)S(1)}, u32[]{:S(2)}, u32[]{:S(2)}) collective-permute-start(bf16[640,384]{1,0:T(8,128)(2,1)S(1)} %shard_map.88), channel_id=1, source_target_pairs={{0,4},{4,0},{8,12},{12,8},{16,20},{20,16},{24,28},{28,24},{1,5},{5... | collective-permute-start | bytes 1474568 | tf_op jit(solution)/shard_map/ppermute | solution.py:17
  73.8 2.9 %shard_map.86 = (f32[384,384]{1,0:T(8,128)S(1)}, f32[640,768]{1,0:T(8,128)S(1)}) custom-call(f32[8,2]{1,0:T(8,128)S(1)} %copy.13.refs_0_, s32[4,8]{1,0:T(4,128)S(1)} %copy-done.6, s32[4,8]{1,0:T(4,128)S(1)} %copy-done.8, f32[4,384]{1,0:T(4,128)S(1)} %copy-done.4, f32[384,4]{1,0:T(8,128)S(1)} %bitcast.38, bf16[640,384]{1,0:T(8,128)(2,1)S(1)} %get-tuple-element.39.refs_5_, ...), custom_call_target="tpu_custom_call" | custom-call | flops 981467136 | bytes 6586368 | tf_op jit(solution)/shard_map/pallas_call | solution.py:183
  76.7 2.9 %shard_map.87 = (f32[384,384]{1,0:T(8,128)S(1)}, f32[640,768]{1,0:T(8,128)S(1)}) custom-call(f32[8,2]{1,0:T(8,128)S(1)} %copy.13.refs_0_, s32[4,8]{1,0:T(4,128)S(1)} %copy-done.6, s32[4,8]{1,0:T(4,128)S(1)} %copy-done.8, f32[4,384]{1,0:T(4,128)S(1)} %copy-done.4, f32[384,4]{1,0:T(8,128)S(1)} %bitcast.39, bf16[640,384]{1,0:T(8,128)(2,1)S(1)} %get-tuple-element.39.refs_5_, ...), custom_call_target="tpu_custom_call" | custom-call | flops 981467136 | bytes 6586368 | tf_op jit(solution)/shard_map/pallas_call | solution.py:183
  79.6 4.0 %collective-permute-done.18.refs_7_.refs_0_ = bf16[640,384]{1,0:T(8,128)(2,1)S(1)} collective-permute-done((bf16[640,384]{1,0:T(8,128)(2,1)S(1)}, bf16[640,384]{1,0:T(8,128)(2,1)S(1)}, u32[]{:S(2)}, u32[]{:S(2)}) %collective-permute-start.18) | collective-permute-done | bytes 491552 | tf_op jit(solution)/shard_map/ppermute | solution.py:17
  83.7 2.7 %shard_map.89 = (bf16[192,384]{1,0:T(8,128)(2,1)}, f32[192,384]{1,0:T(8,128)S(1)}, bf16[768,384]{1,0:T(8,128)(2,1)S(1)}) custom-call(f32[8,2]{1,0:T(8,128)S(1)} %copy.13.refs_0_, s32[4,8]{1,0:T(4,128)S(1)} %copy-done.6, s32[4,8]{1,0:T(4,128)S(1)} %copy-done.8, f32[4,384]{1,0:T(4,128)S(1)} %copy-done.4, f32[384,4]{1,0:T(8,128)S(1)} %bitcast.40, ...), custom_call_target="tpu_custom_call" | custom-call | flops 981467136 | bytes 6586368 | tf_op jit(solution)/shard_map/pallas_call | solution.py:183
  86.4 0.8 copy-done.2
  87.2 1.6 %collective-permute-done.19 = bf16[192,384]{1,0:T(8,128)(2,1)S(1)} collective-permute-done((bf16[192,384]{1,0:T(8,128)(2,1)}, bf16[192,384]{1,0:T(8,128)(2,1)S(1)}, u32[]{:S(2)}, u32[]{:S(2)}) %collective-permute-start.19) | collective-permute-done | bytes 147488 | tf_op jit(solution)/shard_map/ppermute | solution.py:17
  88.8 0.7 dynamic-slice_convert_fusion
  89.5 1.4 %collective-permute-start.20 = (bf16[96,384]{1,0:T(8,128)(2,1)}, bf16[96,384]{1,0:T(8,128)(2,1)}, u32[]{:S(2)}, u32[]{:S(2)}) collective-permute-start(bf16[96,384]{1,0:T(8,128)(2,1)} %dynamic-slice_convert_fusion), channel_id=1, source_target_pairs={{0,2},{1,3},{2,0},{3,1},{4,6},{5,7},{6,4},{7,5},{8,10},{9,11},{10,... | collective-permute-start | bytes 221192 | tf_op jit(solution)/shard_map/ppermute | solution.py:17
  90.9 1.1 copy-done.3
  92.7 1.5 %collective-permute-done.20 = bf16[96,384]{1,0:T(8,128)(2,1)} collective-permute-done((bf16[96,384]{1,0:T(8,128)(2,1)}, bf16[96,384]{1,0:T(8,128)(2,1)}, u32[]{:S(2)}, u32[]{:S(2)}) %collective-permute-start.20) | collective-permute-done | bytes 73760 | tf_op jit(solution)/shard_map/ppermute | solution.py:17
  94.2 0.9 convert_add_fusion.1
  95.1 1.5 %collective-permute-start.21 = (bf16[48,384]{1,0:T(8,128)(2,1)S(1)}, bf16[48,384]{1,0:T(8,128)(2,1)S(1)}, u32[]{:S(2)}, u32[]{:S(2)}) collective-permute-start(bf16[48,384]{1,0:T(8,128)(2,1)S(1)} %dynamic-slice_convert_fusion.1), channel_id=1, source_target_pairs={{0,4},{4,0},{8,12},{12,8},{16,20},{20,16},{24,28},{28,24},{1,5},{5... | collective-permute-start | bytes 110600 | tf_op jit(solution)/shard_map/ppermute | solution.py:17
  96.6 2.5 %collective-permute-done.21 = bf16[48,384]{1,0:T(8,128)(2,1)S(1)} collective-permute-done((bf16[48,384]{1,0:T(8,128)(2,1)S(1)}, bf16[48,384]{1,0:T(8,128)(2,1)S(1)}, u32[]{:S(2)}, u32[]{:S(2)}) %collective-permute-start.21) | collective-permute-done | bytes 36896 | tf_op jit(solution)/shard_map/ppermute | solution.py:17
  99.2 2.4 %collective-permute-start.22 = (bf16[24,384]{1,0:T(8,128)(2,1)S(1)}, bf16[24,384]{1,0:T(8,128)(2,1)S(1)}, u32[]{:S(2)}, u32[]{:S(2)}) collective-permute-start(bf16[24,384]{1,0:T(8,128)(2,1)S(1)} %dynamic-slice_convert_fusion.2), channel_id=1, source_target_pairs={{0,8},{4,12},{8,0},{12,4},{16,24},{20,28},{24,16},{28,20},{1,9},{5... | collective-permute-start | bytes 55304 | tf_op jit(solution)/shard_map/ppermute | solution.py:17
  101.6 1.7 %collective-permute-done.22 = bf16[24,384]{1,0:T(8,128)(2,1)S(1)} collective-permute-done((bf16[24,384]{1,0:T(8,128)(2,1)S(1)}, bf16[24,384]{1,0:T(8,128)(2,1)S(1)}, u32[]{:S(2)}, u32[]{:S(2)}) %collective-permute-start.22) | collective-permute-done | bytes 18464 | tf_op jit(solution)/shard_map/ppermute | solution.py:17
  103.4 3.0 %collective-permute-start.23 = (bf16[12,384]{1,0:T(8,128)(2,1)S(1)}, bf16[12,384]{1,0:T(8,128)(2,1)S(1)}, u32[]{:S(2)}, u32[]{:S(2)}) collective-permute-start(bf16[12,384]{1,0:T(8,128)(2,1)S(1)} %dynamic-slice_convert_fusion.3), channel_id=1, source_target_pairs={{0,16},{4,20},{8,24},{12,28},{16,0},{20,4},{24,8},{28,12},{1,17},{... | collective-permute-start | bytes 27656 | tf_op jit(solution)/shard_map/ppermute | solution.py:17
  106.3 1.2 %reshape.10 = bf16[1,640,1,2,384]{4,3,1,2,0:T(2,128)(2,1)} reshape(bf16[640,768]{1,0:T(8,128)(2,1)S(1)} %shard_map.90) | data formatting | bytes 1966080 | tf_op jit(solution)/shard_map/reshape | solution.py:383
  (67 shorter events, 4.8 us)
Async XLA Ops:
  0.6 0.9 copy-start
  1.6 10.9 %collective-permute-start = (bf16[80,320]{1,0:T(8,128)(2,1)S(1)}, bf16[80,320]{1,0:T(8,128)(2,1)S(1)}, u32[]{:S(2)}, u32[]{:S(2)}) collective-permute-start(bf16[80,320]{1,0:T(8,128)(2,1)S(1)} %constant_dynamic-slice_fusion), channel_id=1, source_target_pairs={{0,16},{4,20},{8,24},{12,28},{16,0},{20,4},{24,8},{28,12},{1,17},{... | collective-permute-start | bytes 153608 | tf_op jit(solution)/shard_map/ppermute | solution.py:17
  5.7 1.2 %copy-start.1 = (bf16[1,80,8,2,384]{4,3,2,1,0:T(2,128)(2,1)S(1)}, bf16[1,80,8,2,384]{4,3,2,1,0:T(2,128)(2,1)}, u32[]{:S(2)}) copy-start(bf16[1,80,8,2,384]{4,3,2,1,0:T(2,128)(2,1)} %param.6) | copy-start | bytes 2949124
  8.1 16.1 %collective-permute-start.4 = (bf16[2,80,384]{2,1,0:T(8,128)(2,1)S(1)}, bf16[2,80,384]{2,1,0:T(8,128)(2,1)S(1)}, u32[]{:S(2)}, u32[]{:S(2)}) collective-permute-start(bf16[2,80,384]{2,1,0:T(8,128)(2,1)S(1)} %get-tuple-element.35), channel_id=1, source_target_pairs={{0,16},{4,20},{8,24},{12,28},{16,0},{20,4},{24,8},{28,12},{1,17},{... | collective-permute-start | bytes 368648 | tf_op jit(solution)/shard_map/ppermute | solution.py:17
  8.1 16.1 %collective-permute-start.5 = (bf16[2,80,384]{2,1,0:T(8,128)(2,1)S(1)}, bf16[2,80,384]{2,1,0:T(8,128)(2,1)S(1)}, u32[]{:S(2)}, u32[]{:S(2)}) collective-permute-start(bf16[2,80,384]{2,1,0:T(8,128)(2,1)S(1)} %get-tuple-element.36), channel_id=1, source_target_pairs={{0,8},{4,12},{8,0},{12,4},{16,24},{20,28},{24,16},{28,20},{1,9},{5... | collective-permute-start | bytes 368648 | tf_op jit(solution)/shard_map/ppermute | solution.py:17
  10.0 14.2 %collective-permute-start.6 = (bf16[2,80,384]{2,1,0:T(8,128)(2,1)S(1)}, bf16[2,80,384]{2,1,0:T(8,128)(2,1)S(1)}, u32[]{:S(2)}, u32[]{:S(2)}) collective-permute-start(bf16[2,80,384]{2,1,0:T(8,128)(2,1)S(1)} %get-tuple-element.37), channel_id=1, source_target_pairs={{0,24},{4,28},{8,16},{12,20},{16,8},{20,12},{24,0},{28,4},{1,25},{... | collective-permute-start | bytes 368648 | tf_op jit(solution)/shard_map/ppermute | solution.py:17
  13.7 18.6 %collective-permute-start.10 = (bf16[4,80,384]{2,1,0:T(8,128)(2,1)S(1)}, bf16[4,80,384]{2,1,0:T(8,128)(2,1)S(1)}, u32[]{:S(2)}, u32[]{:S(2)}) collective-permute-start(bf16[4,80,384]{2,1,0:T(8,128)(2,1)S(1)} %get-tuple-element.42), channel_id=1, source_target_pairs={{0,16},{4,20},{8,24},{12,28},{16,0},{20,4},{24,8},{28,12},{1,17},{... | collective-permute-start | bytes 737288 | tf_op jit(solution)/shard_map/ppermute | solution.py:17
  13.9 13.6 %collective-permute-start.1 = (bf16[160,320]{1,0:T(8,128)(2,1)S(1)}, bf16[160,320]{1,0:T(8,128)(2,1)S(1)}, u32[]{:S(2)}, u32[]{:S(2)}) collective-permute-start(bf16[160,320]{1,0:T(8,128)(2,1)S(1)} %pad_maximum_fusion.7), channel_id=1, source_target_pairs={{0,8},{4,12},{8,0},{12,4},{16,24},{20,28},{24,16},{28,20},{1,9},{5... | collective-permute-start | bytes 307208 | tf_op jit(solution)/shard_map/ppermute | solution.py:17
  24.3 9.6 %collective-permute-start.7 = (bf16[320,384]{1,0:T(8,128)(2,1)S(1)}, bf16[320,384]{1,0:T(8,128)(2,1)S(1)}, u32[]{:S(2)}, u32[]{:S(2)}) collective-permute-start(bf16[320,384]{1,0:T(8,128)(2,1)S(1)} %pad_maximum_fusion.3), channel_id=1, source_target_pairs={{0,4},{4,0},{8,12},{12,8},{16,20},{20,16},{24,28},{28,24},{1,5},{5... | collective-permute-start | bytes 737288 | tf_op jit(solution)/shard_map/ppermute | solution.py:17
  25.9 8.0 %collective-permute-start.8 = (bf16[320,384]{1,0:T(8,128)(2,1)S(1)}, bf16[320,384]{1,0:T(8,128)(2,1)S(1)}, u32[]{:S(2)}, u32[]{:S(2)}) collective-permute-start(bf16[320,384]{1,0:T(8,128)(2,1)S(1)} %pad_maximum_fusion.2.refs_2_), channel_id=1, source_target_pairs={{0,2},{1,3},{2,0},{3,1},{4,6},{5,7},{6,4},{7,5},{8,10},{9,11},{10,... | collective-permute-start | bytes 737288 | tf_op jit(solution)/shard_map/ppermute | solution.py:301
  27.5 6.3 %collective-permute-start.2 = (bf16[320,320]{1,0:T(8,128)(2,1)S(1)}, bf16[320,320]{1,0:T(8,128)(2,1)S(1)}, u32[]{:S(2)}, u32[]{:S(2)}) collective-permute-start(bf16[320,320]{1,0:T(8,128)(2,1)S(1)} %pad_maximum_fusion.1), channel_id=1, source_target_pairs={{0,4},{4,0},{8,12},{12,8},{16,20},{20,16},{24,28},{28,24},{1,5},{5... | collective-permute-start | bytes 614408 | tf_op jit(solution)/shard_map/ppermute | solution.py:17
  32.4 6.9 %collective-permute-start.11 = (bf16[4,80,384]{2,1,0:T(8,128)(2,1)S(1)}, bf16[4,80,384]{2,1,0:T(8,128)(2,1)S(1)}, u32[]{:S(2)}, u32[]{:S(2)}) collective-permute-start(bf16[4,80,384]{2,1,0:T(8,128)(2,1)S(1)} %pad_maximum_fusion.4), channel_id=1, source_target_pairs={{0,8},{4,12},{8,0},{12,4},{16,24},{20,28},{24,16},{28,20},{1,9},{5... | collective-permute-start | bytes 737288 | tf_op jit(solution)/shard_map/ppermute | solution.py:17
  33.8 16.7 %copy-start.4 = (f32[4,384]{1,0:T(4,128)S(1)}, f32[4,384]{1,0:T(4,128)}, u32[]{:S(2)}) copy-start(f32[4,384]{1,0:T(4,128)} %refs_3_.11) | copy-start | bytes 18436
  33.8 16.8 %copy-start.11 = (f32[8,2]{0,1:T(2,128)S(1)}, f32[8,2]{0,1:T(2,128)}, u32[]{:S(2)}) copy-start(f32[8,2]{0,1:T(2,128)} %param.8) | copy-start | bytes 196
  33.9 9.4 %collective-permute-start.3 = (bf16[640,320]{1,0:T(8,128)(2,1)S(1)}, bf16[640,320]{1,0:T(8,128)(2,1)S(1)}, u32[]{:S(2)}, u32[]{:S(2)}) collective-permute-start(bf16[640,320]{1,0:T(8,128)(2,1)S(1)} %pad_maximum_fusion.refs_0_), channel_id=1, source_target_pairs={{0,1},{1,0},{2,3},{3,2},{4,5},{5,4},{6,7},{7,6},{8,9},{9,8},{10,11... | collective-permute-start | bytes 1228808 | tf_op jit(solution)/shard_map/ppermute | solution.py:17
  34.0 8.4 %collective-permute-start.9 = (bf16[320,384]{1,0:T(8,128)(2,1)S(1)}, bf16[320,384]{1,0:T(8,128)(2,1)S(1)}, u32[]{:S(2)}, u32[]{:S(2)}) collective-permute-start(bf16[320,384]{1,0:T(8,128)(2,1)S(1)} %collective-permute-done.7.refs_3_), channel_id=1, source_target_pairs={{0,2},{1,3},{2,0},{3,1},{4,6},{5,7},{6,4},{7,5},{8,10},{9,11},{10,... | collective-permute-start | bytes 737288 | tf_op jit(solution)/shard_map/ppermute | solution.py:304
  39.3 6.3 %collective-permute-start.12 = (bf16[320,384]{1,0:T(8,128)(2,1)S(1)}, bf16[320,384]{1,0:T(8,128)(2,1)S(1)}, u32[]{:S(2)}, u32[]{:S(2)}) collective-permute-start(bf16[320,384]{1,0:T(8,128)(2,1)S(1)} %pad_maximum_fusion.6), channel_id=1, source_target_pairs={{0,4},{4,0},{8,12},{12,8},{16,20},{20,16},{24,28},{28,24},{1,5},{5... | collective-permute-start | bytes 737288 | tf_op jit(solution)/shard_map/ppermute | solution.py:17
  41.0 10.5 %copy-start.5 = (s32[4,8]{1,0:T(4,128)S(1)}, s32[4,8]{1,0:T(4,128)}, u32[]{:S(2)}) copy-start(s32[4,8]{1,0:T(4,128)} %refs_1_.11) | copy-start | bytes 388
  41.0 10.5 %copy-start.7 = (s32[4,8]{1,0:T(4,128)S(1)}, s32[4,8]{1,0:T(4,128)}, u32[]{:S(2)}) copy-start(s32[4,8]{1,0:T(4,128)} %refs_2_.11) | copy-start | bytes 388
  42.3 12.0 %collective-permute-start.15 = (bf16[320,384]{1,0:T(8,128)(2,1)S(1)}, bf16[320,384]{1,0:T(8,128)(2,1)S(1)}, u32[]{:S(2)}, u32[]{:S(2)}) collective-permute-start(bf16[320,384]{1,0:T(8,128)(2,1)S(1)} %pad_maximum_fusion.5.refs_2_), channel_id=1, source_target_pairs={{0,2},{1,3},{2,0},{3,1},{4,6},{5,7},{6,4},{7,5},{8,10},{9,11},{10,... | collective-permute-start | bytes 737288 | tf_op jit(solution)/shard_map/ppermute | solution.py:301
  45.6 9.6 %collective-permute-start.16 = (bf16[320,384]{1,0:T(8,128)(2,1)S(1)}, bf16[320,384]{1,0:T(8,128)(2,1)}, u32[]{:S(2)}, u32[]{:S(2)}) collective-permute-start(bf16[320,384]{1,0:T(8,128)(2,1)S(1)} %collective-permute-done.12.refs_3_), channel_id=1, source_target_pairs={{0,2},{1,3},{2,0},{3,1},{4,6},{5,7},{6,4},{7,5},{8,10},{9,11},{10,... | collective-permute-start | bytes 737288 | tf_op jit(solution)/shard_map/ppermute | solution.py:304
  47.1 14.2 %collective-permute-start.13 = (bf16[640,384]{1,0:T(8,128)(2,1)S(1)}, bf16[640,384]{1,0:T(8,128)(2,1)S(1)}, u32[]{:S(2)}, u32[]{:S(2)}) collective-permute-start(bf16[640,384]{1,0:T(8,128)(2,1)S(1)} %get-tuple-element.49.refs_7_.odd_ref), channel_id=1, source_target_pairs={{0,24},{4,28},{8,0},{12,4},{16,8},{20,12},{24,16},{28,20},{1,25},{... | collective-permute-start | bytes 1474568 | tf_op jit(solution)/shard_map/ppermute | solution.py:23
  56.8 15.4 %collective-permute-start.17 = (bf16[640,384]{1,0:T(8,128)(2,1)S(1)}, bf16[640,384]{1,0:T(8,128)(2,1)S(1)}, u32[]{:S(2)}, u32[]{:S(2)}) collective-permute-start(bf16[640,384]{1,0:T(8,128)(2,1)S(1)} %shard_map.83.refs_7_.odd_ref), channel_id=1, source_target_pairs={{0,24},{4,28},{8,0},{12,4},{16,8},{20,12},{24,16},{28,20},{1,25},{... | collective-permute-start | bytes 1474568 | tf_op jit(solution)/shard_map/ppermute | solution.py:23
  61.5 15.2 %collective-permute-start.14 = (bf16[640,384]{1,0:T(8,128)(2,1)S(1)}, bf16[640,384]{1,0:T(8,128)(2,1)S(1)}, u32[]{:S(2)}, u32[]{:S(2)}) collective-permute-start(bf16[640,384]{1,0:T(8,128)(2,1)S(1)} %shard_map.82), channel_id=1, source_target_pairs={{0,4},{4,0},{8,12},{12,8},{16,20},{20,16},{24,28},{28,24},{1,5},{5... | collective-permute-start | bytes 1474568 | tf_op jit(solution)/shard_map/ppermute | solution.py:17
  65.9 7.9 %copy-start.6 = (s32[4,8]{1,0:T(4,128)S(1)}, s32[4,8]{1,0:T(4,128)}, u32[]{:S(2)}) copy-start(s32[4,8]{1,0:T(4,128)} %refs_1_.11) | copy-start | bytes 388
  66.0 7.8 %copy-start.8 = (s32[4,8]{1,0:T(4,128)S(1)}, s32[4,8]{1,0:T(4,128)}, u32[]{:S(2)}) copy-start(s32[4,8]{1,0:T(4,128)} %refs_2_.11) | copy-start | bytes 388
  72.2 11.5 %collective-permute-start.18 = (bf16[640,384]{1,0:T(8,128)(2,1)S(1)}, bf16[640,384]{1,0:T(8,128)(2,1)S(1)}, u32[]{:S(2)}, u32[]{:S(2)}) collective-permute-start(bf16[640,384]{1,0:T(8,128)(2,1)S(1)} %shard_map.88), channel_id=1, source_target_pairs={{0,4},{4,0},{8,12},{12,8},{16,20},{20,16},{24,28},{28,24},{1,5},{5... | collective-permute-start | bytes 1474568 | tf_op jit(solution)/shard_map/ppermute | solution.py:17
  86.3 0.8 copy-start.2
  87.2 1.6 %collective-permute-start.19 = (bf16[192,384]{1,0:T(8,128)(2,1)}, bf16[192,384]{1,0:T(8,128)(2,1)S(1)}, u32[]{:S(2)}, u32[]{:S(2)}) collective-permute-start(bf16[192,384]{1,0:T(8,128)(2,1)} %get-tuple-element.64), channel_id=1, source_target_pairs={{0,1},{1,0},{2,3},{3,2},{4,5},{5,4},{6,7},{7,6},{8,9},{9,8},{10,11... | collective-permute-start | bytes 442376 | tf_op jit(solution)/shard_map/ppermute | solution.py:17
  88.8 2.1 %copy-start.9 = (f32[192,384]{1,0:T(8,128)}, f32[192,384]{1,0:T(8,128)S(1)}, u32[]{:S(2)}) copy-start(f32[192,384]{1,0:T(8,128)S(1)} %convert_add_fusion) | copy-start | bytes 884740
  89.5 4.7 %collective-permute-start.20 = (bf16[96,384]{1,0:T(8,128)(2,1)}, bf16[96,384]{1,0:T(8,128)(2,1)}, u32[]{:S(2)}, u32[]{:S(2)}) collective-permute-start(bf16[96,384]{1,0:T(8,128)(2,1)} %dynamic-slice_convert_fusion), channel_id=1, source_target_pairs={{0,2},{1,3},{2,0},{3,1},{4,6},{5,7},{6,4},{7,5},{8,10},{9,11},{10,... | collective-permute-start | bytes 221192 | tf_op jit(solution)/shard_map/ppermute | solution.py:17
  90.9 1.1 copy-start.3
  92.0 2.2 %copy-start.10 = (f32[192,384]{1,0:T(8,128)S(1)}, f32[192,384]{1,0:T(8,128)}, u32[]{:S(2)}) copy-start(f32[192,384]{1,0:T(8,128)} %copy-done.9) | copy-start | bytes 884740
  95.1 4.0 %collective-permute-start.21 = (bf16[48,384]{1,0:T(8,128)(2,1)S(1)}, bf16[48,384]{1,0:T(8,128)(2,1)S(1)}, u32[]{:S(2)}, u32[]{:S(2)}) collective-permute-start(bf16[48,384]{1,0:T(8,128)(2,1)S(1)} %dynamic-slice_convert_fusion.1), channel_id=1, source_target_pairs={{0,4},{4,0},{8,12},{12,8},{16,20},{20,16},{24,28},{28,24},{1,5},{5... | collective-permute-start | bytes 110600 | tf_op jit(solution)/shard_map/ppermute | solution.py:17
  99.2 4.2 %collective-permute-start.22 = (bf16[24,384]{1,0:T(8,128)(2,1)S(1)}, bf16[24,384]{1,0:T(8,128)(2,1)S(1)}, u32[]{:S(2)}, u32[]{:S(2)}) collective-permute-start(bf16[24,384]{1,0:T(8,128)(2,1)S(1)} %dynamic-slice_convert_fusion.2), channel_id=1, source_target_pairs={{0,8},{4,12},{8,0},{12,4},{16,24},{20,28},{24,16},{28,20},{1,9},{5... | collective-permute-start | bytes 55304 | tf_op jit(solution)/shard_map/ppermute | solution.py:17
  103.4 4.7 %collective-permute-start.23 = (bf16[12,384]{1,0:T(8,128)(2,1)S(1)}, bf16[12,384]{1,0:T(8,128)(2,1)S(1)}, u32[]{:S(2)}, u32[]{:S(2)}) collective-permute-start(bf16[12,384]{1,0:T(8,128)(2,1)S(1)} %dynamic-slice_convert_fusion.3), channel_id=1, source_target_pairs={{0,16},{4,20},{8,24},{12,28},{16,0},{20,4},{24,8},{28,12},{1,17},{... | collective-permute-start | bytes 27656 | tf_op jit(solution)/shard_map/ppermute | solution.py:17

commit v4 on v3

--- a/solution.py
+++ b/solution.py
@@ -9,6 +9,7 @@
 
 WINDOW = 3
 DIRECT = 8
+STAGE_BITS = (2, 1, 1)
 FAR_PARTS = 1
 
 
@@ -105,7 +106,7 @@
     )(odd, even)
 
 
-def pair_kernel(offset, slot, fars, sums, last, scale_by, *refs):
+def pair_kernel(offset, slot, fars, sums, wanted, scale_by, *refs):
     occ_ref, kpoint_ref, count_ref, row_ref, column_ref = refs[:5]
     occ_slots = occ_ref.shape[1]
     own_refs, refs = refs[5 : 5 + occ_slots], refs[5 + occ_slots :]
@@ -132,57 +133,70 @@
         scale = jnp.where(live, 1.0, 0.0).astype(jnp.float32)
         amplitude = coulomb * (scale / ((occ - vir_own) - vir_far))
         mixed = (2.0 * amplitude - amplitude.T).astype(jnp.bfloat16)
-        if last:
-            outs[-1][columns, :] = mixed
-        else:
+        if "gamma" in wanted:
             three = product(far, mixed, ((1,), (1,)))
-            outs[-1][:, columns] = three if not sums else sum_refs[1][:, columns] + three
-        term = product(mixed, amplitude.astype(jnp.bfloat16), ((1,), (1,)))
-        total = term if total is None else total + term
+            three = three if not sums else sum_refs[-1][:, columns] + three
+            outs[-1][:, columns] = three.astype(outs[-1].dtype)
+        if "density" in wanted:
+            term = product(mixed, amplitude.astype(jnp.bfloat16), ((1,), (1,)))
+            total = term if total is None else total + term
+    if "density" not in wanted:
+        return
     if sums:
         total = sum_refs[0][...] + total
-    if not last:
+    if "gamma" in wanted:
         outs[0][...] = total
         return
     total = total * scale_by
     if len(outs) == 2:
+        part = vir_count // (wide_count * group_count)
+        order = scatter_order(wide_count, group_count)
+        total = jnp.concatenate([total[part * place : part * (place + 1)] for place in order], axis=0)
+        split_parts(total, scatter_stages(wide_count, group_count)[0], outs[:1], outs[1])
+    else:
         outs[0][...] = total
-        return
-    sent_ref, kept_ref = outs[:2]
-    part = vir_count // (wide_count * group_count)
-    order = halving_order(wide_count, group_count)
-    total = jnp.concatenate([total[part * place : part * (place + 1)] for place in order], axis=0)
-    half = vir_count // 2
-    low = group % 2 == 0
-    sent_ref[...] = jnp.where(low, total[half:], total[:half]).astype(jnp.bfloat16)
-    kept_ref[...] = jnp.where(low, total[:half], total[half:])
-
-
-def gamma_kernel(sum_ref, mixed_ref, *refs):
-    far = rows_of(refs[:-1])
-    refs[-1][...] = (sum_ref[...] + product(far, mixed_ref[...], ((1,), (1,)))).astype(refs[-1].dtype)
+
+
+def split_parts(value, bits, sent_refs, kept_ref):
+    count = 2 ** len(bits)
+    rows = value.shape[0] // count
+    places = [lax.axis_index(axis) // mask % 2 for axis, mask in bits]
+
+    def part(flips):
+        candidates = [value[place * rows : (place + 1) * rows] for place in range(count)]
+        for position, place in enumerate(places):
+            upper = place != (flips >> (len(bits) - 1 - position)) % 2
+            half = len(candidates) // 2
+            candidates = [jnp.where(upper, high, low) for low, high in zip(candidates[:half], candidates[half:])]
+        return candidates[0]
+
+    kept_ref[...] = part(0)
+    for flips, sent_ref in enumerate(sent_refs, 1):
+        sent_ref[...] = part(flips).astype(sent_ref.dtype)
 
 
 VMEM = pl.BlockSpec(memory_space=pltpu.VMEM)
 SMEM = pl.BlockSpec(memory_space=pltpu.SMEM)
 
 
-def pair_terms(offset, slot, small, own, far, sums, last=False, scale_by=1.0):
+def pair_terms(offset, slot, small, own, far, sums, wanted=("density", "gamma"), scale_by=1.0):
     aux_count, vir_count = own[0].shape
     width = len(own) * vir_count
     density = jax.ShapeDtypeStruct((vir_count, vir_count), jnp.float32)
-    gamma = jax.ShapeDtypeStruct((aux_count, width), jnp.float32)
-    mixed = jax.ShapeDtypeStruct((width, vir_count), jnp.bfloat16)
     halves = [jax.ShapeDtypeStruct((vir_count // 2, vir_count), kind) for kind in (jnp.bfloat16, jnp.float32)]
-    split = vir_count % (lax.axis_size("wide") * lax.axis_size("narrow")) == 0
-    shapes = ((*halves, mixed) if split else (density, mixed)) if last else (density, gamma)
-    sums = sums[:1] if last else sums
+    if wanted == ("density",):
+        whole = vir_count % (lax.axis_size("wide") * lax.axis_size("narrow")) == 0
+        shapes, sums = (halves if whole else [density]), sums[:1]
+    elif wanted == ("gamma",):
+        shapes, sums = [jax.ShapeDtypeStruct((aux_count, width), jnp.bfloat16)], sums[1:]
+    else:
+        shapes = [density, jax.ShapeDtypeStruct((aux_count, width), jnp.float32)]
     operands = [*small, *own, *far, *sums]
     flops = 4 * aux_count * width * vir_count + 2 * width * vir_count * vir_count
     moved = 2 * aux_count * (width + vir_count) + 8 * vir_count * vir_count + 8 * aux_count * width
     return pl.pallas_call(
-        functools.partial(pair_kernel, offset, slot, len(far), len(sums), last, scale_by),
-        out_shape=shapes,
+        functools.partial(pair_kernel, offset, slot, len(far), len(sums), wanted, scale_by),
+        out_shape=tuple(shapes),
         in_specs=[SMEM] * 3 + [VMEM] * (len(operands) - 3),
         out_specs=tuple([VMEM] * len(shapes)),
         compiler_params=pltpu.CompilerParams(vmem_limit_bytes=32 * 1024 * 1024),
@@ -190,46 +204,75 @@
     )(*operands)
 
 
-def three_index(gamma, mixed, far):
-    aux_count, width = gamma.shape
-    vir_count = mixed.shape[1]
-    return pl.pallas_call(
-        gamma_kernel,
-        out_shape=jax.ShapeDtypeStruct((aux_count, width), jnp.bfloat16),
-        in_specs=[VMEM] * (2 + len(far)),
-        out_specs=VMEM,
-        compiler_params=pltpu.CompilerParams(vmem_limit_bytes=32 * 1024 * 1024),
-        cost_estimate=pl.CostEstimate(
-            flops=2 * aux_count * width * vir_count, bytes_accessed=6 * gamma.size, transcendentals=0
-        ),
-    )(gamma, mixed, *far)
-
-
-def halving_stages(wide_count, group_count):
-    stages = [("narrow", mask) for mask in reversed(bits_of(group_count))]
-    return stages + [("wide", mask) for mask in reversed(bits_of(wide_count))]
-
-
-def halving_order(wide_count, group_count):
+def scatter_stages(wide_count, group_count):
+    bits = [("narrow", mask) for mask in reversed(bits_of(group_count))]
+    bits += [("wide", mask) for mask in reversed(bits_of(wide_count))]
+    stages = [bits[:1]]
+    for size in STAGE_BITS:
+        stages.append(bits[sum(map(len, stages)) :][:size])
+    stages.append(bits[sum(map(len, stages)) :])
+    return [stage for stage in stages if stage]
+
+
+def scatter_order(wide_count, group_count):
     order = [0]
-    for axis, mask in reversed(halving_stages(wide_count, group_count)):
+    for axis, mask in reversed([bit for stage in scatter_stages(wide_count, group_count) for bit in stage]):
         step = mask * group_count if axis == "wide" else mask
         order = order + [place + step for place in order]
     return order
 
 
-def halved_sum(sent, kept, beside):
-    stages = halving_stages(lax.axis_size("wide"), lax.axis_size("narrow"))
-    for position, (axis, mask) in enumerate(stages):
-        value = kept + flip(sent, axis, mask).astype(jnp.float32)
-        if position + 1 < len(stages):
-            axis, mask = stages[position + 1]
-            bit = (lax.axis_index(axis) // mask) % 2
-            half = value.shape[0] // 2
-            sent = lax.dynamic_slice_in_dim(value, (1 - bit) * half, half, 0).astype(jnp.bfloat16)
-            kept = lax.dynamic_slice_in_dim(value, bit * half, half, 0)
-            sent = after(sent, beside) if position == 1 else sent
-    return value.reshape(-1)
+def flipped(value, bits, flips):
+    group_count = lax.axis_size("narrow")
+    masks = [mask * group_count if axis == "wide" else mask for axis, mask in bits]
+    step = sum(mask for place, mask in enumerate(reversed(masks)) if flips >> place & 1)
+    if len(bits) == 1:
+        return flip(value, *bits[0])
+    pairs = [(source, source ^ step) for source in range(lax.axis_size("wide") * group_count)]
+    return lax.ppermute(value, ("wide", "narrow"), pairs)
+
+
+def scatter_kernel(bits, got_count, *refs):
+    value = refs[got_count][...]
+    for got_ref in refs[:got_count]:
+        value = value + got_ref[...].astype(jnp.float32)
+    outs = refs[got_count + 1 :]
+    if bits:
+        split_parts(value, bits, outs[:-1], outs[-1])
+    elif outs[0].shape == value.shape:
+        outs[0][...] = value
+    else:
+        lanes = outs[0].shape[1]
+        tiles = value.shape[1] // lanes
+        for tile in range(tiles):
+            outs[0][pl.ds(tile, value.shape[0], tiles), :] = value[:, tile * lanes : (tile + 1) * lanes]
+
+
+def scattered_parts(sent, kept, beside):
+    stages = scatter_stages(lax.axis_size("wide"), lax.axis_size("narrow"))
+    sents = [sent]
+    for position, bits in enumerate(stages):
+        rows, columns = kept.shape
+        following = stages[position + 1] if position + 1 < len(stages) else []
+        if following:
+            part = (rows // 2 ** len(following), columns)
+            shapes = [jax.ShapeDtypeStruct(part, sent.dtype)] * (2 ** len(following) - 1)
+            shapes.append(jax.ShapeDtypeStruct(part, kept.dtype))
+        else:
+            lanes = 128 if columns % 128 == 0 else columns
+            shapes = [jax.ShapeDtypeStruct((rows * columns // lanes, lanes), kept.dtype)]
+        got = [flipped(value, bits, flips) for flips, value in enumerate(sents, 1)]
+        *sents, kept = pl.pallas_call(
+            functools.partial(scatter_kernel, following, len(got)),
+            out_shape=tuple(shapes),
+            in_specs=[VMEM] * (len(got) + 1),
+            out_specs=tuple([VMEM] * len(shapes)),
+            compiler_params=pltpu.CompilerParams(vmem_limit_bytes=8 * 1024 * 1024),
+            cost_estimate=pl.CostEstimate(flops=rows * columns, bytes_accessed=8 * rows * columns, transcendentals=0),
+        )(*got, kept)
+        if position == 1:
+            sents = [after(value, beside) for value in sents]
+    return kept.reshape(-1)
 
 
 def pack_kernel(slot, sets, raw_ref, *outs):
@@ -259,21 +302,22 @@
     return [jnp.concatenate([message[part] for message in arrived], axis=0) for part in range(2)]
 
 
-def sent_halving(raw, slot, earlier):
+def sent_halving(raw, slot):
     count = lax.axis_size("wide")
-    kept, message = packed(raw, slot, [list(range(count // 2)), list(range(count // 2, count))])
-    held = {offset: [kept[offset]] for offset in range(count // 2)}
-    for mask in bits_of(count)[:-1]:
+    masks = bits_of(count)[-2::-1]
+    sets = [[offset for offset in range(count) if offset & masks[0] == sent] for sent in (0, masks[0])]
+    kept, message = packed(raw, slot, sets)
+    held = {offset: {0: piece} for offset, piece in zip(sets[0], kept)}
+    for mask in masks:
         if message is None:
-            sent = [offset for offset in held if offset & mask]
-            message = jnp.stack([piece for offset in sent for piece in held.pop(offset)])
-            message = after(message, *earlier)
-        pieces = list(flip(message, "wide", mask))
+            sent = [held.pop(offset) for offset in sorted(held) if offset & mask]
+            message = jnp.stack([piece for pieces in sent for piece in pieces.values()])
+        pieces = iter(flip(message, "wide", mask))
         message = None
-        depth = len(pieces) // len(held)
-        for place, offset in enumerate(sorted(held)):
-            held[offset] = held[offset] + pieces[place * depth : (place + 1) * depth]
-    return [jnp.concatenate(held[part], axis=0) for part in range(2)]
+        for offset in sorted(held):
+            held[offset].update({place ^ mask: next(pieces) for place in list(held[offset])})
+    order = doubled(count)[: count // 2]
+    return [jnp.concatenate([held[part][place] for place in order], axis=0) for part in range(2)]
 
 
 def after(value, *earlier):
@@ -293,7 +337,7 @@
     rest = []
     for slot in range(raw.shape[2]):
         if slot:
-            mine, theirs = sent_halving(after(raw, mine_sent), slot, [mine])
+            mine, theirs = sent_halving(after(raw, mine_sent), slot)
             mine, theirs = after(mine, *facing_rows), after(theirs, own_rows[1])
         else:
             mine, theirs = sent_direct(raw, slot)
@@ -301,7 +345,7 @@
         first = lax.ppermute(mine, "narrow", half_turn)
         received = flip(theirs, "wide", 1)
         own_rows = [mine, received]
-        facing_rows = [first, lax.ppermute(after(received, *facing) if slot else after(received, first), "narrow", half_turn)]
+        facing_rows = [first, lax.ppermute(after(received, *facing) if slot else received, "narrow", half_turn)]
         if slot:
             own += fit(metric, [own_rows], [1])[0]
             rest.append(facing_rows)
@@ -374,10 +418,11 @@
     for slot in range(occ_slots - 1):
         sums = pair(1, slot, far=first[slot], sums=sums)
     norm_scale = 1.0 / (group_count * wide_count * vir_count)
-    *terms, mixed = pair(1, occ_slots - 1, far=first[-1], sums=sums, last=True, scale_by=norm_scale)
-    gamma = three_index(sums[1], mixed, first[-1])
+    last = functools.partial(pair, 1, occ_slots - 1, far=first[-1], sums=sums)
+    terms = last(wanted=("density",), scale_by=norm_scale)
+    (gamma,) = last(wanted=("gamma",))
     if len(terms) == 2:
-        virt_density = halved_sum(*terms, gamma)
+        virt_density = scattered_parts(*terms, gamma)
     else:
         virt_density = scattered_sum(*terms)
     return gamma.reshape(1, aux_count, 1, occ_slots, vir_count), virt_density

time: 109 us -> 103 us (0.945)
  waiting for transfers between devices: 36 us -> 32.1 us
  local copies, waits for them, and re-layouts: 6.96 us -> 3.7 us
  Pallas kernels: 23.9 us -> 25.7 us
    ppermute x18 -> x16, waiting for transfers between devices: 30.5 us -> 26.1 us  [flip(): return lax.ppermute(value, axis, pairs)]
    ppermute x2 -> x5, starting transfers between devices: 2.53 us -> 6.66 us  [the longest x3 3.55 us: flipped(): return lax.ppermute(value, ('wide', 'narrow'), pairs)]
    ppermute x18 -> x16, starting transfers between devices: 26.7 us -> 23.9 us  [flip(): return lax.ppermute(value, axis, pairs)]
    unnamed x26 -> x14, local copies, waits for them, and re-layouts: 4.22 us -> 2.32 us
    pallas_call x6 -> x7, Pallas kernels: 17.2 us -> 19 us  [pair_terms(): pl.pallas_call(functools.partial(pair_kernel, offset, slot, len(far), len...]
    ppermute x2, waiting for transfers between devices: 3.28 us -> 5.09 us  [from_ahead(): return lax.ppermute(value, axis, pairs)]
    ppermute x2, starting transfers between devices: 7.86 us -> 6.45 us  [from_ahead(): return lax.ppermute(value, axis, pairs)]
    ppermute x2 -> x5, waiting for transfers between devices: 2.17 us -> 0.89 us  [the longest x3 0.89 us: flipped(): return lax.ppermute(value, ('wide', 'narrow'), pairs)]
  transfers between devices with their start and end apart: 24 -> 25, of which waited for: 14 -> 13; matrix products, arithmetic and copies ran while one was open for 2% -> 2% of each run, Pallas kernels for 20% -> 22%
where the time goes in v4:
time: 103 us
  starting transfers between devices  40.2 us (39%)
  waiting for transfers between devices  32.1 us (31%)
  Pallas kernels  25.7 us (25%)
  local copies, waits for them, and re-layouts  3.7 us (4%)
    ppermute x16, waiting for transfers between devices, flip(): return lax.ppermute(value, axis, pairs)  26.1 us
    ppermute x16, starting transfers between devices, flip(): return lax.ppermute(value, axis, pairs)  23.9 us
    pallas_call x7, Pallas kernels, pair_terms(): pl.pallas_call(functools.partial(pair_kernel, offset, slot, len(far), len...  19 us
    ppermute x2, starting transfers between devices, from_ahead(): return lax.ppermute(value, axis, pairs)  6.45 us
    ppermute x2, waiting for transfers between devices, from_ahead(): return lax.ppermute(value, axis, pairs)  5.09 us
    ppermute x3, starting transfers between devices, flipped(): return lax.ppermute(value, ('wide', 'narrow'), pairs)  3.55 us
    pallas_call x3, Pallas kernels, fit(): pl.pallas_call(functools.partial(fit_kernel, len(metric), len(sources[0])...  3.43 us
    ppermute x2, starting transfers between devices, gathered_rows(): first = lax.ppermute(mine, 'narrow', half_turn)  3.11 us
  transfers between devices with their start and end apart: 25, of which 13 were waited for; matrix products, arithmetic and copies ran while one was open for 2% of the time, Pallas kernels for 22%

profile of v4, /device:TPU:0, one launch (start us, length us, event | category | flops | bytes accessed | tf_op | source)
XLA Modules:
  0.0 103.0 jit_solution(11495397104558401246)
XLA Ops:
  0.7 0.9 copy-done
  1.6 4.1 %collective-permute-start = (bf16[80,320]{1,0:T(8,128)(2,1)S(1)}, bf16[80,320]{1,0:T(8,128)(2,1)S(1)}, u32[]{:S(2)}, u32[]{:S(2)}) collective-permute-start(bf16[80,320]{1,0:T(8,128)(2,1)S(1)} %constant_dynamic-slice_fusion), channel_id=1, source_target_pairs={{0,16},{4,20},{8,24},{12,28},{16,0},{20,4},{24,8},{28,12},{1,17},{... | collective-permute-start | bytes 153608 | tf_op jit(solution)/shard_map/ppermute | solution.py:18
  5.7 1.2 %copy-done.1 = bf16[1,80,8,2,384]{4,3,2,1,0:T(2,128)(2,1)S(1)} copy-done((bf16[1,80,8,2,384]{4,3,2,1,0:T(2,128)(2,1)S(1)}, bf16[1,80,8,2,384]{4,3,2,1,0:T(2,128)(2,1)}, u32[]{:S(2)}) %copy-start.1) | copy-done | bytes 983064
  6.9 1.1 %shard_map.77 = (bf16[2,80,384]{2,1,0:T(8,128)(2,1)S(1)}, bf16[2,80,384]{2,1,0:T(8,128)(2,1)S(1)}, bf16[2,80,384]{2,1,0:T(8,128)(2,1)S(1)}, bf16[2,80,384]{2,1,0:T(8,128)(2,1)S(1)}) custom-call(bf16[80,8,2,384]{3,2,1,0:T(2,128)(2,1)S(1)} %bitcast.43), custom_call_target="tpu_custom_call" | custom-call | bytes 2949120 | tf_op jit(solution)/shard_map/pallas_call | solution.py:287
  8.1 1.9 %collective-permute-start.5 = (bf16[2,80,384]{2,1,0:T(8,128)(2,1)S(1)}, bf16[2,80,384]{2,1,0:T(8,128)(2,1)S(1)}, u32[]{:S(2)}, u32[]{:S(2)}) collective-permute-start(bf16[2,80,384]{2,1,0:T(8,128)(2,1)S(1)} %get-tuple-element.41), channel_id=1, source_target_pairs={{0,8},{4,12},{8,0},{12,4},{16,24},{20,28},{24,16},{28,20},{1,9},{5... | collective-permute-start | bytes 368648 | tf_op jit(solution)/shard_map/ppermute | solution.py:18
  10.0 2.5 %collective-permute-start.6 = (bf16[2,80,384]{2,1,0:T(8,128)(2,1)S(1)}, bf16[2,80,384]{2,1,0:T(8,128)(2,1)S(1)}, u32[]{:S(2)}, u32[]{:S(2)}) collective-permute-start(bf16[2,80,384]{2,1,0:T(8,128)(2,1)S(1)} %get-tuple-element.42), channel_id=1, source_target_pairs={{0,24},{4,28},{8,16},{12,20},{16,8},{20,12},{24,0},{28,4},{1,25},{... | collective-permute-start | bytes 368648 | tf_op jit(solution)/shard_map/ppermute | solution.py:18
  12.6 0.7 collective-permute-start.1
  13.3 1.1 %shard_map.79 = (bf16[4,80,384]{2,1,0:T(8,128)(2,1)S(1)}, bf16[4,80,384]{2,1,0:T(8,128)(2,1)S(1)}) custom-call(bf16[80,8,2,384]{3,2,1,0:T(2,128)(2,1)S(1)} %bitcast.44), custom_call_target="tpu_custom_call" | custom-call | bytes 2949120 | tf_op jit(solution)/shard_map/pallas_call | solution.py:287
  14.4 1.4 %collective-permute-start.10 = (bf16[4,80,384]{2,1,0:T(8,128)(2,1)S(1)}, bf16[4,80,384]{2,1,0:T(8,128)(2,1)S(1)}, u32[]{:S(2)}, u32[]{:S(2)}) collective-permute-start(bf16[4,80,384]{2,1,0:T(8,128)(2,1)S(1)} %get-tuple-element.46), channel_id=1, source_target_pairs={{0,8},{4,12},{8,0},{12,4},{16,24},{20,28},{24,16},{28,20},{1,9},{5... | collective-permute-start | bytes 737288 | tf_op jit(solution)/shard_map/ppermute | solution.py:18
  15.9 3.0 %collective-permute-done.4 = bf16[2,80,384]{2,1,0:T(8,128)(2,1)S(1)} collective-permute-done((bf16[2,80,384]{2,1,0:T(8,128)(2,1)S(1)}, bf16[2,80,384]{2,1,0:T(8,128)(2,1)S(1)}, u32[]{:S(2)}, u32[]{:S(2)}) %collective-permute-start.4) | collective-permute-done | bytes 122912 | tf_op jit(solution)/shard_map/ppermute | solution.py:18
  19.0 2.6 %collective-permute-done.6 = bf16[2,80,384]{2,1,0:T(8,128)(2,1)S(1)} collective-permute-done((bf16[2,80,384]{2,1,0:T(8,128)(2,1)S(1)}, bf16[2,80,384]{2,1,0:T(8,128)(2,1)S(1)}, u32[]{:S(2)}, u32[]{:S(2)}) %collective-permute-start.6) | collective-permute-done | bytes 122912 | tf_op jit(solution)/shard_map/ppermute | solution.py:18
  21.6 1.6 %collective-permute-start.7 = (bf16[320,384]{1,0:T(8,128)(2,1)S(1)}, bf16[320,384]{1,0:T(8,128)(2,1)S(1)}, u32[]{:S(2)}, u32[]{:S(2)}) collective-permute-start(bf16[320,384]{1,0:T(8,128)(2,1)S(1)} %pad_maximum_fusion.3), channel_id=1, source_target_pairs={{0,4},{4,0},{8,12},{12,8},{16,20},{20,16},{24,28},{28,24},{1,5},{5... | collective-permute-start | bytes 737288 | tf_op jit(solution)/shard_map/ppermute | solution.py:18
  23.8 2.4 %collective-permute-done.10 = bf16[4,80,384]{2,1,0:T(8,128)(2,1)S(1)} collective-permute-done((bf16[4,80,384]{2,1,0:T(8,128)(2,1)S(1)}, bf16[4,80,384]{2,1,0:T(8,128)(2,1)S(1)}, u32[]{:S(2)}, u32[]{:S(2)}) %collective-permute-start.10) | collective-permute-done | bytes 245792 | tf_op jit(solution)/shard_map/ppermute | solution.py:18
  26.2 2.5 %collective-permute-start.11 = (bf16[4,80,384]{2,1,0:T(8,128)(2,1)S(1)}, bf16[4,80,384]{2,1,0:T(8,128)(2,1)S(1)}, u32[]{:S(2)}, u32[]{:S(2)}) collective-permute-start(bf16[4,80,384]{2,1,0:T(8,128)(2,1)S(1)} %pad_maximum_fusion.4), channel_id=1, source_target_pairs={{0,16},{4,20},{8,24},{12,28},{16,0},{20,4},{24,8},{28,12},{1,17},{... | collective-permute-start | bytes 737288 | tf_op jit(solution)/shard_map/ppermute | solution.py:18
  28.8 1.6 %collective-permute-start.8 = (bf16[320,384]{1,0:T(8,128)(2,1)S(1)}, bf16[320,384]{1,0:T(8,128)(2,1)S(1)}, u32[]{:S(2)}, u32[]{:S(2)}) collective-permute-start(bf16[320,384]{1,0:T(8,128)(2,1)S(1)} %pad_maximum_fusion.2.refs_2_), channel_id=1, source_target_pairs={{0,2},{1,3},{2,0},{3,1},{4,6},{5,7},{6,4},{7,5},{8,10},{9,11},{10,... | collective-permute-start | bytes 737288 | tf_op jit(solution)/shard_map/ppermute | solution.py:345
  30.3 1.4 %collective-permute-done.2 = bf16[320,320]{1,0:T(8,128)(2,1)S(1)} collective-permute-done((bf16[320,320]{1,0:T(8,128)(2,1)S(1)}, bf16[320,320]{1,0:T(8,128)(2,1)S(1)}, u32[]{:S(2)}, u32[]{:S(2)}) %collective-permute-start.2) | collective-permute-done | bytes 204832 | tf_op jit(solution)/shard_map/ppermute | solution.py:18
  31.9 1.6 %collective-permute-start.9 = (bf16[320,384]{1,0:T(8,128)(2,1)S(1)}, bf16[320,384]{1,0:T(8,128)(2,1)S(1)}, u32[]{:S(2)}, u32[]{:S(2)}) collective-permute-start(bf16[320,384]{1,0:T(8,128)(2,1)S(1)} %collective-permute-done.7.refs_3_), channel_id=1, source_target_pairs={{0,2},{1,3},{2,0},{3,1},{4,6},{5,7},{6,4},{7,5},{8,10},{9,11},{10,... | collective-permute-start | bytes 737288 | tf_op jit(solution)/shard_map/ppermute | solution.py:348
  33.5 5.6 %collective-permute-done.11 = bf16[4,80,384]{2,1,0:T(8,128)(2,1)S(1)} collective-permute-done((bf16[4,80,384]{2,1,0:T(8,128)(2,1)S(1)}, bf16[4,80,384]{2,1,0:T(8,128)(2,1)S(1)}, u32[]{:S(2)}, u32[]{:S(2)}) %collective-permute-start.11) | collective-permute-done | bytes 245792 | tf_op jit(solution)/shard_map/ppermute | solution.py:18
  39.2 1.6 %collective-permute-start.12 = (bf16[320,384]{1,0:T(8,128)(2,1)S(1)}, bf16[320,384]{1,0:T(8,128)(2,1)S(1)}, u32[]{:S(2)}, u32[]{:S(2)}) collective-permute-start(bf16[320,384]{1,0:T(8,128)(2,1)S(1)} %pad_maximum_fusion.6), channel_id=1, source_target_pairs={{0,4},{4,0},{8,12},{12,8},{16,20},{20,16},{24,28},{28,24},{1,5},{5... | collective-permute-start | bytes 737288 | tf_op jit(solution)/shard_map/ppermute | solution.py:18
  40.9 1.6 %collective-permute-start.13 = (bf16[320,384]{1,0:T(8,128)(2,1)S(1)}, bf16[320,384]{1,0:T(8,128)(2,1)S(1)}, u32[]{:S(2)}, u32[]{:S(2)}) collective-permute-start(bf16[320,384]{1,0:T(8,128)(2,1)S(1)} %pad_maximum_fusion.5.refs_2_), channel_id=1, source_target_pairs={{0,2},{1,3},{2,0},{3,1},{4,6},{5,7},{6,4},{7,5},{8,10},{9,11},{10,... | collective-permute-start | bytes 737288 | tf_op jit(solution)/shard_map/ppermute | solution.py:345
  42.4 1.1 %shard_map.78 = (bf16[640,384]{1,0:T(8,128)(2,1)S(1)}, bf16[640,384]{1,0:T(8,128)(2,1)S(1)}) custom-call(bf16[640,320]{1,0:T(8,128)(2,1)S(1)} %pad_maximum_fusion.refs_0_, bf16[640,320]{1,0:T(8,128)(2,1)S(1)} %collective-permute-done.3.refs_1_, bf16[320,384]{1,0:T(8,128)(2,1)S(1)} %pad_maximum_fusion.2.refs_2_, ...), custom_call_target="tpu_custom_call" | custom-call | flops 629145600 | bytes 2785280 | tf_op jit(solution)/shard_map/pallas_call | solution.py:75
  43.6 2.1 %collective-permute-done.12.refs_3_ = bf16[320,384]{1,0:T(8,128)(2,1)S(1)} collective-permute-done((bf16[320,384]{1,0:T(8,128)(2,1)S(1)}, bf16[320,384]{1,0:T(8,128)(2,1)S(1)}, u32[]{:S(2)}, u32[]{:S(2)}) %collective-permute-start.12) | collective-permute-done | bytes 245792 | tf_op jit(solution)/shard_map/ppermute | solution.py:18
  45.7 1.6 %collective-permute-start.14 = (bf16[320,384]{1,0:T(8,128)(2,1)S(1)}, bf16[320,384]{1,0:T(8,128)(2,1)}, u32[]{:S(2)}, u32[]{:S(2)}) collective-permute-start(bf16[320,384]{1,0:T(8,128)(2,1)S(1)} %collective-permute-done.12.refs_3_), channel_id=1, source_target_pairs={{0,2},{1,3},{2,0},{3,1},{4,6},{5,7},{6,4},{7,5},{8,10},{9,11},{10,... | collective-permute-start | bytes 737288 | tf_op jit(solution)/shard_map/ppermute | solution.py:348
  47.3 4.6 %collective-permute-start.15 = (bf16[640,384]{1,0:T(8,128)(2,1)S(1)}, bf16[640,384]{1,0:T(8,128)(2,1)S(1)}, u32[]{:S(2)}, u32[]{:S(2)}) collective-permute-start(bf16[640,384]{1,0:T(8,128)(2,1)S(1)} %get-tuple-element.54.refs_7_.odd_ref), channel_id=1, source_target_pairs={{0,24},{4,28},{8,0},{12,4},{16,8},{20,12},{24,16},{28,20},{1,25},{... | collective-permute-start | bytes 1474568 | tf_op jit(solution)/shard_map/ppermute | solution.py:24
  52.1 0.7 shard_map.80.refs_6_
  52.8 2.9 %shard_map.81 = (f32[384,384]{1,0:T(8,128)S(1)}, f32[640,768]{1,0:T(8,128)S(1)}) custom-call(f32[8,2]{1,0:T(8,128)S(1)} %copy.14.refs_0_, s32[4,8]{1,0:T(4,128)S(1)} %copy-done.3, s32[4,8]{1,0:T(4,128)S(1)} %copy-done.4, f32[4,384]{1,0:T(4,128)S(1)} %copy-done.2, f32[384,4]{1,0:T(8,128)S(1)} %bitcast.36, bf16[640,384]{1,0:T(8,128)(2,1)S(1)} %get-tuple-element.43.refs_5_, ...), custom_call_target="tpu_custom_call" | custom-call | flops 981467136 | bytes 6586368 | tf_op jit(solution)/shard_map/pallas_call | solution.py:197
  55.7 1.6 %shard_map.82.refs_7_.odd_ref = bf16[640,384]{1,0:T(8,128)(2,1)S(1)} custom-call(bf16[640,320]{1,0:T(8,128)(2,1)S(1)} %pad_maximum_fusion.refs_0_, bf16[640,320]{1,0:T(8,128)(2,1)S(1)} %collective-permute-done.3.refs_1_, bf16[320,384]{1,0:T(8,128)(2,1)S(1)} %collective-permute-done.13.refs_2_, bf16[320,384]{1,0:T(8,128)(2,1)} %collective-permute-done.14.refs_3_), custom_call_target="tpu_custom_call" | custom-call | flops 314572800 | bytes 1802240 | tf_op jit(solution)/shard_map/pallas_call | solution.py:75
  57.3 1.9 %collective-permute-start.16 = (bf16[640,384]{1,0:T(8,128)(2,1)S(1)}, bf16[640,384]{1,0:T(8,128)(2,1)S(1)}, u32[]{:S(2)}, u32[]{:S(2)}) collective-permute-start(bf16[640,384]{1,0:T(8,128)(2,1)S(1)} %shard_map.82.refs_7_.odd_ref), channel_id=1, source_target_pairs={{0,24},{4,28},{8,0},{12,4},{16,8},{20,12},{24,16},{28,20},{1,25},{... | collective-permute-start | bytes 1474568 | tf_op jit(solution)/shard_map/ppermute | solution.py:24
  59.2 4.4 %collective-permute-done.15.even_ref.refs_7_ = bf16[640,384]{1,0:T(8,128)(2,1)S(1)} collective-permute-done((bf16[640,384]{1,0:T(8,128)(2,1)S(1)}, bf16[640,384]{1,0:T(8,128)(2,1)S(1)}, u32[]{:S(2)}, u32[]{:S(2)}) %collective-permute-start.15) | collective-permute-done | bytes 491552 | tf_op jit(solution)/shard_map/ppermute | solution.py:24
  63.8 1.6 %collective-permute-start.18 = (bf16[640,384]{1,0:T(8,128)(2,1)S(1)}, bf16[640,384]{1,0:T(8,128)(2,1)S(1)}, u32[]{:S(2)}, u32[]{:S(2)}) collective-permute-start(bf16[640,384]{1,0:T(8,128)(2,1)S(1)} %shard_map.83), channel_id=1, source_target_pairs={{0,4},{4,0},{8,12},{12,8},{16,20},{20,16},{24,28},{28,24},{1,5},{5... | collective-permute-start | bytes 1474568 | tf_op jit(solution)/shard_map/ppermute | solution.py:18
  65.3 2.9 %shard_map.84 = (f32[384,384]{1,0:T(8,128)S(1)}, f32[640,768]{1,0:T(8,128)S(1)}) custom-call(f32[8,2]{1,0:T(8,128)S(1)} %copy.14.refs_0_, s32[4,8]{1,0:T(4,128)S(1)} %copy-done.3, s32[4,8]{1,0:T(4,128)S(1)} %copy-done.4, f32[4,384]{1,0:T(4,128)S(1)} %copy-done.2, f32[384,4]{1,0:T(8,128)S(1)} %bitcast.37, bf16[640,384]{1,0:T(8,128)(2,1)S(1)} %get-tuple-element.43.refs_5_, ...), custom_call_target="tpu_custom_call" | custom-call | flops 981467136 | bytes 6586368 | tf_op jit(solution)/shard_map/pallas_call | solution.py:197
  68.3 2.9 %shard_map.85 = (f32[384,384]{1,0:T(8,128)S(1)}, f32[640,768]{1,0:T(8,128)S(1)}) custom-call(f32[8,2]{1,0:T(8,128)S(1)} %copy.14.refs_0_, s32[4,8]{1,0:T(4,128)S(1)} %copy-done.3, s32[4,8]{1,0:T(4,128)S(1)} %copy-done.4, f32[4,384]{1,0:T(4,128)S(1)} %copy-done.2, f32[384,4]{1,0:T(8,128)S(1)} %bitcast.38, bf16[640,384]{1,0:T(8,128)(2,1)S(1)} %get-tuple-element.43.refs_5_, ...), custom_call_target="tpu_custom_call" | custom-call | flops 981467136 | bytes 6586368 | tf_op jit(solution)/shard_map/pallas_call | solution.py:197
  71.2 0.7 collective-permute-done.16.even_ref.refs_7_
  72.0 1.6 %collective-permute-start.17 = (bf16[640,384]{1,0:T(8,128)(2,1)S(1)}, bf16[640,384]{1,0:T(8,128)(2,1)S(1)}, u32[]{:S(2)}, u32[]{:S(2)}) collective-permute-start(bf16[640,384]{1,0:T(8,128)(2,1)S(1)} %shard_map.86), channel_id=1, source_target_pairs={{0,4},{4,0},{8,12},{12,8},{16,20},{20,16},{24,28},{28,24},{1,5},{5... | collective-permute-start | bytes 1474568 | tf_op jit(solution)/shard_map/ppermute | solution.py:18
  73.6 2.9 %shard_map.87 = (f32[384,384]{1,0:T(8,128)S(1)}, f32[640,768]{1,0:T(8,128)S(1)}) custom-call(f32[8,2]{1,0:T(8,128)S(1)} %copy.14.refs_0_, s32[4,8]{1,0:T(4,128)S(1)} %copy-done.3, s32[4,8]{1,0:T(4,128)S(1)} %copy-done.4, f32[4,384]{1,0:T(4,128)S(1)} %copy-done.2, f32[384,4]{1,0:T(8,128)S(1)} %bitcast.39, bf16[640,384]{1,0:T(8,128)(2,1)S(1)} %get-tuple-element.43.refs_5_, ...), custom_call_target="tpu_custom_call" | custom-call | flops 981467136 | bytes 6586368 | tf_op jit(solution)/shard_map/pallas_call | solution.py:197
  76.5 2.9 %shard_map.88 = (f32[384,384]{1,0:T(8,128)S(1)}, f32[640,768]{1,0:T(8,128)S(1)}) custom-call(f32[8,2]{1,0:T(8,128)S(1)} %copy.14.refs_0_, s32[4,8]{1,0:T(4,128)S(1)} %copy-done.3, s32[4,8]{1,0:T(4,128)S(1)} %copy-done.4, f32[4,384]{1,0:T(4,128)S(1)} %copy-done.2, f32[384,4]{1,0:T(8,128)S(1)} %bitcast.40, bf16[640,384]{1,0:T(8,128)(2,1)S(1)} %get-tuple-element.43.refs_5_, ...), custom_call_target="tpu_custom_call" | custom-call | flops 981467136 | bytes 6586368 | tf_op jit(solution)/shard_map/pallas_call | solution.py:197
  79.4 3.9 %collective-permute-done.17.refs_7_ = bf16[640,384]{1,0:T(8,128)(2,1)S(1)} collective-permute-done((bf16[640,384]{1,0:T(8,128)(2,1)S(1)}, bf16[640,384]{1,0:T(8,128)(2,1)S(1)}, u32[]{:S(2)}, u32[]{:S(2)}) %collective-permute-start.17) | collective-permute-done | bytes 491552 | tf_op jit(solution)/shard_map/ppermute | solution.py:18
  83.3 2.0 %shard_map.90 = (bf16[192,384]{1,0:T(8,128)(2,1)S(1)}, f32[192,384]{1,0:T(8,128)S(1)}) custom-call(f32[8,2]{1,0:T(8,128)S(1)} %copy.14.refs_0_, s32[4,8]{1,0:T(4,128)S(1)} %copy-done.3, s32[4,8]{1,0:T(4,128)S(1)} %copy-done.4, f32[4,384]{1,0:T(4,128)S(1)} %copy-done.2, f32[384,4]{1,0:T(8,128)S(1)} %bitcast.41, ...), custom_call_target="tpu_custom_call" | custom-call | flops 981467136 | bytes 6586368 | tf_op jit(solution)/shard_map/pallas_call | solution.py:197
  85.4 1.4 %collective-permute-done.19.refs_0_ = bf16[192,384]{1,0:T(8,128)(2,1)S(1)} collective-permute-done((bf16[192,384]{1,0:T(8,128)(2,1)S(1)}, bf16[192,384]{1,0:T(8,128)(2,1)S(1)}, u32[]{:S(2)}, u32[]{:S(2)}) %collective-permute-start.19) | collective-permute-done | bytes 147488 | tf_op jit(solution)/shard_map/ppermute | solution.py:18
  86.8 1.6 %collective-permute-start.20 = (bf16[48,384]{1,0:T(8,128)(2,1)S(1)}, bf16[48,384]{1,0:T(8,128)(2,1)S(1)}, u32[]{:S(2)}, u32[]{:S(2)}) collective-permute-start(bf16[48,384]{1,0:T(8,128)(2,1)S(1)} %get-tuple-element.67), channel_id=1, source_target_pairs={{0,4},{1,5},{2,6},{3,7},{4,0},{5,1},{6,2},{7,3},{8,12},{9,13},{10,... | collective-permute-start | bytes 110600 | tf_op jit(solution)/shard_map/ppermute | solution.py:232
  88.9 1.4 %collective-permute-start.22 = (bf16[48,384]{1,0:T(8,128)(2,1)S(1)}, bf16[48,384]{1,0:T(8,128)(2,1)S(1)}, u32[]{:S(2)}, u32[]{:S(2)}) collective-permute-start(bf16[48,384]{1,0:T(8,128)(2,1)S(1)} %get-tuple-element.69), channel_id=1, source_target_pairs={{0,6},{1,7},{2,4},{3,5},{4,2},{5,3},{6,0},{7,1},{8,14},{9,15},{10,... | collective-permute-start | bytes 110600 | tf_op jit(solution)/shard_map/ppermute | solution.py:232
  90.4 2.5 %shard_map.89 = bf16[640,768]{1,0:T(8,128)(2,1)S(1)} custom-call(f32[8,2]{1,0:T(8,128)S(1)} %copy.14.refs_0_, s32[4,8]{1,0:T(4,128)S(1)} %copy-done.3, s32[4,8]{1,0:T(4,128)S(1)} %copy-done.4, f32[4,384]{1,0:T(4,128)S(1)} %copy-done.2, f32[384,4]{1,0:T(8,128)S(1)} %bitcast.42, bf16[640,384]{1,0:T(8,128)(2,1)S(1)} %get-tuple-element.43.refs_5_, ...), custom_call_target="tpu_custom_call" | custom-call | flops 981467136 | bytes 6586368 | tf_op jit(solution)/shard_map/pallas_call | solution.py:197
  92.9 0.9 collective-permute-done.22.refs_2_
  93.8 0.8 collective-permute-start.23
  94.6 3.0 %collective-permute-done.23.refs_0_ = bf16[24,384]{1,0:T(8,128)(2,1)S(1)} collective-permute-done((bf16[24,384]{1,0:T(8,128)(2,1)S(1)}, bf16[24,384]{1,0:T(8,128)(2,1)S(1)}, u32[]{:S(2)}, u32[]{:S(2)}) %collective-permute-start.23) | collective-permute-done | bytes 18464 | tf_op jit(solution)/shard_map/ppermute | solution.py:18
  97.7 2.9 %collective-permute-start.24 = (bf16[12,384]{1,0:T(8,128)(2,1)S(1)}, bf16[12,384]{1,0:T(8,128)(2,1)S(1)}, u32[]{:S(2)}, u32[]{:S(2)}) collective-permute-start(bf16[12,384]{1,0:T(8,128)(2,1)S(1)} %get-tuple-element.74), channel_id=1, source_target_pairs={{0,16},{4,20},{8,24},{12,28},{16,0},{20,4},{24,8},{28,12},{1,17},{... | collective-permute-start | bytes 27656 | tf_op jit(solution)/shard_map/ppermute | solution.py:18
  100.6 1.2 %reshape.10 = bf16[1,640,1,2,384]{4,3,1,2,0:T(2,128)(2,1)} reshape(bf16[640,768]{1,0:T(8,128)(2,1)S(1)} %shard_map.89) | data formatting | bytes 1966080 | tf_op jit(solution)/shard_map/reshape | solution.py:428
  102.3 0.6 shard_map.94
  (51 shorter events, 3.0 us)
Async XLA Ops:
  0.6 0.9 copy-start
  1.6 10.9 %collective-permute-start = (bf16[80,320]{1,0:T(8,128)(2,1)S(1)}, bf16[80,320]{1,0:T(8,128)(2,1)S(1)}, u32[]{:S(2)}, u32[]{:S(2)}) collective-permute-start(bf16[80,320]{1,0:T(8,128)(2,1)S(1)} %constant_dynamic-slice_fusion), channel_id=1, source_target_pairs={{0,16},{4,20},{8,24},{12,28},{16,0},{20,4},{24,8},{28,12},{1,17},{... | collective-permute-start | bytes 153608 | tf_op jit(solution)/shard_map/ppermute | solution.py:18
  5.7 1.2 %copy-start.1 = (bf16[1,80,8,2,384]{4,3,2,1,0:T(2,128)(2,1)S(1)}, bf16[1,80,8,2,384]{4,3,2,1,0:T(2,128)(2,1)}, u32[]{:S(2)}) copy-start(bf16[1,80,8,2,384]{4,3,2,1,0:T(2,128)(2,1)} %param.6) | copy-start | bytes 2949124
  8.1 10.9 %collective-permute-start.4 = (bf16[2,80,384]{2,1,0:T(8,128)(2,1)S(1)}, bf16[2,80,384]{2,1,0:T(8,128)(2,1)S(1)}, u32[]{:S(2)}, u32[]{:S(2)}) collective-permute-start(bf16[2,80,384]{2,1,0:T(8,128)(2,1)S(1)} %get-tuple-element.40), channel_id=1, source_target_pairs={{0,16},{4,20},{8,24},{12,28},{16,0},{20,4},{24,8},{28,12},{1,17},{... | collective-permute-start | bytes 368648 | tf_op jit(solution)/shard_map/ppermute | solution.py:18
  8.1 10.8 %collective-permute-start.5 = (bf16[2,80,384]{2,1,0:T(8,128)(2,1)S(1)}, bf16[2,80,384]{2,1,0:T(8,128)(2,1)S(1)}, u32[]{:S(2)}, u32[]{:S(2)}) collective-permute-start(bf16[2,80,384]{2,1,0:T(8,128)(2,1)S(1)} %get-tuple-element.41), channel_id=1, source_target_pairs={{0,8},{4,12},{8,0},{12,4},{16,24},{20,28},{24,16},{28,20},{1,9},{5... | collective-permute-start | bytes 368648 | tf_op jit(solution)/shard_map/ppermute | solution.py:18
  10.0 11.5 %collective-permute-start.6 = (bf16[2,80,384]{2,1,0:T(8,128)(2,1)S(1)}, bf16[2,80,384]{2,1,0:T(8,128)(2,1)S(1)}, u32[]{:S(2)}, u32[]{:S(2)}) collective-permute-start(bf16[2,80,384]{2,1,0:T(8,128)(2,1)S(1)} %get-tuple-element.42), channel_id=1, source_target_pairs={{0,24},{4,28},{8,16},{12,20},{16,8},{20,12},{24,0},{28,4},{1,25},{... | collective-permute-start | bytes 368648 | tf_op jit(solution)/shard_map/ppermute | solution.py:18
  12.6 10.6 %collective-permute-start.1 = (bf16[160,320]{1,0:T(8,128)(2,1)S(1)}, bf16[160,320]{1,0:T(8,128)(2,1)S(1)}, u32[]{:S(2)}, u32[]{:S(2)}) collective-permute-start(bf16[160,320]{1,0:T(8,128)(2,1)S(1)} %pad_maximum_fusion.7), channel_id=1, source_target_pairs={{0,8},{4,12},{8,0},{12,4},{16,24},{20,28},{24,16},{28,20},{1,9},{5... | collective-permute-start | bytes 307208 | tf_op jit(solution)/shard_map/ppermute | solution.py:18
  14.4 11.7 %collective-permute-start.10 = (bf16[4,80,384]{2,1,0:T(8,128)(2,1)S(1)}, bf16[4,80,384]{2,1,0:T(8,128)(2,1)S(1)}, u32[]{:S(2)}, u32[]{:S(2)}) collective-permute-start(bf16[4,80,384]{2,1,0:T(8,128)(2,1)S(1)} %get-tuple-element.46), channel_id=1, source_target_pairs={{0,8},{4,12},{8,0},{12,4},{16,24},{20,28},{24,16},{28,20},{1,9},{5... | collective-permute-start | bytes 737288 | tf_op jit(solution)/shard_map/ppermute | solution.py:18
  21.6 10.3 %collective-permute-start.7 = (bf16[320,384]{1,0:T(8,128)(2,1)S(1)}, bf16[320,384]{1,0:T(8,128)(2,1)S(1)}, u32[]{:S(2)}, u32[]{:S(2)}) collective-permute-start(bf16[320,384]{1,0:T(8,128)(2,1)S(1)} %pad_maximum_fusion.3), channel_id=1, source_target_pairs={{0,4},{4,0},{8,12},{12,8},{16,20},{20,16},{24,28},{28,24},{1,5},{5... | collective-permute-start | bytes 737288 | tf_op jit(solution)/shard_map/ppermute | solution.py:18
  23.2 8.5 %collective-permute-start.2 = (bf16[320,320]{1,0:T(8,128)(2,1)S(1)}, bf16[320,320]{1,0:T(8,128)(2,1)S(1)}, u32[]{:S(2)}, u32[]{:S(2)}) collective-permute-start(bf16[320,320]{1,0:T(8,128)(2,1)S(1)} %pad_maximum_fusion.1), channel_id=1, source_target_pairs={{0,4},{4,0},{8,12},{12,8},{16,20},{20,16},{24,28},{28,24},{1,5},{5... | collective-permute-start | bytes 614408 | tf_op jit(solution)/shard_map/ppermute | solution.py:18
  26.2 12.9 %collective-permute-start.11 = (bf16[4,80,384]{2,1,0:T(8,128)(2,1)S(1)}, bf16[4,80,384]{2,1,0:T(8,128)(2,1)S(1)}, u32[]{:S(2)}, u32[]{:S(2)}) collective-permute-start(bf16[4,80,384]{2,1,0:T(8,128)(2,1)S(1)} %pad_maximum_fusion.4), channel_id=1, source_target_pairs={{0,16},{4,20},{8,24},{12,28},{16,0},{20,4},{24,8},{28,12},{1,17},{... | collective-permute-start | bytes 737288 | tf_op jit(solution)/shard_map/ppermute | solution.py:18
  28.8 12.1 %collective-permute-start.8 = (bf16[320,384]{1,0:T(8,128)(2,1)S(1)}, bf16[320,384]{1,0:T(8,128)(2,1)S(1)}, u32[]{:S(2)}, u32[]{:S(2)}) collective-permute-start(bf16[320,384]{1,0:T(8,128)(2,1)S(1)} %pad_maximum_fusion.2.refs_2_), channel_id=1, source_target_pairs={{0,2},{1,3},{2,0},{3,1},{4,6},{5,7},{6,4},{7,5},{8,10},{9,11},{10,... | collective-permute-start | bytes 737288 | tf_op jit(solution)/shard_map/ppermute | solution.py:345
  31.8 20.0 %copy-start.5 = (f32[8,2]{0,1:T(2,128)S(1)}, f32[8,2]{0,1:T(2,128)}, u32[]{:S(2)}) copy-start(f32[8,2]{0,1:T(2,128)} %param.8) | copy-start | bytes 196
  31.8 20.1 %copy-start.2 = (f32[4,384]{1,0:T(4,128)S(1)}, f32[4,384]{1,0:T(4,128)}, u32[]{:S(2)}) copy-start(f32[4,384]{1,0:T(4,128)} %refs_3_.13) | copy-start | bytes 18436
  31.9 10.6 %collective-permute-start.3 = (bf16[640,320]{1,0:T(8,128)(2,1)S(1)}, bf16[640,320]{1,0:T(8,128)(2,1)S(1)}, u32[]{:S(2)}, u32[]{:S(2)}) collective-permute-start(bf16[640,320]{1,0:T(8,128)(2,1)S(1)} %pad_maximum_fusion.refs_0_), channel_id=1, source_target_pairs={{0,1},{1,0},{2,3},{3,2},{4,5},{5,4},{6,7},{7,6},{8,9},{9,8},{10,11... | collective-permute-start | bytes 1228808 | tf_op jit(solution)/shard_map/ppermute | solution.py:18
  31.9 8.9 %collective-permute-start.9 = (bf16[320,384]{1,0:T(8,128)(2,1)S(1)}, bf16[320,384]{1,0:T(8,128)(2,1)S(1)}, u32[]{:S(2)}, u32[]{:S(2)}) collective-permute-start(bf16[320,384]{1,0:T(8,128)(2,1)S(1)} %collective-permute-done.7.refs_3_), channel_id=1, source_target_pairs={{0,2},{1,3},{2,0},{3,1},{4,6},{5,7},{6,4},{7,5},{8,10},{9,11},{10,... | collective-permute-start | bytes 737288 | tf_op jit(solution)/shard_map/ppermute | solution.py:348
  39.2 6.5 %collective-permute-start.12 = (bf16[320,384]{1,0:T(8,128)(2,1)S(1)}, bf16[320,384]{1,0:T(8,128)(2,1)S(1)}, u32[]{:S(2)}, u32[]{:S(2)}) collective-permute-start(bf16[320,384]{1,0:T(8,128)(2,1)S(1)} %pad_maximum_fusion.6), channel_id=1, source_target_pairs={{0,4},{4,0},{8,12},{12,8},{16,20},{20,16},{24,28},{28,24},{1,5},{5... | collective-permute-start | bytes 737288 | tf_op jit(solution)/shard_map/ppermute | solution.py:18
  40.8 11.9 %copy-start.3 = (s32[4,8]{1,0:T(4,128)S(1)}, s32[4,8]{1,0:T(4,128)}, u32[]{:S(2)}) copy-start(s32[4,8]{1,0:T(4,128)} %refs_1_.13) | copy-start | bytes 388
  40.8 11.9 %copy-start.4 = (s32[4,8]{1,0:T(4,128)S(1)}, s32[4,8]{1,0:T(4,128)}, u32[]{:S(2)}) copy-start(s32[4,8]{1,0:T(4,128)} %refs_2_.13) | copy-start | bytes 388
  40.9 14.8 %collective-permute-start.13 = (bf16[320,384]{1,0:T(8,128)(2,1)S(1)}, bf16[320,384]{1,0:T(8,128)(2,1)S(1)}, u32[]{:S(2)}, u32[]{:S(2)}) collective-permute-start(bf16[320,384]{1,0:T(8,128)(2,1)S(1)} %pad_maximum_fusion.5.refs_2_), channel_id=1, source_target_pairs={{0,2},{1,3},{2,0},{3,1},{4,6},{5,7},{6,4},{7,5},{8,10},{9,11},{10,... | collective-permute-start | bytes 737288 | tf_op jit(solution)/shard_map/ppermute | solution.py:345
  45.7 10.0 %collective-permute-start.14 = (bf16[320,384]{1,0:T(8,128)(2,1)S(1)}, bf16[320,384]{1,0:T(8,128)(2,1)}, u32[]{:S(2)}, u32[]{:S(2)}) collective-permute-start(bf16[320,384]{1,0:T(8,128)(2,1)S(1)} %collective-permute-done.12.refs_3_), channel_id=1, source_target_pairs={{0,2},{1,3},{2,0},{3,1},{4,6},{5,7},{6,4},{7,5},{8,10},{9,11},{10,... | collective-permute-start | bytes 737288 | tf_op jit(solution)/shard_map/ppermute | solution.py:348
  47.3 16.3 %collective-permute-start.15 = (bf16[640,384]{1,0:T(8,128)(2,1)S(1)}, bf16[640,384]{1,0:T(8,128)(2,1)S(1)}, u32[]{:S(2)}, u32[]{:S(2)}) collective-permute-start(bf16[640,384]{1,0:T(8,128)(2,1)S(1)} %get-tuple-element.54.refs_7_.odd_ref), channel_id=1, source_target_pairs={{0,24},{4,28},{8,0},{12,4},{16,8},{20,12},{24,16},{28,20},{1,25},{... | collective-permute-start | bytes 1474568 | tf_op jit(solution)/shard_map/ppermute | solution.py:24
  57.3 14.6 %collective-permute-start.16 = (bf16[640,384]{1,0:T(8,128)(2,1)S(1)}, bf16[640,384]{1,0:T(8,128)(2,1)S(1)}, u32[]{:S(2)}, u32[]{:S(2)}) collective-permute-start(bf16[640,384]{1,0:T(8,128)(2,1)S(1)} %shard_map.82.refs_7_.odd_ref), channel_id=1, source_target_pairs={{0,24},{4,28},{8,0},{12,4},{16,8},{20,12},{24,16},{28,20},{1,25},{... | collective-permute-start | bytes 1474568 | tf_op jit(solution)/shard_map/ppermute | solution.py:24
  63.8 12.7 %collective-permute-start.18 = (bf16[640,384]{1,0:T(8,128)(2,1)S(1)}, bf16[640,384]{1,0:T(8,128)(2,1)S(1)}, u32[]{:S(2)}, u32[]{:S(2)}) collective-permute-start(bf16[640,384]{1,0:T(8,128)(2,1)S(1)} %shard_map.83), channel_id=1, source_target_pairs={{0,4},{4,0},{8,12},{12,8},{16,20},{20,16},{24,28},{28,24},{1,5},{5... | collective-permute-start | bytes 1474568 | tf_op jit(solution)/shard_map/ppermute | solution.py:18
  72.0 11.3 %collective-permute-start.17 = (bf16[640,384]{1,0:T(8,128)(2,1)S(1)}, bf16[640,384]{1,0:T(8,128)(2,1)S(1)}, u32[]{:S(2)}, u32[]{:S(2)}) collective-permute-start(bf16[640,384]{1,0:T(8,128)(2,1)S(1)} %shard_map.86), channel_id=1, source_target_pairs={{0,4},{4,0},{8,12},{12,8},{16,20},{20,16},{24,28},{28,24},{1,5},{5... | collective-permute-start | bytes 1474568 | tf_op jit(solution)/shard_map/ppermute | solution.py:18
  85.3 1.4 %collective-permute-start.19 = (bf16[192,384]{1,0:T(8,128)(2,1)S(1)}, bf16[192,384]{1,0:T(8,128)(2,1)S(1)}, u32[]{:S(2)}, u32[]{:S(2)}) collective-permute-start(bf16[192,384]{1,0:T(8,128)(2,1)S(1)} %get-tuple-element.65), channel_id=1, source_target_pairs={{0,1},{1,0},{2,3},{3,2},{4,5},{5,4},{6,7},{7,6},{8,9},{9,8},{10,11... | collective-permute-start | bytes 442376 | tf_op jit(solution)/shard_map/ppermute | solution.py:18
  86.8 6.1 %collective-permute-start.20 = (bf16[48,384]{1,0:T(8,128)(2,1)S(1)}, bf16[48,384]{1,0:T(8,128)(2,1)S(1)}, u32[]{:S(2)}, u32[]{:S(2)}) collective-permute-start(bf16[48,384]{1,0:T(8,128)(2,1)S(1)} %get-tuple-element.67), channel_id=1, source_target_pairs={{0,4},{1,5},{2,6},{3,7},{4,0},{5,1},{6,2},{7,3},{8,12},{9,13},{10,... | collective-permute-start | bytes 110600 | tf_op jit(solution)/shard_map/ppermute | solution.py:232
  88.4 4.5 %collective-permute-start.21 = (bf16[48,384]{1,0:T(8,128)(2,1)S(1)}, bf16[48,384]{1,0:T(8,128)(2,1)S(1)}, u32[]{:S(2)}, u32[]{:S(2)}) collective-permute-start(bf16[48,384]{1,0:T(8,128)(2,1)S(1)} %get-tuple-element.68), channel_id=1, source_target_pairs={{0,2},{1,3},{2,0},{3,1},{4,6},{5,7},{6,4},{7,5},{8,10},{9,11},{10,... | collective-permute-start | bytes 110600 | tf_op jit(solution)/shard_map/ppermute | solution.py:232
  88.9 4.9 %collective-permute-start.22 = (bf16[48,384]{1,0:T(8,128)(2,1)S(1)}, bf16[48,384]{1,0:T(8,128)(2,1)S(1)}, u32[]{:S(2)}, u32[]{:S(2)}) collective-permute-start(bf16[48,384]{1,0:T(8,128)(2,1)S(1)} %get-tuple-element.69), channel_id=1, source_target_pairs={{0,6},{1,7},{2,4},{3,5},{4,2},{5,3},{6,0},{7,1},{8,14},{9,15},{10,... | collective-permute-start | bytes 110600 | tf_op jit(solution)/shard_map/ppermute | solution.py:232
  93.8 3.8 %collective-permute-start.23 = (bf16[24,384]{1,0:T(8,128)(2,1)S(1)}, bf16[24,384]{1,0:T(8,128)(2,1)S(1)}, u32[]{:S(2)}, u32[]{:S(2)}) collective-permute-start(bf16[24,384]{1,0:T(8,128)(2,1)S(1)} %get-tuple-element.72), channel_id=1, source_target_pairs={{0,8},{4,12},{8,0},{12,4},{16,24},{20,28},{24,16},{28,20},{1,9},{5... | collective-permute-start | bytes 55304 | tf_op jit(solution)/shard_map/ppermute | solution.py:18
  97.7 4.7 %collective-permute-start.24 = (bf16[12,384]{1,0:T(8,128)(2,1)S(1)}, bf16[12,384]{1,0:T(8,128)(2,1)S(1)}, u32[]{:S(2)}, u32[]{:S(2)}) collective-permute-start(bf16[12,384]{1,0:T(8,128)(2,1)S(1)} %get-tuple-element.74), channel_id=1, source_target_pairs={{0,16},{4,20},{8,24},{12,28},{16,0},{20,4},{24,8},{28,12},{1,17},{... | collective-permute-start | bytes 27656 | tf_op jit(solution)/shard_map/ppermute | solution.py:18

commit v5 on v4

--- a/solution.py
+++ b/solution.py
@@ -179,7 +179,7 @@
 SMEM = pl.BlockSpec(memory_space=pltpu.SMEM)
 
 
-def pair_terms(offset, slot, small, own, far, sums, wanted=("density", "gamma"), scale_by=1.0):
+def pair_terms(offset, slot, small, own, far, sums, wanted=("density", "gamma"), scale_by=1.0, weight=1):
     aux_count, vir_count = own[0].shape
     width = len(own) * vir_count
     density = jax.ShapeDtypeStruct((vir_count, vir_count), jnp.float32)
@@ -192,8 +192,8 @@
     else:
         shapes = [density, jax.ShapeDtypeStruct((aux_count, width), jnp.float32)]
     operands = [*small, *own, *far, *sums]
-    flops = 4 * aux_count * width * vir_count + 2 * width * vir_count * vir_count
-    moved = 2 * aux_count * (width + vir_count) + 8 * vir_count * vir_count + 8 * aux_count * width
+    flops = weight * (4 * aux_count * width * vir_count + 2 * width * vir_count * vir_count)
+    moved = weight * (2 * aux_count * (width + vir_count) + 8 * vir_count * vir_count + 8 * aux_count * width)
     return pl.pallas_call(
         functools.partial(pair_kernel, offset, slot, len(far), len(sums), wanted, scale_by),
         out_shape=tuple(shapes),
@@ -404,7 +404,7 @@
         ahead.append(facing)
         second.append([from_ahead(part, "wide", 2) for part in facing])
         if slot == 0:
-            sums = pair(0, slot, far=facing, sums=sums)
+            sums = pair(0, slot, far=facing, sums=sums, weight=8)
     for slot in range(occ_slots):
         if wide_count % 2 == 0:
             chosen = [choice(after(odd, *sums), even) for odd, even in zip(ahead[slot], second[slot])]

time: 103 us -> 101 us (0.981)
  starting transfers between devices: 40.2 us -> 35.9 us
  waiting for transfers between devices: 32.1 us -> 35 us
    ppermute x16, starting transfers between devices: 23.9 us -> 20.5 us  [flip(): return lax.ppermute(value, axis, pairs)]
    ppermute x2, waiting for transfers between devices: 5.09 us -> 1.93 us  [from_ahead(): return lax.ppermute(value, axis, pairs)]
    ppermute x2, waiting for transfers between devices: 0.01 us -> 2.9 us  [gathered_rows(): lax.ppermute(after(received, *facing) if slot else received, 'narrow', ha...]
    ppermute x16, waiting for transfers between devices: 26.1 us -> 28.4 us  [flip(): return lax.ppermute(value, axis, pairs)]
  transfers between devices with their start and end apart: 25 -> 25, of which waited for: 13 -> 12; matrix products, arithmetic and copies ran while one was open for 2% -> 2% of each run, Pallas kernels for 22% -> 22%
where the time goes in v5:
time: 101 us
  starting transfers between devices  35.9 us (36%)
  waiting for transfers between devices  35 us (35%)
  Pallas kernels  24.8 us (25%)
  local copies, waits for them, and re-layouts  3.7 us (4%)
  between operations  1.01 us (1%)
    ppermute x16, waiting for transfers between devices, flip(): return lax.ppermute(value, axis, pairs)  28.4 us
    ppermute x16, starting transfers between devices, flip(): return lax.ppermute(value, axis, pairs)  20.5 us
    pallas_call x7, Pallas kernels, pair_terms(): pl.pallas_call(functools.partial(pair_kernel, offset, slot, len(far), len...  19 us
    ppermute x2, starting transfers between devices, from_ahead(): return lax.ppermute(value, axis, pairs)  6.59 us
    ppermute x3, starting transfers between devices, flipped(): return lax.ppermute(value, ('wide', 'narrow'), pairs)  3.55 us
    ppermute x2, starting transfers between devices, gathered_rows(): first = lax.ppermute(mine, 'narrow', half_turn)  3.11 us
    ppermute x2, waiting for transfers between devices, gathered_rows(): lax.ppermute(after(received, *facing) if slot else received, 'narrow', ha...  2.9 us
    pallas_call x3, Pallas kernels, fit(): pl.pallas_call(functools.partial(fit_kernel, len(metric), len(sources[0])...  2.5 us
  transfers between devices with their start and end apart: 25, of which 12 were waited for; matrix products, arithmetic and copies ran while one was open for 2% of the time, Pallas kernels for 22%

profile of v5, /device:TPU:0, one launch (start us, length us, event | category | flops | bytes accessed | tf_op | source)
XLA Modules:
  0.0 100.7 jit_solution(15076758713022259414)
XLA Ops:
  0.7 0.9 copy-done
  1.6 4.1 %collective-permute-start = (bf16[80,320]{1,0:T(8,128)(2,1)S(1)}, bf16[80,320]{1,0:T(8,128)(2,1)S(1)}, u32[]{:S(2)}, u32[]{:S(2)}) collective-permute-start(bf16[80,320]{1,0:T(8,128)(2,1)S(1)} %constant_dynamic-slice_fusion), channel_id=1, source_target_pairs={{0,16},{4,20},{8,24},{12,28},{16,0},{20,4},{24,8},{28,12},{1,17},{... | collective-permute-start | bytes 153608 | tf_op jit(solution)/shard_map/ppermute | solution.py:18
  5.7 1.2 %copy-done.1 = bf16[1,80,8,2,384]{4,3,2,1,0:T(2,128)(2,1)S(1)} copy-done((bf16[1,80,8,2,384]{4,3,2,1,0:T(2,128)(2,1)S(1)}, bf16[1,80,8,2,384]{4,3,2,1,0:T(2,128)(2,1)}, u32[]{:S(2)}) %copy-start.1) | copy-done | bytes 983064
  6.9 1.1 %shard_map.77 = (bf16[2,80,384]{2,1,0:T(8,128)(2,1)S(1)}, bf16[2,80,384]{2,1,0:T(8,128)(2,1)S(1)}, bf16[2,80,384]{2,1,0:T(8,128)(2,1)S(1)}, bf16[2,80,384]{2,1,0:T(8,128)(2,1)S(1)}) custom-call(bf16[80,8,2,384]{3,2,1,0:T(2,128)(2,1)S(1)} %bitcast.43), custom_call_target="tpu_custom_call" | custom-call | bytes 2949120 | tf_op jit(solution)/shard_map/pallas_call | solution.py:287
  8.1 1.9 %collective-permute-start.5 = (bf16[2,80,384]{2,1,0:T(8,128)(2,1)S(1)}, bf16[2,80,384]{2,1,0:T(8,128)(2,1)S(1)}, u32[]{:S(2)}, u32[]{:S(2)}) collective-permute-start(bf16[2,80,384]{2,1,0:T(8,128)(2,1)S(1)} %get-tuple-element.41), channel_id=1, source_target_pairs={{0,8},{4,12},{8,0},{12,4},{16,24},{20,28},{24,16},{28,20},{1,9},{5... | collective-permute-start | bytes 368648 | tf_op jit(solution)/shard_map/ppermute | solution.py:18
  10.0 2.5 %collective-permute-start.6 = (bf16[2,80,384]{2,1,0:T(8,128)(2,1)S(1)}, bf16[2,80,384]{2,1,0:T(8,128)(2,1)S(1)}, u32[]{:S(2)}, u32[]{:S(2)}) collective-permute-start(bf16[2,80,384]{2,1,0:T(8,128)(2,1)S(1)} %get-tuple-element.42), channel_id=1, source_target_pairs={{0,24},{4,28},{8,16},{12,20},{16,8},{20,12},{24,0},{28,4},{1,25},{... | collective-permute-start | bytes 368648 | tf_op jit(solution)/shard_map/ppermute | solution.py:18
  12.6 0.7 collective-permute-start.1
  13.3 1.1 %shard_map.79 = (bf16[4,80,384]{2,1,0:T(8,128)(2,1)S(1)}, bf16[4,80,384]{2,1,0:T(8,128)(2,1)S(1)}) custom-call(bf16[80,8,2,384]{3,2,1,0:T(2,128)(2,1)S(1)} %bitcast.44), custom_call_target="tpu_custom_call" | custom-call | bytes 2949120 | tf_op jit(solution)/shard_map/pallas_call | solution.py:287
  14.4 1.4 %collective-permute-start.10 = (bf16[4,80,384]{2,1,0:T(8,128)(2,1)S(1)}, bf16[4,80,384]{2,1,0:T(8,128)(2,1)S(1)}, u32[]{:S(2)}, u32[]{:S(2)}) collective-permute-start(bf16[4,80,384]{2,1,0:T(8,128)(2,1)S(1)} %get-tuple-element.46), channel_id=1, source_target_pairs={{0,8},{4,12},{8,0},{12,4},{16,24},{20,28},{24,16},{28,20},{1,9},{5... | collective-permute-start | bytes 737288 | tf_op jit(solution)/shard_map/ppermute | solution.py:18
  15.9 3.0 %collective-permute-done.4 = bf16[2,80,384]{2,1,0:T(8,128)(2,1)S(1)} collective-permute-done((bf16[2,80,384]{2,1,0:T(8,128)(2,1)S(1)}, bf16[2,80,384]{2,1,0:T(8,128)(2,1)S(1)}, u32[]{:S(2)}, u32[]{:S(2)}) %collective-permute-start.4) | collective-permute-done | bytes 122912 | tf_op jit(solution)/shard_map/ppermute | solution.py:18
  19.0 2.6 %collective-permute-done.6 = bf16[2,80,384]{2,1,0:T(8,128)(2,1)S(1)} collective-permute-done((bf16[2,80,384]{2,1,0:T(8,128)(2,1)S(1)}, bf16[2,80,384]{2,1,0:T(8,128)(2,1)S(1)}, u32[]{:S(2)}, u32[]{:S(2)}) %collective-permute-start.6) | collective-permute-done | bytes 122912 | tf_op jit(solution)/shard_map/ppermute | solution.py:18
  21.6 1.6 %collective-permute-start.7 = (bf16[320,384]{1,0:T(8,128)(2,1)S(1)}, bf16[320,384]{1,0:T(8,128)(2,1)S(1)}, u32[]{:S(2)}, u32[]{:S(2)}) collective-permute-start(bf16[320,384]{1,0:T(8,128)(2,1)S(1)} %pad_maximum_fusion.3), channel_id=1, source_target_pairs={{0,4},{4,0},{8,12},{12,8},{16,20},{20,16},{24,28},{28,24},{1,5},{5... | collective-permute-start | bytes 737288 | tf_op jit(solution)/shard_map/ppermute | solution.py:18
  23.2 0.6 collective-permute-start.2
  23.8 2.3 %collective-permute-done.10 = bf16[4,80,384]{2,1,0:T(8,128)(2,1)S(1)} collective-permute-done((bf16[4,80,384]{2,1,0:T(8,128)(2,1)S(1)}, bf16[4,80,384]{2,1,0:T(8,128)(2,1)S(1)}, u32[]{:S(2)}, u32[]{:S(2)}) %collective-permute-start.10) | collective-permute-done | bytes 245792 | tf_op jit(solution)/shard_map/ppermute | solution.py:18
  26.2 2.5 %collective-permute-start.11 = (bf16[4,80,384]{2,1,0:T(8,128)(2,1)S(1)}, bf16[4,80,384]{2,1,0:T(8,128)(2,1)S(1)}, u32[]{:S(2)}, u32[]{:S(2)}) collective-permute-start(bf16[4,80,384]{2,1,0:T(8,128)(2,1)S(1)} %pad_maximum_fusion.4), channel_id=1, source_target_pairs={{0,16},{4,20},{8,24},{12,28},{16,0},{20,4},{24,8},{28,12},{1,17},{... | collective-permute-start | bytes 737288 | tf_op jit(solution)/shard_map/ppermute | solution.py:18
  28.8 1.6 %collective-permute-start.8 = (bf16[320,384]{1,0:T(8,128)(2,1)S(1)}, bf16[320,384]{1,0:T(8,128)(2,1)S(1)}, u32[]{:S(2)}, u32[]{:S(2)}) collective-permute-start(bf16[320,384]{1,0:T(8,128)(2,1)S(1)} %pad_maximum_fusion.2.refs_2_), channel_id=1, source_target_pairs={{0,2},{1,3},{2,0},{3,1},{4,6},{5,7},{6,4},{7,5},{8,10},{9,11},{10,... | collective-permute-start | bytes 737288 | tf_op jit(solution)/shard_map/ppermute | solution.py:345
  30.3 1.5 %collective-permute-done.2 = bf16[320,320]{1,0:T(8,128)(2,1)S(1)} collective-permute-done((bf16[320,320]{1,0:T(8,128)(2,1)S(1)}, bf16[320,320]{1,0:T(8,128)(2,1)S(1)}, u32[]{:S(2)}, u32[]{:S(2)}) %collective-permute-start.2) | collective-permute-done | bytes 204832 | tf_op jit(solution)/shard_map/ppermute | solution.py:18
  31.9 1.6 %collective-permute-start.9 = (bf16[320,384]{1,0:T(8,128)(2,1)S(1)}, bf16[320,384]{1,0:T(8,128)(2,1)S(1)}, u32[]{:S(2)}, u32[]{:S(2)}) collective-permute-start(bf16[320,384]{1,0:T(8,128)(2,1)S(1)} %collective-permute-done.7.refs_3_), channel_id=1, source_target_pairs={{0,2},{1,3},{2,0},{3,1},{4,6},{5,7},{6,4},{7,5},{8,10},{9,11},{10,... | collective-permute-start | bytes 737288 | tf_op jit(solution)/shard_map/ppermute | solution.py:348
  33.5 5.6 %collective-permute-done.11 = bf16[4,80,384]{2,1,0:T(8,128)(2,1)S(1)} collective-permute-done((bf16[4,80,384]{2,1,0:T(8,128)(2,1)S(1)}, bf16[4,80,384]{2,1,0:T(8,128)(2,1)S(1)}, u32[]{:S(2)}, u32[]{:S(2)}) %collective-permute-start.11) | collective-permute-done | bytes 245792 | tf_op jit(solution)/shard_map/ppermute | solution.py:18
  39.2 1.6 %collective-permute-start.12 = (bf16[320,384]{1,0:T(8,128)(2,1)S(1)}, bf16[320,384]{1,0:T(8,128)(2,1)S(1)}, u32[]{:S(2)}, u32[]{:S(2)}) collective-permute-start(bf16[320,384]{1,0:T(8,128)(2,1)S(1)} %pad_maximum_fusion.6), channel_id=1, source_target_pairs={{0,4},{4,0},{8,12},{12,8},{16,20},{20,16},{24,28},{28,24},{1,5},{5... | collective-permute-start | bytes 737288 | tf_op jit(solution)/shard_map/ppermute | solution.py:18
  41.1 1.6 %collective-permute-start.13 = (bf16[320,384]{1,0:T(8,128)(2,1)S(1)}, bf16[320,384]{1,0:T(8,128)(2,1)S(1)}, u32[]{:S(2)}, u32[]{:S(2)}) collective-permute-start(bf16[320,384]{1,0:T(8,128)(2,1)S(1)} %pad_maximum_fusion.5.refs_2_), channel_id=1, source_target_pairs={{0,2},{1,3},{2,0},{3,1},{4,6},{5,7},{6,4},{7,5},{8,10},{9,11},{10,... | collective-permute-start | bytes 737288 | tf_op jit(solution)/shard_map/ppermute | solution.py:345
  42.7 1.1 %shard_map.78 = (bf16[640,384]{1,0:T(8,128)(2,1)S(1)}, bf16[640,384]{1,0:T(8,128)(2,1)S(1)}) custom-call(bf16[640,320]{1,0:T(8,128)(2,1)S(1)} %pad_maximum_fusion.refs_0_, bf16[640,320]{1,0:T(8,128)(2,1)S(1)} %collective-permute-done.3.refs_1_, bf16[320,384]{1,0:T(8,128)(2,1)S(1)} %pad_maximum_fusion.2.refs_2_, ...), custom_call_target="tpu_custom_call" | custom-call | flops 629145600 | bytes 2785280 | tf_op jit(solution)/shard_map/pallas_call | solution.py:75
  43.8 3.3 %collective-permute-start.15 = (bf16[640,384]{1,0:T(8,128)(2,1)S(1)}, bf16[640,384]{1,0:T(8,128)(2,1)S(1)}, u32[]{:S(2)}, u32[]{:S(2)}) collective-permute-start(bf16[640,384]{1,0:T(8,128)(2,1)S(1)} %get-tuple-element.54.refs_7_.odd_ref), channel_id=1, source_target_pairs={{0,24},{4,28},{8,0},{12,4},{16,8},{20,12},{24,16},{28,20},{1,25},{... | collective-permute-start | bytes 1474568 | tf_op jit(solution)/shard_map/ppermute | solution.py:24
  47.1 0.5 collective-permute-start.14
  47.6 0.7 shard_map.80.refs_6_
  48.3 2.9 %shard_map.81 = (f32[384,384]{1,0:T(8,128)S(1)}, f32[640,768]{1,0:T(8,128)S(1)}) custom-call(f32[8,2]{1,0:T(8,128)S(1)} %copy.14.refs_0_, s32[4,8]{1,0:T(4,128)S(1)} %copy-done.3, s32[4,8]{1,0:T(4,128)S(1)} %copy-done.4, f32[4,384]{1,0:T(4,128)S(1)} %copy-done.2, f32[384,4]{1,0:T(8,128)S(1)} %bitcast.36, bf16[640,384]{1,0:T(8,128)(2,1)S(1)} %get-tuple-element.43.refs_5_, ...), custom_call_target="tpu_custom_call" | custom-call | flops 7851737088 | bytes 52690944 | tf_op jit(solution)/shard_map/pallas_call | solution.py:197
  51.2 2.9 %collective-permute-done.14.refs_3_ = bf16[320,384]{1,0:T(8,128)(2,1)S(1)} collective-permute-done((bf16[320,384]{1,0:T(8,128)(2,1)S(1)}, bf16[320,384]{1,0:T(8,128)(2,1)S(1)}, u32[]{:S(2)}, u32[]{:S(2)}) %collective-permute-start.14) | collective-permute-done | bytes 245792 | tf_op jit(solution)/shard_map/ppermute | solution.py:348
  54.1 0.7 shard_map.82.refs_7_.odd_ref
  54.8 3.3 %collective-permute-start.16 = (bf16[640,384]{1,0:T(8,128)(2,1)S(1)}, bf16[640,384]{1,0:T(8,128)(2,1)S(1)}, u32[]{:S(2)}, u32[]{:S(2)}) collective-permute-start(bf16[640,384]{1,0:T(8,128)(2,1)S(1)} %shard_map.82.refs_7_.odd_ref), channel_id=1, source_target_pairs={{0,24},{4,28},{8,0},{12,4},{16,8},{20,12},{24,16},{28,20},{1,25},{... | collective-permute-start | bytes 1474568 | tf_op jit(solution)/shard_map/ppermute | solution.py:24
  58.4 1.6 %collective-permute-start.18 = (bf16[640,384]{1,0:T(8,128)(2,1)S(1)}, bf16[640,384]{1,0:T(8,128)(2,1)S(1)}, u32[]{:S(2)}, u32[]{:S(2)}) collective-permute-start(bf16[640,384]{1,0:T(8,128)(2,1)S(1)} %shard_map.83), channel_id=1, source_target_pairs={{0,4},{4,0},{8,12},{12,8},{16,20},{20,16},{24,28},{28,24},{1,5},{5... | collective-permute-start | bytes 1474568 | tf_op jit(solution)/shard_map/ppermute | solution.py:18
  59.9 2.9 %shard_map.84 = (f32[384,384]{1,0:T(8,128)S(1)}, f32[640,768]{1,0:T(8,128)S(1)}) custom-call(f32[8,2]{1,0:T(8,128)S(1)} %copy.14.refs_0_, s32[4,8]{1,0:T(4,128)S(1)} %copy-done.3, s32[4,8]{1,0:T(4,128)S(1)} %copy-done.4, f32[4,384]{1,0:T(4,128)S(1)} %copy-done.2, f32[384,4]{1,0:T(8,128)S(1)} %bitcast.37, bf16[640,384]{1,0:T(8,128)(2,1)S(1)} %get-tuple-element.43.refs_5_, ...), custom_call_target="tpu_custom_call" | custom-call | flops 981467136 | bytes 6586368 | tf_op jit(solution)/shard_map/pallas_call | solution.py:197
  62.9 2.9 %shard_map.85 = (f32[384,384]{1,0:T(8,128)S(1)}, f32[640,768]{1,0:T(8,128)S(1)}) custom-call(f32[8,2]{1,0:T(8,128)S(1)} %copy.14.refs_0_, s32[4,8]{1,0:T(4,128)S(1)} %copy-done.3, s32[4,8]{1,0:T(4,128)S(1)} %copy-done.4, f32[4,384]{1,0:T(4,128)S(1)} %copy-done.2, f32[384,4]{1,0:T(8,128)S(1)} %bitcast.38, bf16[640,384]{1,0:T(8,128)(2,1)S(1)} %get-tuple-element.43.refs_5_, ...), custom_call_target="tpu_custom_call" | custom-call | flops 981467136 | bytes 6586368 | tf_op jit(solution)/shard_map/pallas_call | solution.py:197
  65.8 1.9 %collective-permute-done.16.even_ref.refs_7_ = bf16[640,384]{1,0:T(8,128)(2,1)S(1)} collective-permute-done((bf16[640,384]{1,0:T(8,128)(2,1)S(1)}, bf16[640,384]{1,0:T(8,128)(2,1)S(1)}, u32[]{:S(2)}, u32[]{:S(2)}) %collective-permute-start.16) | collective-permute-done | bytes 491552 | tf_op jit(solution)/shard_map/ppermute | solution.py:24
  67.8 0.9 collective-permute-start.17
  68.7 2.9 %shard_map.87 = (f32[384,384]{1,0:T(8,128)S(1)}, f32[640,768]{1,0:T(8,128)S(1)}) custom-call(f32[8,2]{1,0:T(8,128)S(1)} %copy.14.refs_0_, s32[4,8]{1,0:T(4,128)S(1)} %copy-done.3, s32[4,8]{1,0:T(4,128)S(1)} %copy-done.4, f32[4,384]{1,0:T(4,128)S(1)} %copy-done.2, f32[384,4]{1,0:T(8,128)S(1)} %bitcast.39, bf16[640,384]{1,0:T(8,128)(2,1)S(1)} %get-tuple-element.43.refs_5_, ...), custom_call_target="tpu_custom_call" | custom-call | flops 981467136 | bytes 6586368 | tf_op jit(solution)/shard_map/pallas_call | solution.py:197
  71.6 2.9 %shard_map.88 = (f32[384,384]{1,0:T(8,128)S(1)}, f32[640,768]{1,0:T(8,128)S(1)}) custom-call(f32[8,2]{1,0:T(8,128)S(1)} %copy.14.refs_0_, s32[4,8]{1,0:T(4,128)S(1)} %copy-done.3, s32[4,8]{1,0:T(4,128)S(1)} %copy-done.4, f32[4,384]{1,0:T(4,128)S(1)} %copy-done.2, f32[384,4]{1,0:T(8,128)S(1)} %bitcast.40, bf16[640,384]{1,0:T(8,128)(2,1)S(1)} %get-tuple-element.43.refs_5_, ...), custom_call_target="tpu_custom_call" | custom-call | flops 981467136 | bytes 6586368 | tf_op jit(solution)/shard_map/pallas_call | solution.py:197
  74.5 5.6 %collective-permute-done.17.refs_7_ = bf16[640,384]{1,0:T(8,128)(2,1)S(1)} collective-permute-done((bf16[640,384]{1,0:T(8,128)(2,1)S(1)}, bf16[640,384]{1,0:T(8,128)(2,1)S(1)}, u32[]{:S(2)}, u32[]{:S(2)}) %collective-permute-start.17) | collective-permute-done | bytes 491552 | tf_op jit(solution)/shard_map/ppermute | solution.py:18
  80.1 2.0 %shard_map.90 = (bf16[192,384]{1,0:T(8,128)(2,1)S(1)}, f32[192,384]{1,0:T(8,128)S(1)}) custom-call(f32[8,2]{1,0:T(8,128)S(1)} %copy.14.refs_0_, s32[4,8]{1,0:T(4,128)S(1)} %copy-done.3, s32[4,8]{1,0:T(4,128)S(1)} %copy-done.4, f32[4,384]{1,0:T(4,128)S(1)} %copy-done.2, f32[384,4]{1,0:T(8,128)S(1)} %bitcast.41, ...), custom_call_target="tpu_custom_call" | custom-call | flops 981467136 | bytes 6586368 | tf_op jit(solution)/shard_map/pallas_call | solution.py:197
  82.1 1.4 %collective-permute-done.19.refs_0_ = bf16[192,384]{1,0:T(8,128)(2,1)S(1)} collective-permute-done((bf16[192,384]{1,0:T(8,128)(2,1)S(1)}, bf16[192,384]{1,0:T(8,128)(2,1)S(1)}, u32[]{:S(2)}, u32[]{:S(2)}) %collective-permute-start.19) | collective-permute-done | bytes 147488 | tf_op jit(solution)/shard_map/ppermute | solution.py:18
  83.6 1.6 %collective-permute-start.20 = (bf16[48,384]{1,0:T(8,128)(2,1)S(1)}, bf16[48,384]{1,0:T(8,128)(2,1)S(1)}, u32[]{:S(2)}, u32[]{:S(2)}) collective-permute-start(bf16[48,384]{1,0:T(8,128)(2,1)S(1)} %get-tuple-element.67), channel_id=1, source_target_pairs={{0,4},{1,5},{2,6},{3,7},{4,0},{5,1},{6,2},{7,3},{8,12},{9,13},{10,... | collective-permute-start | bytes 110600 | tf_op jit(solution)/shard_map/ppermute | solution.py:232
  85.2 1.5 %collective-permute-start.21 = (bf16[48,384]{1,0:T(8,128)(2,1)S(1)}, bf16[48,384]{1,0:T(8,128)(2,1)S(1)}, u32[]{:S(2)}, u32[]{:S(2)}) collective-permute-start(bf16[48,384]{1,0:T(8,128)(2,1)S(1)} %get-tuple-element.68), channel_id=1, source_target_pairs={{0,2},{1,3},{2,0},{3,1},{4,6},{5,7},{6,4},{7,5},{8,10},{9,11},{10,... | collective-permute-start | bytes 110600 | tf_op jit(solution)/shard_map/ppermute | solution.py:232
  87.1 2.5 %shard_map.89 = bf16[640,768]{1,0:T(8,128)(2,1)S(1)} custom-call(f32[8,2]{1,0:T(8,128)S(1)} %copy.14.refs_0_, s32[4,8]{1,0:T(4,128)S(1)} %copy-done.3, s32[4,8]{1,0:T(4,128)S(1)} %copy-done.4, f32[4,384]{1,0:T(4,128)S(1)} %copy-done.2, f32[384,4]{1,0:T(8,128)S(1)} %bitcast.42, bf16[640,384]{1,0:T(8,128)(2,1)S(1)} %get-tuple-element.43.refs_5_, ...), custom_call_target="tpu_custom_call" | custom-call | flops 981467136 | bytes 6586368 | tf_op jit(solution)/shard_map/pallas_call | solution.py:197
  89.7 1.8 %collective-permute-done.22.refs_2_ = bf16[48,384]{1,0:T(8,128)(2,1)S(1)} collective-permute-done((bf16[48,384]{1,0:T(8,128)(2,1)S(1)}, bf16[48,384]{1,0:T(8,128)(2,1)S(1)}, u32[]{:S(2)}, u32[]{:S(2)}) %collective-permute-start.22) | collective-permute-done | bytes 36896 | tf_op jit(solution)/shard_map/ppermute | solution.py:232
  91.7 3.6 %collective-permute-done.23.refs_0_ = bf16[24,384]{1,0:T(8,128)(2,1)S(1)} collective-permute-done((bf16[24,384]{1,0:T(8,128)(2,1)S(1)}, bf16[24,384]{1,0:T(8,128)(2,1)S(1)}, u32[]{:S(2)}, u32[]{:S(2)}) %collective-permute-start.23) | collective-permute-done | bytes 18464 | tf_op jit(solution)/shard_map/ppermute | solution.py:18
  95.4 0.8 collective-permute-start.24
  96.2 1.2 %reshape.10 = bf16[1,640,1,2,384]{4,3,1,2,0:T(2,128)(2,1)} reshape(bf16[640,768]{1,0:T(8,128)(2,1)S(1)} %shard_map.89) | data formatting | bytes 1966080 | tf_op jit(solution)/shard_map/reshape | solution.py:428
  97.3 2.7 %collective-permute-done.24.refs_0_ = bf16[12,384]{1,0:T(8,128)(2,1)S(1)} collective-permute-done((bf16[12,384]{1,0:T(8,128)(2,1)S(1)}, bf16[12,384]{1,0:T(8,128)(2,1)S(1)}, u32[]{:S(2)}, u32[]{:S(2)}) %collective-permute-start.24) | collective-permute-done | bytes 9248 | tf_op jit(solution)/shard_map/ppermute | solution.py:18
  100.0 0.6 shard_map.94
  (51 shorter events, 2.0 us)
Async XLA Ops:
  0.6 0.9 copy-start
  1.6 10.9 %collective-permute-start = (bf16[80,320]{1,0:T(8,128)(2,1)S(1)}, bf16[80,320]{1,0:T(8,128)(2,1)S(1)}, u32[]{:S(2)}, u32[]{:S(2)}) collective-permute-start(bf16[80,320]{1,0:T(8,128)(2,1)S(1)} %constant_dynamic-slice_fusion), channel_id=1, source_target_pairs={{0,16},{4,20},{8,24},{12,28},{16,0},{20,4},{24,8},{28,12},{1,17},{... | collective-permute-start | bytes 153608 | tf_op jit(solution)/shard_map/ppermute | solution.py:18
  5.7 1.2 %copy-start.1 = (bf16[1,80,8,2,384]{4,3,2,1,0:T(2,128)(2,1)S(1)}, bf16[1,80,8,2,384]{4,3,2,1,0:T(2,128)(2,1)}, u32[]{:S(2)}) copy-start(bf16[1,80,8,2,384]{4,3,2,1,0:T(2,128)(2,1)} %param.6) | copy-start | bytes 2949124
  8.1 10.9 %collective-permute-start.4 = (bf16[2,80,384]{2,1,0:T(8,128)(2,1)S(1)}, bf16[2,80,384]{2,1,0:T(8,128)(2,1)S(1)}, u32[]{:S(2)}, u32[]{:S(2)}) collective-permute-start(bf16[2,80,384]{2,1,0:T(8,128)(2,1)S(1)} %get-tuple-element.40), channel_id=1, source_target_pairs={{0,16},{4,20},{8,24},{12,28},{16,0},{20,4},{24,8},{28,12},{1,17},{... | collective-permute-start | bytes 368648 | tf_op jit(solution)/shard_map/ppermute | solution.py:18
  8.1 10.8 %collective-permute-start.5 = (bf16[2,80,384]{2,1,0:T(8,128)(2,1)S(1)}, bf16[2,80,384]{2,1,0:T(8,128)(2,1)S(1)}, u32[]{:S(2)}, u32[]{:S(2)}) collective-permute-start(bf16[2,80,384]{2,1,0:T(8,128)(2,1)S(1)} %get-tuple-element.41), channel_id=1, source_target_pairs={{0,8},{4,12},{8,0},{12,4},{16,24},{20,28},{24,16},{28,20},{1,9},{5... | collective-permute-start | bytes 368648 | tf_op jit(solution)/shard_map/ppermute | solution.py:18
  10.0 11.5 %collective-permute-start.6 = (bf16[2,80,384]{2,1,0:T(8,128)(2,1)S(1)}, bf16[2,80,384]{2,1,0:T(8,128)(2,1)S(1)}, u32[]{:S(2)}, u32[]{:S(2)}) collective-permute-start(bf16[2,80,384]{2,1,0:T(8,128)(2,1)S(1)} %get-tuple-element.42), channel_id=1, source_target_pairs={{0,24},{4,28},{8,16},{12,20},{16,8},{20,12},{24,0},{28,4},{1,25},{... | collective-permute-start | bytes 368648 | tf_op jit(solution)/shard_map/ppermute | solution.py:18
  12.6 10.7 %collective-permute-start.1 = (bf16[160,320]{1,0:T(8,128)(2,1)S(1)}, bf16[160,320]{1,0:T(8,128)(2,1)S(1)}, u32[]{:S(2)}, u32[]{:S(2)}) collective-permute-start(bf16[160,320]{1,0:T(8,128)(2,1)S(1)} %pad_maximum_fusion.7), channel_id=1, source_target_pairs={{0,8},{4,12},{8,0},{12,4},{16,24},{20,28},{24,16},{28,20},{1,9},{5... | collective-permute-start | bytes 307208 | tf_op jit(solution)/shard_map/ppermute | solution.py:18
  14.4 11.7 %collective-permute-start.10 = (bf16[4,80,384]{2,1,0:T(8,128)(2,1)S(1)}, bf16[4,80,384]{2,1,0:T(8,128)(2,1)S(1)}, u32[]{:S(2)}, u32[]{:S(2)}) collective-permute-start(bf16[4,80,384]{2,1,0:T(8,128)(2,1)S(1)} %get-tuple-element.46), channel_id=1, source_target_pairs={{0,8},{4,12},{8,0},{12,4},{16,24},{20,28},{24,16},{28,20},{1,9},{5... | collective-permute-start | bytes 737288 | tf_op jit(solution)/shard_map/ppermute | solution.py:18
  21.6 19.2 %copy-start.5 = (f32[8,2]{0,1:T(2,128)S(1)}, f32[8,2]{0,1:T(2,128)}, u32[]{:S(2)}) copy-start(f32[8,2]{0,1:T(2,128)} %param.8) | copy-start | bytes 196
  21.6 19.3 %copy-start.2 = (f32[4,384]{1,0:T(4,128)S(1)}, f32[4,384]{1,0:T(4,128)}, u32[]{:S(2)}) copy-start(f32[4,384]{1,0:T(4,128)} %refs_3_.13) | copy-start | bytes 18436
  21.6 10.3 %collective-permute-start.7 = (bf16[320,384]{1,0:T(8,128)(2,1)S(1)}, bf16[320,384]{1,0:T(8,128)(2,1)S(1)}, u32[]{:S(2)}, u32[]{:S(2)}) collective-permute-start(bf16[320,384]{1,0:T(8,128)(2,1)S(1)} %pad_maximum_fusion.3), channel_id=1, source_target_pairs={{0,4},{4,0},{8,12},{12,8},{16,20},{20,16},{24,28},{28,24},{1,5},{5... | collective-permute-start | bytes 737288 | tf_op jit(solution)/shard_map/ppermute | solution.py:18
  23.2 8.5 %collective-permute-start.2 = (bf16[320,320]{1,0:T(8,128)(2,1)S(1)}, bf16[320,320]{1,0:T(8,128)(2,1)S(1)}, u32[]{:S(2)}, u32[]{:S(2)}) collective-permute-start(bf16[320,320]{1,0:T(8,128)(2,1)S(1)} %pad_maximum_fusion.1), channel_id=1, source_target_pairs={{0,4},{4,0},{8,12},{12,8},{16,20},{20,16},{24,28},{28,24},{1,5},{5... | collective-permute-start | bytes 614408 | tf_op jit(solution)/shard_map/ppermute | solution.py:18
  26.2 12.9 %collective-permute-start.11 = (bf16[4,80,384]{2,1,0:T(8,128)(2,1)S(1)}, bf16[4,80,384]{2,1,0:T(8,128)(2,1)S(1)}, u32[]{:S(2)}, u32[]{:S(2)}) collective-permute-start(bf16[4,80,384]{2,1,0:T(8,128)(2,1)S(1)} %pad_maximum_fusion.4), channel_id=1, source_target_pairs={{0,16},{4,20},{8,24},{12,28},{16,0},{20,4},{24,8},{28,12},{1,17},{... | collective-permute-start | bytes 737288 | tf_op jit(solution)/shard_map/ppermute | solution.py:18
  28.8 12.3 %collective-permute-start.8 = (bf16[320,384]{1,0:T(8,128)(2,1)S(1)}, bf16[320,384]{1,0:T(8,128)(2,1)S(1)}, u32[]{:S(2)}, u32[]{:S(2)}) collective-permute-start(bf16[320,384]{1,0:T(8,128)(2,1)S(1)} %pad_maximum_fusion.2.refs_2_), channel_id=1, source_target_pairs={{0,2},{1,3},{2,0},{3,1},{4,6},{5,7},{6,4},{7,5},{8,10},{9,11},{10,... | collective-permute-start | bytes 737288 | tf_op jit(solution)/shard_map/ppermute | solution.py:345
  31.9 10.8 %collective-permute-start.3 = (bf16[640,320]{1,0:T(8,128)(2,1)S(1)}, bf16[640,320]{1,0:T(8,128)(2,1)S(1)}, u32[]{:S(2)}, u32[]{:S(2)}) collective-permute-start(bf16[640,320]{1,0:T(8,128)(2,1)S(1)} %pad_maximum_fusion.refs_0_), channel_id=1, source_target_pairs={{0,1},{1,0},{2,3},{3,2},{4,5},{5,4},{6,7},{7,6},{8,9},{9,8},{10,11... | collective-permute-start | bytes 1228808 | tf_op jit(solution)/shard_map/ppermute | solution.py:18
  31.9 9.2 %collective-permute-start.9 = (bf16[320,384]{1,0:T(8,128)(2,1)S(1)}, bf16[320,384]{1,0:T(8,128)(2,1)S(1)}, u32[]{:S(2)}, u32[]{:S(2)}) collective-permute-start(bf16[320,384]{1,0:T(8,128)(2,1)S(1)} %collective-permute-done.7.refs_3_), channel_id=1, source_target_pairs={{0,2},{1,3},{2,0},{3,1},{4,6},{5,7},{6,4},{7,5},{8,10},{9,11},{10,... | collective-permute-start | bytes 737288 | tf_op jit(solution)/shard_map/ppermute | solution.py:348
  39.2 7.9 %collective-permute-start.12 = (bf16[320,384]{1,0:T(8,128)(2,1)S(1)}, bf16[320,384]{1,0:T(8,128)(2,1)S(1)}, u32[]{:S(2)}, u32[]{:S(2)}) collective-permute-start(bf16[320,384]{1,0:T(8,128)(2,1)S(1)} %pad_maximum_fusion.6), channel_id=1, source_target_pairs={{0,4},{4,0},{8,12},{12,8},{16,20},{20,16},{24,28},{28,24},{1,5},{5... | collective-permute-start | bytes 737288 | tf_op jit(solution)/shard_map/ppermute | solution.py:18
  41.1 7.2 %copy-start.3 = (s32[4,8]{1,0:T(4,128)S(1)}, s32[4,8]{1,0:T(4,128)}, u32[]{:S(2)}) copy-start(s32[4,8]{1,0:T(4,128)} %refs_1_.13) | copy-start | bytes 388
  41.1 7.2 %copy-start.4 = (s32[4,8]{1,0:T(4,128)S(1)}, s32[4,8]{1,0:T(4,128)}, u32[]{:S(2)}) copy-start(s32[4,8]{1,0:T(4,128)} %refs_2_.13) | copy-start | bytes 388
  41.1 10.1 %collective-permute-start.13 = (bf16[320,384]{1,0:T(8,128)(2,1)S(1)}, bf16[320,384]{1,0:T(8,128)(2,1)S(1)}, u32[]{:S(2)}, u32[]{:S(2)}) collective-permute-start(bf16[320,384]{1,0:T(8,128)(2,1)S(1)} %pad_maximum_fusion.5.refs_2_), channel_id=1, source_target_pairs={{0,2},{1,3},{2,0},{3,1},{4,6},{5,7},{6,4},{7,5},{8,10},{9,11},{10,... | collective-permute-start | bytes 737288 | tf_op jit(solution)/shard_map/ppermute | solution.py:345
  43.8 14.3 %collective-permute-start.15 = (bf16[640,384]{1,0:T(8,128)(2,1)S(1)}, bf16[640,384]{1,0:T(8,128)(2,1)S(1)}, u32[]{:S(2)}, u32[]{:S(2)}) collective-permute-start(bf16[640,384]{1,0:T(8,128)(2,1)S(1)} %get-tuple-element.54.refs_7_.odd_ref), channel_id=1, source_target_pairs={{0,24},{4,28},{8,0},{12,4},{16,8},{20,12},{24,16},{28,20},{1,25},{... | collective-permute-start | bytes 1474568 | tf_op jit(solution)/shard_map/ppermute | solution.py:24
  47.1 7.0 %collective-permute-start.14 = (bf16[320,384]{1,0:T(8,128)(2,1)S(1)}, bf16[320,384]{1,0:T(8,128)(2,1)S(1)}, u32[]{:S(2)}, u32[]{:S(2)}) collective-permute-start(bf16[320,384]{1,0:T(8,128)(2,1)S(1)} %collective-permute-done.12.refs_3_), channel_id=1, source_target_pairs={{0,2},{1,3},{2,0},{3,1},{4,6},{5,7},{6,4},{7,5},{8,10},{9,11},{10,... | collective-permute-start | bytes 737288 | tf_op jit(solution)/shard_map/ppermute | solution.py:348
  54.8 12.9 %collective-permute-start.16 = (bf16[640,384]{1,0:T(8,128)(2,1)S(1)}, bf16[640,384]{1,0:T(8,128)(2,1)S(1)}, u32[]{:S(2)}, u32[]{:S(2)}) collective-permute-start(bf16[640,384]{1,0:T(8,128)(2,1)S(1)} %shard_map.82.refs_7_.odd_ref), channel_id=1, source_target_pairs={{0,24},{4,28},{8,0},{12,4},{16,8},{20,12},{24,16},{28,20},{1,25},{... | collective-permute-start | bytes 1474568 | tf_op jit(solution)/shard_map/ppermute | solution.py:24
  58.4 13.2 %collective-permute-start.18 = (bf16[640,384]{1,0:T(8,128)(2,1)S(1)}, bf16[640,384]{1,0:T(8,128)(2,1)S(1)}, u32[]{:S(2)}, u32[]{:S(2)}) collective-permute-start(bf16[640,384]{1,0:T(8,128)(2,1)S(1)} %shard_map.83), channel_id=1, source_target_pairs={{0,4},{4,0},{8,12},{12,8},{16,20},{20,16},{24,28},{28,24},{1,5},{5... | collective-permute-start | bytes 1474568 | tf_op jit(solution)/shard_map/ppermute | solution.py:18
  67.8 12.3 %collective-permute-start.17 = (bf16[640,384]{1,0:T(8,128)(2,1)S(1)}, bf16[640,384]{1,0:T(8,128)(2,1)S(1)}, u32[]{:S(2)}, u32[]{:S(2)}) collective-permute-start(bf16[640,384]{1,0:T(8,128)(2,1)S(1)} %shard_map.86), channel_id=1, source_target_pairs={{0,4},{4,0},{8,12},{12,8},{16,20},{20,16},{24,28},{28,24},{1,5},{5... | collective-permute-start | bytes 1474568 | tf_op jit(solution)/shard_map/ppermute | solution.py:18
  82.1 1.4 %collective-permute-start.19 = (bf16[192,384]{1,0:T(8,128)(2,1)S(1)}, bf16[192,384]{1,0:T(8,128)(2,1)S(1)}, u32[]{:S(2)}, u32[]{:S(2)}) collective-permute-start(bf16[192,384]{1,0:T(8,128)(2,1)S(1)} %get-tuple-element.65), channel_id=1, source_target_pairs={{0,1},{1,0},{2,3},{3,2},{4,5},{5,4},{6,7},{7,6},{8,9},{9,8},{10,11... | collective-permute-start | bytes 442376 | tf_op jit(solution)/shard_map/ppermute | solution.py:18
  83.6 6.1 %collective-permute-start.20 = (bf16[48,384]{1,0:T(8,128)(2,1)S(1)}, bf16[48,384]{1,0:T(8,128)(2,1)S(1)}, u32[]{:S(2)}, u32[]{:S(2)}) collective-permute-start(bf16[48,384]{1,0:T(8,128)(2,1)S(1)} %get-tuple-element.67), channel_id=1, source_target_pairs={{0,4},{1,5},{2,6},{3,7},{4,0},{5,1},{6,2},{7,3},{8,12},{9,13},{10,... | collective-permute-start | bytes 110600 | tf_op jit(solution)/shard_map/ppermute | solution.py:232
  85.2 4.5 %collective-permute-start.21 = (bf16[48,384]{1,0:T(8,128)(2,1)S(1)}, bf16[48,384]{1,0:T(8,128)(2,1)S(1)}, u32[]{:S(2)}, u32[]{:S(2)}) collective-permute-start(bf16[48,384]{1,0:T(8,128)(2,1)S(1)} %get-tuple-element.68), channel_id=1, source_target_pairs={{0,2},{1,3},{2,0},{3,1},{4,6},{5,7},{6,4},{7,5},{8,10},{9,11},{10,... | collective-permute-start | bytes 110600 | tf_op jit(solution)/shard_map/ppermute | solution.py:232
  86.6 4.9 %collective-permute-start.22 = (bf16[48,384]{1,0:T(8,128)(2,1)S(1)}, bf16[48,384]{1,0:T(8,128)(2,1)S(1)}, u32[]{:S(2)}, u32[]{:S(2)}) collective-permute-start(bf16[48,384]{1,0:T(8,128)(2,1)S(1)} %get-tuple-element.69), channel_id=1, source_target_pairs={{0,6},{1,7},{2,4},{3,5},{4,2},{5,3},{6,0},{7,1},{8,14},{9,15},{10,... | collective-permute-start | bytes 110600 | tf_op jit(solution)/shard_map/ppermute | solution.py:232
  91.5 3.8 %collective-permute-start.23 = (bf16[24,384]{1,0:T(8,128)(2,1)S(1)}, bf16[24,384]{1,0:T(8,128)(2,1)S(1)}, u32[]{:S(2)}, u32[]{:S(2)}) collective-permute-start(bf16[24,384]{1,0:T(8,128)(2,1)S(1)} %get-tuple-element.72), channel_id=1, source_target_pairs={{0,8},{4,12},{8,0},{12,4},{16,24},{20,28},{24,16},{28,20},{1,9},{5... | collective-permute-start | bytes 55304 | tf_op jit(solution)/shard_map/ppermute | solution.py:18
  95.4 4.7 %collective-permute-start.24 = (bf16[12,384]{1,0:T(8,128)(2,1)S(1)}, bf16[12,384]{1,0:T(8,128)(2,1)S(1)}, u32[]{:S(2)}, u32[]{:S(2)}) collective-permute-start(bf16[12,384]{1,0:T(8,128)(2,1)S(1)} %get-tuple-element.74), channel_id=1, source_target_pairs={{0,16},{4,20},{8,24},{12,28},{16,0},{20,4},{24,8},{28,12},{1,17},{... | collective-permute-start | bytes 27656 | tf_op jit(solution)/shard_map/ppermute | solution.py:18

commit v6 on v5

--- a/solution.py
+++ b/solution.py
@@ -10,7 +10,7 @@
 WINDOW = 3
 DIRECT = 8
 STAGE_BITS = (2, 1, 1)
-FAR_PARTS = 1
+LAST_PARTS = 2
 
 
 def flip(value, axis, mask):
@@ -350,7 +350,7 @@
             own += fit(metric, [own_rows], [1])[0]
             rest.append(facing_rows)
         else:
-            own, facing = fit(metric, [own_rows, facing_rows], [1, FAR_PARTS])
+            own, facing = fit(metric, [own_rows, facing_rows], [1, 1])
     return own, facing, metric, rest
 
 
@@ -391,32 +391,36 @@
             rows = rows.reshape(wide_count * aux_rows, vir_count)
             own += fit(metric, [[rows]], [1])[0]
             rest.append([lax.ppermute(rows, "narrow", half_turn)])
-        (facing,) = fit(metric, [rest.pop(0)], [FAR_PARTS])
+        (facing,) = fit(metric, [rest.pop(0)], [1])
     aux_count = own[0].shape[0]
 
     pair = functools.partial(pair_terms, small=small, own=own)
-    ahead, second, first = [], [], []
-    sums = ()
+    ahead, second, first = [facing], [], []
+    sums = pair(0, 0, far=facing, sums=(), weight=8)
+    for part, *parts in rest:
+        last = len(ahead) == occ_slots - 1
+        ahead += fit(metric, [[after(part, *sums), *parts]], [LAST_PARTS if last else 1])
+    earlier = []
     for slot in range(occ_slots):
-        if slot:
-            part, *parts = rest[slot - 1]
-            (facing,) = fit(metric, [[after(part, *sums), *parts]], [FAR_PARTS])
-        ahead.append(facing)
-        second.append([from_ahead(part, "wide", 2) for part in facing])
-        if slot == 0:
-            sums = pair(0, slot, far=facing, sums=sums, weight=8)
+        chosen = []
+        second.append([])
+        first.append([])
+        for place, part in enumerate(ahead[slot]):
+            part = after(part, *earlier) if place else part
+            second[slot].append(from_ahead(part, "wide", 2))
+            if wide_count % 2 == 0:
+                gate = () if slot and place == 0 else sums
+                chosen.append(choice(after(part, *gate), second[slot][-1]))
+                first[slot].append(flip(chosen[-1], "wide", 1))
+            else:
+                first[slot].append(from_ahead(part, "wide", 1))
+            if slot and place == 0:
+                sums = pair(0, slot, far=ahead[slot], sums=sums)
+        earlier = chosen
     for slot in range(occ_slots):
-        if wide_count % 2 == 0:
-            chosen = [choice(after(odd, *sums), even) for odd, even in zip(ahead[slot], second[slot])]
-            first.append([flip(part, "wide", 1) for part in chosen])
-        else:
-            chosen = ()
-            first.append([from_ahead(part, "wide", 1) for part in ahead[slot]])
-        if slot + 1 < occ_slots:
-            sums = pair(0, slot + 1, far=[after(part, *chosen) for part in ahead[slot + 1]], sums=sums)
         sums = pair(2, slot, far=second[slot], sums=sums)
     for slot in range(occ_slots - 1):
-        sums = pair(1, slot, far=first[slot], sums=sums)
+        sums = pair(1, slot, far=first[slot], sums=sums, weight=3)
     norm_scale = 1.0 / (group_count * wide_count * vir_count)
     last = functools.partial(pair, 1, occ_slots - 1, far=first[-1], sums=sums)
     terms = last(wanted=("density",), scale_by=norm_scale)

time: 101 us -> 100 us (0.990)
  waiting for transfers between devices: 35 us -> 28.7 us
  starting transfers between devices: 35.9 us -> 41.5 us
    ppermute x16 -> x17, waiting for transfers between devices: 28.4 us -> 20.7 us  [flip(): return lax.ppermute(value, axis, pairs)]
    ppermute x2 -> x3, waiting for transfers between devices: 1.93 us -> 7.04 us  [from_ahead(): return lax.ppermute(value, axis, pairs)]
    ppermute x16 -> x17, starting transfers between devices: 20.5 us -> 24.8 us  [flip(): return lax.ppermute(value, axis, pairs)]
    ppermute x2, waiting for transfers between devices: 2.9 us -> 0.01 us  [gathered_rows(): lax.ppermute(after(received, *facing) if slot else received, 'narrow', ha...]
    ppermute x2 -> x3, starting transfers between devices: 6.59 us -> 7.91 us  [from_ahead(): return lax.ppermute(value, axis, pairs)]
  transfers between devices with their start and end apart: 25 -> 27, of which waited for: 12 -> 13; matrix products, arithmetic and copies ran while one was open for 2% -> 2% of each run, Pallas kernels for 22% -> 22%
where the time goes in v6:
time: 100 us; the launch traced here: 99.8 us
  starting transfers between devices  41.5 us (42%)
  waiting for transfers between devices  28.7 us (29%)
  Pallas kernels  24.7 us (25%)
  local copies, waits for them, and re-layouts  3.7 us (4%)
  between operations  1.01 us (1%)
    ppermute x17, starting transfers between devices, flip(): return lax.ppermute(value, axis, pairs)  24.8 us
    ppermute x17, waiting for transfers between devices, flip(): return lax.ppermute(value, axis, pairs)  20.7 us
    pallas_call x7, Pallas kernels, pair_terms(): pl.pallas_call(functools.partial(pair_kernel, offset, slot, len(far), len...  19.1 us
    ppermute x3, starting transfers between devices, from_ahead(): return lax.ppermute(value, axis, pairs)  7.91 us
    ppermute x3, waiting for transfers between devices, from_ahead(): return lax.ppermute(value, axis, pairs)  7.04 us
    ppermute x3, starting transfers between devices, flipped(): return lax.ppermute(value, ('wide', 'narrow'), pairs)  3.55 us
    ppermute x2, starting transfers between devices, gathered_rows(): first = lax.ppermute(mine, 'narrow', half_turn)  3.11 us
    pallas_call x3, Pallas kernels, fit(): pl.pallas_call(functools.partial(fit_kernel, len(metric), len(sources[0])...  2.49 us
  transfers between devices with their start and end apart: 27, of which 13 were waited for; matrix products, arithmetic and copies ran while one was open for 2% of the time, Pallas kernels for 22%

profile of v6, /device:TPU:0, one launch (start us, length us, event | category | flops | bytes accessed | tf_op | source)
XLA Modules:
  0.0 99.8 jit_solution(12700719935931496608)
XLA Ops:
  0.7 0.9 copy-done
  1.6 4.1 %collective-permute-start = (bf16[80,320]{1,0:T(8,128)(2,1)S(1)}, bf16[80,320]{1,0:T(8,128)(2,1)S(1)}, u32[]{:S(2)}, u32[]{:S(2)}) collective-permute-start(bf16[80,320]{1,0:T(8,128)(2,1)S(1)} %constant_dynamic-slice_fusion), channel_id=1, source_target_pairs={{0,16},{4,20},{8,24},{12,28},{16,0},{20,4},{24,8},{28,12},{1,17},{... | collective-permute-start | bytes 153608 | tf_op jit(solution)/shard_map/ppermute | solution.py:18
  5.7 1.2 %copy-done.1 = bf16[1,80,8,2,384]{4,3,2,1,0:T(2,128)(2,1)S(1)} copy-done((bf16[1,80,8,2,384]{4,3,2,1,0:T(2,128)(2,1)S(1)}, bf16[1,80,8,2,384]{4,3,2,1,0:T(2,128)(2,1)}, u32[]{:S(2)}) %copy-start.1) | copy-done | bytes 983064
  6.9 1.1 %shard_map.77 = (bf16[2,80,384]{2,1,0:T(8,128)(2,1)S(1)}, bf16[2,80,384]{2,1,0:T(8,128)(2,1)S(1)}, bf16[2,80,384]{2,1,0:T(8,128)(2,1)S(1)}, bf16[2,80,384]{2,1,0:T(8,128)(2,1)S(1)}) custom-call(bf16[80,8,2,384]{3,2,1,0:T(2,128)(2,1)S(1)} %bitcast.43), custom_call_target="tpu_custom_call" | custom-call | bytes 2949120 | tf_op jit(solution)/shard_map/pallas_call | solution.py:287
  8.1 1.9 %collective-permute-start.5 = (bf16[2,80,384]{2,1,0:T(8,128)(2,1)S(1)}, bf16[2,80,384]{2,1,0:T(8,128)(2,1)S(1)}, u32[]{:S(2)}, u32[]{:S(2)}) collective-permute-start(bf16[2,80,384]{2,1,0:T(8,128)(2,1)S(1)} %get-tuple-element.43), channel_id=1, source_target_pairs={{0,8},{4,12},{8,0},{12,4},{16,24},{20,28},{24,16},{28,20},{1,9},{5... | collective-permute-start | bytes 368648 | tf_op jit(solution)/shard_map/ppermute | solution.py:18
  10.0 2.5 %collective-permute-start.6 = (bf16[2,80,384]{2,1,0:T(8,128)(2,1)S(1)}, bf16[2,80,384]{2,1,0:T(8,128)(2,1)S(1)}, u32[]{:S(2)}, u32[]{:S(2)}) collective-permute-start(bf16[2,80,384]{2,1,0:T(8,128)(2,1)S(1)} %get-tuple-element.44), channel_id=1, source_target_pairs={{0,24},{4,28},{8,16},{12,20},{16,8},{20,12},{24,0},{28,4},{1,25},{... | collective-permute-start | bytes 368648 | tf_op jit(solution)/shard_map/ppermute | solution.py:18
  12.6 0.7 collective-permute-start.1
  13.3 1.1 %shard_map.79 = (bf16[4,80,384]{2,1,0:T(8,128)(2,1)S(1)}, bf16[4,80,384]{2,1,0:T(8,128)(2,1)S(1)}) custom-call(bf16[80,8,2,384]{3,2,1,0:T(2,128)(2,1)S(1)} %bitcast.44), custom_call_target="tpu_custom_call" | custom-call | bytes 2949120 | tf_op jit(solution)/shard_map/pallas_call | solution.py:287
  14.4 1.4 %collective-permute-start.10 = (bf16[4,80,384]{2,1,0:T(8,128)(2,1)S(1)}, bf16[4,80,384]{2,1,0:T(8,128)(2,1)S(1)}, u32[]{:S(2)}, u32[]{:S(2)}) collective-permute-start(bf16[4,80,384]{2,1,0:T(8,128)(2,1)S(1)} %get-tuple-element.48), channel_id=1, source_target_pairs={{0,8},{4,12},{8,0},{12,4},{16,24},{20,28},{24,16},{28,20},{1,9},{5... | collective-permute-start | bytes 737288 | tf_op jit(solution)/shard_map/ppermute | solution.py:18
  15.9 3.0 %collective-permute-done.4 = bf16[2,80,384]{2,1,0:T(8,128)(2,1)S(1)} collective-permute-done((bf16[2,80,384]{2,1,0:T(8,128)(2,1)S(1)}, bf16[2,80,384]{2,1,0:T(8,128)(2,1)S(1)}, u32[]{:S(2)}, u32[]{:S(2)}) %collective-permute-start.4) | collective-permute-done | bytes 122912 | tf_op jit(solution)/shard_map/ppermute | solution.py:18
  19.0 2.6 %collective-permute-done.6 = bf16[2,80,384]{2,1,0:T(8,128)(2,1)S(1)} collective-permute-done((bf16[2,80,384]{2,1,0:T(8,128)(2,1)S(1)}, bf16[2,80,384]{2,1,0:T(8,128)(2,1)S(1)}, u32[]{:S(2)}, u32[]{:S(2)}) %collective-permute-start.6) | collective-permute-done | bytes 122912 | tf_op jit(solution)/shard_map/ppermute | solution.py:18
  21.6 1.6 %collective-permute-start.7 = (bf16[320,384]{1,0:T(8,128)(2,1)S(1)}, bf16[320,384]{1,0:T(8,128)(2,1)S(1)}, u32[]{:S(2)}, u32[]{:S(2)}) collective-permute-start(bf16[320,384]{1,0:T(8,128)(2,1)S(1)} %pad_maximum_fusion.3), channel_id=1, source_target_pairs={{0,4},{4,0},{8,12},{12,8},{16,20},{20,16},{24,28},{28,24},{1,5},{5... | collective-permute-start | bytes 737288 | tf_op jit(solution)/shard_map/ppermute | solution.py:18
  23.8 2.3 %collective-permute-done.10 = bf16[4,80,384]{2,1,0:T(8,128)(2,1)S(1)} collective-permute-done((bf16[4,80,384]{2,1,0:T(8,128)(2,1)S(1)}, bf16[4,80,384]{2,1,0:T(8,128)(2,1)S(1)}, u32[]{:S(2)}, u32[]{:S(2)}) %collective-permute-start.10) | collective-permute-done | bytes 245792 | tf_op jit(solution)/shard_map/ppermute | solution.py:18
  26.2 2.5 %collective-permute-start.11 = (bf16[4,80,384]{2,1,0:T(8,128)(2,1)S(1)}, bf16[4,80,384]{2,1,0:T(8,128)(2,1)S(1)}, u32[]{:S(2)}, u32[]{:S(2)}) collective-permute-start(bf16[4,80,384]{2,1,0:T(8,128)(2,1)S(1)} %pad_maximum_fusion.4), channel_id=1, source_target_pairs={{0,16},{4,20},{8,24},{12,28},{16,0},{20,4},{24,8},{28,12},{1,17},{... | collective-permute-start | bytes 737288 | tf_op jit(solution)/shard_map/ppermute | solution.py:18
  28.8 1.6 %collective-permute-start.8 = (bf16[320,384]{1,0:T(8,128)(2,1)S(1)}, bf16[320,384]{1,0:T(8,128)(2,1)S(1)}, u32[]{:S(2)}, u32[]{:S(2)}) collective-permute-start(bf16[320,384]{1,0:T(8,128)(2,1)S(1)} %pad_maximum_fusion.2.refs_2_), channel_id=1, source_target_pairs={{0,2},{1,3},{2,0},{3,1},{4,6},{5,7},{6,4},{7,5},{8,10},{9,11},{10,... | collective-permute-start | bytes 737288 | tf_op jit(solution)/shard_map/ppermute | solution.py:345
  30.3 1.5 %collective-permute-done.2 = bf16[320,320]{1,0:T(8,128)(2,1)S(1)} collective-permute-done((bf16[320,320]{1,0:T(8,128)(2,1)S(1)}, bf16[320,320]{1,0:T(8,128)(2,1)S(1)}, u32[]{:S(2)}, u32[]{:S(2)}) %collective-permute-start.2) | collective-permute-done | bytes 204832 | tf_op jit(solution)/shard_map/ppermute | solution.py:18
  31.9 1.6 %collective-permute-start.9 = (bf16[320,384]{1,0:T(8,128)(2,1)S(1)}, bf16[320,384]{1,0:T(8,128)(2,1)S(1)}, u32[]{:S(2)}, u32[]{:S(2)}) collective-permute-start(bf16[320,384]{1,0:T(8,128)(2,1)S(1)} %collective-permute-done.7.refs_3_), channel_id=1, source_target_pairs={{0,2},{1,3},{2,0},{3,1},{4,6},{5,7},{6,4},{7,5},{8,10},{9,11},{10,... | collective-permute-start | bytes 737288 | tf_op jit(solution)/shard_map/ppermute | solution.py:348
  33.5 5.6 %collective-permute-done.11 = bf16[4,80,384]{2,1,0:T(8,128)(2,1)S(1)} collective-permute-done((bf16[4,80,384]{2,1,0:T(8,128)(2,1)S(1)}, bf16[4,80,384]{2,1,0:T(8,128)(2,1)S(1)}, u32[]{:S(2)}, u32[]{:S(2)}) %collective-permute-start.11) | collective-permute-done | bytes 245792 | tf_op jit(solution)/shard_map/ppermute | solution.py:18
  39.2 1.6 %collective-permute-start.12 = (bf16[320,384]{1,0:T(8,128)(2,1)S(1)}, bf16[320,384]{1,0:T(8,128)(2,1)S(1)}, u32[]{:S(2)}, u32[]{:S(2)}) collective-permute-start(bf16[320,384]{1,0:T(8,128)(2,1)S(1)} %pad_maximum_fusion.6), channel_id=1, source_target_pairs={{0,4},{4,0},{8,12},{12,8},{16,20},{20,16},{24,28},{28,24},{1,5},{5... | collective-permute-start | bytes 737288 | tf_op jit(solution)/shard_map/ppermute | solution.py:18
  41.1 1.6 %collective-permute-start.13 = (bf16[320,384]{1,0:T(8,128)(2,1)S(1)}, bf16[320,384]{1,0:T(8,128)(2,1)S(1)}, u32[]{:S(2)}, u32[]{:S(2)}) collective-permute-start(bf16[320,384]{1,0:T(8,128)(2,1)S(1)} %pad_maximum_fusion.5.refs_2_), channel_id=1, source_target_pairs={{0,2},{1,3},{2,0},{3,1},{4,6},{5,7},{6,4},{7,5},{8,10},{9,11},{10,... | collective-permute-start | bytes 737288 | tf_op jit(solution)/shard_map/ppermute | solution.py:345
  42.7 1.1 %shard_map.78 = (bf16[640,384]{1,0:T(8,128)(2,1)S(1)}, bf16[640,384]{1,0:T(8,128)(2,1)S(1)}) custom-call(bf16[640,320]{1,0:T(8,128)(2,1)S(1)} %pad_maximum_fusion.refs_0_, bf16[640,320]{1,0:T(8,128)(2,1)S(1)} %collective-permute-done.3.refs_1_, bf16[320,384]{1,0:T(8,128)(2,1)S(1)} %pad_maximum_fusion.2.refs_2_, ...), custom_call_target="tpu_custom_call" | custom-call | flops 629145600 | bytes 2785280 | tf_op jit(solution)/shard_map/pallas_call | solution.py:75
  43.8 3.3 %collective-permute-start.17 = (bf16[640,384]{1,0:T(8,128)(2,1)S(1)}, bf16[640,384]{1,0:T(8,128)(2,1)S(1)}, u32[]{:S(2)}, u32[]{:S(2)}) collective-permute-start(bf16[640,384]{1,0:T(8,128)(2,1)S(1)} %get-tuple-element.58.refs_7_.odd_ref), channel_id=1, source_target_pairs={{0,24},{4,28},{8,0},{12,4},{16,8},{20,12},{24,16},{28,20},{1,25},{... | collective-permute-start | bytes 1474568 | tf_op jit(solution)/shard_map/ppermute | solution.py:24
  47.6 0.7 shard_map.80.refs_6_
  48.3 2.9 %shard_map.81 = (f32[384,384]{1,0:T(8,128)S(1)}, f32[640,768]{1,0:T(8,128)S(1)}) custom-call(f32[8,2]{1,0:T(8,128)S(1)} %copy.14.refs_0_, s32[4,8]{1,0:T(4,128)S(1)} %copy-done.3, s32[4,8]{1,0:T(4,128)S(1)} %copy-done.4, f32[4,384]{1,0:T(4,128)S(1)} %copy-done.2, f32[384,4]{1,0:T(8,128)S(1)} %bitcast.36, bf16[640,384]{1,0:T(8,128)(2,1)S(1)} %get-tuple-element.45.refs_5_, ...), custom_call_target="tpu_custom_call" | custom-call | flops 7851737088 | bytes 52690944 | tf_op jit(solution)/shard_map/pallas_call | solution.py:197
  51.2 6.0 %collective-permute-done.17.even_ref.refs_7_ = bf16[640,384]{1,0:T(8,128)(2,1)S(1)} collective-permute-done((bf16[640,384]{1,0:T(8,128)(2,1)S(1)}, bf16[640,384]{1,0:T(8,128)(2,1)S(1)}, u32[]{:S(2)}, u32[]{:S(2)}) %collective-permute-start.17) | collective-permute-done | bytes 491552 | tf_op jit(solution)/shard_map/ppermute | solution.py:24
  57.2 0.6 collective-permute-start.20
  57.8 0.7 shard_map.82
  58.5 4.3 %collective-permute-start.15 = (bf16[320,384]{1,0:T(8,128)(2,1)S(1)}, bf16[320,384]{1,0:T(8,128)(2,1)S(1)}, u32[]{:S(2)}, u32[]{:S(2)}) collective-permute-start(bf16[320,384]{1,0:T(8,128)(2,1)S(1)} %get-tuple-element.56.odd_ref.refs_7_), channel_id=1, source_target_pairs={{0,24},{4,28},{8,0},{12,4},{16,8},{20,12},{24,16},{28,20},{1,25},{... | collective-permute-start | bytes 737288 | tf_op jit(solution)/shard_map/ppermute | solution.py:24
  63.2 2.9 %shard_map.85 = (f32[384,384]{1,0:T(8,128)S(1)}, f32[640,768]{1,0:T(8,128)S(1)}) custom-call(f32[8,2]{1,0:T(8,128)S(1)} %copy.14.refs_0_, s32[4,8]{1,0:T(4,128)S(1)} %copy-done.3, s32[4,8]{1,0:T(4,128)S(1)} %copy-done.4, f32[4,384]{1,0:T(4,128)S(1)} %copy-done.2, f32[384,4]{1,0:T(8,128)S(1)} %bitcast.37, bf16[640,384]{1,0:T(8,128)(2,1)S(1)} %get-tuple-element.45.refs_5_, ...), custom_call_target="tpu_custom_call" | custom-call | flops 981467136 | bytes 6586368 | tf_op jit(solution)/shard_map/pallas_call | solution.py:197
  66.1 2.9 %shard_map.87 = (f32[384,384]{1,0:T(8,128)S(1)}, f32[640,768]{1,0:T(8,128)S(1)}) custom-call(f32[8,2]{1,0:T(8,128)S(1)} %copy.14.refs_0_, s32[4,8]{1,0:T(4,128)S(1)} %copy-done.3, s32[4,8]{1,0:T(4,128)S(1)} %copy-done.4, f32[4,384]{1,0:T(4,128)S(1)} %copy-done.2, f32[384,4]{1,0:T(8,128)S(1)} %bitcast.38, bf16[640,384]{1,0:T(8,128)(2,1)S(1)} %get-tuple-element.45.refs_5_, ...), custom_call_target="tpu_custom_call" | custom-call | flops 981467136 | bytes 6586368 | tf_op jit(solution)/shard_map/pallas_call | solution.py:197
  69.1 1.6 %collective-permute-start.16 = (bf16[320,384]{1,0:T(8,128)(2,1)S(1)}, bf16[320,384]{1,0:T(8,128)(2,1)S(1)}, u32[]{:S(2)}, u32[]{:S(2)}) collective-permute-start(bf16[320,384]{1,0:T(8,128)(2,1)S(1)} %shard_map.83), channel_id=1, source_target_pairs={{0,4},{4,0},{8,12},{12,8},{16,20},{20,16},{24,28},{28,24},{1,5},{5... | collective-permute-start | bytes 737288 | tf_op jit(solution)/shard_map/ppermute | solution.py:18
  70.7 1.0 %collective-permute-done.18.even_ref.refs_8_ = bf16[320,384]{1,0:T(8,128)(2,1)S(1)} collective-permute-done((bf16[320,384]{1,0:T(8,128)(2,1)S(1)}, bf16[320,384]{1,0:T(8,128)(2,1)S(1)}, u32[]{:S(2)}, u32[]{:S(2)}) %collective-permute-start.18) | collective-permute-done | bytes 245792 | tf_op jit(solution)/shard_map/ppermute | solution.py:24
  71.8 1.6 %collective-permute-start.19 = (bf16[320,384]{1,0:T(8,128)(2,1)S(1)}, bf16[320,384]{1,0:T(8,128)(2,1)S(1)}, u32[]{:S(2)}, u32[]{:S(2)}) collective-permute-start(bf16[320,384]{1,0:T(8,128)(2,1)S(1)} %shard_map.86), channel_id=1, source_target_pairs={{0,4},{4,0},{8,12},{12,8},{16,20},{20,16},{24,28},{28,24},{1,5},{5... | collective-permute-start | bytes 737288 | tf_op jit(solution)/shard_map/ppermute | solution.py:18
  73.3 2.9 %shard_map.88 = (f32[384,384]{1,0:T(8,128)S(1)}, f32[640,768]{1,0:T(8,128)S(1)}) custom-call(f32[8,2]{1,0:T(8,128)S(1)} %copy.14.refs_0_, s32[4,8]{1,0:T(4,128)S(1)} %copy-done.3, s32[4,8]{1,0:T(4,128)S(1)} %copy-done.4, f32[4,384]{1,0:T(4,128)S(1)} %copy-done.2, f32[384,4]{1,0:T(8,128)S(1)} %bitcast.39, bf16[640,384]{1,0:T(8,128)(2,1)S(1)} %get-tuple-element.45.refs_5_, ...), custom_call_target="tpu_custom_call" | custom-call | flops 981467136 | bytes 6586368 | tf_op jit(solution)/shard_map/pallas_call | solution.py:197
  76.3 2.9 %shard_map.89 = (f32[384,384]{1,0:T(8,128)S(1)}, f32[640,768]{1,0:T(8,128)S(1)}) custom-call(f32[8,2]{1,0:T(8,128)S(1)} %copy.14.refs_0_, s32[4,8]{1,0:T(4,128)S(1)} %copy-done.3, s32[4,8]{1,0:T(4,128)S(1)} %copy-done.4, f32[4,384]{1,0:T(4,128)S(1)} %copy-done.2, f32[384,4]{1,0:T(8,128)S(1)} %bitcast.40, bf16[640,384]{1,0:T(8,128)(2,1)S(1)} %get-tuple-element.45.refs_5_, ...), custom_call_target="tpu_custom_call" | custom-call | flops 2944401408 | bytes 19759104 | tf_op jit(solution)/shard_map/pallas_call | solution.py:197
  79.2 0.9 collective-permute-done.19.refs_8_
  80.1 2.0 %shard_map.91 = (bf16[192,384]{1,0:T(8,128)(2,1)S(1)}, f32[192,384]{1,0:T(8,128)S(1)}) custom-call(f32[8,2]{1,0:T(8,128)S(1)} %copy.14.refs_0_, s32[4,8]{1,0:T(4,128)S(1)} %copy-done.3, s32[4,8]{1,0:T(4,128)S(1)} %copy-done.4, f32[4,384]{1,0:T(4,128)S(1)} %copy-done.2, f32[384,4]{1,0:T(8,128)S(1)} %bitcast.41, ...), custom_call_target="tpu_custom_call" | custom-call | flops 981467136 | bytes 6586368 | tf_op jit(solution)/shard_map/pallas_call | solution.py:197
  82.2 1.4 %collective-permute-done.21.refs_0_ = bf16[192,384]{1,0:T(8,128)(2,1)S(1)} collective-permute-done((bf16[192,384]{1,0:T(8,128)(2,1)S(1)}, bf16[192,384]{1,0:T(8,128)(2,1)S(1)}, u32[]{:S(2)}, u32[]{:S(2)}) %collective-permute-start.21) | collective-permute-done | bytes 147488 | tf_op jit(solution)/shard_map/ppermute | solution.py:18
  83.6 1.6 %collective-permute-start.22 = (bf16[48,384]{1,0:T(8,128)(2,1)S(1)}, bf16[48,384]{1,0:T(8,128)(2,1)S(1)}, u32[]{:S(2)}, u32[]{:S(2)}) collective-permute-start(bf16[48,384]{1,0:T(8,128)(2,1)S(1)} %get-tuple-element.71), channel_id=1, source_target_pairs={{0,4},{1,5},{2,6},{3,7},{4,0},{5,1},{6,2},{7,3},{8,12},{9,13},{10,... | collective-permute-start | bytes 110600 | tf_op jit(solution)/shard_map/ppermute | solution.py:232
  85.8 1.4 %collective-permute-start.24 = (bf16[48,384]{1,0:T(8,128)(2,1)S(1)}, bf16[48,384]{1,0:T(8,128)(2,1)S(1)}, u32[]{:S(2)}, u32[]{:S(2)}) collective-permute-start(bf16[48,384]{1,0:T(8,128)(2,1)S(1)} %get-tuple-element.73), channel_id=1, source_target_pairs={{0,6},{1,7},{2,4},{3,5},{4,2},{5,3},{6,0},{7,1},{8,14},{9,15},{10,... | collective-permute-start | bytes 110600 | tf_op jit(solution)/shard_map/ppermute | solution.py:232
  87.2 2.5 %shard_map.90 = bf16[640,768]{1,0:T(8,128)(2,1)S(1)} custom-call(f32[8,2]{1,0:T(8,128)S(1)} %copy.14.refs_0_, s32[4,8]{1,0:T(4,128)S(1)} %copy-done.3, s32[4,8]{1,0:T(4,128)S(1)} %copy-done.4, f32[4,384]{1,0:T(4,128)S(1)} %copy-done.2, f32[384,4]{1,0:T(8,128)S(1)} %bitcast.42, bf16[640,384]{1,0:T(8,128)(2,1)S(1)} %get-tuple-element.45.refs_5_, ...), custom_call_target="tpu_custom_call" | custom-call | flops 981467136 | bytes 6586368 | tf_op jit(solution)/shard_map/pallas_call | solution.py:197
  89.8 0.9 collective-permute-done.24.refs_2_
  90.7 1.6 %collective-permute-start.25 = (bf16[24,384]{1,0:T(8,128)(2,1)S(1)}, bf16[24,384]{1,0:T(8,128)(2,1)S(1)}, u32[]{:S(2)}, u32[]{:S(2)}) collective-permute-start(bf16[24,384]{1,0:T(8,128)(2,1)S(1)} %get-tuple-element.76), channel_id=1, source_target_pairs={{0,8},{4,12},{8,0},{12,4},{16,24},{20,28},{24,16},{28,20},{1,9},{5... | collective-permute-start | bytes 55304 | tf_op jit(solution)/shard_map/ppermute | solution.py:18
  92.2 2.3 %collective-permute-done.25.refs_0_ = bf16[24,384]{1,0:T(8,128)(2,1)S(1)} collective-permute-done((bf16[24,384]{1,0:T(8,128)(2,1)S(1)}, bf16[24,384]{1,0:T(8,128)(2,1)S(1)}, u32[]{:S(2)}, u32[]{:S(2)}) %collective-permute-start.25) | collective-permute-done | bytes 18464 | tf_op jit(solution)/shard_map/ppermute | solution.py:18
  94.5 2.4 %collective-permute-start.26 = (bf16[12,384]{1,0:T(8,128)(2,1)S(1)}, bf16[12,384]{1,0:T(8,128)(2,1)S(1)}, u32[]{:S(2)}, u32[]{:S(2)}) collective-permute-start(bf16[12,384]{1,0:T(8,128)(2,1)S(1)} %get-tuple-element.78), channel_id=1, source_target_pairs={{0,16},{4,20},{8,24},{12,28},{16,0},{20,4},{24,8},{28,12},{1,17},{... | collective-permute-start | bytes 27656 | tf_op jit(solution)/shard_map/ppermute | solution.py:18
  96.9 1.2 %reshape.10 = bf16[1,640,1,2,384]{4,3,1,2,0:T(2,128)(2,1)} reshape(bf16[640,768]{1,0:T(8,128)(2,1)S(1)} %shard_map.90) | data formatting | bytes 1966080 | tf_op jit(solution)/shard_map/reshape | solution.py:432
  98.1 1.1 %collective-permute-done.26.refs_0_ = bf16[12,384]{1,0:T(8,128)(2,1)S(1)} collective-permute-done((bf16[12,384]{1,0:T(8,128)(2,1)S(1)}, bf16[12,384]{1,0:T(8,128)(2,1)S(1)}, u32[]{:S(2)}, u32[]{:S(2)}) %collective-permute-start.26) | collective-permute-done | bytes 9248 | tf_op jit(solution)/shard_map/ppermute | solution.py:18
  99.2 0.6 shard_map.95
  (56 shorter events, 3.2 us)
Async XLA Ops:
  0.6 0.9 copy-start
  1.6 10.9 %collective-permute-start = (bf16[80,320]{1,0:T(8,128)(2,1)S(1)}, bf16[80,320]{1,0:T(8,128)(2,1)S(1)}, u32[]{:S(2)}, u32[]{:S(2)}) collective-permute-start(bf16[80,320]{1,0:T(8,128)(2,1)S(1)} %constant_dynamic-slice_fusion), channel_id=1, source_target_pairs={{0,16},{4,20},{8,24},{12,28},{16,0},{20,4},{24,8},{28,12},{1,17},{... | collective-permute-start | bytes 153608 | tf_op jit(solution)/shard_map/ppermute | solution.py:18
  5.7 1.2 %copy-start.1 = (bf16[1,80,8,2,384]{4,3,2,1,0:T(2,128)(2,1)S(1)}, bf16[1,80,8,2,384]{4,3,2,1,0:T(2,128)(2,1)}, u32[]{:S(2)}) copy-start(bf16[1,80,8,2,384]{4,3,2,1,0:T(2,128)(2,1)} %param.6) | copy-start | bytes 2949124
  8.1 10.9 %collective-permute-start.4 = (bf16[2,80,384]{2,1,0:T(8,128)(2,1)S(1)}, bf16[2,80,384]{2,1,0:T(8,128)(2,1)S(1)}, u32[]{:S(2)}, u32[]{:S(2)}) collective-permute-start(bf16[2,80,384]{2,1,0:T(8,128)(2,1)S(1)} %get-tuple-element.42), channel_id=1, source_target_pairs={{0,16},{4,20},{8,24},{12,28},{16,0},{20,4},{24,8},{28,12},{1,17},{... | collective-permute-start | bytes 368648 | tf_op jit(solution)/shard_map/ppermute | solution.py:18
  8.1 10.8 %collective-permute-start.5 = (bf16[2,80,384]{2,1,0:T(8,128)(2,1)S(1)}, bf16[2,80,384]{2,1,0:T(8,128)(2,1)S(1)}, u32[]{:S(2)}, u32[]{:S(2)}) collective-permute-start(bf16[2,80,384]{2,1,0:T(8,128)(2,1)S(1)} %get-tuple-element.43), channel_id=1, source_target_pairs={{0,8},{4,12},{8,0},{12,4},{16,24},{20,28},{24,16},{28,20},{1,9},{5... | collective-permute-start | bytes 368648 | tf_op jit(solution)/shard_map/ppermute | solution.py:18
  10.0 11.5 %collective-permute-start.6 = (bf16[2,80,384]{2,1,0:T(8,128)(2,1)S(1)}, bf16[2,80,384]{2,1,0:T(8,128)(2,1)S(1)}, u32[]{:S(2)}, u32[]{:S(2)}) collective-permute-start(bf16[2,80,384]{2,1,0:T(8,128)(2,1)S(1)} %get-tuple-element.44), channel_id=1, source_target_pairs={{0,24},{4,28},{8,16},{12,20},{16,8},{20,12},{24,0},{28,4},{1,25},{... | collective-permute-start | bytes 368648 | tf_op jit(solution)/shard_map/ppermute | solution.py:18
  12.6 10.7 %collective-permute-start.1 = (bf16[160,320]{1,0:T(8,128)(2,1)S(1)}, bf16[160,320]{1,0:T(8,128)(2,1)S(1)}, u32[]{:S(2)}, u32[]{:S(2)}) collective-permute-start(bf16[160,320]{1,0:T(8,128)(2,1)S(1)} %pad_maximum_fusion.7), channel_id=1, source_target_pairs={{0,8},{4,12},{8,0},{12,4},{16,24},{20,28},{24,16},{28,20},{1,9},{5... | collective-permute-start | bytes 307208 | tf_op jit(solution)/shard_map/ppermute | solution.py:18
  14.4 11.7 %collective-permute-start.10 = (bf16[4,80,384]{2,1,0:T(8,128)(2,1)S(1)}, bf16[4,80,384]{2,1,0:T(8,128)(2,1)S(1)}, u32[]{:S(2)}, u32[]{:S(2)}) collective-permute-start(bf16[4,80,384]{2,1,0:T(8,128)(2,1)S(1)} %get-tuple-element.48), channel_id=1, source_target_pairs={{0,8},{4,12},{8,0},{12,4},{16,24},{20,28},{24,16},{28,20},{1,9},{5... | collective-permute-start | bytes 737288 | tf_op jit(solution)/shard_map/ppermute | solution.py:18
  21.6 19.2 %copy-start.5 = (f32[8,2]{0,1:T(2,128)S(1)}, f32[8,2]{0,1:T(2,128)}, u32[]{:S(2)}) copy-start(f32[8,2]{0,1:T(2,128)} %param.8) | copy-start | bytes 196
  21.6 19.3 %copy-start.2 = (f32[4,384]{1,0:T(4,128)S(1)}, f32[4,384]{1,0:T(4,128)}, u32[]{:S(2)}) copy-start(f32[4,384]{1,0:T(4,128)} %refs_3_.13) | copy-start | bytes 18436
  21.6 10.3 %collective-permute-start.7 = (bf16[320,384]{1,0:T(8,128)(2,1)S(1)}, bf16[320,384]{1,0:T(8,128)(2,1)S(1)}, u32[]{:S(2)}, u32[]{:S(2)}) collective-permute-start(bf16[320,384]{1,0:T(8,128)(2,1)S(1)} %pad_maximum_fusion.3), channel_id=1, source_target_pairs={{0,4},{4,0},{8,12},{12,8},{16,20},{20,16},{24,28},{28,24},{1,5},{5... | collective-permute-start | bytes 737288 | tf_op jit(solution)/shard_map/ppermute | solution.py:18
  23.2 8.5 %collective-permute-start.2 = (bf16[320,320]{1,0:T(8,128)(2,1)S(1)}, bf16[320,320]{1,0:T(8,128)(2,1)S(1)}, u32[]{:S(2)}, u32[]{:S(2)}) collective-permute-start(bf16[320,320]{1,0:T(8,128)(2,1)S(1)} %pad_maximum_fusion.1), channel_id=1, source_target_pairs={{0,4},{4,0},{8,12},{12,8},{16,20},{20,16},{24,28},{28,24},{1,5},{5... | collective-permute-start | bytes 614408 | tf_op jit(solution)/shard_map/ppermute | solution.py:18
  26.2 12.9 %collective-permute-start.11 = (bf16[4,80,384]{2,1,0:T(8,128)(2,1)S(1)}, bf16[4,80,384]{2,1,0:T(8,128)(2,1)S(1)}, u32[]{:S(2)}, u32[]{:S(2)}) collective-permute-start(bf16[4,80,384]{2,1,0:T(8,128)(2,1)S(1)} %pad_maximum_fusion.4), channel_id=1, source_target_pairs={{0,16},{4,20},{8,24},{12,28},{16,0},{20,4},{24,8},{28,12},{1,17},{... | collective-permute-start | bytes 737288 | tf_op jit(solution)/shard_map/ppermute | solution.py:18
  28.8 12.3 %collective-permute-start.8 = (bf16[320,384]{1,0:T(8,128)(2,1)S(1)}, bf16[320,384]{1,0:T(8,128)(2,1)S(1)}, u32[]{:S(2)}, u32[]{:S(2)}) collective-permute-start(bf16[320,384]{1,0:T(8,128)(2,1)S(1)} %pad_maximum_fusion.2.refs_2_), channel_id=1, source_target_pairs={{0,2},{1,3},{2,0},{3,1},{4,6},{5,7},{6,4},{7,5},{8,10},{9,11},{10,... | collective-permute-start | bytes 737288 | tf_op jit(solution)/shard_map/ppermute | solution.py:345
  31.9 10.8 %collective-permute-start.3 = (bf16[640,320]{1,0:T(8,128)(2,1)S(1)}, bf16[640,320]{1,0:T(8,128)(2,1)S(1)}, u32[]{:S(2)}, u32[]{:S(2)}) collective-permute-start(bf16[640,320]{1,0:T(8,128)(2,1)S(1)} %pad_maximum_fusion.refs_0_), channel_id=1, source_target_pairs={{0,1},{1,0},{2,3},{3,2},{4,5},{5,4},{6,7},{7,6},{8,9},{9,8},{10,11... | collective-permute-start | bytes 1228808 | tf_op jit(solution)/shard_map/ppermute | solution.py:18
  31.9 9.2 %collective-permute-start.9 = (bf16[320,384]{1,0:T(8,128)(2,1)S(1)}, bf16[320,384]{1,0:T(8,128)(2,1)S(1)}, u32[]{:S(2)}, u32[]{:S(2)}) collective-permute-start(bf16[320,384]{1,0:T(8,128)(2,1)S(1)} %collective-permute-done.7.refs_3_), channel_id=1, source_target_pairs={{0,2},{1,3},{2,0},{3,1},{4,6},{5,7},{6,4},{7,5},{8,10},{9,11},{10,... | collective-permute-start | bytes 737288 | tf_op jit(solution)/shard_map/ppermute | solution.py:348
  39.2 7.9 %collective-permute-start.12 = (bf16[320,384]{1,0:T(8,128)(2,1)S(1)}, bf16[320,384]{1,0:T(8,128)(2,1)S(1)}, u32[]{:S(2)}, u32[]{:S(2)}) collective-permute-start(bf16[320,384]{1,0:T(8,128)(2,1)S(1)} %pad_maximum_fusion.6), channel_id=1, source_target_pairs={{0,4},{4,0},{8,12},{12,8},{16,20},{20,16},{24,28},{28,24},{1,5},{5... | collective-permute-start | bytes 737288 | tf_op jit(solution)/shard_map/ppermute | solution.py:18
  41.1 7.2 %copy-start.3 = (s32[4,8]{1,0:T(4,128)S(1)}, s32[4,8]{1,0:T(4,128)}, u32[]{:S(2)}) copy-start(s32[4,8]{1,0:T(4,128)} %refs_1_.13) | copy-start | bytes 388
  41.1 7.2 %copy-start.4 = (s32[4,8]{1,0:T(4,128)S(1)}, s32[4,8]{1,0:T(4,128)}, u32[]{:S(2)}) copy-start(s32[4,8]{1,0:T(4,128)} %refs_2_.13) | copy-start | bytes 388
  41.1 16.7 %collective-permute-start.13 = (bf16[320,384]{1,0:T(8,128)(2,1)S(1)}, bf16[320,384]{1,0:T(8,128)(2,1)S(1)}, u32[]{:S(2)}, u32[]{:S(2)}) collective-permute-start(bf16[320,384]{1,0:T(8,128)(2,1)S(1)} %pad_maximum_fusion.5.refs_2_), channel_id=1, source_target_pairs={{0,2},{1,3},{2,0},{3,1},{4,6},{5,7},{6,4},{7,5},{8,10},{9,11},{10,... | collective-permute-start | bytes 737288 | tf_op jit(solution)/shard_map/ppermute | solution.py:345
  43.8 13.4 %collective-permute-start.17 = (bf16[640,384]{1,0:T(8,128)(2,1)S(1)}, bf16[640,384]{1,0:T(8,128)(2,1)S(1)}, u32[]{:S(2)}, u32[]{:S(2)}) collective-permute-start(bf16[640,384]{1,0:T(8,128)(2,1)S(1)} %get-tuple-element.58.refs_7_.odd_ref), channel_id=1, source_target_pairs={{0,24},{4,28},{8,0},{12,4},{16,8},{20,12},{24,16},{28,20},{1,25},{... | collective-permute-start | bytes 1474568 | tf_op jit(solution)/shard_map/ppermute | solution.py:24
  47.1 10.8 %collective-permute-start.14 = (bf16[320,384]{1,0:T(8,128)(2,1)S(1)}, bf16[320,384]{1,0:T(8,128)(2,1)S(1)}, u32[]{:S(2)}, u32[]{:S(2)}) collective-permute-start(bf16[320,384]{1,0:T(8,128)(2,1)S(1)} %collective-permute-done.12.refs_3_), channel_id=1, source_target_pairs={{0,2},{1,3},{2,0},{3,1},{4,6},{5,7},{6,4},{7,5},{8,10},{9,11},{10,... | collective-permute-start | bytes 737288 | tf_op jit(solution)/shard_map/ppermute | solution.py:348
  57.2 19.0 %collective-permute-start.20 = (bf16[640,384]{1,0:T(8,128)(2,1)S(1)}, bf16[640,384]{1,0:T(8,128)(2,1)S(1)}, u32[]{:S(2)}, u32[]{:S(2)}) collective-permute-start(bf16[640,384]{1,0:T(8,128)(2,1)S(1)} %shard_map.84), channel_id=1, source_target_pairs={{0,4},{4,0},{8,12},{12,8},{16,20},{20,16},{24,28},{28,24},{1,5},{5... | collective-permute-start | bytes 1474568 | tf_op jit(solution)/shard_map/ppermute | solution.py:18
  58.5 10.6 %collective-permute-start.15 = (bf16[320,384]{1,0:T(8,128)(2,1)S(1)}, bf16[320,384]{1,0:T(8,128)(2,1)S(1)}, u32[]{:S(2)}, u32[]{:S(2)}) collective-permute-start(bf16[320,384]{1,0:T(8,128)(2,1)S(1)} %get-tuple-element.56.odd_ref.refs_7_), channel_id=1, source_target_pairs={{0,24},{4,28},{8,0},{12,4},{16,8},{20,12},{24,16},{28,20},{1,25},{... | collective-permute-start | bytes 737288 | tf_op jit(solution)/shard_map/ppermute | solution.py:24
  62.8 8.9 %collective-permute-start.18 = (bf16[320,384]{1,0:T(8,128)(2,1)S(1)}, bf16[320,384]{1,0:T(8,128)(2,1)S(1)}, u32[]{:S(2)}, u32[]{:S(2)}) collective-permute-start(bf16[320,384]{1,0:T(8,128)(2,1)S(1)} %get-tuple-element.62.refs_8_.odd_ref), channel_id=1, source_target_pairs={{0,24},{4,28},{8,0},{12,4},{16,8},{20,12},{24,16},{28,20},{1,25},{... | collective-permute-start | bytes 737288 | tf_op jit(solution)/shard_map/ppermute | solution.py:24
  69.1 10.1 %collective-permute-start.16 = (bf16[320,384]{1,0:T(8,128)(2,1)S(1)}, bf16[320,384]{1,0:T(8,128)(2,1)S(1)}, u32[]{:S(2)}, u32[]{:S(2)}) collective-permute-start(bf16[320,384]{1,0:T(8,128)(2,1)S(1)} %shard_map.83), channel_id=1, source_target_pairs={{0,4},{4,0},{8,12},{12,8},{16,20},{20,16},{24,28},{28,24},{1,5},{5... | collective-permute-start | bytes 737288 | tf_op jit(solution)/shard_map/ppermute | solution.py:18
  71.8 8.4 %collective-permute-start.19 = (bf16[320,384]{1,0:T(8,128)(2,1)S(1)}, bf16[320,384]{1,0:T(8,128)(2,1)S(1)}, u32[]{:S(2)}, u32[]{:S(2)}) collective-permute-start(bf16[320,384]{1,0:T(8,128)(2,1)S(1)} %shard_map.86), channel_id=1, source_target_pairs={{0,4},{4,0},{8,12},{12,8},{16,20},{20,16},{24,28},{28,24},{1,5},{5... | collective-permute-start | bytes 737288 | tf_op jit(solution)/shard_map/ppermute | solution.py:18
  82.1 1.4 %collective-permute-start.21 = (bf16[192,384]{1,0:T(8,128)(2,1)S(1)}, bf16[192,384]{1,0:T(8,128)(2,1)S(1)}, u32[]{:S(2)}, u32[]{:S(2)}) collective-permute-start(bf16[192,384]{1,0:T(8,128)(2,1)S(1)} %get-tuple-element.69), channel_id=1, source_target_pairs={{0,1},{1,0},{2,3},{3,2},{4,5},{5,4},{6,7},{7,6},{8,9},{9,8},{10,11... | collective-permute-start | bytes 442376 | tf_op jit(solution)/shard_map/ppermute | solution.py:18
  83.6 6.1 %collective-permute-start.22 = (bf16[48,384]{1,0:T(8,128)(2,1)S(1)}, bf16[48,384]{1,0:T(8,128)(2,1)S(1)}, u32[]{:S(2)}, u32[]{:S(2)}) collective-permute-start(bf16[48,384]{1,0:T(8,128)(2,1)S(1)} %get-tuple-element.71), channel_id=1, source_target_pairs={{0,4},{1,5},{2,6},{3,7},{4,0},{5,1},{6,2},{7,3},{8,12},{9,13},{10,... | collective-permute-start | bytes 110600 | tf_op jit(solution)/shard_map/ppermute | solution.py:232
  85.2 4.5 %collective-permute-start.23 = (bf16[48,384]{1,0:T(8,128)(2,1)S(1)}, bf16[48,384]{1,0:T(8,128)(2,1)S(1)}, u32[]{:S(2)}, u32[]{:S(2)}) collective-permute-start(bf16[48,384]{1,0:T(8,128)(2,1)S(1)} %get-tuple-element.72), channel_id=1, source_target_pairs={{0,2},{1,3},{2,0},{3,1},{4,6},{5,7},{6,4},{7,5},{8,10},{9,11},{10,... | collective-permute-start | bytes 110600 | tf_op jit(solution)/shard_map/ppermute | solution.py:232
  85.8 4.9 %collective-permute-start.24 = (bf16[48,384]{1,0:T(8,128)(2,1)S(1)}, bf16[48,384]{1,0:T(8,128)(2,1)S(1)}, u32[]{:S(2)}, u32[]{:S(2)}) collective-permute-start(bf16[48,384]{1,0:T(8,128)(2,1)S(1)} %get-tuple-element.73), channel_id=1, source_target_pairs={{0,6},{1,7},{2,4},{3,5},{4,2},{5,3},{6,0},{7,1},{8,14},{9,15},{10,... | collective-permute-start | bytes 110600 | tf_op jit(solution)/shard_map/ppermute | solution.py:232
  90.7 3.8 %collective-permute-start.25 = (bf16[24,384]{1,0:T(8,128)(2,1)S(1)}, bf16[24,384]{1,0:T(8,128)(2,1)S(1)}, u32[]{:S(2)}, u32[]{:S(2)}) collective-permute-start(bf16[24,384]{1,0:T(8,128)(2,1)S(1)} %get-tuple-element.76), channel_id=1, source_target_pairs={{0,8},{4,12},{8,0},{12,4},{16,24},{20,28},{24,16},{28,20},{1,9},{5... | collective-permute-start | bytes 55304 | tf_op jit(solution)/shard_map/ppermute | solution.py:18
  94.5 4.7 %collective-permute-start.26 = (bf16[12,384]{1,0:T(8,128)(2,1)S(1)}, bf16[12,384]{1,0:T(8,128)(2,1)S(1)}, u32[]{:S(2)}, u32[]{:S(2)}) collective-permute-start(bf16[12,384]{1,0:T(8,128)(2,1)S(1)} %get-tuple-element.78), channel_id=1, source_target_pairs={{0,16},{4,20},{8,24},{12,28},{16,0},{20,4},{24,8},{28,12},{1,17},{... | collective-permute-start | bytes 27656 | tf_op jit(solution)/shard_map/ppermute | solution.py:18

commit v7 on v6

--- a/solution.py
+++ b/solution.py
@@ -302,7 +302,7 @@
     return [jnp.concatenate([message[part] for message in arrived], axis=0) for part in range(2)]
 
 
-def sent_halving(raw, slot):
+def sent_halving(raw, slot, gates=()):
     count = lax.axis_size("wide")
     masks = bits_of(count)[-2::-1]
     sets = [[offset for offset in range(count) if offset & masks[0] == sent] for sent in (0, masks[0])]
@@ -311,7 +311,7 @@
     for mask in masks:
         if message is None:
             sent = [held.pop(offset) for offset in sorted(held) if offset & mask]
-            message = jnp.stack([piece for pieces in sent for piece in pieces.values()])
+            message = after(jnp.stack([piece for pieces in sent for piece in pieces.values()]), *gates)
         pieces = iter(flip(message, "wide", mask))
         message = None
         for offset in sorted(held):
@@ -337,8 +337,8 @@
     rest = []
     for slot in range(raw.shape[2]):
         if slot:
-            mine, theirs = sent_halving(after(raw, mine_sent), slot)
-            mine, theirs = after(mine, *facing_rows), after(theirs, own_rows[1])
+            mine, theirs = sent_halving(after(raw, mine_sent), slot, [received])
+            theirs = after(theirs, own_rows[1])
         else:
             mine, theirs = sent_direct(raw, slot)
             mine_sent = steps[0]

time: 100 us -> 98.3 us (0.983)
  starting transfers between devices: 41.5 us -> 39.2 us
    ppermute x17, waiting for transfers between devices: 20.7 us -> 24.2 us  [flip(): return lax.ppermute(value, axis, pairs)]
    ppermute x3, waiting for transfers between devices: 7.04 us -> 4.21 us  [from_ahead(): return lax.ppermute(value, axis, pairs)]
  transfers between devices with their start and end apart: 27 -> 27, of which waited for: 13 -> 11; matrix products, arithmetic and copies ran while one was open for 2% -> 2% of each run, Pallas kernels for 22% -> 22%
where the time goes in v7:
time: 98.3 us; the launch traced here: 98.1 us
  starting transfers between devices  39.2 us (40%)
  waiting for transfers between devices  29.2 us (30%)
  Pallas kernels  24.7 us (25%)
  local copies, waits for them, and re-layouts  3.7 us (4%)
  between operations  1 us (1%)
    ppermute x17, waiting for transfers between devices, flip(): return lax.ppermute(value, axis, pairs)  24.2 us
    ppermute x17, starting transfers between devices, flip(): return lax.ppermute(value, axis, pairs)  23.8 us
    pallas_call x7, Pallas kernels, pair_terms(): pl.pallas_call(functools.partial(pair_kernel, offset, slot, len(far), len...  19.1 us
    ppermute x3, starting transfers between devices, from_ahead(): return lax.ppermute(value, axis, pairs)  6.99 us
    ppermute x3, waiting for transfers between devices, from_ahead(): return lax.ppermute(value, axis, pairs)  4.21 us
    ppermute x3, starting transfers between devices, flipped(): return lax.ppermute(value, ('wide', 'narrow'), pairs)  3.55 us
    ppermute x2, starting transfers between devices, gathered_rows(): first = lax.ppermute(mine, 'narrow', half_turn)  3.11 us
    pallas_call x3, Pallas kernels, fit(): pl.pallas_call(functools.partial(fit_kernel, len(metric), len(sources[0])...  2.5 us
  transfers between devices with their start and end apart: 27, of which 11 were waited for; matrix products, arithmetic and copies ran while one was open for 2% of the time, Pallas kernels for 22%

profile of v7, /device:TPU:0, one launch (start us, length us, event | category | flops | bytes accessed | tf_op | source)
XLA Modules:
  0.0 98.1 jit_solution(5109723549913439547)
XLA Ops:
  0.7 0.9 copy-done
  1.6 4.1 %collective-permute-start = (bf16[80,320]{1,0:T(8,128)(2,1)S(1)}, bf16[80,320]{1,0:T(8,128)(2,1)S(1)}, u32[]{:S(2)}, u32[]{:S(2)}) collective-permute-start(bf16[80,320]{1,0:T(8,128)(2,1)S(1)} %constant_dynamic-slice_fusion), channel_id=1, source_target_pairs={{0,16},{4,20},{8,24},{12,28},{16,0},{20,4},{24,8},{28,12},{1,17},{... | collective-permute-start | bytes 153608 | tf_op jit(solution)/shard_map/ppermute | solution.py:18
  5.7 1.2 %copy-done.1 = bf16[1,80,8,2,384]{4,3,2,1,0:T(2,128)(2,1)S(1)} copy-done((bf16[1,80,8,2,384]{4,3,2,1,0:T(2,128)(2,1)S(1)}, bf16[1,80,8,2,384]{4,3,2,1,0:T(2,128)(2,1)}, u32[]{:S(2)}) %copy-start.1) | copy-done | bytes 983064
  6.9 1.1 %shard_map.77 = (bf16[2,80,384]{2,1,0:T(8,128)(2,1)S(1)}, bf16[2,80,384]{2,1,0:T(8,128)(2,1)S(1)}, bf16[2,80,384]{2,1,0:T(8,128)(2,1)S(1)}, bf16[2,80,384]{2,1,0:T(8,128)(2,1)S(1)}) custom-call(bf16[80,8,2,384]{3,2,1,0:T(2,128)(2,1)S(1)} %bitcast.43), custom_call_target="tpu_custom_call" | custom-call | bytes 2949120 | tf_op jit(solution)/shard_map/pallas_call | solution.py:287
  8.1 1.9 %collective-permute-start.5 = (bf16[2,80,384]{2,1,0:T(8,128)(2,1)S(1)}, bf16[2,80,384]{2,1,0:T(8,128)(2,1)S(1)}, u32[]{:S(2)}, u32[]{:S(2)}) collective-permute-start(bf16[2,80,384]{2,1,0:T(8,128)(2,1)S(1)} %get-tuple-element.43), channel_id=1, source_target_pairs={{0,8},{4,12},{8,0},{12,4},{16,24},{20,28},{24,16},{28,20},{1,9},{5... | collective-permute-start | bytes 368648 | tf_op jit(solution)/shard_map/ppermute | solution.py:18
  10.0 2.5 %collective-permute-start.6 = (bf16[2,80,384]{2,1,0:T(8,128)(2,1)S(1)}, bf16[2,80,384]{2,1,0:T(8,128)(2,1)S(1)}, u32[]{:S(2)}, u32[]{:S(2)}) collective-permute-start(bf16[2,80,384]{2,1,0:T(8,128)(2,1)S(1)} %get-tuple-element.44), channel_id=1, source_target_pairs={{0,24},{4,28},{8,16},{12,20},{16,8},{20,12},{24,0},{28,4},{1,25},{... | collective-permute-start | bytes 368648 | tf_op jit(solution)/shard_map/ppermute | solution.py:18
  12.6 0.7 collective-permute-start.1
  13.3 1.1 %shard_map.79 = (bf16[4,80,384]{2,1,0:T(8,128)(2,1)S(1)}, bf16[4,80,384]{2,1,0:T(8,128)(2,1)S(1)}) custom-call(bf16[80,8,2,384]{3,2,1,0:T(2,128)(2,1)S(1)} %bitcast.44), custom_call_target="tpu_custom_call" | custom-call | bytes 2949120 | tf_op jit(solution)/shard_map/pallas_call | solution.py:287
  14.4 1.4 %collective-permute-start.10 = (bf16[4,80,384]{2,1,0:T(8,128)(2,1)S(1)}, bf16[4,80,384]{2,1,0:T(8,128)(2,1)S(1)}, u32[]{:S(2)}, u32[]{:S(2)}) collective-permute-start(bf16[4,80,384]{2,1,0:T(8,128)(2,1)S(1)} %get-tuple-element.48), channel_id=1, source_target_pairs={{0,8},{4,12},{8,0},{12,4},{16,24},{20,28},{24,16},{28,20},{1,9},{5... | collective-permute-start | bytes 737288 | tf_op jit(solution)/shard_map/ppermute | solution.py:18
  15.9 3.0 %collective-permute-done.4 = bf16[2,80,384]{2,1,0:T(8,128)(2,1)S(1)} collective-permute-done((bf16[2,80,384]{2,1,0:T(8,128)(2,1)S(1)}, bf16[2,80,384]{2,1,0:T(8,128)(2,1)S(1)}, u32[]{:S(2)}, u32[]{:S(2)}) %collective-permute-start.4) | collective-permute-done | bytes 122912 | tf_op jit(solution)/shard_map/ppermute | solution.py:18
  19.0 2.6 %collective-permute-done.6 = bf16[2,80,384]{2,1,0:T(8,128)(2,1)S(1)} collective-permute-done((bf16[2,80,384]{2,1,0:T(8,128)(2,1)S(1)}, bf16[2,80,384]{2,1,0:T(8,128)(2,1)S(1)}, u32[]{:S(2)}, u32[]{:S(2)}) %collective-permute-start.6) | collective-permute-done | bytes 122912 | tf_op jit(solution)/shard_map/ppermute | solution.py:18
  21.6 1.6 %collective-permute-start.7 = (bf16[320,384]{1,0:T(8,128)(2,1)S(1)}, bf16[320,384]{1,0:T(8,128)(2,1)S(1)}, u32[]{:S(2)}, u32[]{:S(2)}) collective-permute-start(bf16[320,384]{1,0:T(8,128)(2,1)S(1)} %pad_maximum_fusion.3), channel_id=1, source_target_pairs={{0,4},{4,0},{8,12},{12,8},{16,20},{20,16},{24,28},{28,24},{1,5},{5... | collective-permute-start | bytes 737288 | tf_op jit(solution)/shard_map/ppermute | solution.py:18
  23.8 2.3 %collective-permute-done.10 = bf16[4,80,384]{2,1,0:T(8,128)(2,1)S(1)} collective-permute-done((bf16[4,80,384]{2,1,0:T(8,128)(2,1)S(1)}, bf16[4,80,384]{2,1,0:T(8,128)(2,1)S(1)}, u32[]{:S(2)}, u32[]{:S(2)}) %collective-permute-start.10) | collective-permute-done | bytes 245792 | tf_op jit(solution)/shard_map/ppermute | solution.py:18
  26.2 2.9 %collective-permute-done.7.refs_3_ = bf16[320,384]{1,0:T(8,128)(2,1)S(1)} collective-permute-done((bf16[320,384]{1,0:T(8,128)(2,1)S(1)}, bf16[320,384]{1,0:T(8,128)(2,1)S(1)}, u32[]{:S(2)}, u32[]{:S(2)}) %collective-permute-start.7) | collective-permute-done | bytes 245792 | tf_op jit(solution)/shard_map/ppermute | solution.py:18
  29.2 2.1 %collective-permute-start.11 = (bf16[4,80,384]{2,1,0:T(8,128)(2,1)S(1)}, bf16[4,80,384]{2,1,0:T(8,128)(2,1)S(1)}, u32[]{:S(2)}, u32[]{:S(2)}) collective-permute-start(bf16[4,80,384]{2,1,0:T(8,128)(2,1)S(1)} %pad_maximum_fusion.4), channel_id=1, source_target_pairs={{0,16},{4,20},{8,24},{12,28},{16,0},{20,4},{24,8},{28,12},{1,17},{... | collective-permute-start | bytes 737288 | tf_op jit(solution)/shard_map/ppermute | solution.py:18
  31.3 1.6 %collective-permute-start.8 = (bf16[320,384]{1,0:T(8,128)(2,1)S(1)}, bf16[320,384]{1,0:T(8,128)(2,1)S(1)}, u32[]{:S(2)}, u32[]{:S(2)}) collective-permute-start(bf16[320,384]{1,0:T(8,128)(2,1)S(1)} %pad_maximum_fusion.2.refs_2_), channel_id=1, source_target_pairs={{0,2},{1,3},{2,0},{3,1},{4,6},{5,7},{6,4},{7,5},{8,10},{9,11},{10,... | collective-permute-start | bytes 737288 | tf_op jit(solution)/shard_map/ppermute | solution.py:345
  33.6 7.0 %collective-permute-done.11 = bf16[4,80,384]{2,1,0:T(8,128)(2,1)S(1)} collective-permute-done((bf16[4,80,384]{2,1,0:T(8,128)(2,1)S(1)}, bf16[4,80,384]{2,1,0:T(8,128)(2,1)S(1)}, u32[]{:S(2)}, u32[]{:S(2)}) %collective-permute-start.11) | collective-permute-done | bytes 245792 | tf_op jit(solution)/shard_map/ppermute | solution.py:18
  40.6 1.5 %collective-permute-start.12 = (bf16[320,384]{1,0:T(8,128)(2,1)S(1)}, bf16[320,384]{1,0:T(8,128)(2,1)S(1)}, u32[]{:S(2)}, u32[]{:S(2)}) collective-permute-start(bf16[320,384]{1,0:T(8,128)(2,1)S(1)} %pad_maximum_fusion.6), channel_id=1, source_target_pairs={{0,4},{4,0},{8,12},{12,8},{16,20},{20,16},{24,28},{28,24},{1,5},{5... | collective-permute-start | bytes 737288 | tf_op jit(solution)/shard_map/ppermute | solution.py:18
  42.4 1.6 %collective-permute-start.13 = (bf16[320,384]{1,0:T(8,128)(2,1)S(1)}, bf16[320,384]{1,0:T(8,128)(2,1)S(1)}, u32[]{:S(2)}, u32[]{:S(2)}) collective-permute-start(bf16[320,384]{1,0:T(8,128)(2,1)S(1)} %pad_maximum_fusion.5.refs_2_), channel_id=1, source_target_pairs={{0,2},{1,3},{2,0},{3,1},{4,6},{5,7},{6,4},{7,5},{8,10},{9,11},{10,... | collective-permute-start | bytes 737288 | tf_op jit(solution)/shard_map/ppermute | solution.py:345
  44.0 1.1 %shard_map.78 = (bf16[640,384]{1,0:T(8,128)(2,1)S(1)}, bf16[640,384]{1,0:T(8,128)(2,1)S(1)}) custom-call(bf16[640,320]{1,0:T(8,128)(2,1)S(1)} %pad_maximum_fusion.refs_0_, bf16[640,320]{1,0:T(8,128)(2,1)S(1)} %collective-permute-done.3.refs_1_, bf16[320,384]{1,0:T(8,128)(2,1)S(1)} %pad_maximum_fusion.2.refs_2_, ...), custom_call_target="tpu_custom_call" | custom-call | flops 629145600 | bytes 2785280 | tf_op jit(solution)/shard_map/pallas_call | solution.py:75
  45.1 2.7 %collective-permute-start.17 = (bf16[640,384]{1,0:T(8,128)(2,1)S(1)}, bf16[640,384]{1,0:T(8,128)(2,1)S(1)}, u32[]{:S(2)}, u32[]{:S(2)}) collective-permute-start(bf16[640,384]{1,0:T(8,128)(2,1)S(1)} %get-tuple-element.58.refs_7_.odd_ref), channel_id=1, source_target_pairs={{0,24},{4,28},{8,0},{12,4},{16,8},{20,12},{24,16},{28,20},{1,25},{... | collective-permute-start | bytes 1474568 | tf_op jit(solution)/shard_map/ppermute | solution.py:24
  47.8 1.1 %collective-permute-start.14 = (bf16[320,384]{1,0:T(8,128)(2,1)S(1)}, bf16[320,384]{1,0:T(8,128)(2,1)S(1)}, u32[]{:S(2)}, u32[]{:S(2)}) collective-permute-start(bf16[320,384]{1,0:T(8,128)(2,1)S(1)} %collective-permute-done.12.refs_3_), channel_id=1, source_target_pairs={{0,2},{1,3},{2,0},{3,1},{4,6},{5,7},{6,4},{7,5},{8,10},{9,11},{10,... | collective-permute-start | bytes 737288 | tf_op jit(solution)/shard_map/ppermute | solution.py:348
  48.9 0.7 shard_map.80.refs_6_
  49.6 2.9 %shard_map.81 = (f32[384,384]{1,0:T(8,128)S(1)}, f32[640,768]{1,0:T(8,128)S(1)}) custom-call(f32[8,2]{1,0:T(8,128)S(1)} %copy.14.refs_0_, s32[4,8]{1,0:T(4,128)S(1)} %copy-done.3, s32[4,8]{1,0:T(4,128)S(1)} %copy-done.4, f32[4,384]{1,0:T(4,128)S(1)} %copy-done.2, f32[384,4]{1,0:T(8,128)S(1)} %bitcast.36, bf16[640,384]{1,0:T(8,128)(2,1)S(1)} %get-tuple-element.45.refs_5_, ...), custom_call_target="tpu_custom_call" | custom-call | flops 7851737088 | bytes 52690944 | tf_op jit(solution)/shard_map/pallas_call | solution.py:197
  52.5 4.2 %collective-permute-done.17.even_ref.refs_7_ = bf16[640,384]{1,0:T(8,128)(2,1)S(1)} collective-permute-done((bf16[640,384]{1,0:T(8,128)(2,1)S(1)}, bf16[640,384]{1,0:T(8,128)(2,1)S(1)}, u32[]{:S(2)}, u32[]{:S(2)}) %collective-permute-start.17) | collective-permute-done | bytes 491552 | tf_op jit(solution)/shard_map/ppermute | solution.py:24
  56.8 0.6 collective-permute-start.20
  57.4 0.7 shard_map.82
  58.1 4.0 %collective-permute-start.15 = (bf16[320,384]{1,0:T(8,128)(2,1)S(1)}, bf16[320,384]{1,0:T(8,128)(2,1)S(1)}, u32[]{:S(2)}, u32[]{:S(2)}) collective-permute-start(bf16[320,384]{1,0:T(8,128)(2,1)S(1)} %get-tuple-element.56.odd_ref.refs_7_), channel_id=1, source_target_pairs={{0,24},{4,28},{8,0},{12,4},{16,8},{20,12},{24,16},{28,20},{1,25},{... | collective-permute-start | bytes 737288 | tf_op jit(solution)/shard_map/ppermute | solution.py:24
  62.4 2.9 %shard_map.85 = (f32[384,384]{1,0:T(8,128)S(1)}, f32[640,768]{1,0:T(8,128)S(1)}) custom-call(f32[8,2]{1,0:T(8,128)S(1)} %copy.14.refs_0_, s32[4,8]{1,0:T(4,128)S(1)} %copy-done.3, s32[4,8]{1,0:T(4,128)S(1)} %copy-done.4, f32[4,384]{1,0:T(4,128)S(1)} %copy-done.2, f32[384,4]{1,0:T(8,128)S(1)} %bitcast.37, bf16[640,384]{1,0:T(8,128)(2,1)S(1)} %get-tuple-element.45.refs_5_, ...), custom_call_target="tpu_custom_call" | custom-call | flops 981467136 | bytes 6586368 | tf_op jit(solution)/shard_map/pallas_call | solution.py:197
  65.4 2.9 %shard_map.87 = (f32[384,384]{1,0:T(8,128)S(1)}, f32[640,768]{1,0:T(8,128)S(1)}) custom-call(f32[8,2]{1,0:T(8,128)S(1)} %copy.14.refs_0_, s32[4,8]{1,0:T(4,128)S(1)} %copy-done.3, s32[4,8]{1,0:T(4,128)S(1)} %copy-done.4, f32[4,384]{1,0:T(4,128)S(1)} %copy-done.2, f32[384,4]{1,0:T(8,128)S(1)} %bitcast.38, bf16[640,384]{1,0:T(8,128)(2,1)S(1)} %get-tuple-element.45.refs_5_, ...), custom_call_target="tpu_custom_call" | custom-call | flops 981467136 | bytes 6586368 | tf_op jit(solution)/shard_map/pallas_call | solution.py:197
  68.3 1.5 %collective-permute-start.16 = (bf16[320,384]{1,0:T(8,128)(2,1)S(1)}, bf16[320,384]{1,0:T(8,128)(2,1)S(1)}, u32[]{:S(2)}, u32[]{:S(2)}) collective-permute-start(bf16[320,384]{1,0:T(8,128)(2,1)S(1)} %shard_map.83), channel_id=1, source_target_pairs={{0,4},{4,0},{8,12},{12,8},{16,20},{20,16},{24,28},{28,24},{1,5},{5... | collective-permute-start | bytes 737288 | tf_op jit(solution)/shard_map/ppermute | solution.py:18
  69.9 1.3 %collective-permute-start.19 = (bf16[320,384]{1,0:T(8,128)(2,1)S(1)}, bf16[320,384]{1,0:T(8,128)(2,1)S(1)}, u32[]{:S(2)}, u32[]{:S(2)}) collective-permute-start(bf16[320,384]{1,0:T(8,128)(2,1)S(1)} %shard_map.86), channel_id=1, source_target_pairs={{0,4},{4,0},{8,12},{12,8},{16,20},{20,16},{24,28},{28,24},{1,5},{5... | collective-permute-start | bytes 737288 | tf_op jit(solution)/shard_map/ppermute | solution.py:18
  71.1 2.9 %shard_map.88 = (f32[384,384]{1,0:T(8,128)S(1)}, f32[640,768]{1,0:T(8,128)S(1)}) custom-call(f32[8,2]{1,0:T(8,128)S(1)} %copy.14.refs_0_, s32[4,8]{1,0:T(4,128)S(1)} %copy-done.3, s32[4,8]{1,0:T(4,128)S(1)} %copy-done.4, f32[4,384]{1,0:T(4,128)S(1)} %copy-done.2, f32[384,4]{1,0:T(8,128)S(1)} %bitcast.39, bf16[640,384]{1,0:T(8,128)(2,1)S(1)} %get-tuple-element.45.refs_5_, ...), custom_call_target="tpu_custom_call" | custom-call | flops 981467136 | bytes 6586368 | tf_op jit(solution)/shard_map/pallas_call | solution.py:197
  74.1 2.9 %shard_map.89 = (f32[384,384]{1,0:T(8,128)S(1)}, f32[640,768]{1,0:T(8,128)S(1)}) custom-call(f32[8,2]{1,0:T(8,128)S(1)} %copy.14.refs_0_, s32[4,8]{1,0:T(4,128)S(1)} %copy-done.3, s32[4,8]{1,0:T(4,128)S(1)} %copy-done.4, f32[4,384]{1,0:T(4,128)S(1)} %copy-done.2, f32[384,4]{1,0:T(8,128)S(1)} %bitcast.40, bf16[640,384]{1,0:T(8,128)(2,1)S(1)} %get-tuple-element.45.refs_5_, ...), custom_call_target="tpu_custom_call" | custom-call | flops 2944401408 | bytes 19759104 | tf_op jit(solution)/shard_map/pallas_call | solution.py:197
  77.0 1.5 %collective-permute-done.19.refs_8_ = bf16[320,384]{1,0:T(8,128)(2,1)S(1)} collective-permute-done((bf16[320,384]{1,0:T(8,128)(2,1)S(1)}, bf16[320,384]{1,0:T(8,128)(2,1)S(1)}, u32[]{:S(2)}, u32[]{:S(2)}) %collective-permute-start.19) | collective-permute-done | bytes 245792 | tf_op jit(solution)/shard_map/ppermute | solution.py:18
  78.5 2.0 %shard_map.91 = (bf16[192,384]{1,0:T(8,128)(2,1)S(1)}, f32[192,384]{1,0:T(8,128)S(1)}) custom-call(f32[8,2]{1,0:T(8,128)S(1)} %copy.14.refs_0_, s32[4,8]{1,0:T(4,128)S(1)} %copy-done.3, s32[4,8]{1,0:T(4,128)S(1)} %copy-done.4, f32[4,384]{1,0:T(4,128)S(1)} %copy-done.2, f32[384,4]{1,0:T(8,128)S(1)} %bitcast.41, ...), custom_call_target="tpu_custom_call" | custom-call | flops 981467136 | bytes 6586368 | tf_op jit(solution)/shard_map/pallas_call | solution.py:197
  80.6 1.4 %collective-permute-done.21.refs_0_ = bf16[192,384]{1,0:T(8,128)(2,1)S(1)} collective-permute-done((bf16[192,384]{1,0:T(8,128)(2,1)S(1)}, bf16[192,384]{1,0:T(8,128)(2,1)S(1)}, u32[]{:S(2)}, u32[]{:S(2)}) %collective-permute-start.21) | collective-permute-done | bytes 147488 | tf_op jit(solution)/shard_map/ppermute | solution.py:18
  82.0 1.0 %collective-permute-start.22 = (bf16[48,384]{1,0:T(8,128)(2,1)S(1)}, bf16[48,384]{1,0:T(8,128)(2,1)S(1)}, u32[]{:S(2)}, u32[]{:S(2)}) collective-permute-start(bf16[48,384]{1,0:T(8,128)(2,1)S(1)} %get-tuple-element.71), channel_id=1, source_target_pairs={{0,4},{1,5},{2,6},{3,7},{4,0},{5,1},{6,2},{7,3},{8,12},{9,13},{10,... | collective-permute-start | bytes 110600 | tf_op jit(solution)/shard_map/ppermute | solution.py:232
  83.0 1.0 %collective-permute-start.23 = (bf16[48,384]{1,0:T(8,128)(2,1)S(1)}, bf16[48,384]{1,0:T(8,128)(2,1)S(1)}, u32[]{:S(2)}, u32[]{:S(2)}) collective-permute-start(bf16[48,384]{1,0:T(8,128)(2,1)S(1)} %get-tuple-element.72), channel_id=1, source_target_pairs={{0,2},{1,3},{2,0},{3,1},{4,6},{5,7},{6,4},{7,5},{8,10},{9,11},{10,... | collective-permute-start | bytes 110600 | tf_op jit(solution)/shard_map/ppermute | solution.py:232
  84.1 1.5 %collective-permute-start.24 = (bf16[48,384]{1,0:T(8,128)(2,1)S(1)}, bf16[48,384]{1,0:T(8,128)(2,1)S(1)}, u32[]{:S(2)}, u32[]{:S(2)}) collective-permute-start(bf16[48,384]{1,0:T(8,128)(2,1)S(1)} %get-tuple-element.73), channel_id=1, source_target_pairs={{0,6},{1,7},{2,4},{3,5},{4,2},{5,3},{6,0},{7,1},{8,14},{9,15},{10,... | collective-permute-start | bytes 110600 | tf_op jit(solution)/shard_map/ppermute | solution.py:232
  85.6 2.5 %shard_map.90 = bf16[640,768]{1,0:T(8,128)(2,1)S(1)} custom-call(f32[8,2]{1,0:T(8,128)S(1)} %copy.14.refs_0_, s32[4,8]{1,0:T(4,128)S(1)} %copy-done.3, s32[4,8]{1,0:T(4,128)S(1)} %copy-done.4, f32[4,384]{1,0:T(4,128)S(1)} %copy-done.2, f32[384,4]{1,0:T(8,128)S(1)} %bitcast.42, bf16[640,384]{1,0:T(8,128)(2,1)S(1)} %get-tuple-element.45.refs_5_, ...), custom_call_target="tpu_custom_call" | custom-call | flops 981467136 | bytes 6586368 | tf_op jit(solution)/shard_map/pallas_call | solution.py:197
  88.1 0.8 collective-permute-done.24.refs_2_
  89.0 1.1 %collective-permute-start.25 = (bf16[24,384]{1,0:T(8,128)(2,1)S(1)}, bf16[24,384]{1,0:T(8,128)(2,1)S(1)}, u32[]{:S(2)}, u32[]{:S(2)}) collective-permute-start(bf16[24,384]{1,0:T(8,128)(2,1)S(1)} %get-tuple-element.76), channel_id=1, source_target_pairs={{0,8},{4,12},{8,0},{12,4},{16,24},{20,28},{24,16},{28,20},{1,9},{5... | collective-permute-start | bytes 55304 | tf_op jit(solution)/shard_map/ppermute | solution.py:18
  90.1 2.7 %collective-permute-done.25.refs_0_ = bf16[24,384]{1,0:T(8,128)(2,1)S(1)} collective-permute-done((bf16[24,384]{1,0:T(8,128)(2,1)S(1)}, bf16[24,384]{1,0:T(8,128)(2,1)S(1)}, u32[]{:S(2)}, u32[]{:S(2)}) %collective-permute-start.25) | collective-permute-done | bytes 18464 | tf_op jit(solution)/shard_map/ppermute | solution.py:18
  92.8 2.7 %collective-permute-start.26 = (bf16[12,384]{1,0:T(8,128)(2,1)S(1)}, bf16[12,384]{1,0:T(8,128)(2,1)S(1)}, u32[]{:S(2)}, u32[]{:S(2)}) collective-permute-start(bf16[12,384]{1,0:T(8,128)(2,1)S(1)} %get-tuple-element.78), channel_id=1, source_target_pairs={{0,16},{4,20},{8,24},{12,28},{16,0},{20,4},{24,8},{28,12},{1,17},{... | collective-permute-start | bytes 27656 | tf_op jit(solution)/shard_map/ppermute | solution.py:18
  95.6 1.2 %reshape.10 = bf16[1,640,1,2,384]{4,3,1,2,0:T(2,128)(2,1)} reshape(bf16[640,768]{1,0:T(8,128)(2,1)S(1)} %shard_map.90) | data formatting | bytes 1966080 | tf_op jit(solution)/shard_map/reshape | solution.py:432
  96.7 0.7 collective-permute-done.26.refs_0_
  97.5 0.6 shard_map.95
  (56 shorter events, 2.6 us)
Async XLA Ops:
  0.6 0.9 copy-start
  1.6 10.9 %collective-permute-start = (bf16[80,320]{1,0:T(8,128)(2,1)S(1)}, bf16[80,320]{1,0:T(8,128)(2,1)S(1)}, u32[]{:S(2)}, u32[]{:S(2)}) collective-permute-start(bf16[80,320]{1,0:T(8,128)(2,1)S(1)} %constant_dynamic-slice_fusion), channel_id=1, source_target_pairs={{0,16},{4,20},{8,24},{12,28},{16,0},{20,4},{24,8},{28,12},{1,17},{... | collective-permute-start | bytes 153608 | tf_op jit(solution)/shard_map/ppermute | solution.py:18
  5.7 1.2 %copy-start.1 = (bf16[1,80,8,2,384]{4,3,2,1,0:T(2,128)(2,1)S(1)}, bf16[1,80,8,2,384]{4,3,2,1,0:T(2,128)(2,1)}, u32[]{:S(2)}) copy-start(bf16[1,80,8,2,384]{4,3,2,1,0:T(2,128)(2,1)} %param.6) | copy-start | bytes 2949124
  8.1 10.9 %collective-permute-start.4 = (bf16[2,80,384]{2,1,0:T(8,128)(2,1)S(1)}, bf16[2,80,384]{2,1,0:T(8,128)(2,1)S(1)}, u32[]{:S(2)}, u32[]{:S(2)}) collective-permute-start(bf16[2,80,384]{2,1,0:T(8,128)(2,1)S(1)} %get-tuple-element.42), channel_id=1, source_target_pairs={{0,16},{4,20},{8,24},{12,28},{16,0},{20,4},{24,8},{28,12},{1,17},{... | collective-permute-start | bytes 368648 | tf_op jit(solution)/shard_map/ppermute | solution.py:18
  8.1 10.8 %collective-permute-start.5 = (bf16[2,80,384]{2,1,0:T(8,128)(2,1)S(1)}, bf16[2,80,384]{2,1,0:T(8,128)(2,1)S(1)}, u32[]{:S(2)}, u32[]{:S(2)}) collective-permute-start(bf16[2,80,384]{2,1,0:T(8,128)(2,1)S(1)} %get-tuple-element.43), channel_id=1, source_target_pairs={{0,8},{4,12},{8,0},{12,4},{16,24},{20,28},{24,16},{28,20},{1,9},{5... | collective-permute-start | bytes 368648 | tf_op jit(solution)/shard_map/ppermute | solution.py:18
  10.0 11.5 %collective-permute-start.6 = (bf16[2,80,384]{2,1,0:T(8,128)(2,1)S(1)}, bf16[2,80,384]{2,1,0:T(8,128)(2,1)S(1)}, u32[]{:S(2)}, u32[]{:S(2)}) collective-permute-start(bf16[2,80,384]{2,1,0:T(8,128)(2,1)S(1)} %get-tuple-element.44), channel_id=1, source_target_pairs={{0,24},{4,28},{8,16},{12,20},{16,8},{20,12},{24,0},{28,4},{1,25},{... | collective-permute-start | bytes 368648 | tf_op jit(solution)/shard_map/ppermute | solution.py:18
  12.6 10.7 %collective-permute-start.1 = (bf16[160,320]{1,0:T(8,128)(2,1)S(1)}, bf16[160,320]{1,0:T(8,128)(2,1)S(1)}, u32[]{:S(2)}, u32[]{:S(2)}) collective-permute-start(bf16[160,320]{1,0:T(8,128)(2,1)S(1)} %pad_maximum_fusion.7), channel_id=1, source_target_pairs={{0,8},{4,12},{8,0},{12,4},{16,24},{20,28},{24,16},{28,20},{1,9},{5... | collective-permute-start | bytes 307208 | tf_op jit(solution)/shard_map/ppermute | solution.py:18
  14.4 11.7 %collective-permute-start.10 = (bf16[4,80,384]{2,1,0:T(8,128)(2,1)S(1)}, bf16[4,80,384]{2,1,0:T(8,128)(2,1)S(1)}, u32[]{:S(2)}, u32[]{:S(2)}) collective-permute-start(bf16[4,80,384]{2,1,0:T(8,128)(2,1)S(1)} %get-tuple-element.48), channel_id=1, source_target_pairs={{0,8},{4,12},{8,0},{12,4},{16,24},{20,28},{24,16},{28,20},{1,9},{5... | collective-permute-start | bytes 737288 | tf_op jit(solution)/shard_map/ppermute | solution.py:18
  21.6 20.5 %copy-start.5 = (f32[8,2]{0,1:T(2,128)S(1)}, f32[8,2]{0,1:T(2,128)}, u32[]{:S(2)}) copy-start(f32[8,2]{0,1:T(2,128)} %param.8) | copy-start | bytes 196
  21.6 20.6 %copy-start.2 = (f32[4,384]{1,0:T(4,128)S(1)}, f32[4,384]{1,0:T(4,128)}, u32[]{:S(2)}) copy-start(f32[4,384]{1,0:T(4,128)} %refs_3_.13) | copy-start | bytes 18436
  21.6 7.5 %collective-permute-start.7 = (bf16[320,384]{1,0:T(8,128)(2,1)S(1)}, bf16[320,384]{1,0:T(8,128)(2,1)S(1)}, u32[]{:S(2)}, u32[]{:S(2)}) collective-permute-start(bf16[320,384]{1,0:T(8,128)(2,1)S(1)} %pad_maximum_fusion.3), channel_id=1, source_target_pairs={{0,4},{4,0},{8,12},{12,8},{16,20},{20,16},{24,28},{28,24},{1,5},{5... | collective-permute-start | bytes 737288 | tf_op jit(solution)/shard_map/ppermute | solution.py:18
  23.2 9.6 %collective-permute-start.2 = (bf16[320,320]{1,0:T(8,128)(2,1)S(1)}, bf16[320,320]{1,0:T(8,128)(2,1)S(1)}, u32[]{:S(2)}, u32[]{:S(2)}) collective-permute-start(bf16[320,320]{1,0:T(8,128)(2,1)S(1)} %pad_maximum_fusion.1), channel_id=1, source_target_pairs={{0,4},{4,0},{8,12},{12,8},{16,20},{20,16},{24,28},{28,24},{1,5},{5... | collective-permute-start | bytes 614408 | tf_op jit(solution)/shard_map/ppermute | solution.py:18
  29.2 11.4 %collective-permute-start.11 = (bf16[4,80,384]{2,1,0:T(8,128)(2,1)S(1)}, bf16[4,80,384]{2,1,0:T(8,128)(2,1)S(1)}, u32[]{:S(2)}, u32[]{:S(2)}) collective-permute-start(bf16[4,80,384]{2,1,0:T(8,128)(2,1)S(1)} %pad_maximum_fusion.4), channel_id=1, source_target_pairs={{0,16},{4,20},{8,24},{12,28},{16,0},{20,4},{24,8},{28,12},{1,17},{... | collective-permute-start | bytes 737288 | tf_op jit(solution)/shard_map/ppermute | solution.py:18
  31.3 12.7 %collective-permute-start.8 = (bf16[320,384]{1,0:T(8,128)(2,1)S(1)}, bf16[320,384]{1,0:T(8,128)(2,1)S(1)}, u32[]{:S(2)}, u32[]{:S(2)}) collective-permute-start(bf16[320,384]{1,0:T(8,128)(2,1)S(1)} %pad_maximum_fusion.2.refs_2_), channel_id=1, source_target_pairs={{0,2},{1,3},{2,0},{3,1},{4,6},{5,7},{6,4},{7,5},{8,10},{9,11},{10,... | collective-permute-start | bytes 737288 | tf_op jit(solution)/shard_map/ppermute | solution.py:345
  32.9 11.1 %collective-permute-start.3 = (bf16[640,320]{1,0:T(8,128)(2,1)S(1)}, bf16[640,320]{1,0:T(8,128)(2,1)S(1)}, u32[]{:S(2)}, u32[]{:S(2)}) collective-permute-start(bf16[640,320]{1,0:T(8,128)(2,1)S(1)} %pad_maximum_fusion.refs_0_), channel_id=1, source_target_pairs={{0,1},{1,0},{2,3},{3,2},{4,5},{5,4},{6,7},{7,6},{8,9},{9,8},{10,11... | collective-permute-start | bytes 1228808 | tf_op jit(solution)/shard_map/ppermute | solution.py:18
  32.9 11.0 %collective-permute-start.9 = (bf16[320,384]{1,0:T(8,128)(2,1)S(1)}, bf16[320,384]{1,0:T(8,128)(2,1)S(1)}, u32[]{:S(2)}, u32[]{:S(2)}) collective-permute-start(bf16[320,384]{1,0:T(8,128)(2,1)S(1)} %collective-permute-done.7.refs_3_), channel_id=1, source_target_pairs={{0,2},{1,3},{2,0},{3,1},{4,6},{5,7},{6,4},{7,5},{8,10},{9,11},{10,... | collective-permute-start | bytes 737288 | tf_op jit(solution)/shard_map/ppermute | solution.py:348
  40.6 7.2 %collective-permute-start.12 = (bf16[320,384]{1,0:T(8,128)(2,1)S(1)}, bf16[320,384]{1,0:T(8,128)(2,1)S(1)}, u32[]{:S(2)}, u32[]{:S(2)}) collective-permute-start(bf16[320,384]{1,0:T(8,128)(2,1)S(1)} %pad_maximum_fusion.6), channel_id=1, source_target_pairs={{0,4},{4,0},{8,12},{12,8},{16,20},{20,16},{24,28},{28,24},{1,5},{5... | collective-permute-start | bytes 737288 | tf_op jit(solution)/shard_map/ppermute | solution.py:18
  42.4 7.2 %copy-start.3 = (s32[4,8]{1,0:T(4,128)S(1)}, s32[4,8]{1,0:T(4,128)}, u32[]{:S(2)}) copy-start(s32[4,8]{1,0:T(4,128)} %refs_1_.13) | copy-start | bytes 388
  42.4 7.2 %copy-start.4 = (s32[4,8]{1,0:T(4,128)S(1)}, s32[4,8]{1,0:T(4,128)}, u32[]{:S(2)}) copy-start(s32[4,8]{1,0:T(4,128)} %refs_2_.13) | copy-start | bytes 388
  42.4 15.0 %collective-permute-start.13 = (bf16[320,384]{1,0:T(8,128)(2,1)S(1)}, bf16[320,384]{1,0:T(8,128)(2,1)S(1)}, u32[]{:S(2)}, u32[]{:S(2)}) collective-permute-start(bf16[320,384]{1,0:T(8,128)(2,1)S(1)} %pad_maximum_fusion.5.refs_2_), channel_id=1, source_target_pairs={{0,2},{1,3},{2,0},{3,1},{4,6},{5,7},{6,4},{7,5},{8,10},{9,11},{10,... | collective-permute-start | bytes 737288 | tf_op jit(solution)/shard_map/ppermute | solution.py:345
  45.1 11.6 %collective-permute-start.17 = (bf16[640,384]{1,0:T(8,128)(2,1)S(1)}, bf16[640,384]{1,0:T(8,128)(2,1)S(1)}, u32[]{:S(2)}, u32[]{:S(2)}) collective-permute-start(bf16[640,384]{1,0:T(8,128)(2,1)S(1)} %get-tuple-element.58.refs_7_.odd_ref), channel_id=1, source_target_pairs={{0,24},{4,28},{8,0},{12,4},{16,8},{20,12},{24,16},{28,20},{1,25},{... | collective-permute-start | bytes 1474568 | tf_op jit(solution)/shard_map/ppermute | solution.py:24
  47.8 9.6 %collective-permute-start.14 = (bf16[320,384]{1,0:T(8,128)(2,1)S(1)}, bf16[320,384]{1,0:T(8,128)(2,1)S(1)}, u32[]{:S(2)}, u32[]{:S(2)}) collective-permute-start(bf16[320,384]{1,0:T(8,128)(2,1)S(1)} %collective-permute-done.12.refs_3_), channel_id=1, source_target_pairs={{0,2},{1,3},{2,0},{3,1},{4,6},{5,7},{6,4},{7,5},{8,10},{9,11},{10,... | collective-permute-start | bytes 737288 | tf_op jit(solution)/shard_map/ppermute | solution.py:348
  56.8 17.3 %collective-permute-start.20 = (bf16[640,384]{1,0:T(8,128)(2,1)S(1)}, bf16[640,384]{1,0:T(8,128)(2,1)S(1)}, u32[]{:S(2)}, u32[]{:S(2)}) collective-permute-start(bf16[640,384]{1,0:T(8,128)(2,1)S(1)} %shard_map.84), channel_id=1, source_target_pairs={{0,4},{4,0},{8,12},{12,8},{16,20},{20,16},{24,28},{28,24},{1,5},{5... | collective-permute-start | bytes 1474568 | tf_op jit(solution)/shard_map/ppermute | solution.py:18
  58.1 10.2 %collective-permute-start.15 = (bf16[320,384]{1,0:T(8,128)(2,1)S(1)}, bf16[320,384]{1,0:T(8,128)(2,1)S(1)}, u32[]{:S(2)}, u32[]{:S(2)}) collective-permute-start(bf16[320,384]{1,0:T(8,128)(2,1)S(1)} %get-tuple-element.56.odd_ref.refs_7_), channel_id=1, source_target_pairs={{0,24},{4,28},{8,0},{12,4},{16,8},{20,12},{24,16},{28,20},{1,25},{... | collective-permute-start | bytes 737288 | tf_op jit(solution)/shard_map/ppermute | solution.py:24
  62.2 7.7 %collective-permute-start.18 = (bf16[320,384]{1,0:T(8,128)(2,1)S(1)}, bf16[320,384]{1,0:T(8,128)(2,1)S(1)}, u32[]{:S(2)}, u32[]{:S(2)}) collective-permute-start(bf16[320,384]{1,0:T(8,128)(2,1)S(1)} %get-tuple-element.62.refs_8_.odd_ref), channel_id=1, source_target_pairs={{0,24},{4,28},{8,0},{12,4},{16,8},{20,12},{24,16},{28,20},{1,25},{... | collective-permute-start | bytes 737288 | tf_op jit(solution)/shard_map/ppermute | solution.py:24
  68.3 8.7 %collective-permute-start.16 = (bf16[320,384]{1,0:T(8,128)(2,1)S(1)}, bf16[320,384]{1,0:T(8,128)(2,1)S(1)}, u32[]{:S(2)}, u32[]{:S(2)}) collective-permute-start(bf16[320,384]{1,0:T(8,128)(2,1)S(1)} %shard_map.83), channel_id=1, source_target_pairs={{0,4},{4,0},{8,12},{12,8},{16,20},{20,16},{24,28},{28,24},{1,5},{5... | collective-permute-start | bytes 737288 | tf_op jit(solution)/shard_map/ppermute | solution.py:18
  69.9 8.6 %collective-permute-start.19 = (bf16[320,384]{1,0:T(8,128)(2,1)S(1)}, bf16[320,384]{1,0:T(8,128)(2,1)S(1)}, u32[]{:S(2)}, u32[]{:S(2)}) collective-permute-start(bf16[320,384]{1,0:T(8,128)(2,1)S(1)} %shard_map.86), channel_id=1, source_target_pairs={{0,4},{4,0},{8,12},{12,8},{16,20},{20,16},{24,28},{28,24},{1,5},{5... | collective-permute-start | bytes 737288 | tf_op jit(solution)/shard_map/ppermute | solution.py:18
  80.5 1.4 %collective-permute-start.21 = (bf16[192,384]{1,0:T(8,128)(2,1)S(1)}, bf16[192,384]{1,0:T(8,128)(2,1)S(1)}, u32[]{:S(2)}, u32[]{:S(2)}) collective-permute-start(bf16[192,384]{1,0:T(8,128)(2,1)S(1)} %get-tuple-element.69), channel_id=1, source_target_pairs={{0,1},{1,0},{2,3},{3,2},{4,5},{5,4},{6,7},{7,6},{8,9},{9,8},{10,11... | collective-permute-start | bytes 442376 | tf_op jit(solution)/shard_map/ppermute | solution.py:18
  82.0 6.1 %collective-permute-start.22 = (bf16[48,384]{1,0:T(8,128)(2,1)S(1)}, bf16[48,384]{1,0:T(8,128)(2,1)S(1)}, u32[]{:S(2)}, u32[]{:S(2)}) collective-permute-start(bf16[48,384]{1,0:T(8,128)(2,1)S(1)} %get-tuple-element.71), channel_id=1, source_target_pairs={{0,4},{1,5},{2,6},{3,7},{4,0},{5,1},{6,2},{7,3},{8,12},{9,13},{10,... | collective-permute-start | bytes 110600 | tf_op jit(solution)/shard_map/ppermute | solution.py:232
  83.0 5.1 %collective-permute-start.23 = (bf16[48,384]{1,0:T(8,128)(2,1)S(1)}, bf16[48,384]{1,0:T(8,128)(2,1)S(1)}, u32[]{:S(2)}, u32[]{:S(2)}) collective-permute-start(bf16[48,384]{1,0:T(8,128)(2,1)S(1)} %get-tuple-element.72), channel_id=1, source_target_pairs={{0,2},{1,3},{2,0},{3,1},{4,6},{5,7},{6,4},{7,5},{8,10},{9,11},{10,... | collective-permute-start | bytes 110600 | tf_op jit(solution)/shard_map/ppermute | solution.py:232
  84.1 4.9 %collective-permute-start.24 = (bf16[48,384]{1,0:T(8,128)(2,1)S(1)}, bf16[48,384]{1,0:T(8,128)(2,1)S(1)}, u32[]{:S(2)}, u32[]{:S(2)}) collective-permute-start(bf16[48,384]{1,0:T(8,128)(2,1)S(1)} %get-tuple-element.73), channel_id=1, source_target_pairs={{0,6},{1,7},{2,4},{3,5},{4,2},{5,3},{6,0},{7,1},{8,14},{9,15},{10,... | collective-permute-start | bytes 110600 | tf_op jit(solution)/shard_map/ppermute | solution.py:232
  89.0 3.8 %collective-permute-start.25 = (bf16[24,384]{1,0:T(8,128)(2,1)S(1)}, bf16[24,384]{1,0:T(8,128)(2,1)S(1)}, u32[]{:S(2)}, u32[]{:S(2)}) collective-permute-start(bf16[24,384]{1,0:T(8,128)(2,1)S(1)} %get-tuple-element.76), channel_id=1, source_target_pairs={{0,8},{4,12},{8,0},{12,4},{16,24},{20,28},{24,16},{28,20},{1,9},{5... | collective-permute-start | bytes 55304 | tf_op jit(solution)/shard_map/ppermute | solution.py:18
  92.8 4.7 %collective-permute-start.26 = (bf16[12,384]{1,0:T(8,128)(2,1)S(1)}, bf16[12,384]{1,0:T(8,128)(2,1)S(1)}, u32[]{:S(2)}, u32[]{:S(2)}) collective-permute-start(bf16[12,384]{1,0:T(8,128)(2,1)S(1)} %get-tuple-element.78), channel_id=1, source_target_pairs={{0,16},{4,20},{8,24},{12,28},{16,0},{20,4},{24,8},{28,12},{1,17},{... | collective-permute-start | bytes 27656 | tf_op jit(solution)/shard_map/ppermute | solution.py:18

commit v8 on v7

--- a/solution.py
+++ b/solution.py
@@ -338,7 +338,6 @@
     for slot in range(raw.shape[2]):
         if slot:
             mine, theirs = sent_halving(after(raw, mine_sent), slot, [received])
-            theirs = after(theirs, own_rows[1])
         else:
             mine, theirs = sent_direct(raw, slot)
             mine_sent = steps[0]

time: 98.3 us -> 98.3 us (level)
  no operation moved by 1% of the time
where the time goes in v8:
time: 98.3 us; the launch traced here: 98.1 us
  starting transfers between devices  39.2 us (40%)
  waiting for transfers between devices  29.2 us (30%)
  Pallas kernels  24.7 us (25%)
  local copies, waits for them, and re-layouts  3.7 us (4%)
  between operations  1 us (1%)
    ppermute x17, waiting for transfers between devices, flip(): return lax.ppermute(value, axis, pairs)  24.2 us
    ppermute x17, starting transfers between devices, flip(): return lax.ppermute(value, axis, pairs)  23.8 us
    pallas_call x7, Pallas kernels, pair_terms(): pl.pallas_call(functools.partial(pair_kernel, offset, slot, len(far), len...  19.1 us
    ppermute x3, starting transfers between devices, from_ahead(): return lax.ppermute(value, axis, pairs)  6.99 us
    ppermute x3, waiting for transfers between devices, from_ahead(): return lax.ppermute(value, axis, pairs)  4.21 us
    ppermute x3, starting transfers between devices, flipped(): return lax.ppermute(value, ('wide', 'narrow'), pairs)  3.55 us
    ppermute x2, starting transfers between devices, gathered_rows(): first = lax.ppermute(mine, 'narrow', half_turn)  3.11 us
    pallas_call x3, Pallas kernels, fit(): pl.pallas_call(functools.partial(fit_kernel, len(metric), len(sources[0])...  2.5 us
  transfers between devices with their start and end apart: 27, of which 11 were waited for; matrix products, arithmetic and copies ran while one was open for 2% of the time, Pallas kernels for 22%

profile of v8, /device:TPU:0, one launch (start us, length us, event | category | flops | bytes accessed | tf_op | source)
XLA Modules:
  0.0 98.1 jit_solution(5109723549913439547)
XLA Ops:
  0.7 0.9 copy-done
  1.6 4.1 %collective-permute-start = (bf16[80,320]{1,0:T(8,128)(2,1)S(1)}, bf16[80,320]{1,0:T(8,128)(2,1)S(1)}, u32[]{:S(2)}, u32[]{:S(2)}) collective-permute-start(bf16[80,320]{1,0:T(8,128)(2,1)S(1)} %constant_dynamic-slice_fusion), channel_id=1, source_target_pairs={{0,16},{4,20},{8,24},{12,28},{16,0},{20,4},{24,8},{28,12},{1,17},{... | collective-permute-start | bytes 153608 | tf_op jit(solution)/shard_map/ppermute | solution.py:18
  5.7 1.2 %copy-done.1 = bf16[1,80,8,2,384]{4,3,2,1,0:T(2,128)(2,1)S(1)} copy-done((bf16[1,80,8,2,384]{4,3,2,1,0:T(2,128)(2,1)S(1)}, bf16[1,80,8,2,384]{4,3,2,1,0:T(2,128)(2,1)}, u32[]{:S(2)}) %copy-start.1) | copy-done | bytes 983064
  6.9 1.1 %shard_map.77 = (bf16[2,80,384]{2,1,0:T(8,128)(2,1)S(1)}, bf16[2,80,384]{2,1,0:T(8,128)(2,1)S(1)}, bf16[2,80,384]{2,1,0:T(8,128)(2,1)S(1)}, bf16[2,80,384]{2,1,0:T(8,128)(2,1)S(1)}) custom-call(bf16[80,8,2,384]{3,2,1,0:T(2,128)(2,1)S(1)} %bitcast.43), custom_call_target="tpu_custom_call" | custom-call | bytes 2949120 | tf_op jit(solution)/shard_map/pallas_call | solution.py:287
  8.1 1.9 %collective-permute-start.5 = (bf16[2,80,384]{2,1,0:T(8,128)(2,1)S(1)}, bf16[2,80,384]{2,1,0:T(8,128)(2,1)S(1)}, u32[]{:S(2)}, u32[]{:S(2)}) collective-permute-start(bf16[2,80,384]{2,1,0:T(8,128)(2,1)S(1)} %get-tuple-element.42), channel_id=1, source_target_pairs={{0,8},{4,12},{8,0},{12,4},{16,24},{20,28},{24,16},{28,20},{1,9},{5... | collective-permute-start | bytes 368648 | tf_op jit(solution)/shard_map/ppermute | solution.py:18
  10.0 2.5 %collective-permute-start.6 = (bf16[2,80,384]{2,1,0:T(8,128)(2,1)S(1)}, bf16[2,80,384]{2,1,0:T(8,128)(2,1)S(1)}, u32[]{:S(2)}, u32[]{:S(2)}) collective-permute-start(bf16[2,80,384]{2,1,0:T(8,128)(2,1)S(1)} %get-tuple-element.43), channel_id=1, source_target_pairs={{0,24},{4,28},{8,16},{12,20},{16,8},{20,12},{24,0},{28,4},{1,25},{... | collective-permute-start | bytes 368648 | tf_op jit(solution)/shard_map/ppermute | solution.py:18
  12.6 0.7 collective-permute-start.1
  13.3 1.1 %shard_map.79 = (bf16[4,80,384]{2,1,0:T(8,128)(2,1)S(1)}, bf16[4,80,384]{2,1,0:T(8,128)(2,1)S(1)}) custom-call(bf16[80,8,2,384]{3,2,1,0:T(2,128)(2,1)S(1)} %bitcast.44), custom_call_target="tpu_custom_call" | custom-call | bytes 2949120 | tf_op jit(solution)/shard_map/pallas_call | solution.py:287
  14.4 1.4 %collective-permute-start.10 = (bf16[4,80,384]{2,1,0:T(8,128)(2,1)S(1)}, bf16[4,80,384]{2,1,0:T(8,128)(2,1)S(1)}, u32[]{:S(2)}, u32[]{:S(2)}) collective-permute-start(bf16[4,80,384]{2,1,0:T(8,128)(2,1)S(1)} %get-tuple-element.47), channel_id=1, source_target_pairs={{0,8},{4,12},{8,0},{12,4},{16,24},{20,28},{24,16},{28,20},{1,9},{5... | collective-permute-start | bytes 737288 | tf_op jit(solution)/shard_map/ppermute | solution.py:18
  15.9 3.0 %collective-permute-done.4 = bf16[2,80,384]{2,1,0:T(8,128)(2,1)S(1)} collective-permute-done((bf16[2,80,384]{2,1,0:T(8,128)(2,1)S(1)}, bf16[2,80,384]{2,1,0:T(8,128)(2,1)S(1)}, u32[]{:S(2)}, u32[]{:S(2)}) %collective-permute-start.4) | collective-permute-done | bytes 122912 | tf_op jit(solution)/shard_map/ppermute | solution.py:18
  19.0 2.6 %collective-permute-done.6 = bf16[2,80,384]{2,1,0:T(8,128)(2,1)S(1)} collective-permute-done((bf16[2,80,384]{2,1,0:T(8,128)(2,1)S(1)}, bf16[2,80,384]{2,1,0:T(8,128)(2,1)S(1)}, u32[]{:S(2)}, u32[]{:S(2)}) %collective-permute-start.6) | collective-permute-done | bytes 122912 | tf_op jit(solution)/shard_map/ppermute | solution.py:18
  21.6 1.6 %collective-permute-start.7 = (bf16[320,384]{1,0:T(8,128)(2,1)S(1)}, bf16[320,384]{1,0:T(8,128)(2,1)S(1)}, u32[]{:S(2)}, u32[]{:S(2)}) collective-permute-start(bf16[320,384]{1,0:T(8,128)(2,1)S(1)} %pad_maximum_fusion.3), channel_id=1, source_target_pairs={{0,4},{4,0},{8,12},{12,8},{16,20},{20,16},{24,28},{28,24},{1,5},{5... | collective-permute-start | bytes 737288 | tf_op jit(solution)/shard_map/ppermute | solution.py:18
  23.8 2.3 %collective-permute-done.10 = bf16[4,80,384]{2,1,0:T(8,128)(2,1)S(1)} collective-permute-done((bf16[4,80,384]{2,1,0:T(8,128)(2,1)S(1)}, bf16[4,80,384]{2,1,0:T(8,128)(2,1)S(1)}, u32[]{:S(2)}, u32[]{:S(2)}) %collective-permute-start.10) | collective-permute-done | bytes 245792 | tf_op jit(solution)/shard_map/ppermute | solution.py:18
  26.2 2.9 %collective-permute-done.7.refs_3_ = bf16[320,384]{1,0:T(8,128)(2,1)S(1)} collective-permute-done((bf16[320,384]{1,0:T(8,128)(2,1)S(1)}, bf16[320,384]{1,0:T(8,128)(2,1)S(1)}, u32[]{:S(2)}, u32[]{:S(2)}) %collective-permute-start.7) | collective-permute-done | bytes 245792 | tf_op jit(solution)/shard_map/ppermute | solution.py:18
  29.2 2.1 %collective-permute-start.11 = (bf16[4,80,384]{2,1,0:T(8,128)(2,1)S(1)}, bf16[4,80,384]{2,1,0:T(8,128)(2,1)S(1)}, u32[]{:S(2)}, u32[]{:S(2)}) collective-permute-start(bf16[4,80,384]{2,1,0:T(8,128)(2,1)S(1)} %pad_maximum_fusion.4), channel_id=1, source_target_pairs={{0,16},{4,20},{8,24},{12,28},{16,0},{20,4},{24,8},{28,12},{1,17},{... | collective-permute-start | bytes 737288 | tf_op jit(solution)/shard_map/ppermute | solution.py:18
  31.3 1.6 %collective-permute-start.8 = (bf16[320,384]{1,0:T(8,128)(2,1)S(1)}, bf16[320,384]{1,0:T(8,128)(2,1)S(1)}, u32[]{:S(2)}, u32[]{:S(2)}) collective-permute-start(bf16[320,384]{1,0:T(8,128)(2,1)S(1)} %pad_maximum_fusion.2.refs_2_), channel_id=1, source_target_pairs={{0,2},{1,3},{2,0},{3,1},{4,6},{5,7},{6,4},{7,5},{8,10},{9,11},{10,... | collective-permute-start | bytes 737288 | tf_op jit(solution)/shard_map/ppermute | solution.py:344
  33.6 7.0 %collective-permute-done.11 = bf16[4,80,384]{2,1,0:T(8,128)(2,1)S(1)} collective-permute-done((bf16[4,80,384]{2,1,0:T(8,128)(2,1)S(1)}, bf16[4,80,384]{2,1,0:T(8,128)(2,1)S(1)}, u32[]{:S(2)}, u32[]{:S(2)}) %collective-permute-start.11) | collective-permute-done | bytes 245792 | tf_op jit(solution)/shard_map/ppermute | solution.py:18
  40.6 1.5 %collective-permute-start.12 = (bf16[320,384]{1,0:T(8,128)(2,1)S(1)}, bf16[320,384]{1,0:T(8,128)(2,1)S(1)}, u32[]{:S(2)}, u32[]{:S(2)}) collective-permute-start(bf16[320,384]{1,0:T(8,128)(2,1)S(1)} %pad_maximum_fusion.6), channel_id=1, source_target_pairs={{0,4},{4,0},{8,12},{12,8},{16,20},{20,16},{24,28},{28,24},{1,5},{5... | collective-permute-start | bytes 737288 | tf_op jit(solution)/shard_map/ppermute | solution.py:18
  42.4 1.6 %collective-permute-start.13 = (bf16[320,384]{1,0:T(8,128)(2,1)S(1)}, bf16[320,384]{1,0:T(8,128)(2,1)S(1)}, u32[]{:S(2)}, u32[]{:S(2)}) collective-permute-start(bf16[320,384]{1,0:T(8,128)(2,1)S(1)} %pad_maximum_fusion.5.refs_2_), channel_id=1, source_target_pairs={{0,2},{1,3},{2,0},{3,1},{4,6},{5,7},{6,4},{7,5},{8,10},{9,11},{10,... | collective-permute-start | bytes 737288 | tf_op jit(solution)/shard_map/ppermute | solution.py:344
  44.0 1.1 %shard_map.78 = (bf16[640,384]{1,0:T(8,128)(2,1)S(1)}, bf16[640,384]{1,0:T(8,128)(2,1)S(1)}) custom-call(bf16[640,320]{1,0:T(8,128)(2,1)S(1)} %pad_maximum_fusion.refs_0_, bf16[640,320]{1,0:T(8,128)(2,1)S(1)} %collective-permute-done.3.refs_1_, bf16[320,384]{1,0:T(8,128)(2,1)S(1)} %pad_maximum_fusion.2.refs_2_, ...), custom_call_target="tpu_custom_call" | custom-call | flops 629145600 | bytes 2785280 | tf_op jit(solution)/shard_map/pallas_call | solution.py:75
  45.1 2.7 %collective-permute-start.17 = (bf16[640,384]{1,0:T(8,128)(2,1)S(1)}, bf16[640,384]{1,0:T(8,128)(2,1)S(1)}, u32[]{:S(2)}, u32[]{:S(2)}) collective-permute-start(bf16[640,384]{1,0:T(8,128)(2,1)S(1)} %get-tuple-element.56.refs_7_.odd_ref), channel_id=1, source_target_pairs={{0,24},{4,28},{8,0},{12,4},{16,8},{20,12},{24,16},{28,20},{1,25},{... | collective-permute-start | bytes 1474568 | tf_op jit(solution)/shard_map/ppermute | solution.py:24
  47.8 1.1 %collective-permute-start.14 = (bf16[320,384]{1,0:T(8,128)(2,1)S(1)}, bf16[320,384]{1,0:T(8,128)(2,1)S(1)}, u32[]{:S(2)}, u32[]{:S(2)}) collective-permute-start(bf16[320,384]{1,0:T(8,128)(2,1)S(1)} %collective-permute-done.12.refs_3_), channel_id=1, source_target_pairs={{0,2},{1,3},{2,0},{3,1},{4,6},{5,7},{6,4},{7,5},{8,10},{9,11},{10,... | collective-permute-start | bytes 737288 | tf_op jit(solution)/shard_map/ppermute | solution.py:347
  48.9 0.7 shard_map.80.refs_6_
  49.6 2.9 %shard_map.81 = (f32[384,384]{1,0:T(8,128)S(1)}, f32[640,768]{1,0:T(8,128)S(1)}) custom-call(f32[8,2]{1,0:T(8,128)S(1)} %copy.14.refs_0_, s32[4,8]{1,0:T(4,128)S(1)} %copy-done.3, s32[4,8]{1,0:T(4,128)S(1)} %copy-done.4, f32[4,384]{1,0:T(4,128)S(1)} %copy-done.2, f32[384,4]{1,0:T(8,128)S(1)} %bitcast.36, bf16[640,384]{1,0:T(8,128)(2,1)S(1)} %get-tuple-element.44.refs_5_, ...), custom_call_target="tpu_custom_call" | custom-call | flops 7851737088 | bytes 52690944 | tf_op jit(solution)/shard_map/pallas_call | solution.py:197
  52.5 4.2 %collective-permute-done.17.even_ref.refs_7_ = bf16[640,384]{1,0:T(8,128)(2,1)S(1)} collective-permute-done((bf16[640,384]{1,0:T(8,128)(2,1)S(1)}, bf16[640,384]{1,0:T(8,128)(2,1)S(1)}, u32[]{:S(2)}, u32[]{:S(2)}) %collective-permute-start.17) | collective-permute-done | bytes 491552 | tf_op jit(solution)/shard_map/ppermute | solution.py:24
  56.8 0.6 collective-permute-start.20
  57.4 0.7 shard_map.82
  58.1 4.0 %collective-permute-start.15 = (bf16[320,384]{1,0:T(8,128)(2,1)S(1)}, bf16[320,384]{1,0:T(8,128)(2,1)S(1)}, u32[]{:S(2)}, u32[]{:S(2)}) collective-permute-start(bf16[320,384]{1,0:T(8,128)(2,1)S(1)} %get-tuple-element.54.odd_ref.refs_7_), channel_id=1, source_target_pairs={{0,24},{4,28},{8,0},{12,4},{16,8},{20,12},{24,16},{28,20},{1,25},{... | collective-permute-start | bytes 737288 | tf_op jit(solution)/shard_map/ppermute | solution.py:24
  62.4 2.9 %shard_map.85 = (f32[384,384]{1,0:T(8,128)S(1)}, f32[640,768]{1,0:T(8,128)S(1)}) custom-call(f32[8,2]{1,0:T(8,128)S(1)} %copy.14.refs_0_, s32[4,8]{1,0:T(4,128)S(1)} %copy-done.3, s32[4,8]{1,0:T(4,128)S(1)} %copy-done.4, f32[4,384]{1,0:T(4,128)S(1)} %copy-done.2, f32[384,4]{1,0:T(8,128)S(1)} %bitcast.37, bf16[640,384]{1,0:T(8,128)(2,1)S(1)} %get-tuple-element.44.refs_5_, ...), custom_call_target="tpu_custom_call" | custom-call | flops 981467136 | bytes 6586368 | tf_op jit(solution)/shard_map/pallas_call | solution.py:197
  65.4 2.9 %shard_map.87 = (f32[384,384]{1,0:T(8,128)S(1)}, f32[640,768]{1,0:T(8,128)S(1)}) custom-call(f32[8,2]{1,0:T(8,128)S(1)} %copy.14.refs_0_, s32[4,8]{1,0:T(4,128)S(1)} %copy-done.3, s32[4,8]{1,0:T(4,128)S(1)} %copy-done.4, f32[4,384]{1,0:T(4,128)S(1)} %copy-done.2, f32[384,4]{1,0:T(8,128)S(1)} %bitcast.38, bf16[640,384]{1,0:T(8,128)(2,1)S(1)} %get-tuple-element.44.refs_5_, ...), custom_call_target="tpu_custom_call" | custom-call | flops 981467136 | bytes 6586368 | tf_op jit(solution)/shard_map/pallas_call | solution.py:197
  68.3 1.5 %collective-permute-start.16 = (bf16[320,384]{1,0:T(8,128)(2,1)S(1)}, bf16[320,384]{1,0:T(8,128)(2,1)S(1)}, u32[]{:S(2)}, u32[]{:S(2)}) collective-permute-start(bf16[320,384]{1,0:T(8,128)(2,1)S(1)} %shard_map.83), channel_id=1, source_target_pairs={{0,4},{4,0},{8,12},{12,8},{16,20},{20,16},{24,28},{28,24},{1,5},{5... | collective-permute-start | bytes 737288 | tf_op jit(solution)/shard_map/ppermute | solution.py:18
  69.9 1.3 %collective-permute-start.19 = (bf16[320,384]{1,0:T(8,128)(2,1)S(1)}, bf16[320,384]{1,0:T(8,128)(2,1)S(1)}, u32[]{:S(2)}, u32[]{:S(2)}) collective-permute-start(bf16[320,384]{1,0:T(8,128)(2,1)S(1)} %shard_map.86), channel_id=1, source_target_pairs={{0,4},{4,0},{8,12},{12,8},{16,20},{20,16},{24,28},{28,24},{1,5},{5... | collective-permute-start | bytes 737288 | tf_op jit(solution)/shard_map/ppermute | solution.py:18
  71.1 2.9 %shard_map.88 = (f32[384,384]{1,0:T(8,128)S(1)}, f32[640,768]{1,0:T(8,128)S(1)}) custom-call(f32[8,2]{1,0:T(8,128)S(1)} %copy.14.refs_0_, s32[4,8]{1,0:T(4,128)S(1)} %copy-done.3, s32[4,8]{1,0:T(4,128)S(1)} %copy-done.4, f32[4,384]{1,0:T(4,128)S(1)} %copy-done.2, f32[384,4]{1,0:T(8,128)S(1)} %bitcast.39, bf16[640,384]{1,0:T(8,128)(2,1)S(1)} %get-tuple-element.44.refs_5_, ...), custom_call_target="tpu_custom_call" | custom-call | flops 981467136 | bytes 6586368 | tf_op jit(solution)/shard_map/pallas_call | solution.py:197
  74.1 2.9 %shard_map.89 = (f32[384,384]{1,0:T(8,128)S(1)}, f32[640,768]{1,0:T(8,128)S(1)}) custom-call(f32[8,2]{1,0:T(8,128)S(1)} %copy.14.refs_0_, s32[4,8]{1,0:T(4,128)S(1)} %copy-done.3, s32[4,8]{1,0:T(4,128)S(1)} %copy-done.4, f32[4,384]{1,0:T(4,128)S(1)} %copy-done.2, f32[384,4]{1,0:T(8,128)S(1)} %bitcast.40, bf16[640,384]{1,0:T(8,128)(2,1)S(1)} %get-tuple-element.44.refs_5_, ...), custom_call_target="tpu_custom_call" | custom-call | flops 2944401408 | bytes 19759104 | tf_op jit(solution)/shard_map/pallas_call | solution.py:197
  77.0 1.5 %collective-permute-done.19.refs_8_ = bf16[320,384]{1,0:T(8,128)(2,1)S(1)} collective-permute-done((bf16[320,384]{1,0:T(8,128)(2,1)S(1)}, bf16[320,384]{1,0:T(8,128)(2,1)S(1)}, u32[]{:S(2)}, u32[]{:S(2)}) %collective-permute-start.19) | collective-permute-done | bytes 245792 | tf_op jit(solution)/shard_map/ppermute | solution.py:18
  78.5 2.0 %shard_map.91 = (bf16[192,384]{1,0:T(8,128)(2,1)S(1)}, f32[192,384]{1,0:T(8,128)S(1)}) custom-call(f32[8,2]{1,0:T(8,128)S(1)} %copy.14.refs_0_, s32[4,8]{1,0:T(4,128)S(1)} %copy-done.3, s32[4,8]{1,0:T(4,128)S(1)} %copy-done.4, f32[4,384]{1,0:T(4,128)S(1)} %copy-done.2, f32[384,4]{1,0:T(8,128)S(1)} %bitcast.41, ...), custom_call_target="tpu_custom_call" | custom-call | flops 981467136 | bytes 6586368 | tf_op jit(solution)/shard_map/pallas_call | solution.py:197
  80.6 1.4 %collective-permute-done.21.refs_0_ = bf16[192,384]{1,0:T(8,128)(2,1)S(1)} collective-permute-done((bf16[192,384]{1,0:T(8,128)(2,1)S(1)}, bf16[192,384]{1,0:T(8,128)(2,1)S(1)}, u32[]{:S(2)}, u32[]{:S(2)}) %collective-permute-start.21) | collective-permute-done | bytes 147488 | tf_op jit(solution)/shard_map/ppermute | solution.py:18
  82.0 1.0 %collective-permute-start.22 = (bf16[48,384]{1,0:T(8,128)(2,1)S(1)}, bf16[48,384]{1,0:T(8,128)(2,1)S(1)}, u32[]{:S(2)}, u32[]{:S(2)}) collective-permute-start(bf16[48,384]{1,0:T(8,128)(2,1)S(1)} %get-tuple-element.69), channel_id=1, source_target_pairs={{0,4},{1,5},{2,6},{3,7},{4,0},{5,1},{6,2},{7,3},{8,12},{9,13},{10,... | collective-permute-start | bytes 110600 | tf_op jit(solution)/shard_map/ppermute | solution.py:232
  83.0 1.0 %collective-permute-start.23 = (bf16[48,384]{1,0:T(8,128)(2,1)S(1)}, bf16[48,384]{1,0:T(8,128)(2,1)S(1)}, u32[]{:S(2)}, u32[]{:S(2)}) collective-permute-start(bf16[48,384]{1,0:T(8,128)(2,1)S(1)} %get-tuple-element.70), channel_id=1, source_target_pairs={{0,2},{1,3},{2,0},{3,1},{4,6},{5,7},{6,4},{7,5},{8,10},{9,11},{10,... | collective-permute-start | bytes 110600 | tf_op jit(solution)/shard_map/ppermute | solution.py:232
  84.1 1.5 %collective-permute-start.24 = (bf16[48,384]{1,0:T(8,128)(2,1)S(1)}, bf16[48,384]{1,0:T(8,128)(2,1)S(1)}, u32[]{:S(2)}, u32[]{:S(2)}) collective-permute-start(bf16[48,384]{1,0:T(8,128)(2,1)S(1)} %get-tuple-element.71), channel_id=1, source_target_pairs={{0,6},{1,7},{2,4},{3,5},{4,2},{5,3},{6,0},{7,1},{8,14},{9,15},{10,... | collective-permute-start | bytes 110600 | tf_op jit(solution)/shard_map/ppermute | solution.py:232
  85.6 2.5 %shard_map.90 = bf16[640,768]{1,0:T(8,128)(2,1)S(1)} custom-call(f32[8,2]{1,0:T(8,128)S(1)} %copy.14.refs_0_, s32[4,8]{1,0:T(4,128)S(1)} %copy-done.3, s32[4,8]{1,0:T(4,128)S(1)} %copy-done.4, f32[4,384]{1,0:T(4,128)S(1)} %copy-done.2, f32[384,4]{1,0:T(8,128)S(1)} %bitcast.42, bf16[640,384]{1,0:T(8,128)(2,1)S(1)} %get-tuple-element.44.refs_5_, ...), custom_call_target="tpu_custom_call" | custom-call | flops 981467136 | bytes 6586368 | tf_op jit(solution)/shard_map/pallas_call | solution.py:197
  88.1 0.8 collective-permute-done.24.refs_2_
  89.0 1.1 %collective-permute-start.25 = (bf16[24,384]{1,0:T(8,128)(2,1)S(1)}, bf16[24,384]{1,0:T(8,128)(2,1)S(1)}, u32[]{:S(2)}, u32[]{:S(2)}) collective-permute-start(bf16[24,384]{1,0:T(8,128)(2,1)S(1)} %get-tuple-element.74), channel_id=1, source_target_pairs={{0,8},{4,12},{8,0},{12,4},{16,24},{20,28},{24,16},{28,20},{1,9},{5... | collective-permute-start | bytes 55304 | tf_op jit(solution)/shard_map/ppermute | solution.py:18
  90.1 2.7 %collective-permute-done.25.refs_0_ = bf16[24,384]{1,0:T(8,128)(2,1)S(1)} collective-permute-done((bf16[24,384]{1,0:T(8,128)(2,1)S(1)}, bf16[24,384]{1,0:T(8,128)(2,1)S(1)}, u32[]{:S(2)}, u32[]{:S(2)}) %collective-permute-start.25) | collective-permute-done | bytes 18464 | tf_op jit(solution)/shard_map/ppermute | solution.py:18
  92.8 2.7 %collective-permute-start.26 = (bf16[12,384]{1,0:T(8,128)(2,1)S(1)}, bf16[12,384]{1,0:T(8,128)(2,1)S(1)}, u32[]{:S(2)}, u32[]{:S(2)}) collective-permute-start(bf16[12,384]{1,0:T(8,128)(2,1)S(1)} %get-tuple-element.76), channel_id=1, source_target_pairs={{0,16},{4,20},{8,24},{12,28},{16,0},{20,4},{24,8},{28,12},{1,17},{... | collective-permute-start | bytes 27656 | tf_op jit(solution)/shard_map/ppermute | solution.py:18
  95.6 1.2 %reshape.10 = bf16[1,640,1,2,384]{4,3,1,2,0:T(2,128)(2,1)} reshape(bf16[640,768]{1,0:T(8,128)(2,1)S(1)} %shard_map.90) | data formatting | bytes 1966080 | tf_op jit(solution)/shard_map/reshape | solution.py:431
  96.7 0.7 collective-permute-done.26.refs_0_
  97.5 0.6 shard_map.95
  (56 shorter events, 2.6 us)
Async XLA Ops:
  0.6 0.9 copy-start
  1.6 10.9 %collective-permute-start = (bf16[80,320]{1,0:T(8,128)(2,1)S(1)}, bf16[80,320]{1,0:T(8,128)(2,1)S(1)}, u32[]{:S(2)}, u32[]{:S(2)}) collective-permute-start(bf16[80,320]{1,0:T(8,128)(2,1)S(1)} %constant_dynamic-slice_fusion), channel_id=1, source_target_pairs={{0,16},{4,20},{8,24},{12,28},{16,0},{20,4},{24,8},{28,12},{1,17},{... | collective-permute-start | bytes 153608 | tf_op jit(solution)/shard_map/ppermute | solution.py:18
  5.7 1.2 %copy-start.1 = (bf16[1,80,8,2,384]{4,3,2,1,0:T(2,128)(2,1)S(1)}, bf16[1,80,8,2,384]{4,3,2,1,0:T(2,128)(2,1)}, u32[]{:S(2)}) copy-start(bf16[1,80,8,2,384]{4,3,2,1,0:T(2,128)(2,1)} %param.6) | copy-start | bytes 2949124
  8.1 10.9 %collective-permute-start.4 = (bf16[2,80,384]{2,1,0:T(8,128)(2,1)S(1)}, bf16[2,80,384]{2,1,0:T(8,128)(2,1)S(1)}, u32[]{:S(2)}, u32[]{:S(2)}) collective-permute-start(bf16[2,80,384]{2,1,0:T(8,128)(2,1)S(1)} %get-tuple-element.41), channel_id=1, source_target_pairs={{0,16},{4,20},{8,24},{12,28},{16,0},{20,4},{24,8},{28,12},{1,17},{... | collective-permute-start | bytes 368648 | tf_op jit(solution)/shard_map/ppermute | solution.py:18
  8.1 10.8 %collective-permute-start.5 = (bf16[2,80,384]{2,1,0:T(8,128)(2,1)S(1)}, bf16[2,80,384]{2,1,0:T(8,128)(2,1)S(1)}, u32[]{:S(2)}, u32[]{:S(2)}) collective-permute-start(bf16[2,80,384]{2,1,0:T(8,128)(2,1)S(1)} %get-tuple-element.42), channel_id=1, source_target_pairs={{0,8},{4,12},{8,0},{12,4},{16,24},{20,28},{24,16},{28,20},{1,9},{5... | collective-permute-start | bytes 368648 | tf_op jit(solution)/shard_map/ppermute | solution.py:18
  10.0 11.5 %collective-permute-start.6 = (bf16[2,80,384]{2,1,0:T(8,128)(2,1)S(1)}, bf16[2,80,384]{2,1,0:T(8,128)(2,1)S(1)}, u32[]{:S(2)}, u32[]{:S(2)}) collective-permute-start(bf16[2,80,384]{2,1,0:T(8,128)(2,1)S(1)} %get-tuple-element.43), channel_id=1, source_target_pairs={{0,24},{4,28},{8,16},{12,20},{16,8},{20,12},{24,0},{28,4},{1,25},{... | collective-permute-start | bytes 368648 | tf_op jit(solution)/shard_map/ppermute | solution.py:18
  12.6 10.7 %collective-permute-start.1 = (bf16[160,320]{1,0:T(8,128)(2,1)S(1)}, bf16[160,320]{1,0:T(8,128)(2,1)S(1)}, u32[]{:S(2)}, u32[]{:S(2)}) collective-permute-start(bf16[160,320]{1,0:T(8,128)(2,1)S(1)} %pad_maximum_fusion.7), channel_id=1, source_target_pairs={{0,8},{4,12},{8,0},{12,4},{16,24},{20,28},{24,16},{28,20},{1,9},{5... | collective-permute-start | bytes 307208 | tf_op jit(solution)/shard_map/ppermute | solution.py:18
  14.4 11.7 %collective-permute-start.10 = (bf16[4,80,384]{2,1,0:T(8,128)(2,1)S(1)}, bf16[4,80,384]{2,1,0:T(8,128)(2,1)S(1)}, u32[]{:S(2)}, u32[]{:S(2)}) collective-permute-start(bf16[4,80,384]{2,1,0:T(8,128)(2,1)S(1)} %get-tuple-element.47), channel_id=1, source_target_pairs={{0,8},{4,12},{8,0},{12,4},{16,24},{20,28},{24,16},{28,20},{1,9},{5... | collective-permute-start | bytes 737288 | tf_op jit(solution)/shard_map/ppermute | solution.py:18
  21.6 20.5 %copy-start.5 = (f32[8,2]{0,1:T(2,128)S(1)}, f32[8,2]{0,1:T(2,128)}, u32[]{:S(2)}) copy-start(f32[8,2]{0,1:T(2,128)} %param.8) | copy-start | bytes 196
  21.6 20.6 %copy-start.2 = (f32[4,384]{1,0:T(4,128)S(1)}, f32[4,384]{1,0:T(4,128)}, u32[]{:S(2)}) copy-start(f32[4,384]{1,0:T(4,128)} %refs_3_.13) | copy-start | bytes 18436
  21.6 7.5 %collective-permute-start.7 = (bf16[320,384]{1,0:T(8,128)(2,1)S(1)}, bf16[320,384]{1,0:T(8,128)(2,1)S(1)}, u32[]{:S(2)}, u32[]{:S(2)}) collective-permute-start(bf16[320,384]{1,0:T(8,128)(2,1)S(1)} %pad_maximum_fusion.3), channel_id=1, source_target_pairs={{0,4},{4,0},{8,12},{12,8},{16,20},{20,16},{24,28},{28,24},{1,5},{5... | collective-permute-start | bytes 737288 | tf_op jit(solution)/shard_map/ppermute | solution.py:18
  23.2 9.6 %collective-permute-start.2 = (bf16[320,320]{1,0:T(8,128)(2,1)S(1)}, bf16[320,320]{1,0:T(8,128)(2,1)S(1)}, u32[]{:S(2)}, u32[]{:S(2)}) collective-permute-start(bf16[320,320]{1,0:T(8,128)(2,1)S(1)} %pad_maximum_fusion.1), channel_id=1, source_target_pairs={{0,4},{4,0},{8,12},{12,8},{16,20},{20,16},{24,28},{28,24},{1,5},{5... | collective-permute-start | bytes 614408 | tf_op jit(solution)/shard_map/ppermute | solution.py:18
  29.2 11.4 %collective-permute-start.11 = (bf16[4,80,384]{2,1,0:T(8,128)(2,1)S(1)}, bf16[4,80,384]{2,1,0:T(8,128)(2,1)S(1)}, u32[]{:S(2)}, u32[]{:S(2)}) collective-permute-start(bf16[4,80,384]{2,1,0:T(8,128)(2,1)S(1)} %pad_maximum_fusion.4), channel_id=1, source_target_pairs={{0,16},{4,20},{8,24},{12,28},{16,0},{20,4},{24,8},{28,12},{1,17},{... | collective-permute-start | bytes 737288 | tf_op jit(solution)/shard_map/ppermute | solution.py:18
  31.3 12.7 %collective-permute-start.8 = (bf16[320,384]{1,0:T(8,128)(2,1)S(1)}, bf16[320,384]{1,0:T(8,128)(2,1)S(1)}, u32[]{:S(2)}, u32[]{:S(2)}) collective-permute-start(bf16[320,384]{1,0:T(8,128)(2,1)S(1)} %pad_maximum_fusion.2.refs_2_), channel_id=1, source_target_pairs={{0,2},{1,3},{2,0},{3,1},{4,6},{5,7},{6,4},{7,5},{8,10},{9,11},{10,... | collective-permute-start | bytes 737288 | tf_op jit(solution)/shard_map/ppermute | solution.py:344
  32.9 11.1 %collective-permute-start.3 = (bf16[640,320]{1,0:T(8,128)(2,1)S(1)}, bf16[640,320]{1,0:T(8,128)(2,1)S(1)}, u32[]{:S(2)}, u32[]{:S(2)}) collective-permute-start(bf16[640,320]{1,0:T(8,128)(2,1)S(1)} %pad_maximum_fusion.refs_0_), channel_id=1, source_target_pairs={{0,1},{1,0},{2,3},{3,2},{4,5},{5,4},{6,7},{7,6},{8,9},{9,8},{10,11... | collective-permute-start | bytes 1228808 | tf_op jit(solution)/shard_map/ppermute | solution.py:18
  32.9 11.0 %collective-permute-start.9 = (bf16[320,384]{1,0:T(8,128)(2,1)S(1)}, bf16[320,384]{1,0:T(8,128)(2,1)S(1)}, u32[]{:S(2)}, u32[]{:S(2)}) collective-permute-start(bf16[320,384]{1,0:T(8,128)(2,1)S(1)} %collective-permute-done.7.refs_3_), channel_id=1, source_target_pairs={{0,2},{1,3},{2,0},{3,1},{4,6},{5,7},{6,4},{7,5},{8,10},{9,11},{10,... | collective-permute-start | bytes 737288 | tf_op jit(solution)/shard_map/ppermute | solution.py:347
  40.6 7.2 %collective-permute-start.12 = (bf16[320,384]{1,0:T(8,128)(2,1)S(1)}, bf16[320,384]{1,0:T(8,128)(2,1)S(1)}, u32[]{:S(2)}, u32[]{:S(2)}) collective-permute-start(bf16[320,384]{1,0:T(8,128)(2,1)S(1)} %pad_maximum_fusion.6), channel_id=1, source_target_pairs={{0,4},{4,0},{8,12},{12,8},{16,20},{20,16},{24,28},{28,24},{1,5},{5... | collective-permute-start | bytes 737288 | tf_op jit(solution)/shard_map/ppermute | solution.py:18
  42.4 7.2 %copy-start.3 = (s32[4,8]{1,0:T(4,128)S(1)}, s32[4,8]{1,0:T(4,128)}, u32[]{:S(2)}) copy-start(s32[4,8]{1,0:T(4,128)} %refs_1_.13) | copy-start | bytes 388
  42.4 7.2 %copy-start.4 = (s32[4,8]{1,0:T(4,128)S(1)}, s32[4,8]{1,0:T(4,128)}, u32[]{:S(2)}) copy-start(s32[4,8]{1,0:T(4,128)} %refs_2_.13) | copy-start | bytes 388
  42.4 15.0 %collective-permute-start.13 = (bf16[320,384]{1,0:T(8,128)(2,1)S(1)}, bf16[320,384]{1,0:T(8,128)(2,1)S(1)}, u32[]{:S(2)}, u32[]{:S(2)}) collective-permute-start(bf16[320,384]{1,0:T(8,128)(2,1)S(1)} %pad_maximum_fusion.5.refs_2_), channel_id=1, source_target_pairs={{0,2},{1,3},{2,0},{3,1},{4,6},{5,7},{6,4},{7,5},{8,10},{9,11},{10,... | collective-permute-start | bytes 737288 | tf_op jit(solution)/shard_map/ppermute | solution.py:344
  45.1 11.6 %collective-permute-start.17 = (bf16[640,384]{1,0:T(8,128)(2,1)S(1)}, bf16[640,384]{1,0:T(8,128)(2,1)S(1)}, u32[]{:S(2)}, u32[]{:S(2)}) collective-permute-start(bf16[640,384]{1,0:T(8,128)(2,1)S(1)} %get-tuple-element.56.refs_7_.odd_ref), channel_id=1, source_target_pairs={{0,24},{4,28},{8,0},{12,4},{16,8},{20,12},{24,16},{28,20},{1,25},{... | collective-permute-start | bytes 1474568 | tf_op jit(solution)/shard_map/ppermute | solution.py:24
  47.8 9.6 %collective-permute-start.14 = (bf16[320,384]{1,0:T(8,128)(2,1)S(1)}, bf16[320,384]{1,0:T(8,128)(2,1)S(1)}, u32[]{:S(2)}, u32[]{:S(2)}) collective-permute-start(bf16[320,384]{1,0:T(8,128)(2,1)S(1)} %collective-permute-done.12.refs_3_), channel_id=1, source_target_pairs={{0,2},{1,3},{2,0},{3,1},{4,6},{5,7},{6,4},{7,5},{8,10},{9,11},{10,... | collective-permute-start | bytes 737288 | tf_op jit(solution)/shard_map/ppermute | solution.py:347
  56.8 17.3 %collective-permute-start.20 = (bf16[640,384]{1,0:T(8,128)(2,1)S(1)}, bf16[640,384]{1,0:T(8,128)(2,1)S(1)}, u32[]{:S(2)}, u32[]{:S(2)}) collective-permute-start(bf16[640,384]{1,0:T(8,128)(2,1)S(1)} %shard_map.84), channel_id=1, source_target_pairs={{0,4},{4,0},{8,12},{12,8},{16,20},{20,16},{24,28},{28,24},{1,5},{5... | collective-permute-start | bytes 1474568 | tf_op jit(solution)/shard_map/ppermute | solution.py:18
  58.1 10.2 %collective-permute-start.15 = (bf16[320,384]{1,0:T(8,128)(2,1)S(1)}, bf16[320,384]{1,0:T(8,128)(2,1)S(1)}, u32[]{:S(2)}, u32[]{:S(2)}) collective-permute-start(bf16[320,384]{1,0:T(8,128)(2,1)S(1)} %get-tuple-element.54.odd_ref.refs_7_), channel_id=1, source_target_pairs={{0,24},{4,28},{8,0},{12,4},{16,8},{20,12},{24,16},{28,20},{1,25},{... | collective-permute-start | bytes 737288 | tf_op jit(solution)/shard_map/ppermute | solution.py:24
  62.2 7.7 %collective-permute-start.18 = (bf16[320,384]{1,0:T(8,128)(2,1)S(1)}, bf16[320,384]{1,0:T(8,128)(2,1)S(1)}, u32[]{:S(2)}, u32[]{:S(2)}) collective-permute-start(bf16[320,384]{1,0:T(8,128)(2,1)S(1)} %get-tuple-element.60.refs_8_.odd_ref), channel_id=1, source_target_pairs={{0,24},{4,28},{8,0},{12,4},{16,8},{20,12},{24,16},{28,20},{1,25},{... | collective-permute-start | bytes 737288 | tf_op jit(solution)/shard_map/ppermute | solution.py:24
  68.3 8.7 %collective-permute-start.16 = (bf16[320,384]{1,0:T(8,128)(2,1)S(1)}, bf16[320,384]{1,0:T(8,128)(2,1)S(1)}, u32[]{:S(2)}, u32[]{:S(2)}) collective-permute-start(bf16[320,384]{1,0:T(8,128)(2,1)S(1)} %shard_map.83), channel_id=1, source_target_pairs={{0,4},{4,0},{8,12},{12,8},{16,20},{20,16},{24,28},{28,24},{1,5},{5... | collective-permute-start | bytes 737288 | tf_op jit(solution)/shard_map/ppermute | solution.py:18
  69.9 8.6 %collective-permute-start.19 = (bf16[320,384]{1,0:T(8,128)(2,1)S(1)}, bf16[320,384]{1,0:T(8,128)(2,1)S(1)}, u32[]{:S(2)}, u32[]{:S(2)}) collective-permute-start(bf16[320,384]{1,0:T(8,128)(2,1)S(1)} %shard_map.86), channel_id=1, source_target_pairs={{0,4},{4,0},{8,12},{12,8},{16,20},{20,16},{24,28},{28,24},{1,5},{5... | collective-permute-start | bytes 737288 | tf_op jit(solution)/shard_map/ppermute | solution.py:18
  80.5 1.4 %collective-permute-start.21 = (bf16[192,384]{1,0:T(8,128)(2,1)S(1)}, bf16[192,384]{1,0:T(8,128)(2,1)S(1)}, u32[]{:S(2)}, u32[]{:S(2)}) collective-permute-start(bf16[192,384]{1,0:T(8,128)(2,1)S(1)} %get-tuple-element.67), channel_id=1, source_target_pairs={{0,1},{1,0},{2,3},{3,2},{4,5},{5,4},{6,7},{7,6},{8,9},{9,8},{10,11... | collective-permute-start | bytes 442376 | tf_op jit(solution)/shard_map/ppermute | solution.py:18
  82.0 6.1 %collective-permute-start.22 = (bf16[48,384]{1,0:T(8,128)(2,1)S(1)}, bf16[48,384]{1,0:T(8,128)(2,1)S(1)}, u32[]{:S(2)}, u32[]{:S(2)}) collective-permute-start(bf16[48,384]{1,0:T(8,128)(2,1)S(1)} %get-tuple-element.69), channel_id=1, source_target_pairs={{0,4},{1,5},{2,6},{3,7},{4,0},{5,1},{6,2},{7,3},{8,12},{9,13},{10,... | collective-permute-start | bytes 110600 | tf_op jit(solution)/shard_map/ppermute | solution.py:232
  83.0 5.1 %collective-permute-start.23 = (bf16[48,384]{1,0:T(8,128)(2,1)S(1)}, bf16[48,384]{1,0:T(8,128)(2,1)S(1)}, u32[]{:S(2)}, u32[]{:S(2)}) collective-permute-start(bf16[48,384]{1,0:T(8,128)(2,1)S(1)} %get-tuple-element.70), channel_id=1, source_target_pairs={{0,2},{1,3},{2,0},{3,1},{4,6},{5,7},{6,4},{7,5},{8,10},{9,11},{10,... | collective-permute-start | bytes 110600 | tf_op jit(solution)/shard_map/ppermute | solution.py:232
  84.1 4.9 %collective-permute-start.24 = (bf16[48,384]{1,0:T(8,128)(2,1)S(1)}, bf16[48,384]{1,0:T(8,128)(2,1)S(1)}, u32[]{:S(2)}, u32[]{:S(2)}) collective-permute-start(bf16[48,384]{1,0:T(8,128)(2,1)S(1)} %get-tuple-element.71), channel_id=1, source_target_pairs={{0,6},{1,7},{2,4},{3,5},{4,2},{5,3},{6,0},{7,1},{8,14},{9,15},{10,... | collective-permute-start | bytes 110600 | tf_op jit(solution)/shard_map/ppermute | solution.py:232
  89.0 3.8 %collective-permute-start.25 = (bf16[24,384]{1,0:T(8,128)(2,1)S(1)}, bf16[24,384]{1,0:T(8,128)(2,1)S(1)}, u32[]{:S(2)}, u32[]{:S(2)}) collective-permute-start(bf16[24,384]{1,0:T(8,128)(2,1)S(1)} %get-tuple-element.74), channel_id=1, source_target_pairs={{0,8},{4,12},{8,0},{12,4},{16,24},{20,28},{24,16},{28,20},{1,9},{5... | collective-permute-start | bytes 55304 | tf_op jit(solution)/shard_map/ppermute | solution.py:18
  92.8 4.7 %collective-permute-start.26 = (bf16[12,384]{1,0:T(8,128)(2,1)S(1)}, bf16[12,384]{1,0:T(8,128)(2,1)S(1)}, u32[]{:S(2)}, u32[]{:S(2)}) collective-permute-start(bf16[12,384]{1,0:T(8,128)(2,1)S(1)} %get-tuple-element.76), channel_id=1, source_target_pairs={{0,16},{4,20},{8,24},{12,28},{16,0},{20,4},{24,8},{28,12},{1,17},{... | collective-permute-start | bytes 27656 | tf_op jit(solution)/shard_map/ppermute | solution.py:18
